TPU v7x, 128 devices: a whole 4x4x4 slice. The times are simulated.
128 devices in a mesh: dp: 128 (over x, z, y, core).
Axes of the slice: x: 4, y: 4, z: 4, core: 2. Of those that a mesh axis runs over, the one named last changes fastest.
Arguments:
- queries: bfloat16 [16384, 768], P('dp'), may hold values from -2 to 2
- documents: bfloat16 [16384, 768], P('dp'), may hold values from -2 to 2
- positives: int32 [16384], P('dp'), may hold values from 0 to 16383, each once
Outputs:
- loss: float32 [], replicated
- grad_queries: float32 [16384, 768], P('dp')
- grad_documents: float32 [16384, 768], P('dp')
Inputs may be any that keep to these rules, and one draw needn't show every extreme that they name: `positives`: every document is the positive of exactly one query.
All inputs are finite; a program needn't handle non-finite values.
Results may differ from a plain program's by a relative error of at most 0.0004.
The roundings to bfloat16 on the way count: a program that leaves them out, or rounds other values in their place, can miss the bound.
Values may be sent and summed in bfloat16 or wider, within the bound.
No kernel may reach another device: no remote copies, remote signals or barrier semaphores. Data moves between devices by JAX's collectives and lax.ppermute only.
A program may use at most 192 MiB of HBM per device.

v0:
```python
import functools

import jax
import jax.numpy as jnp
from jax import lax
from jax.experimental import pallas as pl
from jax.experimental.pallas import tpu as pltpu
from jax.sharding import PartitionSpec as P

PAIRS_A = ((0, 1), (2, 3))
PAIRS_B = ((0, 3), (1, 2))
CUBE = 8
CORES = 2
ROWS = 128
BLOCK = CORES * ROWS
SIDE = CUBE * BLOCK
WIDTH = 768
PAD = 16
LOSS = 8
PER = BLOCK // 128
HALF = CUBE * PER
LOG2E = 1.4426950408889634
FULL = 32760.0
NEAR = (0, 4, 2, 1)
SIDES = (6, 3)
ENDS = (5, 7)
PACKS = (NEAR, SIDES, ENDS)
ALL = NEAR + SIDES + ENDS
PARTS = (
    (NEAR, NEAR),
    (SIDES, NEAR),
    (NEAR + SIDES, SIDES),
    (ENDS, NEAR + SIDES),
    (ALL, ENDS),
)
SPAN = BLOCK + PAD
F32 = jnp.float32
BF16 = jnp.bfloat16


def device_index(x, z, y, core):
    return ((x * 4 + z) * 4 + y) * CORES + core


def partners(bits):
    moves = []
    for x in range(4):
        for z in range(4):
            for y in range(4):
                for core in range(CORES):
                    flip = (lambda v: v ^ 1) if core == 0 else (lambda v: 3 - v)
                    to = [flip(v) if bits & bit else v for v, bit in ((x, 4), (z, 2), (y, 1))]
                    moves.append((device_index(x, z, y, core), device_index(*to, core)))
    return moves


def a_cubes():
    return [
        [device_index(x, z, y, core) for x in px for z in pz for y in py]
        for core in range(CORES)
        for px in PAIRS_A
        for pz in PAIRS_A
        for py in PAIRS_A
    ]


SWAP = [(i, i ^ 1) for i in range(128)]
SUM_GROUPS = a_cubes()


def send(value, bits):
    return lax.ppermute(value, "dp", partners(bits))


def swap(value):
    return lax.ppermute(value, "dp", SWAP)


def near(value):
    return pltpu.with_memory_space_constraint(value, pltpu.VMEM)


def call(kernel, name, out_shape, *args, scratch=(), after=()):
    n = len(args)

    def body(*refs):
        kernel(*refs[:n], *refs[n + len(after) :])

    return pl.pallas_call(
        body,
        name=name,
        out_shape=out_shape,
        scratch_shapes=scratch,
        compiler_params=pltpu.CompilerParams(vmem_limit_bytes=8 * 1024 * 1024),
    )(*args, *[near(v) for v in after])


def role_of():
    return lax.axis_index("dp") & 1


def unit_rows(values):
    wide = values.astype(F32)
    length = jnp.sqrt(jnp.sum(wide * wide, axis=1, keepdims=True) + 1e-06)
    return wide / length, length


def row_ids(ref, at=0):
    tail = ref[at + BLOCK : at + SPAN, :BLOCK].astype(F32)
    return tail[0:1, :] * 128.0 + tail[1:2, :]


def down_rows(row, width):
    wide = jnp.transpose(jnp.broadcast_to(row, (128, row.shape[1])))
    return jnp.concatenate([wide] * (width // 128), axis=1)


def pre_kernel(q_hbm, d_hbm, p_hbm, keep_ref, send_ref, q_ref, d_ref, p_ref, sems):
    copies = [
        pltpu.make_async_copy(src, dst, sems.at[n])
        for n, (src, dst) in enumerate(((q_hbm, q_ref), (d_hbm, d_ref), (p_hbm, p_ref)))
    ]
    for copy in copies:
        copy.start()
    me = lax.axis_index("dp")
    role = role_of()
    for copy in copies:
        copy.wait()

    def fill(ref, values, ids):
        ref[:ROWS, :] = unit_rows(values)[0].astype(BF16)
        high = ids >> 7
        rows = lax.broadcasted_iota(jnp.int32, (PAD, ROWS), 0)
        tail = jnp.where(rows == 0, high, jnp.where(rows == 1, ids - high * 128, 0))
        ref[ROWS:, :] = jnp.zeros((PAD, WIDTH), BF16)
        ref[ROWS:, :ROWS] = tail.astype(F32).astype(BF16)

    mine = me * ROWS + lax.broadcasted_iota(jnp.int32, (1, ROWS), 1)

    @pl.when(role == 0)
    def _():
        fill(keep_ref, q_ref[...], p_ref[...])
        fill(send_ref, d_ref[...], mine)

    @pl.when(role == 1)
    def _():
        fill(keep_ref, d_ref[...], mine)
        fill(send_ref, q_ref[...], p_ref[...])


def join_kernel(keep_ref, come_ref, own_ref):
    def fill(low, high):
        own_ref[:ROWS, :] = low[:ROWS, :]
        own_ref[ROWS:BLOCK, :] = high[:ROWS, :]
        own_ref[BLOCK:, :] = jnp.zeros((PAD, WIDTH), BF16)
        own_ref[BLOCK:, :ROWS] = low[ROWS:, :ROWS]
        own_ref[BLOCK:, ROWS:BLOCK] = high[ROWS:, :ROWS]

    role = role_of()

    @pl.when(role == 0)
    def _():
        fill(keep_ref, come_ref)

    @pl.when(role == 1)
    def _():
        fill(come_ref, keep_ref)


def place_in_cube():
    me = lax.axis_index("dp")
    return ((me >> 5) & 1) * 4 + ((me >> 3) & 1) * 2 + ((me >> 1) & 1)


def pack_kernel(*refs):
    for n, ref in enumerate(refs[:-1]):
        refs[-1][n * SPAN : (n + 1) * SPAN, :] = ref[...]


def packs_of(columns):
    used = [pack for pack in PACKS if set(pack) & set(columns)]
    return used, [
        (p, pack.index(number) * SPAN) for number in columns for p, pack in enumerate(used) if number in pack
    ]


def tile_kernel(part, *refs):
    rows, columns = PARTS[part]
    last = part == len(PARTS) - 1
    used, where = packs_of(columns)
    x, refs = refs[: len(rows)], refs[len(rows) :]
    y, refs = refs[: len(used)], refs[len(used) :]
    if last:
        before, (e_ref, stats_ref, rowsum_ref, colsum_ref) = refs[: 2 * part], refs[2 * part :]
        before = [(before[2 * n], before[2 * n + 1]) for n in range(part)]
    else:
        e_ref, rowsum_ref, colsum_ref = refs
    ids_of_columns = [row_ids(y[p], at) for p, at in where]
    for i in range(len(rows)):
        ids = down_rows(row_ids(x[i]), BLOCK)
        partial = None
        for k, (p, start) in enumerate(where):
            dots = lax.dot_general(
                x[i][:BLOCK, :],
                y[p][start : start + BLOCK, :],
                (((1,), (1,)), ((), ())),
                preferred_element_type=F32,
            )
            e = jnp.exp2(dots * (20.0 * LOG2E) - 20.0 * LOG2E)
            at = slice(k * BLOCK, (k + 1) * BLOCK)
            e_ref[i * BLOCK : (i + 1) * BLOCK, at] = e
            for h in range(PER):
                piece = e[:, h * 128 : (h + 1) * 128]
                partial = piece if partial is None else partial + piece
            hit = jnp.where(ids == ids_of_columns[k], dots, 0.0)
            for n, value in enumerate((e, hit)):
                value = jnp.sum(value.reshape(BLOCK // 8, 8, BLOCK), axis=0)
                to = slice(n * 8, n * 8 + 8)
                colsum_ref[to, at] = value if i == 0 else colsum_ref[to, at] + value
        rowsum_ref[i * BLOCK : (i + 1) * BLOCK, :] = partial

    if last:
        place = place_in_cube()
        sums = before + [(rowsum_ref, colsum_ref)]

        def put(n, number, row):
            at = (place ^ number) * PER + n * HALF
            for h in range(PER):
                for g in range(CUBE):
                    stats_ref[g, pl.ds(at + h, 1), :] = row[:, h * 128 : (h + 1) * 128]

        @pl.when(role_of() == 0)
        def _():
            for number in ALL:
                total = None
                for (these, _), (ref, _) in zip(PARTS, sums):
                    if number in these:
                        at = these.index(number) * BLOCK
                        piece = ref[at : at + BLOCK, :]
                        total = piece if total is None else total + piece
                put(0, number, jnp.sum(jnp.transpose(total), axis=0, keepdims=True))
                put(1, number, jnp.zeros((1, BLOCK), F32))

        @pl.when(role_of() == 1)
        def _():
            for number in ALL:
                for n in range(2):
                    total = None
                    for (_, these), (_, ref) in zip(PARTS, sums):
                        if number in these:
                            at = these.index(number) * BLOCK
                            piece = ref[n * 8 : n * 8 + 8, at : at + BLOCK]
                            total = piece if total is None else total + piece
                    put(n, number, jnp.sum(total, axis=0, keepdims=True))


def encode(out_ref, value, digits):
    largest = None
    for h in range(WIDTH // 128):
        piece = jnp.abs(value[:, h * 128 : (h + 1) * 128])
        largest = piece if largest is None else jnp.maximum(largest, piece)
    largest = jnp.max(jnp.transpose(largest), axis=0, keepdims=True)
    power = jnp.ceil(jnp.log2(jnp.maximum(largest, 1e-35)) * 128.0)
    steps = value * down_rows(FULL * jnp.exp2(power * (-1.0 / 128.0)), WIDTH)
    out_ref[:BLOCK, :] = jnp.floor(steps + 0.5).astype(jnp.int32).astype(jnp.int16)
    at = lax.broadcasted_iota(jnp.int32, (PAD, BLOCK), 0)
    lane = lax.broadcasted_iota(jnp.int32, (PAD, BLOCK), 1)
    tail = jnp.where(at == 0, jnp.broadcast_to(power, (PAD, BLOCK)), 0.0)
    for n, digit in enumerate(digits):
        tail = jnp.where((at == 1) & (lane == n), digit, tail)
    out_ref[BLOCK:, :] = jnp.zeros((PAD, WIDTH), jnp.int16)
    out_ref[BLOCK:, :BLOCK] = tail.astype(jnp.int32).astype(jnp.int16)


def decode(ref):
    tail = ref[BLOCK:, :BLOCK].astype(jnp.int32).astype(F32)
    scale = down_rows(jnp.exp2(tail[0:1, :] * (1.0 / 128.0)) * (1.0 / FULL), WIDTH)
    return ref[:BLOCK, :].astype(jnp.int32).astype(F32) * scale


def digits_of(loss):
    high = jnp.floor(loss * (1.0 / 16.0))
    rest = (loss - high * 16.0) * 1024.0
    middle = jnp.floor(rest)
    low = jnp.floor((rest - middle) * 16384.0)
    return high, middle, low


def loss_of(ref):
    tail = ref[BLOCK:, :BLOCK].astype(jnp.int32).astype(F32)[1:2, :]
    lane = lax.broadcasted_iota(jnp.int32, (1, BLOCK), 1)
    unit = jnp.where(lane == 0, 16.0, jnp.where(lane == 1, 1.0 / 1024.0, 1.0 / (1024.0 * 16384.0)))
    return jnp.sum(jnp.where(lane < 3, tail * unit, 0.0))


def scale_kernel(stats_ref, out_ref):
    total = jnp.sum(stats_ref[:, :HALF, :], axis=0)
    out_ref[:HALF, :] = 1.0 / total
    lse = 20.0 + jnp.log(total)
    picked = 20.0 * jnp.sum(stats_ref[:, HALF:, :], axis=0)
    out_ref[HALF:, :] = jnp.full((8, 128), jnp.sum(lse - picked), F32)


def grad_kernel(number, coded, *refs):
    exps, refs = refs[: len(PARTS)], refs[len(PARTS) :]
    y, refs = refs[: len(PACKS)], refs[len(PACKS) :]
    scale_ref, x_ref, come, out_ref = refs[0], refs[1], refs[2:-1], refs[-1]
    place = place_in_cube()
    role = role_of()
    loss = scale_ref[HALF, 0]
    _, where = packs_of(ALL)

    def scale_of(block):
        at = (place ^ block) * PER
        return jnp.concatenate([scale_ref[pl.ds(at + h, 1), :] for h in range(PER)], axis=1)

    ids = down_rows(row_ids(x_ref), BLOCK)
    down = down_rows(jnp.where(role == 0, scale_of(number), 1.0), BLOCK)
    acc = None
    for column, (p, start) in zip(ALL, where):
        (e,) = [
            ref[
                rows.index(number) * BLOCK : (rows.index(number) + 1) * BLOCK,
                columns.index(column) * BLOCK : (columns.index(column) + 1) * BLOCK,
            ]
            for (rows, columns), ref in zip(PARTS, exps)
            if number in rows and column in columns
        ]
        along = jnp.where(role == 1, scale_of(column), 1.0)
        hit = jnp.where(ids == row_ids(y[p], start), 1.0, 0.0)
        weights = (e * down * along - hit).astype(BF16)
        part = jnp.dot(weights, y[p][start : start + BLOCK, :], preferred_element_type=F32)
        acc = part if acc is None else acc + part
    value = 20.0 * acc
    for ref in come:
        value = value + decode(ref)
        loss = loss + loss_of(ref)
    if coded:
        encode(out_ref, value, digits_of(loss))
    else:
        out_ref[:BLOCK, :] = value
        out_ref[BLOCK:, :] = jnp.full((LOSS, WIDTH), loss, F32)


def split_kernel(own_ref, a_ref, b_ref, c_ref, keep_ref, send_ref):
    value, loss = own_ref[:BLOCK, :], own_ref[BLOCK, 0]
    for ref in (a_ref, b_ref, c_ref):
        value = value + decode(ref)
        loss = loss + loss_of(ref)
    role = role_of()
    keep_ref[ROWS:, :] = jnp.full((LOSS, WIDTH), loss, F32)
    send_ref[ROWS:, :] = jnp.full((LOSS, WIDTH), loss, F32)

    @pl.when(role == 0)
    def _():
        keep_ref[:ROWS, :] = value[:ROWS, :]
        send_ref[:ROWS, :] = value[ROWS:, :]

    @pl.when(role == 1)
    def _():
        keep_ref[:ROWS, :] = value[ROWS:, :]
        send_ref[:ROWS, :] = value[:ROWS, :]


def post_kernel(q_ref, d_ref, keep_ref, come_ref, loss_ref, gq_ref, gd_ref):
    def project(out_ref, grad, values):
        unit, length = unit_rows(values)
        out_ref[...] = (grad - jnp.sum(grad * unit, axis=1, keepdims=True) * unit) / length

    def fill(gq, gd):
        project(gq_ref, gq[:ROWS, :], q_ref[...])
        project(gd_ref, gd[:ROWS, :], d_ref[...])
        loss_ref[...] = gd[ROWS : ROWS + 1, 0:1] * (1.0 / 16384)

    role = role_of()

    @pl.when(role == 0)
    def _():
        fill(keep_ref, come_ref)

    @pl.when(role == 1)
    def _():
        fill(come_ref, keep_ref)


def local(queries, documents, positives):
    piece = pltpu.VMEM((ROWS + PAD, WIDTH), BF16)
    raw = [queries, documents, positives.reshape(1, ROWS)]
    keep, give = pl.pallas_call(
        pre_kernel,
        name="pre",
        in_specs=[pl.BlockSpec(memory_space=pltpu.HBM)] * 3,
        out_shape=[piece, piece],
        scratch_shapes=[
            pltpu.VMEM((ROWS, WIDTH), BF16),
            pltpu.VMEM((ROWS, WIDTH), BF16),
            pltpu.VMEM((1, ROWS), jnp.int32),
            pltpu.SemaphoreType.DMA((3,)),
        ],
        compiler_params=pltpu.CompilerParams(vmem_limit_bytes=8 * 1024 * 1024),
    )(*[pltpu.with_memory_space_constraint(v, pltpu.HBM) for v in raw])
    come = swap(give)
    own = call(join_kernel, "join", pltpu.VMEM((SPAN, WIDTH), BF16), near(keep), near(come))

    def pack(blocks, name, after=()):
        shape = pltpu.VMEM((len(blocks) * SPAN, WIDTH), BF16)
        return call(pack_kernel, name, shape, *[near(x[n]) for n in blocks], after=after)

    x = {0: own}
    for bits in (4, 2, 1):
        x[bits] = send(own, bits)
    x[7] = send(x[4], 3)
    x[6] = send(x[2], 4)
    x[3] = send(x[1], 2)
    x[5] = send(x[1], 4)
    y = [swap(pack(NEAR, "pack_near"))]
    parts = []

    def tile(part, name):
        rows, columns = PARTS[part]
        used, _ = packs_of(columns)
        last = part == len(PARTS) - 1
        e = pltpu.VMEM((len(rows) * BLOCK, len(columns) * BLOCK), F32)
        sums = [pltpu.VMEM((len(rows) * BLOCK, 128), F32), pltpu.VMEM((16, len(columns) * BLOCK), F32)]
        before = [near(v) for done in parts for v in done[1:]] if last else []
        parts.append(
            call(
                functools.partial(tile_kernel, part),
                name,
                [e, pltpu.VMEM((CUBE, 2 * HALF, 128), F32)] if last else [e, *sums],
                *[near(x[n]) for n in rows],
                *[near(y[PACKS.index(pack)]) for pack in used],
                *before,
                scratch=sums if last else [],
            )
        )

    tile(0, "tile_0")
    y.append(swap(pack(SIDES, "pack_sides", after=[parts[0][1]])))
    tile(1, "tile_1")
    y.append(swap(pack(ENDS, "pack_ends", after=[parts[1][1]])))
    tile(2, "tile_2")
    tile(3, "tile_3")
    tile(4, "tile_4")
    stats = lax.all_to_all(parts[-1][1], "dp", 0, 0, axis_index_groups=SUM_GROUPS, tiled=True)
    scales = call(scale_kernel, "scales", pltpu.VMEM((HALF + 8, 128), F32), near(stats))

    coded = pltpu.VMEM((SPAN, WIDTH), jnp.int16)
    plain = pltpu.VMEM((BLOCK + LOSS, WIDTH), F32)

    def grad(number, *come, after, shape=coded):
        return call(
            functools.partial(grad_kernel, number, shape is coded),
            f"grad_{number}",
            shape,
            *[near(v[0]) for v in parts],
            *[near(v) for v in y],
            near(scales),
            near(x[number]),
            *[near(v) for v in come],
            after=after,
        )

    g7 = grad(7, after=[])
    r7 = send(g7, 3)
    g3 = grad(3, after=[])
    r3 = send(g3, 2)
    g5 = grad(5, after=[])
    r5 = send(g5, 1)
    g6 = grad(6, after=[])
    r6 = send(g6, 4)
    g1 = grad(1, r3, after=[])
    r1 = send(g1, 1)
    g2 = grad(2, r6, after=[])
    r2 = send(g2, 2)
    g4 = grad(4, r5, r7, after=[])
    r4 = send(g4, 4)
    g0 = grad(0, after=[], shape=plain)
    part = pltpu.VMEM((ROWS + LOSS, WIDTH), F32)
    keep, give = call(split_kernel, "split", [part, part], *[near(v) for v in (g0, r1, r2, r4)])
    come = swap(give)
    loss, gq, gd = call(
        post_kernel,
        "post",
        [
            jax.ShapeDtypeStruct((1, 1), F32),
            jax.ShapeDtypeStruct((ROWS, WIDTH), F32),
            jax.ShapeDtypeStruct((ROWS, WIDTH), F32),
        ],
        queries,
        documents,
        near(keep),
        near(come),
    )
    return (loss.reshape(()), gq, gd)


def solution(mesh):
    placed = (P("dp", None), P("dp", None), P("dp"))
    return jax.shard_map(
        local,
        mesh=mesh,
        in_specs=placed,
        out_specs=(P(), P("dp", None), P("dp", None)),
        check_vma=False,
    )
```

profile of v0, /device:TPU:1, one launch (start us, length us, event | category | flops | bytes accessed | tf_op | source)
XLA Modules:
  0.0 82.3 jit_solution(12890741291267984058)
XLA Ops:
  0.6 1.2 %pre.1 = (bf16[144,768]{1,0:T(8,128)(2,1)S(1)}, bf16[144,768]{1,0:T(8,128)(2,1)S(1)}) custom-call(bf16[128,768]{1,0:T(8,128)(2,1)} %refs_0_.1, bf16[128,768]{1,0:T(8,128)(2,1)} %refs_1_.1, s32[1,128]{1,0:T(1,128)} %bitcast.2), custom_call_target="tpu_custom_call" | custom-call | tf_op jit(solution)/shard_map/pre/pallas_call | solution.py:389
  1.9 1.5 %collective-permute-start = (bf16[144,768]{1,0:T(8,128)(2,1)S(1)}, bf16[144,768]{1,0:T(8,128)(2,1)S(1)}, u32[]{:S(2)}, u32[]{:S(2)}) collective-permute-start(bf16[144,768]{1,0:T(8,128)(2,1)S(1)} %get-tuple-element.25), channel_id=1, source_target_pairs={{0,1},{1,0},{2,3},{3,2},{4,5},{5,4},{6,7},{7,6},{8,9},{9,8},{10,11... | collective-permute-start | bytes 663560 | tf_op jit(solution)/shard_map/ppermute | solution.py:76
  4.5 2.9 %collective-permute-start.3 = (bf16[272,768]{1,0:T(8,128)(2,1)S(1)}, bf16[272,768]{1,0:T(8,128)(2,1)S(1)}, u32[]{:S(2)}, u32[]{:S(2)}) collective-permute-start(bf16[272,768]{1,0:T(8,128)(2,1)S(1)} %join.1.refs_0_.refs_9_), channel_id=1, source_target_pairs={{0,2},{1,7},{2,0},{3,5},{4,6},{5,3},{6,4},{7,1},{8,10},{9,15},{10,... | collective-permute-start | bytes 1253384 | tf_op jit(solution)/shard_map/ppermute | solution.py:72
  7.4 3.8 %collective-permute-start.2 = (bf16[272,768]{1,0:T(8,128)(2,1)S(1)}, bf16[272,768]{1,0:T(8,128)(2,1)S(1)}, u32[]{:S(2)}, u32[]{:S(2)}) collective-permute-start(bf16[272,768]{1,0:T(8,128)(2,1)S(1)} %join.1.refs_0_.refs_9_), channel_id=1, source_target_pairs={{0,8},{1,25},{2,10},{3,27},{4,12},{5,29},{6,14},{7,31},{8,0},{9,17... | collective-permute-start | bytes 1253384 | tf_op jit(solution)/shard_map/ppermute | solution.py:72
  11.2 2.5 %collective-permute-start.1 = (bf16[272,768]{1,0:T(8,128)(2,1)S(1)}, bf16[272,768]{1,0:T(8,128)(2,1)S(1)}, u32[]{:S(2)}, u32[]{:S(2)}) collective-permute-start(bf16[272,768]{1,0:T(8,128)(2,1)S(1)} %join.1.refs_0_.refs_9_), channel_id=1, source_target_pairs={{0,32},{1,97},{2,34},{3,99},{4,36},{5,101},{6,38},{7,103},{8,40},{... | collective-permute-start | bytes 1253384 | tf_op jit(solution)/shard_map/ppermute | solution.py:72
  13.7 2.9 %collective-permute-done.2.refs_2_.refs_9_ = bf16[272,768]{1,0:T(8,128)(2,1)S(1)} collective-permute-done((bf16[272,768]{1,0:T(8,128)(2,1)S(1)}, bf16[272,768]{1,0:T(8,128)(2,1)S(1)}, u32[]{:S(2)}, u32[]{:S(2)}) %collective-permute-start.2) | collective-permute-done | bytes 417824 | tf_op jit(solution)/shard_map/ppermute | solution.py:72
  16.6 2.7 %collective-permute-done.1.refs_1_.refs_9_ = bf16[272,768]{1,0:T(8,128)(2,1)S(1)} collective-permute-done((bf16[272,768]{1,0:T(8,128)(2,1)S(1)}, bf16[272,768]{1,0:T(8,128)(2,1)S(1)}, u32[]{:S(2)}, u32[]{:S(2)}) %collective-permute-start.1) | collective-permute-done | bytes 417824 | tf_op jit(solution)/shard_map/ppermute | solution.py:72
  19.6 2.6 %collective-permute-start.5 = (bf16[272,768]{1,0:T(8,128)(2,1)S(1)}, bf16[272,768]{1,0:T(8,128)(2,1)S(1)}, u32[]{:S(2)}, u32[]{:S(2)}) collective-permute-start(bf16[272,768]{1,0:T(8,128)(2,1)S(1)} %collective-permute-done.2.refs_2_.refs_9_), channel_id=1, source_target_pairs={{0,32},{1,97},{2,34},{3,99},{4,36},{5,101},{6,38},{7,103},{8,40},{... | collective-permute-start | bytes 1253384 | tf_op jit(solution)/shard_map/ppermute | solution.py:72
  22.3 2.4 %collective-permute-start.9 = (bf16[272,768]{1,0:T(8,128)(2,1)S(1)}, bf16[272,768]{1,0:T(8,128)(2,1)S(1)}, u32[]{:S(2)}, u32[]{:S(2)}) collective-permute-start(bf16[272,768]{1,0:T(8,128)(2,1)S(1)} %collective-permute-done.1.refs_1_.refs_9_), channel_id=1, source_target_pairs={{0,10},{1,31},{2,8},{3,29},{4,14},{5,27},{6,12},{7,25},{8,2},{9,23... | collective-permute-start | bytes 1253384 | tf_op jit(solution)/shard_map/ppermute | solution.py:72
  24.7 2.0 %tile_0.1 = (f32[1024,1024]{1,0:T(8,128)S(1)}, f32[1024,128]{1,0:T(8,128)S(1)}, f32[16,1024]{1,0:T(8,128)S(1)}) custom-call(bf16[272,768]{1,0:T(8,128)(2,1)S(1)} %join.1.refs_0_.refs_9_, bf16[272,768]{1,0:T(8,128)(2,1)S(1)} %collective-permute-done.1.refs_1_.refs_9_, bf16[272,768]{1,0:T(8,128)(2,1)S(1)} %collective-permute-done.2.refs_2_.refs_9_, ...), custom_call_target="tpu_custom_call" | custom-call | tf_op jit(solution)/shard_map/tile_0/pallas_call | solution.py:89
  27.9 4.7 %collective-permute-start.7 = (bf16[544,768]{1,0:T(8,128)(2,1)S(1)}, bf16[544,768]{1,0:T(8,128)(2,1)S(1)}, u32[]{:S(2)}, u32[]{:S(2)}) collective-permute-start(bf16[544,768]{1,0:T(8,128)(2,1)S(1)} %pack_sides.1), channel_id=1, source_target_pairs={{0,1},{1,0},{2,3},{3,2},{4,5},{5,4},{6,7},{7,6},{8,9},{9,8},{10,11... | collective-permute-start | bytes 2506760 | tf_op jit(solution)/shard_map/ppermute | solution.py:76
  32.6 1.1 %tile_1.1 = (f32[512,1024]{1,0:T(8,128)S(1)}, f32[512,128]{1,0:T(8,128)S(1)}, f32[16,1024]{1,0:T(8,128)S(1)}) custom-call(bf16[272,768]{1,0:T(8,128)(2,1)S(1)} %collective-permute-done.5.refs_0_.refs_4_.refs_9_, bf16[272,768]{1,0:T(8,128)(2,1)S(1)} %collective-permute-done.6.refs_1_.refs_5_.refs_9_, ...), custom_call_target="tpu_custom_call" | custom-call | tf_op jit(solution)/shard_map/tile_1/pallas_call | solution.py:89
  34.6 1.6 %tile_3.1 = (f32[512,1536]{1,0:T(8,128)S(1)}, f32[512,128]{1,0:T(8,128)S(1)}, f32[16,1536]{1,0:T(8,128)S(1)}) custom-call(bf16[272,768]{1,0:T(8,128)(2,1)S(1)} %collective-permute-done.8.refs_0_.refs_6_.refs_9_, bf16[272,768]{1,0:T(8,128)(2,1)S(1)} %collective-permute-done.9.refs_1_.refs_7_.refs_9_, ...), custom_call_target="tpu_custom_call" | custom-call | tf_op jit(solution)/shard_map/tile_3/pallas_call | solution.py:89
  36.2 1.5 %tile_2.1 = (f32[1536,512]{1,0:T(8,128)S(1)}, f32[1536,128]{1,0:T(8,128)S(1)}, f32[16,512]{1,0:T(8,128)S(1)}) custom-call(bf16[272,768]{1,0:T(8,128)(2,1)S(1)} %join.1.refs_0_.refs_9_, bf16[272,768]{1,0:T(8,128)(2,1)S(1)} %collective-permute-done.1.refs_1_.refs_9_, bf16[272,768]{1,0:T(8,128)(2,1)S(1)} %collective-permute-done.2.refs_2_.refs_9_, ...), custom_call_target="tpu_custom_call" | custom-call | tf_op jit(solution)/shard_map/tile_2/pallas_call | solution.py:89
  37.8 2.0 %tile_4.1 = (f32[2048,512]{1,0:T(8,128)S(1)}, f32[8,32,128]{2,1,0:T(8,128)S(1)}) custom-call(bf16[272,768]{1,0:T(8,128)(2,1)S(1)} %join.1.refs_0_.refs_9_, bf16[272,768]{1,0:T(8,128)(2,1)S(1)} %collective-permute-done.1.refs_1_.refs_9_, bf16[272,768]{1,0:T(8,128)(2,1)S(1)} %collective-permute-done.2.refs_2_.refs_9_, ...), custom_call_target="tpu_custom_call" | custom-call | tf_op jit(solution)/shard_map/tile_4/pallas_call | solution.py:89
  39.8 7.6 %all_to_all.5.refs_0_ = f32[8,32,128]{2,1,0:T(8,128)S(1)} all-to-all(f32[8,32,128]{2,1,0:T(8,128)S(1)} %get-tuple-element.39), channel_id=1, replica_groups={{0,2,8,10,32,34,40,42},{4,6,12,14,36,38,44,46},{16,18,24,26,48,50,56,58..., dimensions={0} | all-to-all | bytes 262144 | tf_op jit(solution)/shard_map/all_to_all | solution.py:445
  47.6 1.4 %grad_3.1 = s16[272,768]{1,0:T(8,128)(2,1)S(1)} custom-call(f32[1024,1024]{1,0:T(8,128)S(1)} %get-tuple-element.26.refs_0_, f32[512,1024]{1,0:T(8,128)S(1)} %get-tuple-element.27.refs_1_, f32[1536,512]{1,0:T(8,128)S(1)} %get-tuple-element.29.refs_2_, f32[512,1536]{1,0:T(8,128)S(1)} %get-tuple-element.30.refs_3_, f32[2048,512]{1,0:T(8,128)S(1)} %get-tuple-element.38.refs_4_, ...), custom_call_target="tpu_custom_call" | custom-call | tf_op jit(solution)/shard_map/grad_3/pallas_call | solution.py:89
  49.1 1.4 %grad_6.1 = s16[272,768]{1,0:T(8,128)(2,1)S(1)} custom-call(f32[1024,1024]{1,0:T(8,128)S(1)} %get-tuple-element.26.refs_0_, f32[512,1024]{1,0:T(8,128)S(1)} %get-tuple-element.27.refs_1_, f32[1536,512]{1,0:T(8,128)S(1)} %get-tuple-element.29.refs_2_, f32[512,1536]{1,0:T(8,128)S(1)} %get-tuple-element.30.refs_3_, f32[2048,512]{1,0:T(8,128)S(1)} %get-tuple-element.38.refs_4_, ...), custom_call_target="tpu_custom_call" | custom-call | tf_op jit(solution)/shard_map/grad_6/pallas_call | solution.py:89
  50.5 2.1 %collective-permute-start.13 = (s16[272,768]{1,0:T(8,128)(2,1)S(1)}, s16[272,768]{1,0:T(8,128)(2,1)S(1)}, u32[]{:S(2)}, u32[]{:S(2)}) collective-permute-start(s16[272,768]{1,0:T(8,128)(2,1)S(1)} %grad_6.1), channel_id=1, source_target_pairs={{0,32},{1,97},{2,34},{3,99},{4,36},{5,101},{6,38},{7,103},{8,40},{... | collective-permute-start | bytes 1253384 | tf_op jit(solution)/shard_map/ppermute | solution.py:72
  52.7 1.5 %grad_5.1 = s16[272,768]{1,0:T(8,128)(2,1)S(1)} custom-call(f32[1024,1024]{1,0:T(8,128)S(1)} %get-tuple-element.26.refs_0_, f32[512,1024]{1,0:T(8,128)S(1)} %get-tuple-element.27.refs_1_, f32[1536,512]{1,0:T(8,128)S(1)} %get-tuple-element.29.refs_2_, f32[512,1536]{1,0:T(8,128)S(1)} %get-tuple-element.30.refs_3_, f32[2048,512]{1,0:T(8,128)S(1)} %get-tuple-element.38.refs_4_, ...), custom_call_target="tpu_custom_call" | custom-call | tf_op jit(solution)/shard_map/grad_5/pallas_call | solution.py:89
  55.2 1.5 %grad_7.1 = s16[272,768]{1,0:T(8,128)(2,1)S(1)} custom-call(f32[1024,1024]{1,0:T(8,128)S(1)} %get-tuple-element.26.refs_0_, f32[512,1024]{1,0:T(8,128)S(1)} %get-tuple-element.27.refs_1_, f32[1536,512]{1,0:T(8,128)S(1)} %get-tuple-element.29.refs_2_, f32[512,1536]{1,0:T(8,128)S(1)} %get-tuple-element.30.refs_3_, f32[2048,512]{1,0:T(8,128)S(1)} %get-tuple-element.38.refs_4_, ...), custom_call_target="tpu_custom_call" | custom-call | tf_op jit(solution)/shard_map/grad_7/pallas_call | solution.py:89
  56.7 3.7 %collective-permute-start.16 = (s16[272,768]{1,0:T(8,128)(2,1)S(1)}, s16[272,768]{1,0:T(8,128)(2,1)S(1)}, u32[]{:S(2)}, u32[]{:S(2)}) collective-permute-start(s16[272,768]{1,0:T(8,128)(2,1)S(1)} %grad_7.1), channel_id=1, source_target_pairs={{0,10},{1,31},{2,8},{3,29},{4,14},{5,27},{6,12},{7,25},{8,2},{9,23... | collective-permute-start | bytes 1253384 | tf_op jit(solution)/shard_map/ppermute | solution.py:72
  60.4 1.4 %grad_1.1 = s16[272,768]{1,0:T(8,128)(2,1)S(1)} custom-call(f32[1024,1024]{1,0:T(8,128)S(1)} %get-tuple-element.26.refs_0_, f32[512,1024]{1,0:T(8,128)S(1)} %get-tuple-element.27.refs_1_, f32[1536,512]{1,0:T(8,128)S(1)} %get-tuple-element.29.refs_2_, f32[512,1536]{1,0:T(8,128)S(1)} %get-tuple-element.30.refs_3_, f32[2048,512]{1,0:T(8,128)S(1)} %get-tuple-element.38.refs_4_, ...), custom_call_target="tpu_custom_call" | custom-call | tf_op jit(solution)/shard_map/grad_1/pallas_call | solution.py:89
  62.0 1.4 %grad_2.1 = s16[272,768]{1,0:T(8,128)(2,1)S(1)} custom-call(f32[1024,1024]{1,0:T(8,128)S(1)} %get-tuple-element.26.refs_0_, f32[512,1024]{1,0:T(8,128)S(1)} %get-tuple-element.27.refs_1_, f32[1536,512]{1,0:T(8,128)S(1)} %get-tuple-element.29.refs_2_, f32[512,1536]{1,0:T(8,128)S(1)} %get-tuple-element.30.refs_3_, f32[2048,512]{1,0:T(8,128)S(1)} %get-tuple-element.38.refs_4_, ...), custom_call_target="tpu_custom_call" | custom-call | tf_op jit(solution)/shard_map/grad_2/pallas_call | solution.py:89
  63.5 1.4 %collective-permute-start.14 = (s16[272,768]{1,0:T(8,128)(2,1)S(1)}, s16[272,768]{1,0:T(8,128)(2,1)S(1)}, u32[]{:S(2)}, u32[]{:S(2)}) collective-permute-start(s16[272,768]{1,0:T(8,128)(2,1)S(1)} %grad_2.1), channel_id=1, source_target_pairs={{0,8},{1,25},{2,10},{3,27},{4,12},{5,29},{6,14},{7,31},{8,0},{9,17... | collective-permute-start | bytes 1253384 | tf_op jit(solution)/shard_map/ppermute | solution.py:72
  64.9 4.0 %collective-permute-done.16.refs_11_ = s16[272,768]{1,0:T(8,128)(2,1)S(1)} collective-permute-done((s16[272,768]{1,0:T(8,128)(2,1)S(1)}, s16[272,768]{1,0:T(8,128)(2,1)S(1)}, u32[]{:S(2)}, u32[]{:S(2)}) %collective-permute-start.16) | collective-permute-done | bytes 417824 | tf_op jit(solution)/shard_map/ppermute | solution.py:72
  68.9 1.5 %grad_4.1 = s16[272,768]{1,0:T(8,128)(2,1)S(1)} custom-call(f32[1024,1024]{1,0:T(8,128)S(1)} %get-tuple-element.26.refs_0_, f32[512,1024]{1,0:T(8,128)S(1)} %get-tuple-element.27.refs_1_, f32[1536,512]{1,0:T(8,128)S(1)} %get-tuple-element.29.refs_2_, f32[512,1536]{1,0:T(8,128)S(1)} %get-tuple-element.30.refs_3_, f32[2048,512]{1,0:T(8,128)S(1)} %get-tuple-element.38.refs_4_, ...), custom_call_target="tpu_custom_call" | custom-call | tf_op jit(solution)/shard_map/grad_4/pallas_call | solution.py:89
  70.4 1.3 %collective-permute-start.17 = (s16[272,768]{1,0:T(8,128)(2,1)S(1)}, s16[272,768]{1,0:T(8,128)(2,1)S(1)}, u32[]{:S(2)}, u32[]{:S(2)}) collective-permute-start(s16[272,768]{1,0:T(8,128)(2,1)S(1)} %grad_4.1), channel_id=1, source_target_pairs={{0,32},{1,97},{2,34},{3,99},{4,36},{5,101},{6,38},{7,103},{8,40},{... | collective-permute-start | bytes 1253384 | tf_op jit(solution)/shard_map/ppermute | solution.py:72
  71.8 1.1 %grad_0.1.refs_0_ = f32[264,768]{1,0:T(8,128)S(1)} custom-call(f32[1024,1024]{1,0:T(8,128)S(1)} %get-tuple-element.26.refs_0_, f32[512,1024]{1,0:T(8,128)S(1)} %get-tuple-element.27.refs_1_, f32[1536,512]{1,0:T(8,128)S(1)} %get-tuple-element.29.refs_2_, f32[512,1536]{1,0:T(8,128)S(1)} %get-tuple-element.30.refs_3_, ...), custom_call_target="tpu_custom_call" | custom-call | tf_op jit(solution)/shard_map/grad_0/pallas_call | solution.py:89
  73.2 5.6 %collective-permute-done.17.refs_3_ = s16[272,768]{1,0:T(8,128)(2,1)S(1)} collective-permute-done((s16[272,768]{1,0:T(8,128)(2,1)S(1)}, s16[272,768]{1,0:T(8,128)(2,1)S(1)}, u32[]{:S(2)}, u32[]{:S(2)}) %collective-permute-start.17) | collective-permute-done | bytes 417824 | tf_op jit(solution)/shard_map/ppermute | solution.py:72
  79.4 1.7 %collective-permute-done.18.refs_3_ = f32[136,768]{1,0:T(8,128)S(1)} collective-permute-done((f32[136,768]{1,0:T(8,128)S(1)}, f32[136,768]{1,0:T(8,128)S(1)}, u32[]{:S(2)}, u32[]{:S(2)}) %collective-permute-start.18) | collective-permute-done | bytes 417824 | tf_op jit(solution)/shard_map/ppermute | solution.py:76
  81.1 1.2 %post.1 = (f32[1,1]{1,0:T(1,128)}, f32[128,768]{1,0:T(8,128)}, f32[128,768]{1,0:T(8,128)}) custom-call(bf16[128,768]{1,0:T(8,128)(2,1)S(1)} %copy-done, bf16[128,768]{1,0:T(8,128)(2,1)S(1)} %copy-done.1, f32[136,768]{1,0:T(8,128)S(1)} %get-tuple-element.40.refs_2_, f32[136,768]{1,0:T(8,128)S(1)} %collective-permute-done.18.refs_3_), custom_call_target="tpu_custom_call" | custom-call | tf_op jit(solution)/shard_map/post/pallas_call | solution.py:89
  (32 shorter events, 6.0 us)
Async XLA Ops:
  1.9 2.6 %collective-permute-start = (bf16[144,768]{1,0:T(8,128)(2,1)S(1)}, bf16[144,768]{1,0:T(8,128)(2,1)S(1)}, u32[]{:S(2)}, u32[]{:S(2)}) collective-permute-start(bf16[144,768]{1,0:T(8,128)(2,1)S(1)} %get-tuple-element.25), channel_id=1, source_target_pairs={{0,1},{1,0},{2,3},{3,2},{4,5},{5,4},{6,7},{7,6},{8,9},{9,8},{10,11... | collective-permute-start | bytes 663560 | tf_op jit(solution)/shard_map/ppermute | solution.py:76
  4.5 9.1 %collective-permute-start.3 = (bf16[272,768]{1,0:T(8,128)(2,1)S(1)}, bf16[272,768]{1,0:T(8,128)(2,1)S(1)}, u32[]{:S(2)}, u32[]{:S(2)}) collective-permute-start(bf16[272,768]{1,0:T(8,128)(2,1)S(1)} %join.1.refs_0_.refs_9_), channel_id=1, source_target_pairs={{0,2},{1,7},{2,0},{3,5},{4,6},{5,3},{6,4},{7,1},{8,10},{9,15},{10,... | collective-permute-start | bytes 1253384 | tf_op jit(solution)/shard_map/ppermute | solution.py:72
  7.4 9.2 %collective-permute-start.2 = (bf16[272,768]{1,0:T(8,128)(2,1)S(1)}, bf16[272,768]{1,0:T(8,128)(2,1)S(1)}, u32[]{:S(2)}, u32[]{:S(2)}) collective-permute-start(bf16[272,768]{1,0:T(8,128)(2,1)S(1)} %join.1.refs_0_.refs_9_), channel_id=1, source_target_pairs={{0,8},{1,25},{2,10},{3,27},{4,12},{5,29},{6,14},{7,31},{8,0},{9,17... | collective-permute-start | bytes 1253384 | tf_op jit(solution)/shard_map/ppermute | solution.py:72
  11.2 8.1 %collective-permute-start.1 = (bf16[272,768]{1,0:T(8,128)(2,1)S(1)}, bf16[272,768]{1,0:T(8,128)(2,1)S(1)}, u32[]{:S(2)}, u32[]{:S(2)}) collective-permute-start(bf16[272,768]{1,0:T(8,128)(2,1)S(1)} %join.1.refs_0_.refs_9_), channel_id=1, source_target_pairs={{0,32},{1,97},{2,34},{3,99},{4,36},{5,101},{6,38},{7,103},{8,40},{... | collective-permute-start | bytes 1253384 | tf_op jit(solution)/shard_map/ppermute | solution.py:72
  19.4 5.3 %collective-permute-start.4 = (bf16[1088,768]{1,0:T(8,128)(2,1)S(1)}, bf16[1088,768]{1,0:T(8,128)(2,1)S(1)}, u32[]{:S(2)}, u32[]{:S(2)}) collective-permute-start(bf16[1088,768]{1,0:T(8,128)(2,1)S(1)} %pack_near.1), channel_id=1, source_target_pairs={{0,1},{1,0},{2,3},{3,2},{4,5},{5,4},{6,7},{7,6},{8,9},{9,8},{10,11... | collective-permute-start | bytes 5013512 | tf_op jit(solution)/shard_map/ppermute | solution.py:76
  19.5 8.3 %collective-permute-start.6 = (bf16[272,768]{1,0:T(8,128)(2,1)S(1)}, bf16[272,768]{1,0:T(8,128)(2,1)S(1)}, u32[]{:S(2)}, u32[]{:S(2)}) collective-permute-start(bf16[272,768]{1,0:T(8,128)(2,1)S(1)} %collective-permute-done.3.refs_3_.refs_9_), channel_id=1, source_target_pairs={{0,8},{1,25},{2,10},{3,27},{4,12},{5,29},{6,14},{7,31},{8,0},{9,17... | collective-permute-start | bytes 1253384 | tf_op jit(solution)/shard_map/ppermute | solution.py:72
  19.6 8.3 %collective-permute-start.5 = (bf16[272,768]{1,0:T(8,128)(2,1)S(1)}, bf16[272,768]{1,0:T(8,128)(2,1)S(1)}, u32[]{:S(2)}, u32[]{:S(2)}) collective-permute-start(bf16[272,768]{1,0:T(8,128)(2,1)S(1)} %collective-permute-done.2.refs_2_.refs_9_), channel_id=1, source_target_pairs={{0,32},{1,97},{2,34},{3,99},{4,36},{5,101},{6,38},{7,103},{8,40},{... | collective-permute-start | bytes 1253384 | tf_op jit(solution)/shard_map/ppermute | solution.py:72
  22.1 11.6 %collective-permute-start.8 = (bf16[272,768]{1,0:T(8,128)(2,1)S(1)}, bf16[272,768]{1,0:T(8,128)(2,1)S(1)}, u32[]{:S(2)}, u32[]{:S(2)}) collective-permute-start(bf16[272,768]{1,0:T(8,128)(2,1)S(1)} %collective-permute-done.3.refs_3_.refs_9_), channel_id=1, source_target_pairs={{0,32},{1,97},{2,34},{3,99},{4,36},{5,101},{6,38},{7,103},{8,40},{... | collective-permute-start | bytes 1253384 | tf_op jit(solution)/shard_map/ppermute | solution.py:72
  22.3 11.4 %collective-permute-start.9 = (bf16[272,768]{1,0:T(8,128)(2,1)S(1)}, bf16[272,768]{1,0:T(8,128)(2,1)S(1)}, u32[]{:S(2)}, u32[]{:S(2)}) collective-permute-start(bf16[272,768]{1,0:T(8,128)(2,1)S(1)} %collective-permute-done.1.refs_1_.refs_9_), channel_id=1, source_target_pairs={{0,10},{1,31},{2,8},{3,29},{4,14},{5,27},{6,12},{7,25},{8,2},{9,23... | collective-permute-start | bytes 1253384 | tf_op jit(solution)/shard_map/ppermute | solution.py:72
  27.9 6.7 %collective-permute-start.7 = (bf16[544,768]{1,0:T(8,128)(2,1)S(1)}, bf16[544,768]{1,0:T(8,128)(2,1)S(1)}, u32[]{:S(2)}, u32[]{:S(2)}) collective-permute-start(bf16[544,768]{1,0:T(8,128)(2,1)S(1)} %pack_sides.1), channel_id=1, source_target_pairs={{0,1},{1,0},{2,3},{3,2},{4,5},{5,4},{6,7},{7,6},{8,9},{9,8},{10,11... | collective-permute-start | bytes 2506760 | tf_op jit(solution)/shard_map/ppermute | solution.py:76
  33.8 3.9 %collective-permute-start.10 = (bf16[544,768]{1,0:T(8,128)(2,1)S(1)}, bf16[544,768]{1,0:T(8,128)(2,1)S(1)}, u32[]{:S(2)}, u32[]{:S(2)}) collective-permute-start(bf16[544,768]{1,0:T(8,128)(2,1)S(1)} %pack_ends.1), channel_id=1, source_target_pairs={{0,1},{1,0},{2,3},{3,2},{4,5},{5,4},{6,7},{7,6},{8,9},{9,8},{10,11... | collective-permute-start | bytes 2506760 | tf_op jit(solution)/shard_map/ppermute | solution.py:76
  49.0 11.4 %collective-permute-start.11 = (s16[272,768]{1,0:T(8,128)(2,1)S(1)}, s16[272,768]{1,0:T(8,128)(2,1)S(1)}, u32[]{:S(2)}, u32[]{:S(2)}) collective-permute-start(s16[272,768]{1,0:T(8,128)(2,1)S(1)} %grad_3.1), channel_id=1, source_target_pairs={{0,8},{1,25},{2,10},{3,27},{4,12},{5,29},{6,14},{7,31},{8,0},{9,17... | collective-permute-start | bytes 1253384 | tf_op jit(solution)/shard_map/ppermute | solution.py:72
  50.5 11.5 %collective-permute-start.13 = (s16[272,768]{1,0:T(8,128)(2,1)S(1)}, s16[272,768]{1,0:T(8,128)(2,1)S(1)}, u32[]{:S(2)}, u32[]{:S(2)}) collective-permute-start(s16[272,768]{1,0:T(8,128)(2,1)S(1)} %grad_6.1), channel_id=1, source_target_pairs={{0,32},{1,97},{2,34},{3,99},{4,36},{5,101},{6,38},{7,103},{8,40},{... | collective-permute-start | bytes 1253384 | tf_op jit(solution)/shard_map/ppermute | solution.py:72
  54.1 10.8 %collective-permute-start.15 = (s16[272,768]{1,0:T(8,128)(2,1)S(1)}, s16[272,768]{1,0:T(8,128)(2,1)S(1)}, u32[]{:S(2)}, u32[]{:S(2)}) collective-permute-start(s16[272,768]{1,0:T(8,128)(2,1)S(1)} %grad_5.1), channel_id=1, source_target_pairs={{0,2},{1,7},{2,0},{3,5},{4,6},{5,3},{6,4},{7,1},{8,10},{9,15},{10,... | collective-permute-start | bytes 1253384 | tf_op jit(solution)/shard_map/ppermute | solution.py:72
  56.7 12.2 %collective-permute-start.16 = (s16[272,768]{1,0:T(8,128)(2,1)S(1)}, s16[272,768]{1,0:T(8,128)(2,1)S(1)}, u32[]{:S(2)}, u32[]{:S(2)}) collective-permute-start(s16[272,768]{1,0:T(8,128)(2,1)S(1)} %grad_7.1), channel_id=1, source_target_pairs={{0,10},{1,31},{2,8},{3,29},{4,14},{5,27},{6,12},{7,25},{8,2},{9,23... | collective-permute-start | bytes 1253384 | tf_op jit(solution)/shard_map/ppermute | solution.py:72
  61.9 11.0 %collective-permute-start.12 = (s16[272,768]{1,0:T(8,128)(2,1)S(1)}, s16[272,768]{1,0:T(8,128)(2,1)S(1)}, u32[]{:S(2)}, u32[]{:S(2)}) collective-permute-start(s16[272,768]{1,0:T(8,128)(2,1)S(1)} %grad_1.1), channel_id=1, source_target_pairs={{0,2},{1,7},{2,0},{3,5},{4,6},{5,3},{6,4},{7,1},{8,10},{9,15},{10,... | collective-permute-start | bytes 1253384 | tf_op jit(solution)/shard_map/ppermute | solution.py:72
  63.5 9.8 %collective-permute-start.14 = (s16[272,768]{1,0:T(8,128)(2,1)S(1)}, s16[272,768]{1,0:T(8,128)(2,1)S(1)}, u32[]{:S(2)}, u32[]{:S(2)}) collective-permute-start(s16[272,768]{1,0:T(8,128)(2,1)S(1)} %grad_2.1), channel_id=1, source_target_pairs={{0,8},{1,25},{2,10},{3,27},{4,12},{5,29},{6,14},{7,31},{8,0},{9,17... | collective-permute-start | bytes 1253384 | tf_op jit(solution)/shard_map/ppermute | solution.py:72
  70.4 10.7 %copy-start = (bf16[128,768]{1,0:T(8,128)(2,1)S(1)}, bf16[128,768]{1,0:T(8,128)(2,1)}, u32[]{:S(2)}) copy-start(bf16[128,768]{1,0:T(8,128)(2,1)} %refs_0_.1) | copy-start | bytes 589828
  70.4 10.7 %copy-start.1 = (bf16[128,768]{1,0:T(8,128)(2,1)S(1)}, bf16[128,768]{1,0:T(8,128)(2,1)}, u32[]{:S(2)}) copy-start(bf16[128,768]{1,0:T(8,128)(2,1)} %refs_1_.1) | copy-start | bytes 589828
  70.4 8.4 %collective-permute-start.17 = (s16[272,768]{1,0:T(8,128)(2,1)S(1)}, s16[272,768]{1,0:T(8,128)(2,1)S(1)}, u32[]{:S(2)}, u32[]{:S(2)}) collective-permute-start(s16[272,768]{1,0:T(8,128)(2,1)S(1)} %grad_4.1), channel_id=1, source_target_pairs={{0,32},{1,97},{2,34},{3,99},{4,36},{5,101},{6,38},{7,103},{8,40},{... | collective-permute-start | bytes 1253384 | tf_op jit(solution)/shard_map/ppermute | solution.py:72
  79.3 1.8 %collective-permute-start.18 = (f32[136,768]{1,0:T(8,128)S(1)}, f32[136,768]{1,0:T(8,128)S(1)}, u32[]{:S(2)}, u32[]{:S(2)}) collective-permute-start(f32[136,768]{1,0:T(8,128)S(1)} %get-tuple-element.41), channel_id=1, source_target_pairs={{0,1},{1,0},{2,3},{3,2},{4,5},{5,4},{6,7},{7,6},{8,9},{9,8},{10,11... | collective-permute-start | bytes 1253384 | tf_op jit(solution)/shard_map/ppermute | solution.py:76
where the time goes:
time: 82.5 us; the launch traced here: 82.3 us
  starting transfers between devices  30.7 us (37%)
  Pallas kernels  22.9 us (28%)
  waiting for transfers between devices  20.2 us (24%)
  blocking collectives  7.62 us (9%)
  between operations  0.86 us (1%)
    ppermute x14, starting transfers between devices, send(): return lax.ppermute(value, 'dp', partners(bits))  24.3 us
    pallas_call x20, Pallas kernels, call(): pl.pallas_call(body, name=name, out_shape=out_shape, scratch_shapes=scrat...  21.6 us
    ppermute x14, waiting for transfers between devices, send(): return lax.ppermute(value, 'dp', partners(bits))  16.7 us
    all_to_all x1, blocking collectives, local(): lax.all_to_all(parts[-1][1], 'dp', 0, 0, axis_index_groups=SUM_GROUPS, ti...  7.62 us
    ppermute x5, starting transfers between devices, swap(): return lax.ppermute(value, 'dp', SWAP)  6.45 us
    ppermute x5, waiting for transfers between devices, swap(): return lax.ppermute(value, 'dp', SWAP)  3.52 us
  transfers between devices with their start and end apart: 19, of which 10 were waited for; matrix products, arithmetic and copies ran while one was open for 0% of the time, Pallas kernels for 20%

commit v1 on v0

--- a/solution.py
+++ b/solution.py
@@ -22,16 +22,16 @@
 LOG2E = 1.4426950408889634
 FULL = 32760.0
 NEAR = (0, 4, 2, 1)
-SIDES = (6, 3)
-ENDS = (5, 7)
-PACKS = (NEAR, SIDES, ENDS)
-ALL = NEAR + SIDES + ENDS
+SIDES = (3, 6, 5)
+CORNER = (7,)
+PACKS = (NEAR, SIDES, CORNER)
+ALL = NEAR + SIDES + CORNER
 PARTS = (
     (NEAR, NEAR),
     (SIDES, NEAR),
     (NEAR + SIDES, SIDES),
-    (ENDS, NEAR + SIDES),
-    (ALL, ENDS),
+    (CORNER, NEAR + SIDES),
+    (ALL, CORNER),
 )
 SPAN = BLOCK + PAD
 F32 = jnp.float32
@@ -409,14 +409,14 @@
     x = {0: own}
     for bits in (4, 2, 1):
         x[bits] = send(own, bits)
-    x[7] = send(x[4], 3)
+    x[3] = send(x[1], 2)
     x[6] = send(x[2], 4)
-    x[3] = send(x[1], 2)
-    x[5] = send(x[1], 4)
+    x[5] = send(x[4], 1)
+    x[7] = send(x[3], 4)
     y = [swap(pack(NEAR, "pack_near"))]
     parts = []
 
-    def tile(part, name):
+    def tile(part, name, after=()):
         rows, columns = PARTS[part]
         used, _ = packs_of(columns)
         last = part == len(PARTS) - 1
@@ -432,14 +432,15 @@
                 *[near(y[PACKS.index(pack)]) for pack in used],
                 *before,
                 scratch=sums if last else [],
+                after=after,
             )
         )
 
     tile(0, "tile_0")
     y.append(swap(pack(SIDES, "pack_sides", after=[parts[0][1]])))
     tile(1, "tile_1")
-    y.append(swap(pack(ENDS, "pack_ends", after=[parts[1][1]])))
-    tile(2, "tile_2")
+    tile(2, "tile_2", [parts[1][1]])
+    y.append(swap(pack(CORNER, "pack_corner", after=[parts[2][1]])))
     tile(3, "tile_3")
     tile(4, "tile_4")
     stats = lax.all_to_all(parts[-1][1], "dp", 0, 0, axis_index_groups=SUM_GROUPS, tiled=True)
@@ -448,7 +449,7 @@
     coded = pltpu.VMEM((SPAN, WIDTH), jnp.int16)
     plain = pltpu.VMEM((BLOCK + LOSS, WIDTH), F32)
 
-    def grad(number, *come, after, shape=coded):
+    def grad(number, *come, after=(), shape=coded):
         return call(
             functools.partial(grad_kernel, number, shape is coded),
             f"grad_{number}",
@@ -461,21 +462,21 @@
             after=after,
         )
 
-    g7 = grad(7, after=[])
-    r7 = send(g7, 3)
-    g3 = grad(3, after=[])
+    g7 = grad(7)
+    r7 = send(g7, 4)
+    g6 = grad(6)
+    r6 = send(g6, 2)
+    g5 = grad(5)
+    r5 = send(g5, 1)
+    g3 = grad(3, r7)
     r3 = send(g3, 2)
-    g5 = grad(5, after=[])
-    r5 = send(g5, 1)
-    g6 = grad(6, after=[])
-    r6 = send(g6, 4)
-    g1 = grad(1, r3, after=[])
+    g4 = grad(4, r6, r5)
+    r4 = send(g4, 4)
+    g2 = grad(2)
+    r2 = send(g2, 2)
+    g1 = grad(1, r3)
     r1 = send(g1, 1)
-    g2 = grad(2, r6, after=[])
-    r2 = send(g2, 2)
-    g4 = grad(4, r5, r7, after=[])
-    r4 = send(g4, 4)
-    g0 = grad(0, after=[], shape=plain)
+    g0 = grad(0, shape=plain)
     part = pltpu.VMEM((ROWS + LOSS, WIDTH), F32)
     keep, give = call(split_kernel, "split", [part, part], *[near(v) for v in (g0, r1, r2, r4)])
     come = swap(give)

time: 82.5 us -> 83.1 us (level)
  waiting for transfers between devices: 20.2 us -> 27.1 us
  starting transfers between devices: 30.7 us -> 24.6 us
    ppermute x14, waiting for transfers between devices: 16.7 us -> 23.1 us  [send(): return lax.ppermute(value, 'dp', partners(bits))]
    ppermute x14, starting transfers between devices: 24.3 us -> 21.1 us  [send(): return lax.ppermute(value, 'dp', partners(bits))]
    ppermute x5, starting transfers between devices: 6.45 us -> 3.51 us  [swap(): return lax.ppermute(value, 'dp', SWAP)]
  transfers between devices with their start and end apart: 19 -> 19, of which waited for: 10 -> 15; matrix products, arithmetic and copies ran while one was open for 0% -> 0% of each run, Pallas kernels for 20% -> 20%
where the time goes in v1:
time: 83.1 us; the launch traced here: 83 us
  waiting for transfers between devices  27.1 us (33%)
  starting transfers between devices  24.6 us (30%)
  Pallas kernels  22.8 us (27%)
  blocking collectives  7.61 us (9%)
    ppermute x14, waiting for transfers between devices, send(): return lax.ppermute(value, 'dp', partners(bits))  23.1 us
    pallas_call x20, Pallas kernels, call(): pl.pallas_call(body, name=name, out_shape=out_shape, scratch_shapes=scrat...  21.6 us
    ppermute x14, starting transfers between devices, send(): return lax.ppermute(value, 'dp', partners(bits))  21.1 us
    all_to_all x1, blocking collectives, local(): lax.all_to_all(parts[-1][1], 'dp', 0, 0, axis_index_groups=SUM_GROUPS, ti...  7.61 us
    ppermute x5, waiting for transfers between devices, swap(): return lax.ppermute(value, 'dp', SWAP)  4.01 us
    ppermute x5, starting transfers between devices, swap(): return lax.ppermute(value, 'dp', SWAP)  3.51 us
  transfers between devices with their start and end apart: 19, of which 15 were waited for; matrix products, arithmetic and copies ran while one was open for 0% of the time, Pallas kernels for 20%

profile of v1, /device:TPU:1, one launch (start us, length us, event | category | flops | bytes accessed | tf_op | source)
XLA Modules:
  0.0 83.0 jit_solution(14952049963745431640)
XLA Ops:
  1.9 1.5 %collective-permute-start = (bf16[144,768]{1,0:T(8,128)(2,1)S(1)}, bf16[144,768]{1,0:T(8,128)(2,1)S(1)}, u32[]{:S(2)}, u32[]{:S(2)}) collective-permute-start(bf16[144,768]{1,0:T(8,128)(2,1)S(1)} %get-tuple-element.25), channel_id=1, source_target_pairs={{0,1},{1,0},{2,3},{3,2},{4,5},{5,4},{6,7},{7,6},{8,9},{9,8},{10,11... | collective-permute-start | bytes 663560 | tf_op jit(solution)/shard_map/ppermute | solution.py:76
  4.5 2.9 %collective-permute-start.3 = (bf16[272,768]{1,0:T(8,128)(2,1)S(1)}, bf16[272,768]{1,0:T(8,128)(2,1)S(1)}, u32[]{:S(2)}, u32[]{:S(2)}) collective-permute-start(bf16[272,768]{1,0:T(8,128)(2,1)S(1)} %join.1.refs_0_.refs_9_), channel_id=1, source_target_pairs={{0,2},{1,7},{2,0},{3,5},{4,6},{5,3},{6,4},{7,1},{8,10},{9,15},{10,... | collective-permute-start | bytes 1253384 | tf_op jit(solution)/shard_map/ppermute | solution.py:72
  7.4 3.8 %collective-permute-start.2 = (bf16[272,768]{1,0:T(8,128)(2,1)S(1)}, bf16[272,768]{1,0:T(8,128)(2,1)S(1)}, u32[]{:S(2)}, u32[]{:S(2)}) collective-permute-start(bf16[272,768]{1,0:T(8,128)(2,1)S(1)} %join.1.refs_0_.refs_9_), channel_id=1, source_target_pairs={{0,8},{1,25},{2,10},{3,27},{4,12},{5,29},{6,14},{7,31},{8,0},{9,17... | collective-permute-start | bytes 1253384 | tf_op jit(solution)/shard_map/ppermute | solution.py:72
  11.2 2.5 %collective-permute-start.1 = (bf16[272,768]{1,0:T(8,128)(2,1)S(1)}, bf16[272,768]{1,0:T(8,128)(2,1)S(1)}, u32[]{:S(2)}, u32[]{:S(2)}) collective-permute-start(bf16[272,768]{1,0:T(8,128)(2,1)S(1)} %join.1.refs_0_.refs_9_), channel_id=1, source_target_pairs={{0,32},{1,97},{2,34},{3,99},{4,36},{5,101},{6,38},{7,103},{8,40},{... | collective-permute-start | bytes 1253384 | tf_op jit(solution)/shard_map/ppermute | solution.py:72
  13.7 2.9 %collective-permute-done.2.refs_2_.refs_9_ = bf16[272,768]{1,0:T(8,128)(2,1)S(1)} collective-permute-done((bf16[272,768]{1,0:T(8,128)(2,1)S(1)}, bf16[272,768]{1,0:T(8,128)(2,1)S(1)}, u32[]{:S(2)}, u32[]{:S(2)}) %collective-permute-start.2) | collective-permute-done | bytes 417824 | tf_op jit(solution)/shard_map/ppermute | solution.py:72
  16.6 2.7 %collective-permute-done.1.refs_1_.refs_9_ = bf16[272,768]{1,0:T(8,128)(2,1)S(1)} collective-permute-done((bf16[272,768]{1,0:T(8,128)(2,1)S(1)}, bf16[272,768]{1,0:T(8,128)(2,1)S(1)}, u32[]{:S(2)}, u32[]{:S(2)}) %collective-permute-start.1) | collective-permute-done | bytes 417824 | tf_op jit(solution)/shard_map/ppermute | solution.py:72
  19.6 2.6 %collective-permute-start.6 = (bf16[272,768]{1,0:T(8,128)(2,1)S(1)}, bf16[272,768]{1,0:T(8,128)(2,1)S(1)}, u32[]{:S(2)}, u32[]{:S(2)}) collective-permute-start(bf16[272,768]{1,0:T(8,128)(2,1)S(1)} %collective-permute-done.2.refs_2_.refs_9_), channel_id=1, source_target_pairs={{0,32},{1,97},{2,34},{3,99},{4,36},{5,101},{6,38},{7,103},{8,40},{... | collective-permute-start | bytes 1253384 | tf_op jit(solution)/shard_map/ppermute | solution.py:72
  22.1 1.3 %collective-permute-start.7 = (bf16[272,768]{1,0:T(8,128)(2,1)S(1)}, bf16[272,768]{1,0:T(8,128)(2,1)S(1)}, u32[]{:S(2)}, u32[]{:S(2)}) collective-permute-start(bf16[272,768]{1,0:T(8,128)(2,1)S(1)} %collective-permute-done.1.refs_1_.refs_9_), channel_id=1, source_target_pairs={{0,2},{1,7},{2,0},{3,5},{4,6},{5,3},{6,4},{7,1},{8,10},{9,15},{10,... | collective-permute-start | bytes 1253384 | tf_op jit(solution)/shard_map/ppermute | solution.py:72
  23.4 2.0 %tile_0.1 = (f32[1024,1024]{1,0:T(8,128)S(1)}, f32[1024,128]{1,0:T(8,128)S(1)}, f32[16,1024]{1,0:T(8,128)S(1)}) custom-call(bf16[272,768]{1,0:T(8,128)(2,1)S(1)} %join.1.refs_0_.refs_9_, bf16[272,768]{1,0:T(8,128)(2,1)S(1)} %collective-permute-done.1.refs_1_.refs_9_, bf16[272,768]{1,0:T(8,128)(2,1)S(1)} %collective-permute-done.2.refs_2_.refs_9_, ...), custom_call_target="tpu_custom_call" | custom-call | tf_op jit(solution)/shard_map/tile_0/pallas_call | solution.py:89
  25.4 2.2 %collective-permute-done.5.refs_0_.refs_4_.refs_9_ = bf16[272,768]{1,0:T(8,128)(2,1)S(1)} collective-permute-done((bf16[272,768]{1,0:T(8,128)(2,1)S(1)}, bf16[272,768]{1,0:T(8,128)(2,1)S(1)}, u32[]{:S(2)}, u32[]{:S(2)}) %collective-permute-start.5) | collective-permute-done | bytes 417824 | tf_op jit(solution)/shard_map/ppermute | solution.py:72
  27.8 2.5 %collective-permute-done.7.refs_2_.refs_6_.refs_9_ = bf16[272,768]{1,0:T(8,128)(2,1)S(1)} collective-permute-done((bf16[272,768]{1,0:T(8,128)(2,1)S(1)}, bf16[272,768]{1,0:T(8,128)(2,1)S(1)}, u32[]{:S(2)}, u32[]{:S(2)}) %collective-permute-start.7) | collective-permute-done | bytes 417824 | tf_op jit(solution)/shard_map/ppermute | solution.py:72
  30.7 1.6 %tile_1.1 = (f32[768,1024]{1,0:T(8,128)S(1)}, f32[768,128]{1,0:T(8,128)S(1)}, f32[16,1024]{1,0:T(8,128)S(1)}) custom-call(bf16[272,768]{1,0:T(8,128)(2,1)S(1)} %collective-permute-done.5.refs_0_.refs_4_.refs_9_, bf16[272,768]{1,0:T(8,128)(2,1)S(1)} %collective-permute-done.6.refs_1_.refs_5_.refs_9_, ...), custom_call_target="tpu_custom_call" | custom-call | tf_op jit(solution)/shard_map/tile_1/pallas_call | solution.py:89
  33.3 2.5 %tile_2.1 = (f32[1792,768]{1,0:T(8,128)S(1)}, f32[1792,128]{1,0:T(8,128)S(1)}, f32[16,768]{1,0:T(8,128)S(1)}) custom-call(bf16[272,768]{1,0:T(8,128)(2,1)S(1)} %join.1.refs_0_.refs_9_, bf16[272,768]{1,0:T(8,128)(2,1)S(1)} %collective-permute-done.1.refs_1_.refs_9_, bf16[272,768]{1,0:T(8,128)(2,1)S(1)} %collective-permute-done.2.refs_2_.refs_9_, ...), custom_call_target="tpu_custom_call" | custom-call | tf_op jit(solution)/shard_map/tile_2/pallas_call | solution.py:89
  35.9 2.7 %collective-permute-done.9.refs_0_.refs_7_.refs_9_ = bf16[272,768]{1,0:T(8,128)(2,1)S(1)} collective-permute-done((bf16[272,768]{1,0:T(8,128)(2,1)S(1)}, bf16[272,768]{1,0:T(8,128)(2,1)S(1)}, u32[]{:S(2)}, u32[]{:S(2)}) %collective-permute-start.9) | collective-permute-done | bytes 417824 | tf_op jit(solution)/shard_map/ppermute | solution.py:72
  41.7 7.6 %all_to_all.5.refs_0_ = f32[8,32,128]{2,1,0:T(8,128)S(1)} all-to-all(f32[8,32,128]{2,1,0:T(8,128)S(1)} %get-tuple-element.39), channel_id=1, replica_groups={{0,2,8,10,32,34,40,42},{4,6,12,14,36,38,44,46},{16,18,24,26,48,50,56,58..., dimensions={0} | all-to-all | bytes 262144 | tf_op jit(solution)/shard_map/all_to_all | solution.py:446
  49.4 1.4 %grad_7.1 = s16[272,768]{1,0:T(8,128)(2,1)S(1)} custom-call(f32[1024,1024]{1,0:T(8,128)S(1)} %get-tuple-element.26.refs_0_, f32[768,1024]{1,0:T(8,128)S(1)} %get-tuple-element.27.refs_1_, f32[1792,768]{1,0:T(8,128)S(1)} %get-tuple-element.30.refs_2_, f32[256,1792]{1,0:T(8,128)S(1)} %get-tuple-element.31.refs_3_, f32[2048,256]{1,0:T(8,128)S(1)} %get-tuple-element.38.refs_4_, ...), custom_call_target="tpu_custom_call" | custom-call | tf_op jit(solution)/shard_map/grad_7/pallas_call | solution.py:89
  52.0 1.4 %grad_6.1 = s16[272,768]{1,0:T(8,128)(2,1)S(1)} custom-call(f32[1024,1024]{1,0:T(8,128)S(1)} %get-tuple-element.26.refs_0_, f32[768,1024]{1,0:T(8,128)S(1)} %get-tuple-element.27.refs_1_, f32[1792,768]{1,0:T(8,128)S(1)} %get-tuple-element.30.refs_2_, f32[256,1792]{1,0:T(8,128)S(1)} %get-tuple-element.31.refs_3_, f32[2048,256]{1,0:T(8,128)S(1)} %get-tuple-element.38.refs_4_, ...), custom_call_target="tpu_custom_call" | custom-call | tf_op jit(solution)/shard_map/grad_6/pallas_call | solution.py:89
  54.1 1.4 %grad_5.1 = s16[272,768]{1,0:T(8,128)(2,1)S(1)} custom-call(f32[1024,1024]{1,0:T(8,128)S(1)} %get-tuple-element.26.refs_0_, f32[768,1024]{1,0:T(8,128)S(1)} %get-tuple-element.27.refs_1_, f32[1792,768]{1,0:T(8,128)S(1)} %get-tuple-element.30.refs_2_, f32[256,1792]{1,0:T(8,128)S(1)} %get-tuple-element.31.refs_3_, f32[2048,256]{1,0:T(8,128)S(1)} %get-tuple-element.38.refs_4_, ...), custom_call_target="tpu_custom_call" | custom-call | tf_op jit(solution)/shard_map/grad_5/pallas_call | solution.py:89
  55.6 1.2 %collective-permute-start.16 = (s16[272,768]{1,0:T(8,128)(2,1)S(1)}, s16[272,768]{1,0:T(8,128)(2,1)S(1)}, u32[]{:S(2)}, u32[]{:S(2)}) collective-permute-start(s16[272,768]{1,0:T(8,128)(2,1)S(1)} %grad_5.1), channel_id=1, source_target_pairs={{0,2},{1,7},{2,0},{3,5},{4,6},{5,3},{6,4},{7,1},{8,10},{9,15},{10,... | collective-permute-start | bytes 1253384 | tf_op jit(solution)/shard_map/ppermute | solution.py:72
  56.8 2.2 %collective-permute-done.11.refs_10_ = s16[272,768]{1,0:T(8,128)(2,1)S(1)} collective-permute-done((s16[272,768]{1,0:T(8,128)(2,1)S(1)}, s16[272,768]{1,0:T(8,128)(2,1)S(1)}, u32[]{:S(2)}, u32[]{:S(2)}) %collective-permute-start.11) | collective-permute-done | bytes 417824 | tf_op jit(solution)/shard_map/ppermute | solution.py:72
  59.1 1.4 %grad_3.1 = s16[272,768]{1,0:T(8,128)(2,1)S(1)} custom-call(f32[1024,1024]{1,0:T(8,128)S(1)} %get-tuple-element.26.refs_0_, f32[768,1024]{1,0:T(8,128)S(1)} %get-tuple-element.27.refs_1_, f32[1792,768]{1,0:T(8,128)S(1)} %get-tuple-element.30.refs_2_, f32[256,1792]{1,0:T(8,128)S(1)} %get-tuple-element.31.refs_3_, f32[2048,256]{1,0:T(8,128)S(1)} %get-tuple-element.38.refs_4_, ...), custom_call_target="tpu_custom_call" | custom-call | tf_op jit(solution)/shard_map/grad_3/pallas_call | solution.py:89
  60.5 1.3 %collective-permute-start.12 = (s16[272,768]{1,0:T(8,128)(2,1)S(1)}, s16[272,768]{1,0:T(8,128)(2,1)S(1)}, u32[]{:S(2)}, u32[]{:S(2)}) collective-permute-start(s16[272,768]{1,0:T(8,128)(2,1)S(1)} %grad_3.1), channel_id=1, source_target_pairs={{0,8},{1,25},{2,10},{3,27},{4,12},{5,29},{6,14},{7,31},{8,0},{9,17... | collective-permute-start | bytes 1253384 | tf_op jit(solution)/shard_map/ppermute | solution.py:72
  61.8 1.4 %grad_2.1 = s16[272,768]{1,0:T(8,128)(2,1)S(1)} custom-call(f32[1024,1024]{1,0:T(8,128)S(1)} %get-tuple-element.26.refs_0_, f32[768,1024]{1,0:T(8,128)S(1)} %get-tuple-element.27.refs_1_, f32[1792,768]{1,0:T(8,128)S(1)} %get-tuple-element.30.refs_2_, f32[256,1792]{1,0:T(8,128)S(1)} %get-tuple-element.31.refs_3_, f32[2048,256]{1,0:T(8,128)S(1)} %get-tuple-element.38.refs_4_, ...), custom_call_target="tpu_custom_call" | custom-call | tf_op jit(solution)/shard_map/grad_2/pallas_call | solution.py:89
  63.3 1.5 %collective-permute-start.14 = (s16[272,768]{1,0:T(8,128)(2,1)S(1)}, s16[272,768]{1,0:T(8,128)(2,1)S(1)}, u32[]{:S(2)}, u32[]{:S(2)}) collective-permute-start(s16[272,768]{1,0:T(8,128)(2,1)S(1)} %grad_2.1), channel_id=1, source_target_pairs={{0,8},{1,25},{2,10},{3,27},{4,12},{5,29},{6,14},{7,31},{8,0},{9,17... | collective-permute-start | bytes 1253384 | tf_op jit(solution)/shard_map/ppermute | solution.py:72
  64.8 1.5 %grad_4.1 = s16[272,768]{1,0:T(8,128)(2,1)S(1)} custom-call(f32[1024,1024]{1,0:T(8,128)S(1)} %get-tuple-element.26.refs_0_, f32[768,1024]{1,0:T(8,128)S(1)} %get-tuple-element.27.refs_1_, f32[1792,768]{1,0:T(8,128)S(1)} %get-tuple-element.30.refs_2_, f32[256,1792]{1,0:T(8,128)S(1)} %get-tuple-element.31.refs_3_, f32[2048,256]{1,0:T(8,128)S(1)} %get-tuple-element.38.refs_4_, ...), custom_call_target="tpu_custom_call" | custom-call | tf_op jit(solution)/shard_map/grad_4/pallas_call | solution.py:89
  66.3 1.3 %collective-permute-start.17 = (s16[272,768]{1,0:T(8,128)(2,1)S(1)}, s16[272,768]{1,0:T(8,128)(2,1)S(1)}, u32[]{:S(2)}, u32[]{:S(2)}) collective-permute-start(s16[272,768]{1,0:T(8,128)(2,1)S(1)} %grad_4.1), channel_id=1, source_target_pairs={{0,32},{1,97},{2,34},{3,99},{4,36},{5,101},{6,38},{7,103},{8,40},{... | collective-permute-start | bytes 1253384 | tf_op jit(solution)/shard_map/ppermute | solution.py:72
  68.7 1.4 %grad_1.1 = s16[272,768]{1,0:T(8,128)(2,1)S(1)} custom-call(f32[1024,1024]{1,0:T(8,128)S(1)} %get-tuple-element.26.refs_0_, f32[768,1024]{1,0:T(8,128)S(1)} %get-tuple-element.27.refs_1_, f32[1792,768]{1,0:T(8,128)S(1)} %get-tuple-element.30.refs_2_, f32[256,1792]{1,0:T(8,128)S(1)} %get-tuple-element.31.refs_3_, f32[2048,256]{1,0:T(8,128)S(1)} %get-tuple-element.38.refs_4_, ...), custom_call_target="tpu_custom_call" | custom-call | tf_op jit(solution)/shard_map/grad_1/pallas_call | solution.py:89
  71.8 1.3 %collective-permute-done.14.refs_2_ = s16[272,768]{1,0:T(8,128)(2,1)S(1)} collective-permute-done((s16[272,768]{1,0:T(8,128)(2,1)S(1)}, s16[272,768]{1,0:T(8,128)(2,1)S(1)}, u32[]{:S(2)}, u32[]{:S(2)}) %collective-permute-start.14) | collective-permute-done | bytes 417824 | tf_op jit(solution)/shard_map/ppermute | solution.py:72
  73.2 1.3 %collective-permute-done.17.refs_3_ = s16[272,768]{1,0:T(8,128)(2,1)S(1)} collective-permute-done((s16[272,768]{1,0:T(8,128)(2,1)S(1)}, s16[272,768]{1,0:T(8,128)(2,1)S(1)}, u32[]{:S(2)}, u32[]{:S(2)}) %collective-permute-start.17) | collective-permute-done | bytes 417824 | tf_op jit(solution)/shard_map/ppermute | solution.py:72
  74.5 4.0 %collective-permute-done.13.refs_1_ = s16[272,768]{1,0:T(8,128)(2,1)S(1)} collective-permute-done((s16[272,768]{1,0:T(8,128)(2,1)S(1)}, s16[272,768]{1,0:T(8,128)(2,1)S(1)}, u32[]{:S(2)}, u32[]{:S(2)}) %collective-permute-start.13) | collective-permute-done | bytes 417824 | tf_op jit(solution)/shard_map/ppermute | solution.py:72
  79.0 1.4 %collective-permute-start.18 = (f32[136,768]{1,0:T(8,128)S(1)}, f32[136,768]{1,0:T(8,128)S(1)}, u32[]{:S(2)}, u32[]{:S(2)}) collective-permute-start(f32[136,768]{1,0:T(8,128)S(1)} %get-tuple-element.41), channel_id=1, source_target_pairs={{0,1},{1,0},{2,3},{3,2},{4,5},{5,4},{6,7},{7,6},{8,9},{9,8},{10,11... | collective-permute-start | bytes 1253384 | tf_op jit(solution)/shard_map/ppermute | solution.py:76
  80.4 1.4 %collective-permute-done.18.refs_3_ = f32[136,768]{1,0:T(8,128)S(1)} collective-permute-done((f32[136,768]{1,0:T(8,128)S(1)}, f32[136,768]{1,0:T(8,128)S(1)}, u32[]{:S(2)}, u32[]{:S(2)}) %collective-permute-start.18) | collective-permute-done | bytes 417824 | tf_op jit(solution)/shard_map/ppermute | solution.py:76
  (32 shorter events, 13.7 us)
Async XLA Ops:
  1.9 2.6 %collective-permute-start = (bf16[144,768]{1,0:T(8,128)(2,1)S(1)}, bf16[144,768]{1,0:T(8,128)(2,1)S(1)}, u32[]{:S(2)}, u32[]{:S(2)}) collective-permute-start(bf16[144,768]{1,0:T(8,128)(2,1)S(1)} %get-tuple-element.25), channel_id=1, source_target_pairs={{0,1},{1,0},{2,3},{3,2},{4,5},{5,4},{6,7},{7,6},{8,9},{9,8},{10,11... | collective-permute-start | bytes 663560 | tf_op jit(solution)/shard_map/ppermute | solution.py:76
  4.5 9.1 %collective-permute-start.3 = (bf16[272,768]{1,0:T(8,128)(2,1)S(1)}, bf16[272,768]{1,0:T(8,128)(2,1)S(1)}, u32[]{:S(2)}, u32[]{:S(2)}) collective-permute-start(bf16[272,768]{1,0:T(8,128)(2,1)S(1)} %join.1.refs_0_.refs_9_), channel_id=1, source_target_pairs={{0,2},{1,7},{2,0},{3,5},{4,6},{5,3},{6,4},{7,1},{8,10},{9,15},{10,... | collective-permute-start | bytes 1253384 | tf_op jit(solution)/shard_map/ppermute | solution.py:72
  7.4 9.2 %collective-permute-start.2 = (bf16[272,768]{1,0:T(8,128)(2,1)S(1)}, bf16[272,768]{1,0:T(8,128)(2,1)S(1)}, u32[]{:S(2)}, u32[]{:S(2)}) collective-permute-start(bf16[272,768]{1,0:T(8,128)(2,1)S(1)} %join.1.refs_0_.refs_9_), channel_id=1, source_target_pairs={{0,8},{1,25},{2,10},{3,27},{4,12},{5,29},{6,14},{7,31},{8,0},{9,17... | collective-permute-start | bytes 1253384 | tf_op jit(solution)/shard_map/ppermute | solution.py:72
  11.2 8.1 %collective-permute-start.1 = (bf16[272,768]{1,0:T(8,128)(2,1)S(1)}, bf16[272,768]{1,0:T(8,128)(2,1)S(1)}, u32[]{:S(2)}, u32[]{:S(2)}) collective-permute-start(bf16[272,768]{1,0:T(8,128)(2,1)S(1)} %join.1.refs_0_.refs_9_), channel_id=1, source_target_pairs={{0,32},{1,97},{2,34},{3,99},{4,36},{5,101},{6,38},{7,103},{8,40},{... | collective-permute-start | bytes 1253384 | tf_op jit(solution)/shard_map/ppermute | solution.py:72
  19.4 4.0 %collective-permute-start.4 = (bf16[1088,768]{1,0:T(8,128)(2,1)S(1)}, bf16[1088,768]{1,0:T(8,128)(2,1)S(1)}, u32[]{:S(2)}, u32[]{:S(2)}) collective-permute-start(bf16[1088,768]{1,0:T(8,128)(2,1)S(1)} %pack_near.1), channel_id=1, source_target_pairs={{0,1},{1,0},{2,3},{3,2},{4,5},{5,4},{6,7},{7,6},{8,9},{9,8},{10,11... | collective-permute-start | bytes 5013512 | tf_op jit(solution)/shard_map/ppermute | solution.py:76
  19.5 8.2 %collective-permute-start.5 = (bf16[272,768]{1,0:T(8,128)(2,1)S(1)}, bf16[272,768]{1,0:T(8,128)(2,1)S(1)}, u32[]{:S(2)}, u32[]{:S(2)}) collective-permute-start(bf16[272,768]{1,0:T(8,128)(2,1)S(1)} %collective-permute-done.3.refs_3_.refs_9_), channel_id=1, source_target_pairs={{0,8},{1,25},{2,10},{3,27},{4,12},{5,29},{6,14},{7,31},{8,0},{9,17... | collective-permute-start | bytes 1253384 | tf_op jit(solution)/shard_map/ppermute | solution.py:72
  19.6 8.2 %collective-permute-start.6 = (bf16[272,768]{1,0:T(8,128)(2,1)S(1)}, bf16[272,768]{1,0:T(8,128)(2,1)S(1)}, u32[]{:S(2)}, u32[]{:S(2)}) collective-permute-start(bf16[272,768]{1,0:T(8,128)(2,1)S(1)} %collective-permute-done.2.refs_2_.refs_9_), channel_id=1, source_target_pairs={{0,32},{1,97},{2,34},{3,99},{4,36},{5,101},{6,38},{7,103},{8,40},{... | collective-permute-start | bytes 1253384 | tf_op jit(solution)/shard_map/ppermute | solution.py:72
  22.1 8.1 %collective-permute-start.7 = (bf16[272,768]{1,0:T(8,128)(2,1)S(1)}, bf16[272,768]{1,0:T(8,128)(2,1)S(1)}, u32[]{:S(2)}, u32[]{:S(2)}) collective-permute-start(bf16[272,768]{1,0:T(8,128)(2,1)S(1)} %collective-permute-done.1.refs_1_.refs_9_), channel_id=1, source_target_pairs={{0,2},{1,7},{2,0},{3,5},{4,6},{5,3},{6,4},{7,1},{8,10},{9,15},{10,... | collective-permute-start | bytes 1253384 | tf_op jit(solution)/shard_map/ppermute | solution.py:72
  30.3 3.0 %collective-permute-start.8 = (bf16[816,768]{1,0:T(8,128)(2,1)S(1)}, bf16[816,768]{1,0:T(8,128)(2,1)S(1)}, u32[]{:S(2)}, u32[]{:S(2)}) collective-permute-start(bf16[816,768]{1,0:T(8,128)(2,1)S(1)} %pack_sides.1), channel_id=1, source_target_pairs={{0,1},{1,0},{2,3},{3,2},{4,5},{5,4},{6,7},{7,6},{8,9},{9,8},{10,11... | collective-permute-start | bytes 3760136 | tf_op jit(solution)/shard_map/ppermute | solution.py:76
  30.4 8.2 %collective-permute-start.9 = (bf16[272,768]{1,0:T(8,128)(2,1)S(1)}, bf16[272,768]{1,0:T(8,128)(2,1)S(1)}, u32[]{:S(2)}, u32[]{:S(2)}) collective-permute-start(bf16[272,768]{1,0:T(8,128)(2,1)S(1)} %collective-permute-done.5.refs_0_.refs_4_.refs_9_), channel_id=1, source_target_pairs={{0,32},{1,97},{2,34},{3,99},{4,36},{5,101},{6,38},{7,103},{8,40},{... | collective-permute-start | bytes 1253384 | tf_op jit(solution)/shard_map/ppermute | solution.py:72
  38.6 1.8 %collective-permute-start.10 = (bf16[272,768]{1,0:T(8,128)(2,1)S(1)}, bf16[272,768]{1,0:T(8,128)(2,1)S(1)}, u32[]{:S(2)}, u32[]{:S(2)}) collective-permute-start(bf16[272,768]{1,0:T(8,128)(2,1)S(1)} %pack_corner.1), channel_id=1, source_target_pairs={{0,1},{1,0},{2,3},{3,2},{4,5},{5,4},{6,7},{7,6},{8,9},{9,8},{10,11... | collective-permute-start | bytes 1253384 | tf_op jit(solution)/shard_map/ppermute | solution.py:76
  50.9 8.2 %collective-permute-start.11 = (s16[272,768]{1,0:T(8,128)(2,1)S(1)}, s16[272,768]{1,0:T(8,128)(2,1)S(1)}, u32[]{:S(2)}, u32[]{:S(2)}) collective-permute-start(s16[272,768]{1,0:T(8,128)(2,1)S(1)} %grad_7.1), channel_id=1, source_target_pairs={{0,32},{1,97},{2,34},{3,99},{4,36},{5,101},{6,38},{7,103},{8,40},{... | collective-permute-start | bytes 1253384 | tf_op jit(solution)/shard_map/ppermute | solution.py:72
  53.4 11.4 %collective-permute-start.15 = (s16[272,768]{1,0:T(8,128)(2,1)S(1)}, s16[272,768]{1,0:T(8,128)(2,1)S(1)}, u32[]{:S(2)}, u32[]{:S(2)}) collective-permute-start(s16[272,768]{1,0:T(8,128)(2,1)S(1)} %grad_6.1), channel_id=1, source_target_pairs={{0,8},{1,25},{2,10},{3,27},{4,12},{5,29},{6,14},{7,31},{8,0},{9,17... | collective-permute-start | bytes 1253384 | tf_op jit(solution)/shard_map/ppermute | solution.py:72
  55.6 9.2 %collective-permute-start.16 = (s16[272,768]{1,0:T(8,128)(2,1)S(1)}, s16[272,768]{1,0:T(8,128)(2,1)S(1)}, u32[]{:S(2)}, u32[]{:S(2)}) collective-permute-start(s16[272,768]{1,0:T(8,128)(2,1)S(1)} %grad_5.1), channel_id=1, source_target_pairs={{0,2},{1,7},{2,0},{3,5},{4,6},{5,3},{6,4},{7,1},{8,10},{9,15},{10,... | collective-permute-start | bytes 1253384 | tf_op jit(solution)/shard_map/ppermute | solution.py:72
  60.5 8.2 %collective-permute-start.12 = (s16[272,768]{1,0:T(8,128)(2,1)S(1)}, s16[272,768]{1,0:T(8,128)(2,1)S(1)}, u32[]{:S(2)}, u32[]{:S(2)}) collective-permute-start(s16[272,768]{1,0:T(8,128)(2,1)S(1)} %grad_3.1), channel_id=1, source_target_pairs={{0,8},{1,25},{2,10},{3,27},{4,12},{5,29},{6,14},{7,31},{8,0},{9,17... | collective-permute-start | bytes 1253384 | tf_op jit(solution)/shard_map/ppermute | solution.py:72
  63.3 9.9 %collective-permute-start.14 = (s16[272,768]{1,0:T(8,128)(2,1)S(1)}, s16[272,768]{1,0:T(8,128)(2,1)S(1)}, u32[]{:S(2)}, u32[]{:S(2)}) collective-permute-start(s16[272,768]{1,0:T(8,128)(2,1)S(1)} %grad_2.1), channel_id=1, source_target_pairs={{0,8},{1,25},{2,10},{3,27},{4,12},{5,29},{6,14},{7,31},{8,0},{9,17... | collective-permute-start | bytes 1253384 | tf_op jit(solution)/shard_map/ppermute | solution.py:72
  66.3 8.2 %collective-permute-start.17 = (s16[272,768]{1,0:T(8,128)(2,1)S(1)}, s16[272,768]{1,0:T(8,128)(2,1)S(1)}, u32[]{:S(2)}, u32[]{:S(2)}) collective-permute-start(s16[272,768]{1,0:T(8,128)(2,1)S(1)} %grad_4.1), channel_id=1, source_target_pairs={{0,32},{1,97},{2,34},{3,99},{4,36},{5,101},{6,38},{7,103},{8,40},{... | collective-permute-start | bytes 1253384 | tf_op jit(solution)/shard_map/ppermute | solution.py:72
  70.1 8.4 %collective-permute-start.13 = (s16[272,768]{1,0:T(8,128)(2,1)S(1)}, s16[272,768]{1,0:T(8,128)(2,1)S(1)}, u32[]{:S(2)}, u32[]{:S(2)}) collective-permute-start(s16[272,768]{1,0:T(8,128)(2,1)S(1)} %grad_1.1), channel_id=1, source_target_pairs={{0,2},{1,7},{2,0},{3,5},{4,6},{5,3},{6,4},{7,1},{8,10},{9,15},{10,... | collective-permute-start | bytes 1253384 | tf_op jit(solution)/shard_map/ppermute | solution.py:72
  71.8 9.9 %copy-start = (bf16[128,768]{1,0:T(8,128)(2,1)S(1)}, bf16[128,768]{1,0:T(8,128)(2,1)}, u32[]{:S(2)}) copy-start(bf16[128,768]{1,0:T(8,128)(2,1)} %refs_0_.1) | copy-start | bytes 589828
  71.8 9.9 %copy-start.1 = (bf16[128,768]{1,0:T(8,128)(2,1)S(1)}, bf16[128,768]{1,0:T(8,128)(2,1)}, u32[]{:S(2)}) copy-start(bf16[128,768]{1,0:T(8,128)(2,1)} %refs_1_.1) | copy-start | bytes 589828
  79.0 2.8 %collective-permute-start.18 = (f32[136,768]{1,0:T(8,128)S(1)}, f32[136,768]{1,0:T(8,128)S(1)}, u32[]{:S(2)}, u32[]{:S(2)}) collective-permute-start(f32[136,768]{1,0:T(8,128)S(1)} %get-tuple-element.41), channel_id=1, source_target_pairs={{0,1},{1,0},{2,3},{3,2},{4,5},{5,4},{6,7},{7,6},{8,9},{9,8},{10,11... | collective-permute-start | bytes 1253384 | tf_op jit(solution)/shard_map/ppermute | solution.py:76

commit v2 on v1

--- a/solution.py
+++ b/solution.py
@@ -22,16 +22,14 @@
 LOG2E = 1.4426950408889634
 FULL = 32760.0
 NEAR = (0, 4, 2, 1)
-SIDES = (3, 6, 5)
-CORNER = (7,)
-PACKS = (NEAR, SIDES, CORNER)
-ALL = NEAR + SIDES + CORNER
+FAR = (7, 3, 6, 5)
+PACKS = (NEAR, FAR[:2], FAR[2:])
+ALL = NEAR + FAR
 PARTS = (
-    (NEAR, NEAR),
-    (SIDES, NEAR),
-    (NEAR + SIDES, SIDES),
-    (CORNER, NEAR + SIDES),
-    (ALL, CORNER),
+    (NEAR, NEAR, ()),
+    (FAR, NEAR, ()),
+    (ALL, FAR[:2], ()),
+    (ALL, FAR[2:], ()),
 )
 SPAN = BLOCK + PAD
 F32 = jnp.float32
@@ -184,8 +182,13 @@
     ]
 
 
+def has(part, row, column):
+    rows, columns, known = PARTS[part]
+    return row in rows and column in columns and not (row in known and column in known)
+
+
 def tile_kernel(part, *refs):
-    rows, columns = PARTS[part]
+    rows, columns, _ = PARTS[part]
     last = part == len(PARTS) - 1
     used, where = packs_of(columns)
     x, refs = refs[: len(rows)], refs[len(rows) :]
@@ -196,10 +199,13 @@
     else:
         e_ref, rowsum_ref, colsum_ref = refs
     ids_of_columns = [row_ids(y[p], at) for p, at in where]
-    for i in range(len(rows)):
+    begun = set()
+    for i, number in enumerate(rows):
         ids = down_rows(row_ids(x[i]), BLOCK)
         partial = None
         for k, (p, start) in enumerate(where):
+            if not has(part, number, columns[k]):
+                continue
             dots = lax.dot_general(
                 x[i][:BLOCK, :],
                 y[p][start : start + BLOCK, :],
@@ -216,7 +222,8 @@
             for n, value in enumerate((e, hit)):
                 value = jnp.sum(value.reshape(BLOCK // 8, 8, BLOCK), axis=0)
                 to = slice(n * 8, n * 8 + 8)
-                colsum_ref[to, at] = value if i == 0 else colsum_ref[to, at] + value
+                colsum_ref[to, at] = colsum_ref[to, at] + value if k in begun else value
+            begun.add(k)
         rowsum_ref[i * BLOCK : (i + 1) * BLOCK, :] = partial
 
     if last:
@@ -233,7 +240,7 @@
         def _():
             for number in ALL:
                 total = None
-                for (these, _), (ref, _) in zip(PARTS, sums):
+                for (these, _, _), (ref, _) in zip(PARTS, sums):
                     if number in these:
                         at = these.index(number) * BLOCK
                         piece = ref[at : at + BLOCK, :]
@@ -246,7 +253,7 @@
             for number in ALL:
                 for n in range(2):
                     total = None
-                    for (_, these), (_, ref) in zip(PARTS, sums):
+                    for (_, these, _), (_, ref) in zip(PARTS, sums):
                         if number in these:
                             at = these.index(number) * BLOCK
                             piece = ref[n * 8 : n * 8 + 8, at : at + BLOCK]
@@ -323,14 +330,14 @@
                 rows.index(number) * BLOCK : (rows.index(number) + 1) * BLOCK,
                 columns.index(column) * BLOCK : (columns.index(column) + 1) * BLOCK,
             ]
-            for (rows, columns), ref in zip(PARTS, exps)
-            if number in rows and column in columns
+            for part, ((rows, columns, _), ref) in enumerate(zip(PARTS, exps))
+            if has(part, number, column)
         ]
         along = jnp.where(role == 1, scale_of(column), 1.0)
         hit = jnp.where(ids == row_ids(y[p], start), 1.0, 0.0)
         weights = (e * down * along - hit).astype(BF16)
-        part = jnp.dot(weights, y[p][start : start + BLOCK, :], preferred_element_type=F32)
-        acc = part if acc is None else acc + part
+        piece = jnp.dot(weights, y[p][start : start + BLOCK, :], preferred_element_type=F32)
+        acc = piece if acc is None else acc + piece
     value = 20.0 * acc
     for ref in come:
         value = value + decode(ref)
@@ -342,9 +349,9 @@
         out_ref[BLOCK:, :] = jnp.full((LOSS, WIDTH), loss, F32)
 
 
-def split_kernel(own_ref, a_ref, b_ref, c_ref, keep_ref, send_ref):
+def split_kernel(own_ref, a_ref, b_ref, c_ref, d_ref, keep_ref, send_ref):
     value, loss = own_ref[:BLOCK, :], own_ref[BLOCK, 0]
-    for ref in (a_ref, b_ref, c_ref):
+    for ref in (a_ref, b_ref, c_ref, d_ref):
         value = value + decode(ref)
         loss = loss + loss_of(ref)
     role = role_of()
@@ -407,17 +414,17 @@
         return call(pack_kernel, name, shape, *[near(x[n]) for n in blocks], after=after)
 
     x = {0: own}
+    x[7] = send(own, 7)
     for bits in (4, 2, 1):
         x[bits] = send(own, bits)
     x[3] = send(x[1], 2)
     x[6] = send(x[2], 4)
     x[5] = send(x[4], 1)
-    x[7] = send(x[3], 4)
     y = [swap(pack(NEAR, "pack_near"))]
     parts = []
 
     def tile(part, name, after=()):
-        rows, columns = PARTS[part]
+        rows, columns, _ = PARTS[part]
         used, _ = packs_of(columns)
         last = part == len(PARTS) - 1
         e = pltpu.VMEM((len(rows) * BLOCK, len(columns) * BLOCK), F32)
@@ -437,12 +444,11 @@
         )
 
     tile(0, "tile_0")
-    y.append(swap(pack(SIDES, "pack_sides", after=[parts[0][1]])))
-    tile(1, "tile_1")
+    y.append(swap(pack(FAR[:2], "pack_first", after=[parts[0][1]])))
+    y.append(swap(pack(FAR[2:], "pack_second")))
+    tile(1, "tile_1", [parts[0][1]])
     tile(2, "tile_2", [parts[1][1]])
-    y.append(swap(pack(CORNER, "pack_corner", after=[parts[2][1]])))
     tile(3, "tile_3")
-    tile(4, "tile_4")
     stats = lax.all_to_all(parts[-1][1], "dp", 0, 0, axis_index_groups=SUM_GROUPS, tiled=True)
     scales = call(scale_kernel, "scales", pltpu.VMEM((HALF + 8, 128), F32), near(stats))
 
@@ -462,23 +468,23 @@
             after=after,
         )
 
-    g7 = grad(7)
-    r7 = send(g7, 4)
+    g3 = grad(3)
+    r3 = send(g3, 2)
     g6 = grad(6)
-    r6 = send(g6, 2)
+    r6 = send(g6, 4)
     g5 = grad(5)
     r5 = send(g5, 1)
-    g3 = grad(3, r7)
-    r3 = send(g3, 2)
-    g4 = grad(4, r6, r5)
-    r4 = send(g4, 4)
-    g2 = grad(2)
-    r2 = send(g2, 2)
+    g7 = grad(7)
+    r7 = send(g7, 7)
     g1 = grad(1, r3)
     r1 = send(g1, 1)
+    g2 = grad(2, r6)
+    r2 = send(g2, 2)
+    g4 = grad(4, r5)
+    r4 = send(g4, 4)
     g0 = grad(0, shape=plain)
     part = pltpu.VMEM((ROWS + LOSS, WIDTH), F32)
-    keep, give = call(split_kernel, "split", [part, part], *[near(v) for v in (g0, r1, r2, r4)])
+    keep, give = call(split_kernel, "split", [part, part], *[near(v) for v in (g0, r7, r1, r2, r4)])
     come = swap(give)
     loss, gq, gd = call(
         post_kernel,

time: 83.1 us -> 82.8 us (level)
  starting transfers between devices: 24.6 us -> 32.2 us
  waiting for transfers between devices: 27.1 us -> 19.6 us
    ppermute x14, starting transfers between devices: 21.1 us -> 28.5 us  [send(): return lax.ppermute(value, 'dp', partners(bits))]
    ppermute x14, waiting for transfers between devices: 23.1 us -> 17.1 us  [send(): return lax.ppermute(value, 'dp', partners(bits))]
    ppermute x5, waiting for transfers between devices: 4.01 us -> 2.5 us  [swap(): return lax.ppermute(value, 'dp', SWAP)]
    pallas_call x20 -> x19, Pallas kernels: 21.6 us -> 21.3 us  [call(): pl.pallas_call(body, name=name, out_shape=out_shape, scratch_shapes=scrat...]
  transfers between devices with their start and end apart: 19 -> 19, of which waited for: 15 -> 9; matrix products, arithmetic and copies ran while one was open for 0% -> 0% of each run, Pallas kernels for 20% -> 19%
where the time goes in v2:
time: 82.8 us; the launch traced here: 82.6 us
  starting transfers between devices  32.2 us (39%)
  Pallas kernels  22.6 us (27%)
  waiting for transfers between devices  19.6 us (24%)
  blocking collectives  7.35 us (9%)
  between operations  0.85 us (1%)
    ppermute x14, starting transfers between devices, send(): return lax.ppermute(value, 'dp', partners(bits))  28.5 us
    pallas_call x19, Pallas kernels, call(): pl.pallas_call(body, name=name, out_shape=out_shape, scratch_shapes=scrat...  21.3 us
    ppermute x14, waiting for transfers between devices, send(): return lax.ppermute(value, 'dp', partners(bits))  17.1 us
    all_to_all x1, blocking collectives, local(): lax.all_to_all(parts[-1][1], 'dp', 0, 0, axis_index_groups=SUM_GROUPS, ti...  7.35 us
    ppermute x5, starting transfers between devices, swap(): return lax.ppermute(value, 'dp', SWAP)  3.72 us
    ppermute x5, waiting for transfers between devices, swap(): return lax.ppermute(value, 'dp', SWAP)  2.5 us
  transfers between devices with their start and end apart: 19, of which 9 were waited for; matrix products, arithmetic and copies ran while one was open for 0% of the time, Pallas kernels for 19%

profile of v2, /device:TPU:1, one launch (start us, length us, event | category | flops | bytes accessed | tf_op | source)
XLA Modules:
  0.0 82.6 jit_solution(13897397664313997787)
XLA Ops:
  1.9 1.5 %collective-permute-start = (bf16[144,768]{1,0:T(8,128)(2,1)S(1)}, bf16[144,768]{1,0:T(8,128)(2,1)S(1)}, u32[]{:S(2)}, u32[]{:S(2)}) collective-permute-start(bf16[144,768]{1,0:T(8,128)(2,1)S(1)} %get-tuple-element.22), channel_id=1, source_target_pairs={{0,1},{1,0},{2,3},{3,2},{4,5},{5,4},{6,7},{7,6},{8,9},{9,8},{10,11... | collective-permute-start | bytes 663560 | tf_op jit(solution)/shard_map/ppermute | solution.py:74
  4.5 2.9 %collective-permute-start.3 = (bf16[272,768]{1,0:T(8,128)(2,1)S(1)}, bf16[272,768]{1,0:T(8,128)(2,1)S(1)}, u32[]{:S(2)}, u32[]{:S(2)}) collective-permute-start(bf16[272,768]{1,0:T(8,128)(2,1)S(1)} %join.1.refs_0_.refs_8_), channel_id=1, source_target_pairs={{0,2},{1,7},{2,0},{3,5},{4,6},{5,3},{6,4},{7,1},{8,10},{9,15},{10,... | collective-permute-start | bytes 1253384 | tf_op jit(solution)/shard_map/ppermute | solution.py:70
  7.4 3.8 %collective-permute-start.2 = (bf16[272,768]{1,0:T(8,128)(2,1)S(1)}, bf16[272,768]{1,0:T(8,128)(2,1)S(1)}, u32[]{:S(2)}, u32[]{:S(2)}) collective-permute-start(bf16[272,768]{1,0:T(8,128)(2,1)S(1)} %join.1.refs_0_.refs_8_), channel_id=1, source_target_pairs={{0,8},{1,25},{2,10},{3,27},{4,12},{5,29},{6,14},{7,31},{8,0},{9,17... | collective-permute-start | bytes 1253384 | tf_op jit(solution)/shard_map/ppermute | solution.py:70
  11.2 2.5 %collective-permute-start.1 = (bf16[272,768]{1,0:T(8,128)(2,1)S(1)}, bf16[272,768]{1,0:T(8,128)(2,1)S(1)}, u32[]{:S(2)}, u32[]{:S(2)}) collective-permute-start(bf16[272,768]{1,0:T(8,128)(2,1)S(1)} %join.1.refs_0_.refs_8_), channel_id=1, source_target_pairs={{0,32},{1,97},{2,34},{3,99},{4,36},{5,101},{6,38},{7,103},{8,40},{... | collective-permute-start | bytes 1253384 | tf_op jit(solution)/shard_map/ppermute | solution.py:70
  13.7 2.9 %collective-permute-done.2.refs_2_.refs_8_ = bf16[272,768]{1,0:T(8,128)(2,1)S(1)} collective-permute-done((bf16[272,768]{1,0:T(8,128)(2,1)S(1)}, bf16[272,768]{1,0:T(8,128)(2,1)S(1)}, u32[]{:S(2)}, u32[]{:S(2)}) %collective-permute-start.2) | collective-permute-done | bytes 417824 | tf_op jit(solution)/shard_map/ppermute | solution.py:70
  16.6 2.7 %collective-permute-done.1.refs_1_.refs_8_ = bf16[272,768]{1,0:T(8,128)(2,1)S(1)} collective-permute-done((bf16[272,768]{1,0:T(8,128)(2,1)S(1)}, bf16[272,768]{1,0:T(8,128)(2,1)S(1)}, u32[]{:S(2)}, u32[]{:S(2)}) %collective-permute-start.1) | collective-permute-done | bytes 417824 | tf_op jit(solution)/shard_map/ppermute | solution.py:70
  19.5 3.4 %collective-permute-start.5 = (bf16[272,768]{1,0:T(8,128)(2,1)S(1)}, bf16[272,768]{1,0:T(8,128)(2,1)S(1)}, u32[]{:S(2)}, u32[]{:S(2)}) collective-permute-start(bf16[272,768]{1,0:T(8,128)(2,1)S(1)} %join.1.refs_0_.refs_8_), channel_id=1, source_target_pairs={{0,42},{1,127},{2,40},{3,125},{4,46},{5,123},{6,44},{7,121},{8,34}... | collective-permute-start | bytes 1253384 | tf_op jit(solution)/shard_map/ppermute | solution.py:70
  22.8 1.4 %collective-permute-start.6 = (bf16[272,768]{1,0:T(8,128)(2,1)S(1)}, bf16[272,768]{1,0:T(8,128)(2,1)S(1)}, u32[]{:S(2)}, u32[]{:S(2)}) collective-permute-start(bf16[272,768]{1,0:T(8,128)(2,1)S(1)} %collective-permute-done.3.refs_3_.refs_8_), channel_id=1, source_target_pairs={{0,8},{1,25},{2,10},{3,27},{4,12},{5,29},{6,14},{7,31},{8,0},{9,17... | collective-permute-start | bytes 1253384 | tf_op jit(solution)/shard_map/ppermute | solution.py:70
  24.4 2.6 %collective-permute-start.8 = (bf16[272,768]{1,0:T(8,128)(2,1)S(1)}, bf16[272,768]{1,0:T(8,128)(2,1)S(1)}, u32[]{:S(2)}, u32[]{:S(2)}) collective-permute-start(bf16[272,768]{1,0:T(8,128)(2,1)S(1)} %collective-permute-done.1.refs_1_.refs_8_), channel_id=1, source_target_pairs={{0,2},{1,7},{2,0},{3,5},{4,6},{5,3},{6,4},{7,1},{8,10},{9,15},{10,... | collective-permute-start | bytes 1253384 | tf_op jit(solution)/shard_map/ppermute | solution.py:70
  27.0 2.0 %tile_0.1 = (f32[1024,1024]{1,0:T(8,128)S(1)}, f32[1024,128]{1,0:T(8,128)S(1)}, f32[16,1024]{1,0:T(8,128)S(1)}) custom-call(bf16[272,768]{1,0:T(8,128)(2,1)S(1)} %join.1.refs_0_.refs_8_, bf16[272,768]{1,0:T(8,128)(2,1)S(1)} %collective-permute-done.1.refs_1_.refs_8_, bf16[272,768]{1,0:T(8,128)(2,1)S(1)} %collective-permute-done.2.refs_2_.refs_8_, ...), custom_call_target="tpu_custom_call" | custom-call | tf_op jit(solution)/shard_map/tile_0/pallas_call | solution.py:87
  29.0 3.0 %collective-permute-done.5.refs_0_.refs_4_.refs_8_ = bf16[272,768]{1,0:T(8,128)(2,1)S(1)} collective-permute-done((bf16[272,768]{1,0:T(8,128)(2,1)S(1)}, bf16[272,768]{1,0:T(8,128)(2,1)S(1)}, u32[]{:S(2)}, u32[]{:S(2)}) %collective-permute-start.5) | collective-permute-done | bytes 417824 | tf_op jit(solution)/shard_map/ppermute | solution.py:70
  32.0 3.4 %collective-permute-done.6.refs_1_.refs_5_.refs_8_ = bf16[272,768]{1,0:T(8,128)(2,1)S(1)} collective-permute-done((bf16[272,768]{1,0:T(8,128)(2,1)S(1)}, bf16[272,768]{1,0:T(8,128)(2,1)S(1)}, u32[]{:S(2)}, u32[]{:S(2)}) %collective-permute-start.6) | collective-permute-done | bytes 417824 | tf_op jit(solution)/shard_map/ppermute | solution.py:70
  36.2 2.0 %tile_1.1 = (f32[1024,1024]{1,0:T(8,128)S(1)}, f32[1024,128]{1,0:T(8,128)S(1)}, f32[16,1024]{1,0:T(8,128)S(1)}) custom-call(bf16[272,768]{1,0:T(8,128)(2,1)S(1)} %collective-permute-done.5.refs_0_.refs_4_.refs_8_, bf16[272,768]{1,0:T(8,128)(2,1)S(1)} %collective-permute-done.6.refs_1_.refs_5_.refs_8_, ...), custom_call_target="tpu_custom_call" | custom-call | tf_op jit(solution)/shard_map/tile_1/pallas_call | solution.py:87
  38.2 1.9 %tile_2.1 = (f32[2048,512]{1,0:T(8,128)S(1)}, f32[2048,128]{1,0:T(8,128)S(1)}, f32[16,512]{1,0:T(8,128)S(1)}) custom-call(bf16[272,768]{1,0:T(8,128)(2,1)S(1)} %join.1.refs_0_.refs_8_, bf16[272,768]{1,0:T(8,128)(2,1)S(1)} %collective-permute-done.1.refs_1_.refs_8_, bf16[272,768]{1,0:T(8,128)(2,1)S(1)} %collective-permute-done.2.refs_2_.refs_8_, ...), custom_call_target="tpu_custom_call" | custom-call | tf_op jit(solution)/shard_map/tile_2/pallas_call | solution.py:87
  40.2 2.1 %tile_3.1 = (f32[2048,512]{1,0:T(8,128)S(1)}, f32[8,32,128]{2,1,0:T(8,128)S(1)}) custom-call(bf16[272,768]{1,0:T(8,128)(2,1)S(1)} %join.1.refs_0_.refs_8_, bf16[272,768]{1,0:T(8,128)(2,1)S(1)} %collective-permute-done.1.refs_1_.refs_8_, bf16[272,768]{1,0:T(8,128)(2,1)S(1)} %collective-permute-done.2.refs_2_.refs_8_, ...), custom_call_target="tpu_custom_call" | custom-call | tf_op jit(solution)/shard_map/tile_3/pallas_call | solution.py:87
  42.3 7.4 %all_to_all.5.refs_0_ = f32[8,32,128]{2,1,0:T(8,128)S(1)} all-to-all(f32[8,32,128]{2,1,0:T(8,128)S(1)} %get-tuple-element.33), channel_id=1, replica_groups={{0,2,8,10,32,34,40,42},{4,6,12,14,36,38,44,46},{16,18,24,26,48,50,56,58..., dimensions={0} | all-to-all | bytes 262144 | tf_op jit(solution)/shard_map/all_to_all | solution.py:452
  49.8 1.4 %grad_3.1 = s16[272,768]{1,0:T(8,128)(2,1)S(1)} custom-call(f32[1024,1024]{1,0:T(8,128)S(1)} %get-tuple-element.23.refs_0_, f32[1024,1024]{1,0:T(8,128)S(1)} %get-tuple-element.25.refs_1_, f32[2048,512]{1,0:T(8,128)S(1)} %get-tuple-element.27.refs_2_, f32[2048,512]{1,0:T(8,128)S(1)} %get-tuple-element.32.refs_3_, ...), custom_call_target="tpu_custom_call" | custom-call | tf_op jit(solution)/shard_map/grad_3/pallas_call | solution.py:87
  51.4 1.4 %grad_6.1 = s16[272,768]{1,0:T(8,128)(2,1)S(1)} custom-call(f32[1024,1024]{1,0:T(8,128)S(1)} %get-tuple-element.23.refs_0_, f32[1024,1024]{1,0:T(8,128)S(1)} %get-tuple-element.25.refs_1_, f32[2048,512]{1,0:T(8,128)S(1)} %get-tuple-element.27.refs_2_, f32[2048,512]{1,0:T(8,128)S(1)} %get-tuple-element.32.refs_3_, ...), custom_call_target="tpu_custom_call" | custom-call | tf_op jit(solution)/shard_map/grad_6/pallas_call | solution.py:87
  52.9 2.2 %collective-permute-start.14 = (s16[272,768]{1,0:T(8,128)(2,1)S(1)}, s16[272,768]{1,0:T(8,128)(2,1)S(1)}, u32[]{:S(2)}, u32[]{:S(2)}) collective-permute-start(s16[272,768]{1,0:T(8,128)(2,1)S(1)} %grad_6.1), channel_id=1, source_target_pairs={{0,32},{1,97},{2,34},{3,99},{4,36},{5,101},{6,38},{7,103},{8,40},{... | collective-permute-start | bytes 1253384 | tf_op jit(solution)/shard_map/ppermute | solution.py:70
  55.0 1.4 %grad_5.1 = s16[272,768]{1,0:T(8,128)(2,1)S(1)} custom-call(f32[1024,1024]{1,0:T(8,128)S(1)} %get-tuple-element.23.refs_0_, f32[1024,1024]{1,0:T(8,128)S(1)} %get-tuple-element.25.refs_1_, f32[2048,512]{1,0:T(8,128)S(1)} %get-tuple-element.27.refs_2_, f32[2048,512]{1,0:T(8,128)S(1)} %get-tuple-element.32.refs_3_, ...), custom_call_target="tpu_custom_call" | custom-call | tf_op jit(solution)/shard_map/grad_5/pallas_call | solution.py:87
  56.5 1.4 %collective-permute-start.16 = (s16[272,768]{1,0:T(8,128)(2,1)S(1)}, s16[272,768]{1,0:T(8,128)(2,1)S(1)}, u32[]{:S(2)}, u32[]{:S(2)}) collective-permute-start(s16[272,768]{1,0:T(8,128)(2,1)S(1)} %grad_5.1), channel_id=1, source_target_pairs={{0,2},{1,7},{2,0},{3,5},{4,6},{5,3},{6,4},{7,1},{8,10},{9,15},{10,... | collective-permute-start | bytes 1253384 | tf_op jit(solution)/shard_map/ppermute | solution.py:70
  57.9 1.4 %grad_7.1 = s16[272,768]{1,0:T(8,128)(2,1)S(1)} custom-call(f32[1024,1024]{1,0:T(8,128)S(1)} %get-tuple-element.23.refs_0_, f32[1024,1024]{1,0:T(8,128)S(1)} %get-tuple-element.25.refs_1_, f32[2048,512]{1,0:T(8,128)S(1)} %get-tuple-element.27.refs_2_, f32[2048,512]{1,0:T(8,128)S(1)} %get-tuple-element.32.refs_3_, ...), custom_call_target="tpu_custom_call" | custom-call | tf_op jit(solution)/shard_map/grad_7/pallas_call | solution.py:87
  59.3 4.0 %collective-permute-start.11 = (s16[272,768]{1,0:T(8,128)(2,1)S(1)}, s16[272,768]{1,0:T(8,128)(2,1)S(1)}, u32[]{:S(2)}, u32[]{:S(2)}) collective-permute-start(s16[272,768]{1,0:T(8,128)(2,1)S(1)} %grad_7.1), channel_id=1, source_target_pairs={{0,42},{1,127},{2,40},{3,125},{4,46},{5,123},{6,44},{7,121},{8,34}... | collective-permute-start | bytes 1253384 | tf_op jit(solution)/shard_map/ppermute | solution.py:70
  63.3 1.4 %grad_1.1 = s16[272,768]{1,0:T(8,128)(2,1)S(1)} custom-call(f32[1024,1024]{1,0:T(8,128)S(1)} %get-tuple-element.23.refs_0_, f32[1024,1024]{1,0:T(8,128)S(1)} %get-tuple-element.25.refs_1_, f32[2048,512]{1,0:T(8,128)S(1)} %get-tuple-element.27.refs_2_, f32[2048,512]{1,0:T(8,128)S(1)} %get-tuple-element.32.refs_3_, ...), custom_call_target="tpu_custom_call" | custom-call | tf_op jit(solution)/shard_map/grad_1/pallas_call | solution.py:87
  65.0 1.4 %grad_2.1 = s16[272,768]{1,0:T(8,128)(2,1)S(1)} custom-call(f32[1024,1024]{1,0:T(8,128)S(1)} %get-tuple-element.23.refs_0_, f32[1024,1024]{1,0:T(8,128)S(1)} %get-tuple-element.25.refs_1_, f32[2048,512]{1,0:T(8,128)S(1)} %get-tuple-element.27.refs_2_, f32[2048,512]{1,0:T(8,128)S(1)} %get-tuple-element.32.refs_3_, ...), custom_call_target="tpu_custom_call" | custom-call | tf_op jit(solution)/shard_map/grad_2/pallas_call | solution.py:87
  66.4 1.7 %collective-permute-start.15 = (s16[272,768]{1,0:T(8,128)(2,1)S(1)}, s16[272,768]{1,0:T(8,128)(2,1)S(1)}, u32[]{:S(2)}, u32[]{:S(2)}) collective-permute-start(s16[272,768]{1,0:T(8,128)(2,1)S(1)} %grad_2.1), channel_id=1, source_target_pairs={{0,8},{1,25},{2,10},{3,27},{4,12},{5,29},{6,14},{7,31},{8,0},{9,17... | collective-permute-start | bytes 1253384 | tf_op jit(solution)/shard_map/ppermute | solution.py:70
  68.1 1.4 %grad_4.1 = s16[272,768]{1,0:T(8,128)(2,1)S(1)} custom-call(f32[1024,1024]{1,0:T(8,128)S(1)} %get-tuple-element.23.refs_0_, f32[1024,1024]{1,0:T(8,128)S(1)} %get-tuple-element.25.refs_1_, f32[2048,512]{1,0:T(8,128)S(1)} %get-tuple-element.27.refs_2_, f32[2048,512]{1,0:T(8,128)S(1)} %get-tuple-element.32.refs_3_, ...), custom_call_target="tpu_custom_call" | custom-call | tf_op jit(solution)/shard_map/grad_4/pallas_call | solution.py:87
  69.6 2.1 %collective-permute-start.17 = (s16[272,768]{1,0:T(8,128)(2,1)S(1)}, s16[272,768]{1,0:T(8,128)(2,1)S(1)}, u32[]{:S(2)}, u32[]{:S(2)}) collective-permute-start(s16[272,768]{1,0:T(8,128)(2,1)S(1)} %grad_4.1), channel_id=1, source_target_pairs={{0,32},{1,97},{2,34},{3,99},{4,36},{5,101},{6,38},{7,103},{8,40},{... | collective-permute-start | bytes 1253384 | tf_op jit(solution)/shard_map/ppermute | solution.py:70
  72.8 1.6 %collective-permute-done.13.refs_2_ = s16[272,768]{1,0:T(8,128)(2,1)S(1)} collective-permute-done((s16[272,768]{1,0:T(8,128)(2,1)S(1)}, s16[272,768]{1,0:T(8,128)(2,1)S(1)}, u32[]{:S(2)}, u32[]{:S(2)}) %collective-permute-start.13) | collective-permute-done | bytes 417824 | tf_op jit(solution)/shard_map/ppermute | solution.py:70
  74.5 1.9 %collective-permute-done.15.refs_3_ = s16[272,768]{1,0:T(8,128)(2,1)S(1)} collective-permute-done((s16[272,768]{1,0:T(8,128)(2,1)S(1)}, s16[272,768]{1,0:T(8,128)(2,1)S(1)}, u32[]{:S(2)}, u32[]{:S(2)}) %collective-permute-start.15) | collective-permute-done | bytes 417824 | tf_op jit(solution)/shard_map/ppermute | solution.py:70
  76.3 1.7 %collective-permute-done.17.refs_4_ = s16[272,768]{1,0:T(8,128)(2,1)S(1)} collective-permute-done((s16[272,768]{1,0:T(8,128)(2,1)S(1)}, s16[272,768]{1,0:T(8,128)(2,1)S(1)}, u32[]{:S(2)}, u32[]{:S(2)}) %collective-permute-start.17) | collective-permute-done | bytes 417824 | tf_op jit(solution)/shard_map/ppermute | solution.py:70
  78.5 1.5 %collective-permute-start.18 = (f32[136,768]{1,0:T(8,128)S(1)}, f32[136,768]{1,0:T(8,128)S(1)}, u32[]{:S(2)}, u32[]{:S(2)}) collective-permute-start(f32[136,768]{1,0:T(8,128)S(1)} %get-tuple-element.35), channel_id=1, source_target_pairs={{0,1},{1,0},{2,3},{3,2},{4,5},{5,4},{6,7},{7,6},{8,9},{9,8},{10,11... | collective-permute-start | bytes 1253384 | tf_op jit(solution)/shard_map/ppermute | solution.py:74
  (31 shorter events, 8.4 us)
Async XLA Ops:
  1.9 2.6 %collective-permute-start = (bf16[144,768]{1,0:T(8,128)(2,1)S(1)}, bf16[144,768]{1,0:T(8,128)(2,1)S(1)}, u32[]{:S(2)}, u32[]{:S(2)}) collective-permute-start(bf16[144,768]{1,0:T(8,128)(2,1)S(1)} %get-tuple-element.22), channel_id=1, source_target_pairs={{0,1},{1,0},{2,3},{3,2},{4,5},{5,4},{6,7},{7,6},{8,9},{9,8},{10,11... | collective-permute-start | bytes 663560 | tf_op jit(solution)/shard_map/ppermute | solution.py:74
  4.5 9.1 %collective-permute-start.3 = (bf16[272,768]{1,0:T(8,128)(2,1)S(1)}, bf16[272,768]{1,0:T(8,128)(2,1)S(1)}, u32[]{:S(2)}, u32[]{:S(2)}) collective-permute-start(bf16[272,768]{1,0:T(8,128)(2,1)S(1)} %join.1.refs_0_.refs_8_), channel_id=1, source_target_pairs={{0,2},{1,7},{2,0},{3,5},{4,6},{5,3},{6,4},{7,1},{8,10},{9,15},{10,... | collective-permute-start | bytes 1253384 | tf_op jit(solution)/shard_map/ppermute | solution.py:70
  7.4 9.2 %collective-permute-start.2 = (bf16[272,768]{1,0:T(8,128)(2,1)S(1)}, bf16[272,768]{1,0:T(8,128)(2,1)S(1)}, u32[]{:S(2)}, u32[]{:S(2)}) collective-permute-start(bf16[272,768]{1,0:T(8,128)(2,1)S(1)} %join.1.refs_0_.refs_8_), channel_id=1, source_target_pairs={{0,8},{1,25},{2,10},{3,27},{4,12},{5,29},{6,14},{7,31},{8,0},{9,17... | collective-permute-start | bytes 1253384 | tf_op jit(solution)/shard_map/ppermute | solution.py:70
  11.2 8.1 %collective-permute-start.1 = (bf16[272,768]{1,0:T(8,128)(2,1)S(1)}, bf16[272,768]{1,0:T(8,128)(2,1)S(1)}, u32[]{:S(2)}, u32[]{:S(2)}) collective-permute-start(bf16[272,768]{1,0:T(8,128)(2,1)S(1)} %join.1.refs_0_.refs_8_), channel_id=1, source_target_pairs={{0,32},{1,97},{2,34},{3,99},{4,36},{5,101},{6,38},{7,103},{8,40},{... | collective-permute-start | bytes 1253384 | tf_op jit(solution)/shard_map/ppermute | solution.py:70
  19.4 7.6 %collective-permute-start.4 = (bf16[1088,768]{1,0:T(8,128)(2,1)S(1)}, bf16[1088,768]{1,0:T(8,128)(2,1)S(1)}, u32[]{:S(2)}, u32[]{:S(2)}) collective-permute-start(bf16[1088,768]{1,0:T(8,128)(2,1)S(1)} %pack_near.1), channel_id=1, source_target_pairs={{0,1},{1,0},{2,3},{3,2},{4,5},{5,4},{6,7},{7,6},{8,9},{9,8},{10,11... | collective-permute-start | bytes 5013512 | tf_op jit(solution)/shard_map/ppermute | solution.py:74
  19.5 12.6 %collective-permute-start.5 = (bf16[272,768]{1,0:T(8,128)(2,1)S(1)}, bf16[272,768]{1,0:T(8,128)(2,1)S(1)}, u32[]{:S(2)}, u32[]{:S(2)}) collective-permute-start(bf16[272,768]{1,0:T(8,128)(2,1)S(1)} %join.1.refs_0_.refs_8_), channel_id=1, source_target_pairs={{0,42},{1,127},{2,40},{3,125},{4,46},{5,123},{6,44},{7,121},{8,34}... | collective-permute-start | bytes 1253384 | tf_op jit(solution)/shard_map/ppermute | solution.py:70
  22.8 12.6 %collective-permute-start.6 = (bf16[272,768]{1,0:T(8,128)(2,1)S(1)}, bf16[272,768]{1,0:T(8,128)(2,1)S(1)}, u32[]{:S(2)}, u32[]{:S(2)}) collective-permute-start(bf16[272,768]{1,0:T(8,128)(2,1)S(1)} %collective-permute-done.3.refs_3_.refs_8_), channel_id=1, source_target_pairs={{0,8},{1,25},{2,10},{3,27},{4,12},{5,29},{6,14},{7,31},{8,0},{9,17... | collective-permute-start | bytes 1253384 | tf_op jit(solution)/shard_map/ppermute | solution.py:70
  24.2 11.3 %collective-permute-start.7 = (bf16[272,768]{1,0:T(8,128)(2,1)S(1)}, bf16[272,768]{1,0:T(8,128)(2,1)S(1)}, u32[]{:S(2)}, u32[]{:S(2)}) collective-permute-start(bf16[272,768]{1,0:T(8,128)(2,1)S(1)} %collective-permute-done.2.refs_2_.refs_8_), channel_id=1, source_target_pairs={{0,32},{1,97},{2,34},{3,99},{4,36},{5,101},{6,38},{7,103},{8,40},{... | collective-permute-start | bytes 1253384 | tf_op jit(solution)/shard_map/ppermute | solution.py:70
  24.4 11.1 %collective-permute-start.8 = (bf16[272,768]{1,0:T(8,128)(2,1)S(1)}, bf16[272,768]{1,0:T(8,128)(2,1)S(1)}, u32[]{:S(2)}, u32[]{:S(2)}) collective-permute-start(bf16[272,768]{1,0:T(8,128)(2,1)S(1)} %collective-permute-done.1.refs_1_.refs_8_), channel_id=1, source_target_pairs={{0,2},{1,7},{2,0},{3,5},{4,6},{5,3},{6,4},{7,1},{8,10},{9,15},{10,... | collective-permute-start | bytes 1253384 | tf_op jit(solution)/shard_map/ppermute | solution.py:70
  35.5 2.8 %collective-permute-start.9 = (bf16[544,768]{1,0:T(8,128)(2,1)S(1)}, bf16[544,768]{1,0:T(8,128)(2,1)S(1)}, u32[]{:S(2)}, u32[]{:S(2)}) collective-permute-start(bf16[544,768]{1,0:T(8,128)(2,1)S(1)} %pack_first.1), channel_id=1, source_target_pairs={{0,1},{1,0},{2,3},{3,2},{4,5},{5,4},{6,7},{7,6},{8,9},{9,8},{10,11... | collective-permute-start | bytes 2506760 | tf_op jit(solution)/shard_map/ppermute | solution.py:74
  35.7 4.5 %collective-permute-start.10 = (bf16[544,768]{1,0:T(8,128)(2,1)S(1)}, bf16[544,768]{1,0:T(8,128)(2,1)S(1)}, u32[]{:S(2)}, u32[]{:S(2)}) collective-permute-start(bf16[544,768]{1,0:T(8,128)(2,1)S(1)} %pack_second.1), channel_id=1, source_target_pairs={{0,1},{1,0},{2,3},{3,2},{4,5},{5,4},{6,7},{7,6},{8,9},{9,8},{10,11... | collective-permute-start | bytes 2506760 | tf_op jit(solution)/shard_map/ppermute | solution.py:74
  51.2 12.1 %collective-permute-start.12 = (s16[272,768]{1,0:T(8,128)(2,1)S(1)}, s16[272,768]{1,0:T(8,128)(2,1)S(1)}, u32[]{:S(2)}, u32[]{:S(2)}) collective-permute-start(s16[272,768]{1,0:T(8,128)(2,1)S(1)} %grad_3.1), channel_id=1, source_target_pairs={{0,8},{1,25},{2,10},{3,27},{4,12},{5,29},{6,14},{7,31},{8,0},{9,17... | collective-permute-start | bytes 1253384 | tf_op jit(solution)/shard_map/ppermute | solution.py:70
  52.9 12.1 %collective-permute-start.14 = (s16[272,768]{1,0:T(8,128)(2,1)S(1)}, s16[272,768]{1,0:T(8,128)(2,1)S(1)}, u32[]{:S(2)}, u32[]{:S(2)}) collective-permute-start(s16[272,768]{1,0:T(8,128)(2,1)S(1)} %grad_6.1), channel_id=1, source_target_pairs={{0,32},{1,97},{2,34},{3,99},{4,36},{5,101},{6,38},{7,103},{8,40},{... | collective-permute-start | bytes 1253384 | tf_op jit(solution)/shard_map/ppermute | solution.py:70
  56.5 11.6 %collective-permute-start.16 = (s16[272,768]{1,0:T(8,128)(2,1)S(1)}, s16[272,768]{1,0:T(8,128)(2,1)S(1)}, u32[]{:S(2)}, u32[]{:S(2)}) collective-permute-start(s16[272,768]{1,0:T(8,128)(2,1)S(1)} %grad_5.1), channel_id=1, source_target_pairs={{0,2},{1,7},{2,0},{3,5},{4,6},{5,3},{6,4},{7,1},{8,10},{9,15},{10,... | collective-permute-start | bytes 1253384 | tf_op jit(solution)/shard_map/ppermute | solution.py:70
  59.3 13.5 %collective-permute-start.11 = (s16[272,768]{1,0:T(8,128)(2,1)S(1)}, s16[272,768]{1,0:T(8,128)(2,1)S(1)}, u32[]{:S(2)}, u32[]{:S(2)}) collective-permute-start(s16[272,768]{1,0:T(8,128)(2,1)S(1)} %grad_7.1), channel_id=1, source_target_pairs={{0,42},{1,127},{2,40},{3,125},{4,46},{5,123},{6,44},{7,121},{8,34}... | collective-permute-start | bytes 1253384 | tf_op jit(solution)/shard_map/ppermute | solution.py:70
  64.8 9.7 %collective-permute-start.13 = (s16[272,768]{1,0:T(8,128)(2,1)S(1)}, s16[272,768]{1,0:T(8,128)(2,1)S(1)}, u32[]{:S(2)}, u32[]{:S(2)}) collective-permute-start(s16[272,768]{1,0:T(8,128)(2,1)S(1)} %grad_1.1), channel_id=1, source_target_pairs={{0,2},{1,7},{2,0},{3,5},{4,6},{5,3},{6,4},{7,1},{8,10},{9,15},{10,... | collective-permute-start | bytes 1253384 | tf_op jit(solution)/shard_map/ppermute | solution.py:70
  66.4 9.9 %collective-permute-start.15 = (s16[272,768]{1,0:T(8,128)(2,1)S(1)}, s16[272,768]{1,0:T(8,128)(2,1)S(1)}, u32[]{:S(2)}, u32[]{:S(2)}) collective-permute-start(s16[272,768]{1,0:T(8,128)(2,1)S(1)} %grad_2.1), channel_id=1, source_target_pairs={{0,8},{1,25},{2,10},{3,27},{4,12},{5,29},{6,14},{7,31},{8,0},{9,17... | collective-permute-start | bytes 1253384 | tf_op jit(solution)/shard_map/ppermute | solution.py:70
  69.6 11.9 %copy-start = (bf16[128,768]{1,0:T(8,128)(2,1)S(1)}, bf16[128,768]{1,0:T(8,128)(2,1)}, u32[]{:S(2)}) copy-start(bf16[128,768]{1,0:T(8,128)(2,1)} %refs_0_.1) | copy-start | bytes 589828
  69.6 11.8 %copy-start.1 = (bf16[128,768]{1,0:T(8,128)(2,1)S(1)}, bf16[128,768]{1,0:T(8,128)(2,1)}, u32[]{:S(2)}) copy-start(bf16[128,768]{1,0:T(8,128)(2,1)} %refs_1_.1) | copy-start | bytes 589828
  69.6 8.4 %collective-permute-start.17 = (s16[272,768]{1,0:T(8,128)(2,1)S(1)}, s16[272,768]{1,0:T(8,128)(2,1)S(1)}, u32[]{:S(2)}, u32[]{:S(2)}) collective-permute-start(s16[272,768]{1,0:T(8,128)(2,1)S(1)} %grad_4.1), channel_id=1, source_target_pairs={{0,32},{1,97},{2,34},{3,99},{4,36},{5,101},{6,38},{7,103},{8,40},{... | collective-permute-start | bytes 1253384 | tf_op jit(solution)/shard_map/ppermute | solution.py:70
  78.5 2.9 %collective-permute-start.18 = (f32[136,768]{1,0:T(8,128)S(1)}, f32[136,768]{1,0:T(8,128)S(1)}, u32[]{:S(2)}, u32[]{:S(2)}) collective-permute-start(f32[136,768]{1,0:T(8,128)S(1)} %get-tuple-element.35), channel_id=1, source_target_pairs={{0,1},{1,0},{2,3},{3,2},{4,5},{5,4},{6,7},{7,6},{8,9},{9,8},{10,11... | collective-permute-start | bytes 1253384 | tf_op jit(solution)/shard_map/ppermute | solution.py:74

commit v3 on v2

--- a/solution.py
+++ b/solution.py
@@ -22,13 +22,14 @@
 LOG2E = 1.4426950408889634
 FULL = 32760.0
 NEAR = (0, 4, 2, 1)
-FAR = (7, 3, 6, 5)
+FAR = (7, 5, 3, 6)
 PACKS = (NEAR, FAR[:2], FAR[2:])
 ALL = NEAR + FAR
 PARTS = (
     (NEAR, NEAR, ()),
-    (FAR, NEAR, ()),
-    (ALL, FAR[:2], ()),
+    (FAR[:2], NEAR, ()),
+    (NEAR + FAR[:2], FAR[:2], ()),
+    (FAR[2:], NEAR + FAR[:2], ()),
     (ALL, FAR[2:], ()),
 )
 SPAN = BLOCK + PAD
@@ -279,10 +280,10 @@
     out_ref[BLOCK:, :BLOCK] = tail.astype(jnp.int32).astype(jnp.int16)
 
 
-def decode(ref):
+def decode(ref, at=slice(0, BLOCK)):
     tail = ref[BLOCK:, :BLOCK].astype(jnp.int32).astype(F32)
-    scale = down_rows(jnp.exp2(tail[0:1, :] * (1.0 / 128.0)) * (1.0 / FULL), WIDTH)
-    return ref[:BLOCK, :].astype(jnp.int32).astype(F32) * scale
+    scale = down_rows(jnp.exp2(tail[0:1, at] * (1.0 / 128.0)) * (1.0 / FULL), WIDTH)
+    return ref[at, :].astype(jnp.int32).astype(F32) * scale
 
 
 def digits_of(loss):
@@ -349,9 +350,10 @@
         out_ref[BLOCK:, :] = jnp.full((LOSS, WIDTH), loss, F32)
 
 
-def split_kernel(own_ref, a_ref, b_ref, c_ref, d_ref, keep_ref, send_ref):
+def split_kernel(own_ref, *refs):
+    come, (keep_ref, send_ref) = refs[:-2], refs[-2:]
     value, loss = own_ref[:BLOCK, :], own_ref[BLOCK, 0]
-    for ref in (a_ref, b_ref, c_ref, d_ref):
+    for ref in come:
         value = value + decode(ref)
         loss = loss + loss_of(ref)
     role = role_of()
@@ -369,25 +371,26 @@
         send_ref[:ROWS, :] = value[:ROWS, :]
 
 
-def post_kernel(q_ref, d_ref, keep_ref, come_ref, loss_ref, gq_ref, gd_ref):
+def post_kernel(q_ref, d_ref, keep_ref, come_ref, last_ref, other_ref, loss_ref, gq_ref, gd_ref):
     def project(out_ref, grad, values):
         unit, length = unit_rows(values)
         out_ref[...] = (grad - jnp.sum(grad * unit, axis=1, keepdims=True) * unit) / length
 
-    def fill(gq, gd):
-        project(gq_ref, gq[:ROWS, :], q_ref[...])
-        project(gd_ref, gd[:ROWS, :], d_ref[...])
-        loss_ref[...] = gd[ROWS : ROWS + 1, 0:1] * (1.0 / 16384)
+    def fill(gq, last_q, gd, last_d, half):
+        at = slice(half * ROWS, (half + 1) * ROWS)
+        project(gq_ref, gq[:ROWS, :] + decode(last_q, at), q_ref[...])
+        project(gd_ref, gd[:ROWS, :] + decode(last_d, at), d_ref[...])
+        loss_ref[...] = (gd[ROWS : ROWS + 1, 0:1] + loss_of(last_d)) * (1.0 / 16384)
 
     role = role_of()
 
     @pl.when(role == 0)
     def _():
-        fill(keep_ref, come_ref)
+        fill(keep_ref, last_ref, come_ref, other_ref, 0)
 
     @pl.when(role == 1)
     def _():
-        fill(come_ref, keep_ref)
+        fill(come_ref, other_ref, keep_ref, last_ref, 1)
 
 
 def local(queries, documents, positives):
@@ -414,12 +417,12 @@
         return call(pack_kernel, name, shape, *[near(x[n]) for n in blocks], after=after)
 
     x = {0: own}
-    x[7] = send(own, 7)
     for bits in (4, 2, 1):
         x[bits] = send(own, bits)
+    x[5] = send(x[4], 1)
+    x[6] = send(x[2], 4)
     x[3] = send(x[1], 2)
-    x[6] = send(x[2], 4)
-    x[5] = send(x[4], 1)
+    x[7] = send(x[1], 6)
     y = [swap(pack(NEAR, "pack_near"))]
     parts = []
 
@@ -443,12 +446,13 @@
             )
         )
 
-    tile(0, "tile_0")
+    tile(0, "tile_0", [])
     y.append(swap(pack(FAR[:2], "pack_first", after=[parts[0][1]])))
-    y.append(swap(pack(FAR[2:], "pack_second")))
     tile(1, "tile_1", [parts[0][1]])
     tile(2, "tile_2", [parts[1][1]])
-    tile(3, "tile_3")
+    y.append(swap(pack(FAR[2:], "pack_second", after=[parts[1][1]])))
+    tile(3, "tile_3", [parts[2][1]])
+    tile(4, "tile_4")
     stats = lax.all_to_all(parts[-1][1], "dp", 0, 0, axis_index_groups=SUM_GROUPS, tiled=True)
     scales = call(scale_kernel, "scales", pltpu.VMEM((HALF + 8, 128), F32), near(stats))
 
@@ -484,8 +488,9 @@
     r4 = send(g4, 4)
     g0 = grad(0, shape=plain)
     part = pltpu.VMEM((ROWS + LOSS, WIDTH), F32)
-    keep, give = call(split_kernel, "split", [part, part], *[near(v) for v in (g0, r7, r1, r2, r4)])
+    keep, give = call(split_kernel, "split", [part, part], *[near(v) for v in (g0, r7, r1, r2)])
     come = swap(give)
+    other = swap(r4)
     loss, gq, gd = call(
         post_kernel,
         "post",
@@ -496,8 +501,7 @@
         ],
         queries,
         documents,
-        near(keep),
-        near(come),
+        *[near(v) for v in (keep, come, r4, other)],
     )
     return (loss.reshape(()), gq, gd)
 

time: 82.8 us -> 80.1 us (0.967)
  starting transfers between devices: 32.2 us -> 30.3 us
  waiting for transfers between devices: 19.6 us -> 18.3 us
    ppermute x14, starting transfers between devices: 28.5 us -> 25.7 us  [send(): return lax.ppermute(value, 'dp', partners(bits))]
    ppermute x14, waiting for transfers between devices: 17.1 us -> 15.8 us  [send(): return lax.ppermute(value, 'dp', partners(bits))]
    ppermute x5 -> x6, starting transfers between devices: 3.72 us -> 4.61 us  [swap(): return lax.ppermute(value, 'dp', SWAP)]
    pallas_call x19 -> x20, Pallas kernels: 21.3 us -> 21.7 us  [call(): pl.pallas_call(body, name=name, out_shape=out_shape, scratch_shapes=scrat...]
    ppermute x5 -> x6, waiting for transfers between devices: 2.5 us -> 2.5 us  [swap(): return lax.ppermute(value, 'dp', SWAP)]
  transfers between devices with their start and end apart: 19 -> 20, of which waited for: 9 -> 9; matrix products, arithmetic and copies ran while one was open for 0% -> 0% of each run, Pallas kernels for 19% -> 21%
where the time goes in v3:
time: 80.1 us; the launch traced here: 79.9 us
  starting transfers between devices  30.3 us (38%)
  Pallas kernels  22.9 us (29%)
  waiting for transfers between devices  18.3 us (23%)
  blocking collectives  7.53 us (9%)
  between operations  0.87 us (1%)
    ppermute x14, starting transfers between devices, send(): return lax.ppermute(value, 'dp', partners(bits))  25.7 us
    pallas_call x20, Pallas kernels, call(): pl.pallas_call(body, name=name, out_shape=out_shape, scratch_shapes=scrat...  21.7 us
    ppermute x14, waiting for transfers between devices, send(): return lax.ppermute(value, 'dp', partners(bits))  15.8 us
    all_to_all x1, blocking collectives, local(): lax.all_to_all(parts[-1][1], 'dp', 0, 0, axis_index_groups=SUM_GROUPS, ti...  7.53 us
    ppermute x6, starting transfers between devices, swap(): return lax.ppermute(value, 'dp', SWAP)  4.61 us
    ppermute x6, waiting for transfers between devices, swap(): return lax.ppermute(value, 'dp', SWAP)  2.5 us
  transfers between devices with their start and end apart: 20, of which 9 were waited for; matrix products, arithmetic and copies ran while one was open for 0% of the time, Pallas kernels for 21%

profile of v3, /device:TPU:1, one launch (start us, length us, event | category | flops | bytes accessed | tf_op | source)
XLA Modules:
  0.0 79.9 jit_solution(3659538724620865517)
XLA Ops:
  0.6 1.2 %pre.1 = (bf16[144,768]{1,0:T(8,128)(2,1)S(1)}, bf16[144,768]{1,0:T(8,128)(2,1)S(1)}) custom-call(bf16[128,768]{1,0:T(8,128)(2,1)} %refs_0_.1, bf16[128,768]{1,0:T(8,128)(2,1)} %refs_1_.1, s32[1,128]{1,0:T(1,128)} %bitcast.2), custom_call_target="tpu_custom_call" | custom-call | tf_op jit(solution)/shard_map/pre/pallas_call | solution.py:399
  1.9 1.5 %collective-permute-start = (bf16[144,768]{1,0:T(8,128)(2,1)S(1)}, bf16[144,768]{1,0:T(8,128)(2,1)S(1)}, u32[]{:S(2)}, u32[]{:S(2)}) collective-permute-start(bf16[144,768]{1,0:T(8,128)(2,1)S(1)} %get-tuple-element.25), channel_id=1, source_target_pairs={{0,1},{1,0},{2,3},{3,2},{4,5},{5,4},{6,7},{7,6},{8,9},{9,8},{10,11... | collective-permute-start | bytes 663560 | tf_op jit(solution)/shard_map/ppermute | solution.py:75
  4.5 2.9 %collective-permute-start.3 = (bf16[272,768]{1,0:T(8,128)(2,1)S(1)}, bf16[272,768]{1,0:T(8,128)(2,1)S(1)}, u32[]{:S(2)}, u32[]{:S(2)}) collective-permute-start(bf16[272,768]{1,0:T(8,128)(2,1)S(1)} %join.1.refs_0_.refs_9_), channel_id=1, source_target_pairs={{0,2},{1,7},{2,0},{3,5},{4,6},{5,3},{6,4},{7,1},{8,10},{9,15},{10,... | collective-permute-start | bytes 1253384 | tf_op jit(solution)/shard_map/ppermute | solution.py:71
  7.4 3.8 %collective-permute-start.2 = (bf16[272,768]{1,0:T(8,128)(2,1)S(1)}, bf16[272,768]{1,0:T(8,128)(2,1)S(1)}, u32[]{:S(2)}, u32[]{:S(2)}) collective-permute-start(bf16[272,768]{1,0:T(8,128)(2,1)S(1)} %join.1.refs_0_.refs_9_), channel_id=1, source_target_pairs={{0,8},{1,25},{2,10},{3,27},{4,12},{5,29},{6,14},{7,31},{8,0},{9,17... | collective-permute-start | bytes 1253384 | tf_op jit(solution)/shard_map/ppermute | solution.py:71
  11.2 2.5 %collective-permute-start.1 = (bf16[272,768]{1,0:T(8,128)(2,1)S(1)}, bf16[272,768]{1,0:T(8,128)(2,1)S(1)}, u32[]{:S(2)}, u32[]{:S(2)}) collective-permute-start(bf16[272,768]{1,0:T(8,128)(2,1)S(1)} %join.1.refs_0_.refs_9_), channel_id=1, source_target_pairs={{0,32},{1,97},{2,34},{3,99},{4,36},{5,101},{6,38},{7,103},{8,40},{... | collective-permute-start | bytes 1253384 | tf_op jit(solution)/shard_map/ppermute | solution.py:71
  13.7 2.9 %collective-permute-done.2.refs_2_.refs_9_ = bf16[272,768]{1,0:T(8,128)(2,1)S(1)} collective-permute-done((bf16[272,768]{1,0:T(8,128)(2,1)S(1)}, bf16[272,768]{1,0:T(8,128)(2,1)S(1)}, u32[]{:S(2)}, u32[]{:S(2)}) %collective-permute-start.2) | collective-permute-done | bytes 417824 | tf_op jit(solution)/shard_map/ppermute | solution.py:71
  16.6 2.7 %collective-permute-done.1.refs_1_.refs_9_ = bf16[272,768]{1,0:T(8,128)(2,1)S(1)} collective-permute-done((bf16[272,768]{1,0:T(8,128)(2,1)S(1)}, bf16[272,768]{1,0:T(8,128)(2,1)S(1)}, u32[]{:S(2)}, u32[]{:S(2)}) %collective-permute-start.1) | collective-permute-done | bytes 417824 | tf_op jit(solution)/shard_map/ppermute | solution.py:71
  19.5 2.3 %collective-permute-start.5 = (bf16[272,768]{1,0:T(8,128)(2,1)S(1)}, bf16[272,768]{1,0:T(8,128)(2,1)S(1)}, u32[]{:S(2)}, u32[]{:S(2)}) collective-permute-start(bf16[272,768]{1,0:T(8,128)(2,1)S(1)} %collective-permute-done.3.refs_3_.refs_9_), channel_id=1, source_target_pairs={{0,40},{1,121},{2,42},{3,123},{4,44},{5,125},{6,46},{7,127},{8,32}... | collective-permute-start | bytes 1253384 | tf_op jit(solution)/shard_map/ppermute | solution.py:71
  21.8 1.4 %collective-permute-start.6 = (bf16[272,768]{1,0:T(8,128)(2,1)S(1)}, bf16[272,768]{1,0:T(8,128)(2,1)S(1)}, u32[]{:S(2)}, u32[]{:S(2)}) collective-permute-start(bf16[272,768]{1,0:T(8,128)(2,1)S(1)} %collective-permute-done.1.refs_1_.refs_9_), channel_id=1, source_target_pairs={{0,2},{1,7},{2,0},{3,5},{4,6},{5,3},{6,4},{7,1},{8,10},{9,15},{10,... | collective-permute-start | bytes 1253384 | tf_op jit(solution)/shard_map/ppermute | solution.py:71
  23.1 1.4 %collective-permute-start.8 = (bf16[272,768]{1,0:T(8,128)(2,1)S(1)}, bf16[272,768]{1,0:T(8,128)(2,1)S(1)}, u32[]{:S(2)}, u32[]{:S(2)}) collective-permute-start(bf16[272,768]{1,0:T(8,128)(2,1)S(1)} %collective-permute-done.3.refs_3_.refs_9_), channel_id=1, source_target_pairs={{0,8},{1,25},{2,10},{3,27},{4,12},{5,29},{6,14},{7,31},{8,0},{9,17... | collective-permute-start | bytes 1253384 | tf_op jit(solution)/shard_map/ppermute | solution.py:71
  24.7 2.0 %tile_0.1 = (f32[1024,1024]{1,0:T(8,128)S(1)}, f32[1024,128]{1,0:T(8,128)S(1)}, f32[16,1024]{1,0:T(8,128)S(1)}) custom-call(bf16[272,768]{1,0:T(8,128)(2,1)S(1)} %join.1.refs_0_.refs_9_, bf16[272,768]{1,0:T(8,128)(2,1)S(1)} %collective-permute-done.1.refs_1_.refs_9_, bf16[272,768]{1,0:T(8,128)(2,1)S(1)} %collective-permute-done.2.refs_2_.refs_9_, ...), custom_call_target="tpu_custom_call" | custom-call | tf_op jit(solution)/shard_map/tile_0/pallas_call | solution.py:88
  26.7 3.1 %collective-permute-done.5.refs_0_.refs_4_.refs_9_ = bf16[272,768]{1,0:T(8,128)(2,1)S(1)} collective-permute-done((bf16[272,768]{1,0:T(8,128)(2,1)S(1)}, bf16[272,768]{1,0:T(8,128)(2,1)S(1)}, u32[]{:S(2)}, u32[]{:S(2)}) %collective-permute-start.5) | collective-permute-done | bytes 417824 | tf_op jit(solution)/shard_map/ppermute | solution.py:71
  31.2 3.1 %collective-permute-done.8.refs_0_.refs_6_.refs_9_ = bf16[272,768]{1,0:T(8,128)(2,1)S(1)} collective-permute-done((bf16[272,768]{1,0:T(8,128)(2,1)S(1)}, bf16[272,768]{1,0:T(8,128)(2,1)S(1)}, u32[]{:S(2)}, u32[]{:S(2)}) %collective-permute-start.8) | collective-permute-done | bytes 417824 | tf_op jit(solution)/shard_map/ppermute | solution.py:71
  34.4 1.5 %tile_2.1 = (f32[1536,512]{1,0:T(8,128)S(1)}, f32[1536,128]{1,0:T(8,128)S(1)}, f32[16,512]{1,0:T(8,128)S(1)}) custom-call(bf16[272,768]{1,0:T(8,128)(2,1)S(1)} %join.1.refs_0_.refs_9_, bf16[272,768]{1,0:T(8,128)(2,1)S(1)} %collective-permute-done.1.refs_1_.refs_9_, bf16[272,768]{1,0:T(8,128)(2,1)S(1)} %collective-permute-done.2.refs_2_.refs_9_, ...), custom_call_target="tpu_custom_call" | custom-call | tf_op jit(solution)/shard_map/tile_2/pallas_call | solution.py:88
  35.9 1.6 %tile_3.1 = (f32[512,1536]{1,0:T(8,128)S(1)}, f32[512,128]{1,0:T(8,128)S(1)}, f32[16,1536]{1,0:T(8,128)S(1)}) custom-call(bf16[272,768]{1,0:T(8,128)(2,1)S(1)} %collective-permute-done.8.refs_0_.refs_6_.refs_9_, bf16[272,768]{1,0:T(8,128)(2,1)S(1)} %collective-permute-done.9.refs_1_.refs_7_.refs_9_, ...), custom_call_target="tpu_custom_call" | custom-call | tf_op jit(solution)/shard_map/tile_3/pallas_call | solution.py:88
  37.6 2.0 %tile_4.1 = (f32[2048,512]{1,0:T(8,128)S(1)}, f32[8,32,128]{2,1,0:T(8,128)S(1)}) custom-call(bf16[272,768]{1,0:T(8,128)(2,1)S(1)} %join.1.refs_0_.refs_9_, bf16[272,768]{1,0:T(8,128)(2,1)S(1)} %collective-permute-done.1.refs_1_.refs_9_, bf16[272,768]{1,0:T(8,128)(2,1)S(1)} %collective-permute-done.2.refs_2_.refs_9_, ...), custom_call_target="tpu_custom_call" | custom-call | tf_op jit(solution)/shard_map/tile_4/pallas_call | solution.py:88
  39.6 7.5 %all_to_all.5.refs_0_ = f32[8,32,128]{2,1,0:T(8,128)S(1)} all-to-all(f32[8,32,128]{2,1,0:T(8,128)S(1)} %get-tuple-element.39), channel_id=1, replica_groups={{0,2,8,10,32,34,40,42},{4,6,12,14,36,38,44,46},{16,18,24,26,48,50,56,58..., dimensions={0} | all-to-all | bytes 262144 | tf_op jit(solution)/shard_map/all_to_all | solution.py:456
  47.3 1.4 %grad_3.1 = s16[272,768]{1,0:T(8,128)(2,1)S(1)} custom-call(f32[1024,1024]{1,0:T(8,128)S(1)} %get-tuple-element.26.refs_0_, f32[512,1024]{1,0:T(8,128)S(1)} %get-tuple-element.28.refs_1_, f32[1536,512]{1,0:T(8,128)S(1)} %get-tuple-element.30.refs_2_, f32[512,1536]{1,0:T(8,128)S(1)} %get-tuple-element.32.refs_3_, f32[2048,512]{1,0:T(8,128)S(1)} %get-tuple-element.38.refs_4_, ...), custom_call_target="tpu_custom_call" | custom-call | tf_op jit(solution)/shard_map/grad_3/pallas_call | solution.py:88
  48.8 1.4 %grad_6.1 = s16[272,768]{1,0:T(8,128)(2,1)S(1)} custom-call(f32[1024,1024]{1,0:T(8,128)S(1)} %get-tuple-element.26.refs_0_, f32[512,1024]{1,0:T(8,128)S(1)} %get-tuple-element.28.refs_1_, f32[1536,512]{1,0:T(8,128)S(1)} %get-tuple-element.30.refs_2_, f32[512,1536]{1,0:T(8,128)S(1)} %get-tuple-element.32.refs_3_, f32[2048,512]{1,0:T(8,128)S(1)} %get-tuple-element.38.refs_4_, ...), custom_call_target="tpu_custom_call" | custom-call | tf_op jit(solution)/shard_map/grad_6/pallas_call | solution.py:88
  50.3 1.9 %collective-permute-start.14 = (s16[272,768]{1,0:T(8,128)(2,1)S(1)}, s16[272,768]{1,0:T(8,128)(2,1)S(1)}, u32[]{:S(2)}, u32[]{:S(2)}) collective-permute-start(s16[272,768]{1,0:T(8,128)(2,1)S(1)} %grad_6.1), channel_id=1, source_target_pairs={{0,32},{1,97},{2,34},{3,99},{4,36},{5,101},{6,38},{7,103},{8,40},{... | collective-permute-start | bytes 1253384 | tf_op jit(solution)/shard_map/ppermute | solution.py:71
  52.1 1.4 %grad_5.1 = s16[272,768]{1,0:T(8,128)(2,1)S(1)} custom-call(f32[1024,1024]{1,0:T(8,128)S(1)} %get-tuple-element.26.refs_0_, f32[512,1024]{1,0:T(8,128)S(1)} %get-tuple-element.28.refs_1_, f32[1536,512]{1,0:T(8,128)S(1)} %get-tuple-element.30.refs_2_, f32[512,1536]{1,0:T(8,128)S(1)} %get-tuple-element.32.refs_3_, f32[2048,512]{1,0:T(8,128)S(1)} %get-tuple-element.38.refs_4_, ...), custom_call_target="tpu_custom_call" | custom-call | tf_op jit(solution)/shard_map/grad_5/pallas_call | solution.py:88
  53.6 1.4 %collective-permute-start.17 = (s16[272,768]{1,0:T(8,128)(2,1)S(1)}, s16[272,768]{1,0:T(8,128)(2,1)S(1)}, u32[]{:S(2)}, u32[]{:S(2)}) collective-permute-start(s16[272,768]{1,0:T(8,128)(2,1)S(1)} %grad_5.1), channel_id=1, source_target_pairs={{0,2},{1,7},{2,0},{3,5},{4,6},{5,3},{6,4},{7,1},{8,10},{9,15},{10,... | collective-permute-start | bytes 1253384 | tf_op jit(solution)/shard_map/ppermute | solution.py:71
  55.0 1.4 %grad_7.1 = s16[272,768]{1,0:T(8,128)(2,1)S(1)} custom-call(f32[1024,1024]{1,0:T(8,128)S(1)} %get-tuple-element.26.refs_0_, f32[512,1024]{1,0:T(8,128)S(1)} %get-tuple-element.28.refs_1_, f32[1536,512]{1,0:T(8,128)S(1)} %get-tuple-element.30.refs_2_, f32[512,1536]{1,0:T(8,128)S(1)} %get-tuple-element.32.refs_3_, f32[2048,512]{1,0:T(8,128)S(1)} %get-tuple-element.38.refs_4_, ...), custom_call_target="tpu_custom_call" | custom-call | tf_op jit(solution)/shard_map/grad_7/pallas_call | solution.py:88
  56.4 4.5 %collective-permute-start.11 = (s16[272,768]{1,0:T(8,128)(2,1)S(1)}, s16[272,768]{1,0:T(8,128)(2,1)S(1)}, u32[]{:S(2)}, u32[]{:S(2)}) collective-permute-start(s16[272,768]{1,0:T(8,128)(2,1)S(1)} %grad_7.1), channel_id=1, source_target_pairs={{0,42},{1,127},{2,40},{3,125},{4,46},{5,123},{6,44},{7,121},{8,34}... | collective-permute-start | bytes 1253384 | tf_op jit(solution)/shard_map/ppermute | solution.py:71
  60.9 1.4 %grad_1.1 = s16[272,768]{1,0:T(8,128)(2,1)S(1)} custom-call(f32[1024,1024]{1,0:T(8,128)S(1)} %get-tuple-element.26.refs_0_, f32[512,1024]{1,0:T(8,128)S(1)} %get-tuple-element.28.refs_1_, f32[1536,512]{1,0:T(8,128)S(1)} %get-tuple-element.30.refs_2_, f32[512,1536]{1,0:T(8,128)S(1)} %get-tuple-element.32.refs_3_, f32[2048,512]{1,0:T(8,128)S(1)} %get-tuple-element.38.refs_4_, ...), custom_call_target="tpu_custom_call" | custom-call | tf_op jit(solution)/shard_map/grad_1/pallas_call | solution.py:88
  62.4 1.4 %grad_2.1 = s16[272,768]{1,0:T(8,128)(2,1)S(1)} custom-call(f32[1024,1024]{1,0:T(8,128)S(1)} %get-tuple-element.26.refs_0_, f32[512,1024]{1,0:T(8,128)S(1)} %get-tuple-element.28.refs_1_, f32[1536,512]{1,0:T(8,128)S(1)} %get-tuple-element.30.refs_2_, f32[512,1536]{1,0:T(8,128)S(1)} %get-tuple-element.32.refs_3_, f32[2048,512]{1,0:T(8,128)S(1)} %get-tuple-element.38.refs_4_, ...), custom_call_target="tpu_custom_call" | custom-call | tf_op jit(solution)/shard_map/grad_2/pallas_call | solution.py:88
  64.6 1.4 %grad_4.1 = s16[272,768]{1,0:T(8,128)(2,1)S(1)} custom-call(f32[1024,1024]{1,0:T(8,128)S(1)} %get-tuple-element.26.refs_0_, f32[512,1024]{1,0:T(8,128)S(1)} %get-tuple-element.28.refs_1_, f32[1536,512]{1,0:T(8,128)S(1)} %get-tuple-element.30.refs_2_, f32[512,1536]{1,0:T(8,128)S(1)} %get-tuple-element.32.refs_3_, f32[2048,512]{1,0:T(8,128)S(1)} %get-tuple-element.38.refs_4_, ...), custom_call_target="tpu_custom_call" | custom-call | tf_op jit(solution)/shard_map/grad_4/pallas_call | solution.py:88
  66.0 2.8 %collective-permute-start.18 = (s16[272,768]{1,0:T(8,128)(2,1)S(1)}, s16[272,768]{1,0:T(8,128)(2,1)S(1)}, u32[]{:S(2)}, u32[]{:S(2)}) collective-permute-start(s16[272,768]{1,0:T(8,128)(2,1)S(1)} %grad_4.1), channel_id=1, source_target_pairs={{0,32},{1,97},{2,34},{3,99},{4,36},{5,101},{6,38},{7,103},{8,40},{... | collective-permute-start | bytes 1253384 | tf_op jit(solution)/shard_map/ppermute | solution.py:71
  69.9 2.2 %collective-permute-done.13.refs_2_ = s16[272,768]{1,0:T(8,128)(2,1)S(1)} collective-permute-done((s16[272,768]{1,0:T(8,128)(2,1)S(1)}, s16[272,768]{1,0:T(8,128)(2,1)S(1)}, u32[]{:S(2)}, u32[]{:S(2)}) %collective-permute-start.13) | collective-permute-done | bytes 417824 | tf_op jit(solution)/shard_map/ppermute | solution.py:71
  74.4 2.8 %collective-permute-start.19 = (s16[272,768]{1,0:T(8,128)(2,1)S(1)}, s16[272,768]{1,0:T(8,128)(2,1)S(1)}, u32[]{:S(2)}, u32[]{:S(2)}) collective-permute-start(s16[272,768]{1,0:T(8,128)(2,1)S(1)} %collective-permute-done.18.refs_4_), channel_id=1, source_target_pairs={{0,1},{1,0},{2,3},{3,2},{4,5},{5,4},{6,7},{7,6},{8,9},{9,8},{10,11... | collective-permute-start | bytes 1253384 | tf_op jit(solution)/shard_map/ppermute | solution.py:75
  77.2 1.4 %collective-permute-done.19.refs_5_ = s16[272,768]{1,0:T(8,128)(2,1)S(1)} collective-permute-done((s16[272,768]{1,0:T(8,128)(2,1)S(1)}, s16[272,768]{1,0:T(8,128)(2,1)S(1)}, u32[]{:S(2)}, u32[]{:S(2)}) %collective-permute-start.19) | collective-permute-done | bytes 417824 | tf_op jit(solution)/shard_map/ppermute | solution.py:75
  78.6 1.3 %post.1 = (f32[1,1]{1,0:T(1,128)}, f32[128,768]{1,0:T(8,128)}, f32[128,768]{1,0:T(8,128)}) custom-call(bf16[128,768]{1,0:T(8,128)(2,1)S(1)} %copy-done, bf16[128,768]{1,0:T(8,128)(2,1)S(1)} %copy-done.1, f32[136,768]{1,0:T(8,128)S(1)} %get-tuple-element.40.refs_2_, f32[136,768]{1,0:T(8,128)S(1)} %collective-permute-done.16.refs_3_, ...), custom_call_target="tpu_custom_call" | custom-call | tf_op jit(solution)/shard_map/post/pallas_call | solution.py:88
  (34 shorter events, 7.4 us)
Async XLA Ops:
  1.9 2.6 %collective-permute-start = (bf16[144,768]{1,0:T(8,128)(2,1)S(1)}, bf16[144,768]{1,0:T(8,128)(2,1)S(1)}, u32[]{:S(2)}, u32[]{:S(2)}) collective-permute-start(bf16[144,768]{1,0:T(8,128)(2,1)S(1)} %get-tuple-element.25), channel_id=1, source_target_pairs={{0,1},{1,0},{2,3},{3,2},{4,5},{5,4},{6,7},{7,6},{8,9},{9,8},{10,11... | collective-permute-start | bytes 663560 | tf_op jit(solution)/shard_map/ppermute | solution.py:75
  4.5 9.1 %collective-permute-start.3 = (bf16[272,768]{1,0:T(8,128)(2,1)S(1)}, bf16[272,768]{1,0:T(8,128)(2,1)S(1)}, u32[]{:S(2)}, u32[]{:S(2)}) collective-permute-start(bf16[272,768]{1,0:T(8,128)(2,1)S(1)} %join.1.refs_0_.refs_9_), channel_id=1, source_target_pairs={{0,2},{1,7},{2,0},{3,5},{4,6},{5,3},{6,4},{7,1},{8,10},{9,15},{10,... | collective-permute-start | bytes 1253384 | tf_op jit(solution)/shard_map/ppermute | solution.py:71
  7.4 9.2 %collective-permute-start.2 = (bf16[272,768]{1,0:T(8,128)(2,1)S(1)}, bf16[272,768]{1,0:T(8,128)(2,1)S(1)}, u32[]{:S(2)}, u32[]{:S(2)}) collective-permute-start(bf16[272,768]{1,0:T(8,128)(2,1)S(1)} %join.1.refs_0_.refs_9_), channel_id=1, source_target_pairs={{0,8},{1,25},{2,10},{3,27},{4,12},{5,29},{6,14},{7,31},{8,0},{9,17... | collective-permute-start | bytes 1253384 | tf_op jit(solution)/shard_map/ppermute | solution.py:71
  11.2 8.1 %collective-permute-start.1 = (bf16[272,768]{1,0:T(8,128)(2,1)S(1)}, bf16[272,768]{1,0:T(8,128)(2,1)S(1)}, u32[]{:S(2)}, u32[]{:S(2)}) collective-permute-start(bf16[272,768]{1,0:T(8,128)(2,1)S(1)} %join.1.refs_0_.refs_9_), channel_id=1, source_target_pairs={{0,32},{1,97},{2,34},{3,99},{4,36},{5,101},{6,38},{7,103},{8,40},{... | collective-permute-start | bytes 1253384 | tf_op jit(solution)/shard_map/ppermute | solution.py:71
  19.4 5.3 %collective-permute-start.4 = (bf16[1088,768]{1,0:T(8,128)(2,1)S(1)}, bf16[1088,768]{1,0:T(8,128)(2,1)S(1)}, u32[]{:S(2)}, u32[]{:S(2)}) collective-permute-start(bf16[1088,768]{1,0:T(8,128)(2,1)S(1)} %pack_near.1), channel_id=1, source_target_pairs={{0,1},{1,0},{2,3},{3,2},{4,5},{5,4},{6,7},{7,6},{8,9},{9,8},{10,11... | collective-permute-start | bytes 5013512 | tf_op jit(solution)/shard_map/ppermute | solution.py:75
  19.5 10.4 %collective-permute-start.5 = (bf16[272,768]{1,0:T(8,128)(2,1)S(1)}, bf16[272,768]{1,0:T(8,128)(2,1)S(1)}, u32[]{:S(2)}, u32[]{:S(2)}) collective-permute-start(bf16[272,768]{1,0:T(8,128)(2,1)S(1)} %collective-permute-done.3.refs_3_.refs_9_), channel_id=1, source_target_pairs={{0,40},{1,121},{2,42},{3,123},{4,44},{5,125},{6,46},{7,127},{8,32}... | collective-permute-start | bytes 1253384 | tf_op jit(solution)/shard_map/ppermute | solution.py:71
  21.8 8.1 %collective-permute-start.6 = (bf16[272,768]{1,0:T(8,128)(2,1)S(1)}, bf16[272,768]{1,0:T(8,128)(2,1)S(1)}, u32[]{:S(2)}, u32[]{:S(2)}) collective-permute-start(bf16[272,768]{1,0:T(8,128)(2,1)S(1)} %collective-permute-done.1.refs_1_.refs_9_), channel_id=1, source_target_pairs={{0,2},{1,7},{2,0},{3,5},{4,6},{5,3},{6,4},{7,1},{8,10},{9,15},{10,... | collective-permute-start | bytes 1253384 | tf_op jit(solution)/shard_map/ppermute | solution.py:71
  23.1 11.1 %collective-permute-start.8 = (bf16[272,768]{1,0:T(8,128)(2,1)S(1)}, bf16[272,768]{1,0:T(8,128)(2,1)S(1)}, u32[]{:S(2)}, u32[]{:S(2)}) collective-permute-start(bf16[272,768]{1,0:T(8,128)(2,1)S(1)} %collective-permute-done.3.refs_3_.refs_9_), channel_id=1, source_target_pairs={{0,8},{1,25},{2,10},{3,27},{4,12},{5,29},{6,14},{7,31},{8,0},{9,17... | collective-permute-start | bytes 1253384 | tf_op jit(solution)/shard_map/ppermute | solution.py:71
  24.5 9.7 %collective-permute-start.9 = (bf16[272,768]{1,0:T(8,128)(2,1)S(1)}, bf16[272,768]{1,0:T(8,128)(2,1)S(1)}, u32[]{:S(2)}, u32[]{:S(2)}) collective-permute-start(bf16[272,768]{1,0:T(8,128)(2,1)S(1)} %collective-permute-done.2.refs_2_.refs_9_), channel_id=1, source_target_pairs={{0,32},{1,97},{2,34},{3,99},{4,36},{5,101},{6,38},{7,103},{8,40},{... | collective-permute-start | bytes 1253384 | tf_op jit(solution)/shard_map/ppermute | solution.py:71
  29.9 4.5 %collective-permute-start.7 = (bf16[544,768]{1,0:T(8,128)(2,1)S(1)}, bf16[544,768]{1,0:T(8,128)(2,1)S(1)}, u32[]{:S(2)}, u32[]{:S(2)}) collective-permute-start(bf16[544,768]{1,0:T(8,128)(2,1)S(1)} %pack_first.1), channel_id=1, source_target_pairs={{0,1},{1,0},{2,3},{3,2},{4,5},{5,4},{6,7},{7,6},{8,9},{9,8},{10,11... | collective-permute-start | bytes 2506760 | tf_op jit(solution)/shard_map/ppermute | solution.py:75
  34.3 3.3 %collective-permute-start.10 = (bf16[544,768]{1,0:T(8,128)(2,1)S(1)}, bf16[544,768]{1,0:T(8,128)(2,1)S(1)}, u32[]{:S(2)}, u32[]{:S(2)}) collective-permute-start(bf16[544,768]{1,0:T(8,128)(2,1)S(1)} %pack_second.1), channel_id=1, source_target_pairs={{0,1},{1,0},{2,3},{3,2},{4,5},{5,4},{6,7},{7,6},{8,9},{9,8},{10,11... | collective-permute-start | bytes 2506760 | tf_op jit(solution)/shard_map/ppermute | solution.py:75
  48.7 12.1 %collective-permute-start.12 = (s16[272,768]{1,0:T(8,128)(2,1)S(1)}, s16[272,768]{1,0:T(8,128)(2,1)S(1)}, u32[]{:S(2)}, u32[]{:S(2)}) collective-permute-start(s16[272,768]{1,0:T(8,128)(2,1)S(1)} %grad_3.1), channel_id=1, source_target_pairs={{0,8},{1,25},{2,10},{3,27},{4,12},{5,29},{6,14},{7,31},{8,0},{9,17... | collective-permute-start | bytes 1253384 | tf_op jit(solution)/shard_map/ppermute | solution.py:71
  50.3 12.1 %collective-permute-start.14 = (s16[272,768]{1,0:T(8,128)(2,1)S(1)}, s16[272,768]{1,0:T(8,128)(2,1)S(1)}, u32[]{:S(2)}, u32[]{:S(2)}) collective-permute-start(s16[272,768]{1,0:T(8,128)(2,1)S(1)} %grad_6.1), channel_id=1, source_target_pairs={{0,32},{1,97},{2,34},{3,99},{4,36},{5,101},{6,38},{7,103},{8,40},{... | collective-permute-start | bytes 1253384 | tf_op jit(solution)/shard_map/ppermute | solution.py:71
  53.6 11.0 %collective-permute-start.17 = (s16[272,768]{1,0:T(8,128)(2,1)S(1)}, s16[272,768]{1,0:T(8,128)(2,1)S(1)}, u32[]{:S(2)}, u32[]{:S(2)}) collective-permute-start(s16[272,768]{1,0:T(8,128)(2,1)S(1)} %grad_5.1), channel_id=1, source_target_pairs={{0,2},{1,7},{2,0},{3,5},{4,6},{5,3},{6,4},{7,1},{8,10},{9,15},{10,... | collective-permute-start | bytes 1253384 | tf_op jit(solution)/shard_map/ppermute | solution.py:71
  56.4 13.5 %collective-permute-start.11 = (s16[272,768]{1,0:T(8,128)(2,1)S(1)}, s16[272,768]{1,0:T(8,128)(2,1)S(1)}, u32[]{:S(2)}, u32[]{:S(2)}) collective-permute-start(s16[272,768]{1,0:T(8,128)(2,1)S(1)} %grad_7.1), channel_id=1, source_target_pairs={{0,42},{1,127},{2,40},{3,125},{4,46},{5,123},{6,44},{7,121},{8,34}... | collective-permute-start | bytes 1253384 | tf_op jit(solution)/shard_map/ppermute | solution.py:71
  62.3 9.8 %collective-permute-start.13 = (s16[272,768]{1,0:T(8,128)(2,1)S(1)}, s16[272,768]{1,0:T(8,128)(2,1)S(1)}, u32[]{:S(2)}, u32[]{:S(2)}) collective-permute-start(s16[272,768]{1,0:T(8,128)(2,1)S(1)} %grad_1.1), channel_id=1, source_target_pairs={{0,2},{1,7},{2,0},{3,5},{4,6},{5,3},{6,4},{7,1},{8,10},{9,15},{10,... | collective-permute-start | bytes 1253384 | tf_op jit(solution)/shard_map/ppermute | solution.py:71
  63.9 9.5 %collective-permute-start.15 = (s16[272,768]{1,0:T(8,128)(2,1)S(1)}, s16[272,768]{1,0:T(8,128)(2,1)S(1)}, u32[]{:S(2)}, u32[]{:S(2)}) collective-permute-start(s16[272,768]{1,0:T(8,128)(2,1)S(1)} %grad_2.1), channel_id=1, source_target_pairs={{0,8},{1,25},{2,10},{3,27},{4,12},{5,29},{6,14},{7,31},{8,0},{9,17... | collective-permute-start | bytes 1253384 | tf_op jit(solution)/shard_map/ppermute | solution.py:71
  66.0 12.6 %copy-start = (bf16[128,768]{1,0:T(8,128)(2,1)S(1)}, bf16[128,768]{1,0:T(8,128)(2,1)}, u32[]{:S(2)}) copy-start(bf16[128,768]{1,0:T(8,128)(2,1)} %refs_0_.1) | copy-start | bytes 589828
  66.0 12.6 %copy-start.1 = (bf16[128,768]{1,0:T(8,128)(2,1)S(1)}, bf16[128,768]{1,0:T(8,128)(2,1)}, u32[]{:S(2)}) copy-start(bf16[128,768]{1,0:T(8,128)(2,1)} %refs_1_.1) | copy-start | bytes 589828
  66.0 8.4 %collective-permute-start.18 = (s16[272,768]{1,0:T(8,128)(2,1)S(1)}, s16[272,768]{1,0:T(8,128)(2,1)S(1)}, u32[]{:S(2)}, u32[]{:S(2)}) collective-permute-start(s16[272,768]{1,0:T(8,128)(2,1)S(1)} %grad_4.1), channel_id=1, source_target_pairs={{0,32},{1,97},{2,34},{3,99},{4,36},{5,101},{6,38},{7,103},{8,40},{... | collective-permute-start | bytes 1253384 | tf_op jit(solution)/shard_map/ppermute | solution.py:71
  73.8 3.4 %collective-permute-start.16 = (f32[136,768]{1,0:T(8,128)S(1)}, f32[136,768]{1,0:T(8,128)S(1)}, u32[]{:S(2)}, u32[]{:S(2)}) collective-permute-start(f32[136,768]{1,0:T(8,128)S(1)} %get-tuple-element.41), channel_id=1, source_target_pairs={{0,1},{1,0},{2,3},{3,2},{4,5},{5,4},{6,7},{7,6},{8,9},{9,8},{10,11... | collective-permute-start | bytes 1253384 | tf_op jit(solution)/shard_map/ppermute | solution.py:75
  74.4 4.2 %collective-permute-start.19 = (s16[272,768]{1,0:T(8,128)(2,1)S(1)}, s16[272,768]{1,0:T(8,128)(2,1)S(1)}, u32[]{:S(2)}, u32[]{:S(2)}) collective-permute-start(s16[272,768]{1,0:T(8,128)(2,1)S(1)} %collective-permute-done.18.refs_4_), channel_id=1, source_target_pairs={{0,1},{1,0},{2,3},{3,2},{4,5},{5,4},{6,7},{7,6},{8,9},{9,8},{10,11... | collective-permute-start | bytes 1253384 | tf_op jit(solution)/shard_map/ppermute | solution.py:75

commit v4 on v3

--- a/solution.py
+++ b/solution.py
@@ -267,13 +267,14 @@
     for h in range(WIDTH // 128):
         piece = jnp.abs(value[:, h * 128 : (h + 1) * 128])
         largest = piece if largest is None else jnp.maximum(largest, piece)
-    largest = jnp.max(jnp.transpose(largest), axis=0, keepdims=True)
+    largest = jnp.max(largest, axis=1, keepdims=True)
     power = jnp.ceil(jnp.log2(jnp.maximum(largest, 1e-35)) * 128.0)
-    steps = value * down_rows(FULL * jnp.exp2(power * (-1.0 / 128.0)), WIDTH)
+    steps = value * (FULL * jnp.exp2(power * (-1.0 / 128.0)))
     out_ref[:BLOCK, :] = jnp.floor(steps + 0.5).astype(jnp.int32).astype(jnp.int16)
     at = lax.broadcasted_iota(jnp.int32, (PAD, BLOCK), 0)
     lane = lax.broadcasted_iota(jnp.int32, (PAD, BLOCK), 1)
-    tail = jnp.where(at == 0, jnp.broadcast_to(power, (PAD, BLOCK)), 0.0)
+    power = jnp.transpose(jnp.broadcast_to(power, (BLOCK, 128)))[:PAD, :]
+    tail = jnp.where(at == 0, power, 0.0)
     for n, digit in enumerate(digits):
         tail = jnp.where((at == 1) & (lane == n), digit, tail)
     out_ref[BLOCK:, :] = jnp.zeros((PAD, WIDTH), jnp.int16)

time: 80.1 us -> 79.8 us (level)
  transfers between devices with their start and end apart: 20 -> 20, of which waited for: 9 -> 9; matrix products, arithmetic and copies ran while one was open for 0% -> 0% of each run, Pallas kernels for 21% -> 20%
where the time goes in v4:
time: 79.8 us; the launch traced here: 79.7 us
  starting transfers between devices  30.4 us (38%)
  Pallas kernels  22.6 us (28%)
  waiting for transfers between devices  18.3 us (23%)
  blocking collectives  7.53 us (9%)
  between operations  0.81 us (1%)
    ppermute x14, starting transfers between devices, send(): return lax.ppermute(value, 'dp', partners(bits))  25.7 us
    pallas_call x20, Pallas kernels, call(): pl.pallas_call(body, name=name, out_shape=out_shape, scratch_shapes=scrat...  21.3 us
    ppermute x14, waiting for transfers between devices, send(): return lax.ppermute(value, 'dp', partners(bits))  15.8 us
    all_to_all x1, blocking collectives, local(): lax.all_to_all(parts[-1][1], 'dp', 0, 0, axis_index_groups=SUM_GROUPS, ti...  7.53 us
    ppermute x6, starting transfers between devices, swap(): return lax.ppermute(value, 'dp', SWAP)  4.78 us
    ppermute x6, waiting for transfers between devices, swap(): return lax.ppermute(value, 'dp', SWAP)  2.5 us
  transfers between devices with their start and end apart: 20, of which 9 were waited for; matrix products, arithmetic and copies ran while one was open for 0% of the time, Pallas kernels for 20%

profile of v4, /device:TPU:1, one launch (start us, length us, event | category | flops | bytes accessed | tf_op | source)
XLA Modules:
  0.0 79.7 jit_solution(4951861014818927253)
XLA Ops:
  0.6 1.2 %pre.1 = (bf16[144,768]{1,0:T(8,128)(2,1)S(1)}, bf16[144,768]{1,0:T(8,128)(2,1)S(1)}) custom-call(bf16[128,768]{1,0:T(8,128)(2,1)} %refs_0_.1, bf16[128,768]{1,0:T(8,128)(2,1)} %refs_1_.1, s32[1,128]{1,0:T(1,128)} %bitcast.2), custom_call_target="tpu_custom_call" | custom-call | tf_op jit(solution)/shard_map/pre/pallas_call | solution.py:400
  1.9 1.5 %collective-permute-start = (bf16[144,768]{1,0:T(8,128)(2,1)S(1)}, bf16[144,768]{1,0:T(8,128)(2,1)S(1)}, u32[]{:S(2)}, u32[]{:S(2)}) collective-permute-start(bf16[144,768]{1,0:T(8,128)(2,1)S(1)} %get-tuple-element.25), channel_id=1, source_target_pairs={{0,1},{1,0},{2,3},{3,2},{4,5},{5,4},{6,7},{7,6},{8,9},{9,8},{10,11... | collective-permute-start | bytes 663560 | tf_op jit(solution)/shard_map/ppermute | solution.py:75
  4.5 2.9 %collective-permute-start.3 = (bf16[272,768]{1,0:T(8,128)(2,1)S(1)}, bf16[272,768]{1,0:T(8,128)(2,1)S(1)}, u32[]{:S(2)}, u32[]{:S(2)}) collective-permute-start(bf16[272,768]{1,0:T(8,128)(2,1)S(1)} %join.1.refs_0_.refs_9_), channel_id=1, source_target_pairs={{0,2},{1,7},{2,0},{3,5},{4,6},{5,3},{6,4},{7,1},{8,10},{9,15},{10,... | collective-permute-start | bytes 1253384 | tf_op jit(solution)/shard_map/ppermute | solution.py:71
  7.4 3.8 %collective-permute-start.2 = (bf16[272,768]{1,0:T(8,128)(2,1)S(1)}, bf16[272,768]{1,0:T(8,128)(2,1)S(1)}, u32[]{:S(2)}, u32[]{:S(2)}) collective-permute-start(bf16[272,768]{1,0:T(8,128)(2,1)S(1)} %join.1.refs_0_.refs_9_), channel_id=1, source_target_pairs={{0,8},{1,25},{2,10},{3,27},{4,12},{5,29},{6,14},{7,31},{8,0},{9,17... | collective-permute-start | bytes 1253384 | tf_op jit(solution)/shard_map/ppermute | solution.py:71
  11.2 2.5 %collective-permute-start.1 = (bf16[272,768]{1,0:T(8,128)(2,1)S(1)}, bf16[272,768]{1,0:T(8,128)(2,1)S(1)}, u32[]{:S(2)}, u32[]{:S(2)}) collective-permute-start(bf16[272,768]{1,0:T(8,128)(2,1)S(1)} %join.1.refs_0_.refs_9_), channel_id=1, source_target_pairs={{0,32},{1,97},{2,34},{3,99},{4,36},{5,101},{6,38},{7,103},{8,40},{... | collective-permute-start | bytes 1253384 | tf_op jit(solution)/shard_map/ppermute | solution.py:71
  13.7 2.9 %collective-permute-done.2.refs_2_.refs_9_ = bf16[272,768]{1,0:T(8,128)(2,1)S(1)} collective-permute-done((bf16[272,768]{1,0:T(8,128)(2,1)S(1)}, bf16[272,768]{1,0:T(8,128)(2,1)S(1)}, u32[]{:S(2)}, u32[]{:S(2)}) %collective-permute-start.2) | collective-permute-done | bytes 417824 | tf_op jit(solution)/shard_map/ppermute | solution.py:71
  16.6 2.7 %collective-permute-done.1.refs_1_.refs_9_ = bf16[272,768]{1,0:T(8,128)(2,1)S(1)} collective-permute-done((bf16[272,768]{1,0:T(8,128)(2,1)S(1)}, bf16[272,768]{1,0:T(8,128)(2,1)S(1)}, u32[]{:S(2)}, u32[]{:S(2)}) %collective-permute-start.1) | collective-permute-done | bytes 417824 | tf_op jit(solution)/shard_map/ppermute | solution.py:71
  19.5 2.3 %collective-permute-start.5 = (bf16[272,768]{1,0:T(8,128)(2,1)S(1)}, bf16[272,768]{1,0:T(8,128)(2,1)S(1)}, u32[]{:S(2)}, u32[]{:S(2)}) collective-permute-start(bf16[272,768]{1,0:T(8,128)(2,1)S(1)} %collective-permute-done.3.refs_3_.refs_9_), channel_id=1, source_target_pairs={{0,40},{1,121},{2,42},{3,123},{4,44},{5,125},{6,46},{7,127},{8,32}... | collective-permute-start | bytes 1253384 | tf_op jit(solution)/shard_map/ppermute | solution.py:71
  21.8 1.4 %collective-permute-start.6 = (bf16[272,768]{1,0:T(8,128)(2,1)S(1)}, bf16[272,768]{1,0:T(8,128)(2,1)S(1)}, u32[]{:S(2)}, u32[]{:S(2)}) collective-permute-start(bf16[272,768]{1,0:T(8,128)(2,1)S(1)} %collective-permute-done.1.refs_1_.refs_9_), channel_id=1, source_target_pairs={{0,2},{1,7},{2,0},{3,5},{4,6},{5,3},{6,4},{7,1},{8,10},{9,15},{10,... | collective-permute-start | bytes 1253384 | tf_op jit(solution)/shard_map/ppermute | solution.py:71
  23.1 1.4 %collective-permute-start.8 = (bf16[272,768]{1,0:T(8,128)(2,1)S(1)}, bf16[272,768]{1,0:T(8,128)(2,1)S(1)}, u32[]{:S(2)}, u32[]{:S(2)}) collective-permute-start(bf16[272,768]{1,0:T(8,128)(2,1)S(1)} %collective-permute-done.3.refs_3_.refs_9_), channel_id=1, source_target_pairs={{0,8},{1,25},{2,10},{3,27},{4,12},{5,29},{6,14},{7,31},{8,0},{9,17... | collective-permute-start | bytes 1253384 | tf_op jit(solution)/shard_map/ppermute | solution.py:71
  24.7 2.0 %tile_0.1 = (f32[1024,1024]{1,0:T(8,128)S(1)}, f32[1024,128]{1,0:T(8,128)S(1)}, f32[16,1024]{1,0:T(8,128)S(1)}) custom-call(bf16[272,768]{1,0:T(8,128)(2,1)S(1)} %join.1.refs_0_.refs_9_, bf16[272,768]{1,0:T(8,128)(2,1)S(1)} %collective-permute-done.1.refs_1_.refs_9_, bf16[272,768]{1,0:T(8,128)(2,1)S(1)} %collective-permute-done.2.refs_2_.refs_9_, ...), custom_call_target="tpu_custom_call" | custom-call | tf_op jit(solution)/shard_map/tile_0/pallas_call | solution.py:88
  26.7 3.1 %collective-permute-done.5.refs_0_.refs_4_.refs_9_ = bf16[272,768]{1,0:T(8,128)(2,1)S(1)} collective-permute-done((bf16[272,768]{1,0:T(8,128)(2,1)S(1)}, bf16[272,768]{1,0:T(8,128)(2,1)S(1)}, u32[]{:S(2)}, u32[]{:S(2)}) %collective-permute-start.5) | collective-permute-done | bytes 417824 | tf_op jit(solution)/shard_map/ppermute | solution.py:71
  31.2 3.1 %collective-permute-done.8.refs_0_.refs_6_.refs_9_ = bf16[272,768]{1,0:T(8,128)(2,1)S(1)} collective-permute-done((bf16[272,768]{1,0:T(8,128)(2,1)S(1)}, bf16[272,768]{1,0:T(8,128)(2,1)S(1)}, u32[]{:S(2)}, u32[]{:S(2)}) %collective-permute-start.8) | collective-permute-done | bytes 417824 | tf_op jit(solution)/shard_map/ppermute | solution.py:71
  34.4 1.5 %tile_2.1 = (f32[1536,512]{1,0:T(8,128)S(1)}, f32[1536,128]{1,0:T(8,128)S(1)}, f32[16,512]{1,0:T(8,128)S(1)}) custom-call(bf16[272,768]{1,0:T(8,128)(2,1)S(1)} %join.1.refs_0_.refs_9_, bf16[272,768]{1,0:T(8,128)(2,1)S(1)} %collective-permute-done.1.refs_1_.refs_9_, bf16[272,768]{1,0:T(8,128)(2,1)S(1)} %collective-permute-done.2.refs_2_.refs_9_, ...), custom_call_target="tpu_custom_call" | custom-call | tf_op jit(solution)/shard_map/tile_2/pallas_call | solution.py:88
  35.9 1.6 %tile_3.1 = (f32[512,1536]{1,0:T(8,128)S(1)}, f32[512,128]{1,0:T(8,128)S(1)}, f32[16,1536]{1,0:T(8,128)S(1)}) custom-call(bf16[272,768]{1,0:T(8,128)(2,1)S(1)} %collective-permute-done.8.refs_0_.refs_6_.refs_9_, bf16[272,768]{1,0:T(8,128)(2,1)S(1)} %collective-permute-done.9.refs_1_.refs_7_.refs_9_, ...), custom_call_target="tpu_custom_call" | custom-call | tf_op jit(solution)/shard_map/tile_3/pallas_call | solution.py:88
  37.6 2.0 %tile_4.1 = (f32[2048,512]{1,0:T(8,128)S(1)}, f32[8,32,128]{2,1,0:T(8,128)S(1)}) custom-call(bf16[272,768]{1,0:T(8,128)(2,1)S(1)} %join.1.refs_0_.refs_9_, bf16[272,768]{1,0:T(8,128)(2,1)S(1)} %collective-permute-done.1.refs_1_.refs_9_, bf16[272,768]{1,0:T(8,128)(2,1)S(1)} %collective-permute-done.2.refs_2_.refs_9_, ...), custom_call_target="tpu_custom_call" | custom-call | tf_op jit(solution)/shard_map/tile_4/pallas_call | solution.py:88
  39.6 7.5 %all_to_all.5.refs_0_ = f32[8,32,128]{2,1,0:T(8,128)S(1)} all-to-all(f32[8,32,128]{2,1,0:T(8,128)S(1)} %get-tuple-element.39), channel_id=1, replica_groups={{0,2,8,10,32,34,40,42},{4,6,12,14,36,38,44,46},{16,18,24,26,48,50,56,58..., dimensions={0} | all-to-all | bytes 262144 | tf_op jit(solution)/shard_map/all_to_all | solution.py:457
  47.3 1.4 %grad_3.1 = s16[272,768]{1,0:T(8,128)(2,1)S(1)} custom-call(f32[1024,1024]{1,0:T(8,128)S(1)} %get-tuple-element.26.refs_0_, f32[512,1024]{1,0:T(8,128)S(1)} %get-tuple-element.28.refs_1_, f32[1536,512]{1,0:T(8,128)S(1)} %get-tuple-element.30.refs_2_, f32[512,1536]{1,0:T(8,128)S(1)} %get-tuple-element.32.refs_3_, f32[2048,512]{1,0:T(8,128)S(1)} %get-tuple-element.38.refs_4_, ...), custom_call_target="tpu_custom_call" | custom-call | tf_op jit(solution)/shard_map/grad_3/pallas_call | solution.py:88
  48.8 1.4 %grad_6.1 = s16[272,768]{1,0:T(8,128)(2,1)S(1)} custom-call(f32[1024,1024]{1,0:T(8,128)S(1)} %get-tuple-element.26.refs_0_, f32[512,1024]{1,0:T(8,128)S(1)} %get-tuple-element.28.refs_1_, f32[1536,512]{1,0:T(8,128)S(1)} %get-tuple-element.30.refs_2_, f32[512,1536]{1,0:T(8,128)S(1)} %get-tuple-element.32.refs_3_, f32[2048,512]{1,0:T(8,128)S(1)} %get-tuple-element.38.refs_4_, ...), custom_call_target="tpu_custom_call" | custom-call | tf_op jit(solution)/shard_map/grad_6/pallas_call | solution.py:88
  50.2 1.9 %collective-permute-start.14 = (s16[272,768]{1,0:T(8,128)(2,1)S(1)}, s16[272,768]{1,0:T(8,128)(2,1)S(1)}, u32[]{:S(2)}, u32[]{:S(2)}) collective-permute-start(s16[272,768]{1,0:T(8,128)(2,1)S(1)} %grad_6.1), channel_id=1, source_target_pairs={{0,32},{1,97},{2,34},{3,99},{4,36},{5,101},{6,38},{7,103},{8,40},{... | collective-permute-start | bytes 1253384 | tf_op jit(solution)/shard_map/ppermute | solution.py:71
  52.0 1.4 %grad_5.1 = s16[272,768]{1,0:T(8,128)(2,1)S(1)} custom-call(f32[1024,1024]{1,0:T(8,128)S(1)} %get-tuple-element.26.refs_0_, f32[512,1024]{1,0:T(8,128)S(1)} %get-tuple-element.28.refs_1_, f32[1536,512]{1,0:T(8,128)S(1)} %get-tuple-element.30.refs_2_, f32[512,1536]{1,0:T(8,128)S(1)} %get-tuple-element.32.refs_3_, f32[2048,512]{1,0:T(8,128)S(1)} %get-tuple-element.38.refs_4_, ...), custom_call_target="tpu_custom_call" | custom-call | tf_op jit(solution)/shard_map/grad_5/pallas_call | solution.py:88
  53.4 1.4 %collective-permute-start.17 = (s16[272,768]{1,0:T(8,128)(2,1)S(1)}, s16[272,768]{1,0:T(8,128)(2,1)S(1)}, u32[]{:S(2)}, u32[]{:S(2)}) collective-permute-start(s16[272,768]{1,0:T(8,128)(2,1)S(1)} %grad_5.1), channel_id=1, source_target_pairs={{0,2},{1,7},{2,0},{3,5},{4,6},{5,3},{6,4},{7,1},{8,10},{9,15},{10,... | collective-permute-start | bytes 1253384 | tf_op jit(solution)/shard_map/ppermute | solution.py:71
  54.8 1.4 %grad_7.1 = s16[272,768]{1,0:T(8,128)(2,1)S(1)} custom-call(f32[1024,1024]{1,0:T(8,128)S(1)} %get-tuple-element.26.refs_0_, f32[512,1024]{1,0:T(8,128)S(1)} %get-tuple-element.28.refs_1_, f32[1536,512]{1,0:T(8,128)S(1)} %get-tuple-element.30.refs_2_, f32[512,1536]{1,0:T(8,128)S(1)} %get-tuple-element.32.refs_3_, f32[2048,512]{1,0:T(8,128)S(1)} %get-tuple-element.38.refs_4_, ...), custom_call_target="tpu_custom_call" | custom-call | tf_op jit(solution)/shard_map/grad_7/pallas_call | solution.py:88
  56.1 4.4 %collective-permute-start.11 = (s16[272,768]{1,0:T(8,128)(2,1)S(1)}, s16[272,768]{1,0:T(8,128)(2,1)S(1)}, u32[]{:S(2)}, u32[]{:S(2)}) collective-permute-start(s16[272,768]{1,0:T(8,128)(2,1)S(1)} %grad_7.1), channel_id=1, source_target_pairs={{0,42},{1,127},{2,40},{3,125},{4,46},{5,123},{6,44},{7,121},{8,34}... | collective-permute-start | bytes 1253384 | tf_op jit(solution)/shard_map/ppermute | solution.py:71
  60.6 1.4 %grad_1.1 = s16[272,768]{1,0:T(8,128)(2,1)S(1)} custom-call(f32[1024,1024]{1,0:T(8,128)S(1)} %get-tuple-element.26.refs_0_, f32[512,1024]{1,0:T(8,128)S(1)} %get-tuple-element.28.refs_1_, f32[1536,512]{1,0:T(8,128)S(1)} %get-tuple-element.30.refs_2_, f32[512,1536]{1,0:T(8,128)S(1)} %get-tuple-element.32.refs_3_, f32[2048,512]{1,0:T(8,128)S(1)} %get-tuple-element.38.refs_4_, ...), custom_call_target="tpu_custom_call" | custom-call | tf_op jit(solution)/shard_map/grad_1/pallas_call | solution.py:88
  62.1 1.4 %grad_2.1 = s16[272,768]{1,0:T(8,128)(2,1)S(1)} custom-call(f32[1024,1024]{1,0:T(8,128)S(1)} %get-tuple-element.26.refs_0_, f32[512,1024]{1,0:T(8,128)S(1)} %get-tuple-element.28.refs_1_, f32[1536,512]{1,0:T(8,128)S(1)} %get-tuple-element.30.refs_2_, f32[512,1536]{1,0:T(8,128)S(1)} %get-tuple-element.32.refs_3_, f32[2048,512]{1,0:T(8,128)S(1)} %get-tuple-element.38.refs_4_, ...), custom_call_target="tpu_custom_call" | custom-call | tf_op jit(solution)/shard_map/grad_2/pallas_call | solution.py:88
  64.2 1.4 %grad_4.1 = s16[272,768]{1,0:T(8,128)(2,1)S(1)} custom-call(f32[1024,1024]{1,0:T(8,128)S(1)} %get-tuple-element.26.refs_0_, f32[512,1024]{1,0:T(8,128)S(1)} %get-tuple-element.28.refs_1_, f32[1536,512]{1,0:T(8,128)S(1)} %get-tuple-element.30.refs_2_, f32[512,1536]{1,0:T(8,128)S(1)} %get-tuple-element.32.refs_3_, f32[2048,512]{1,0:T(8,128)S(1)} %get-tuple-element.38.refs_4_, ...), custom_call_target="tpu_custom_call" | custom-call | tf_op jit(solution)/shard_map/grad_4/pallas_call | solution.py:88
  65.6 2.8 %collective-permute-start.18 = (s16[272,768]{1,0:T(8,128)(2,1)S(1)}, s16[272,768]{1,0:T(8,128)(2,1)S(1)}, u32[]{:S(2)}, u32[]{:S(2)}) collective-permute-start(s16[272,768]{1,0:T(8,128)(2,1)S(1)} %grad_4.1), channel_id=1, source_target_pairs={{0,32},{1,97},{2,34},{3,99},{4,36},{5,101},{6,38},{7,103},{8,40},{... | collective-permute-start | bytes 1253384 | tf_op jit(solution)/shard_map/ppermute | solution.py:71
  69.5 2.4 %collective-permute-done.13.refs_2_ = s16[272,768]{1,0:T(8,128)(2,1)S(1)} collective-permute-done((s16[272,768]{1,0:T(8,128)(2,1)S(1)}, s16[272,768]{1,0:T(8,128)(2,1)S(1)}, u32[]{:S(2)}, u32[]{:S(2)}) %collective-permute-start.13) | collective-permute-done | bytes 417824 | tf_op jit(solution)/shard_map/ppermute | solution.py:71
  74.0 2.9 %collective-permute-start.19 = (s16[272,768]{1,0:T(8,128)(2,1)S(1)}, s16[272,768]{1,0:T(8,128)(2,1)S(1)}, u32[]{:S(2)}, u32[]{:S(2)}) collective-permute-start(s16[272,768]{1,0:T(8,128)(2,1)S(1)} %collective-permute-done.18.refs_4_), channel_id=1, source_target_pairs={{0,1},{1,0},{2,3},{3,2},{4,5},{5,4},{6,7},{7,6},{8,9},{9,8},{10,11... | collective-permute-start | bytes 1253384 | tf_op jit(solution)/shard_map/ppermute | solution.py:75
  76.9 1.4 %collective-permute-done.19.refs_5_ = s16[272,768]{1,0:T(8,128)(2,1)S(1)} collective-permute-done((s16[272,768]{1,0:T(8,128)(2,1)S(1)}, s16[272,768]{1,0:T(8,128)(2,1)S(1)}, u32[]{:S(2)}, u32[]{:S(2)}) %collective-permute-start.19) | collective-permute-done | bytes 417824 | tf_op jit(solution)/shard_map/ppermute | solution.py:75
  78.3 1.3 %post.1 = (f32[1,1]{1,0:T(1,128)}, f32[128,768]{1,0:T(8,128)}, f32[128,768]{1,0:T(8,128)}) custom-call(bf16[128,768]{1,0:T(8,128)(2,1)S(1)} %copy-done, bf16[128,768]{1,0:T(8,128)(2,1)S(1)} %copy-done.1, f32[136,768]{1,0:T(8,128)S(1)} %get-tuple-element.40.refs_2_, f32[136,768]{1,0:T(8,128)S(1)} %collective-permute-done.16.refs_3_, ...), custom_call_target="tpu_custom_call" | custom-call | tf_op jit(solution)/shard_map/post/pallas_call | solution.py:88
  (34 shorter events, 7.2 us)
Async XLA Ops:
  1.9 2.6 %collective-permute-start = (bf16[144,768]{1,0:T(8,128)(2,1)S(1)}, bf16[144,768]{1,0:T(8,128)(2,1)S(1)}, u32[]{:S(2)}, u32[]{:S(2)}) collective-permute-start(bf16[144,768]{1,0:T(8,128)(2,1)S(1)} %get-tuple-element.25), channel_id=1, source_target_pairs={{0,1},{1,0},{2,3},{3,2},{4,5},{5,4},{6,7},{7,6},{8,9},{9,8},{10,11... | collective-permute-start | bytes 663560 | tf_op jit(solution)/shard_map/ppermute | solution.py:75
  4.5 9.1 %collective-permute-start.3 = (bf16[272,768]{1,0:T(8,128)(2,1)S(1)}, bf16[272,768]{1,0:T(8,128)(2,1)S(1)}, u32[]{:S(2)}, u32[]{:S(2)}) collective-permute-start(bf16[272,768]{1,0:T(8,128)(2,1)S(1)} %join.1.refs_0_.refs_9_), channel_id=1, source_target_pairs={{0,2},{1,7},{2,0},{3,5},{4,6},{5,3},{6,4},{7,1},{8,10},{9,15},{10,... | collective-permute-start | bytes 1253384 | tf_op jit(solution)/shard_map/ppermute | solution.py:71
  7.4 9.2 %collective-permute-start.2 = (bf16[272,768]{1,0:T(8,128)(2,1)S(1)}, bf16[272,768]{1,0:T(8,128)(2,1)S(1)}, u32[]{:S(2)}, u32[]{:S(2)}) collective-permute-start(bf16[272,768]{1,0:T(8,128)(2,1)S(1)} %join.1.refs_0_.refs_9_), channel_id=1, source_target_pairs={{0,8},{1,25},{2,10},{3,27},{4,12},{5,29},{6,14},{7,31},{8,0},{9,17... | collective-permute-start | bytes 1253384 | tf_op jit(solution)/shard_map/ppermute | solution.py:71
  11.2 8.1 %collective-permute-start.1 = (bf16[272,768]{1,0:T(8,128)(2,1)S(1)}, bf16[272,768]{1,0:T(8,128)(2,1)S(1)}, u32[]{:S(2)}, u32[]{:S(2)}) collective-permute-start(bf16[272,768]{1,0:T(8,128)(2,1)S(1)} %join.1.refs_0_.refs_9_), channel_id=1, source_target_pairs={{0,32},{1,97},{2,34},{3,99},{4,36},{5,101},{6,38},{7,103},{8,40},{... | collective-permute-start | bytes 1253384 | tf_op jit(solution)/shard_map/ppermute | solution.py:71
  19.4 5.3 %collective-permute-start.4 = (bf16[1088,768]{1,0:T(8,128)(2,1)S(1)}, bf16[1088,768]{1,0:T(8,128)(2,1)S(1)}, u32[]{:S(2)}, u32[]{:S(2)}) collective-permute-start(bf16[1088,768]{1,0:T(8,128)(2,1)S(1)} %pack_near.1), channel_id=1, source_target_pairs={{0,1},{1,0},{2,3},{3,2},{4,5},{5,4},{6,7},{7,6},{8,9},{9,8},{10,11... | collective-permute-start | bytes 5013512 | tf_op jit(solution)/shard_map/ppermute | solution.py:75
  19.5 10.4 %collective-permute-start.5 = (bf16[272,768]{1,0:T(8,128)(2,1)S(1)}, bf16[272,768]{1,0:T(8,128)(2,1)S(1)}, u32[]{:S(2)}, u32[]{:S(2)}) collective-permute-start(bf16[272,768]{1,0:T(8,128)(2,1)S(1)} %collective-permute-done.3.refs_3_.refs_9_), channel_id=1, source_target_pairs={{0,40},{1,121},{2,42},{3,123},{4,44},{5,125},{6,46},{7,127},{8,32}... | collective-permute-start | bytes 1253384 | tf_op jit(solution)/shard_map/ppermute | solution.py:71
  21.8 8.1 %collective-permute-start.6 = (bf16[272,768]{1,0:T(8,128)(2,1)S(1)}, bf16[272,768]{1,0:T(8,128)(2,1)S(1)}, u32[]{:S(2)}, u32[]{:S(2)}) collective-permute-start(bf16[272,768]{1,0:T(8,128)(2,1)S(1)} %collective-permute-done.1.refs_1_.refs_9_), channel_id=1, source_target_pairs={{0,2},{1,7},{2,0},{3,5},{4,6},{5,3},{6,4},{7,1},{8,10},{9,15},{10,... | collective-permute-start | bytes 1253384 | tf_op jit(solution)/shard_map/ppermute | solution.py:71
  23.1 11.1 %collective-permute-start.8 = (bf16[272,768]{1,0:T(8,128)(2,1)S(1)}, bf16[272,768]{1,0:T(8,128)(2,1)S(1)}, u32[]{:S(2)}, u32[]{:S(2)}) collective-permute-start(bf16[272,768]{1,0:T(8,128)(2,1)S(1)} %collective-permute-done.3.refs_3_.refs_9_), channel_id=1, source_target_pairs={{0,8},{1,25},{2,10},{3,27},{4,12},{5,29},{6,14},{7,31},{8,0},{9,17... | collective-permute-start | bytes 1253384 | tf_op jit(solution)/shard_map/ppermute | solution.py:71
  24.5 9.7 %collective-permute-start.9 = (bf16[272,768]{1,0:T(8,128)(2,1)S(1)}, bf16[272,768]{1,0:T(8,128)(2,1)S(1)}, u32[]{:S(2)}, u32[]{:S(2)}) collective-permute-start(bf16[272,768]{1,0:T(8,128)(2,1)S(1)} %collective-permute-done.2.refs_2_.refs_9_), channel_id=1, source_target_pairs={{0,32},{1,97},{2,34},{3,99},{4,36},{5,101},{6,38},{7,103},{8,40},{... | collective-permute-start | bytes 1253384 | tf_op jit(solution)/shard_map/ppermute | solution.py:71
  29.9 4.5 %collective-permute-start.7 = (bf16[544,768]{1,0:T(8,128)(2,1)S(1)}, bf16[544,768]{1,0:T(8,128)(2,1)S(1)}, u32[]{:S(2)}, u32[]{:S(2)}) collective-permute-start(bf16[544,768]{1,0:T(8,128)(2,1)S(1)} %pack_first.1), channel_id=1, source_target_pairs={{0,1},{1,0},{2,3},{3,2},{4,5},{5,4},{6,7},{7,6},{8,9},{9,8},{10,11... | collective-permute-start | bytes 2506760 | tf_op jit(solution)/shard_map/ppermute | solution.py:75
  34.3 3.3 %collective-permute-start.10 = (bf16[544,768]{1,0:T(8,128)(2,1)S(1)}, bf16[544,768]{1,0:T(8,128)(2,1)S(1)}, u32[]{:S(2)}, u32[]{:S(2)}) collective-permute-start(bf16[544,768]{1,0:T(8,128)(2,1)S(1)} %pack_second.1), channel_id=1, source_target_pairs={{0,1},{1,0},{2,3},{3,2},{4,5},{5,4},{6,7},{7,6},{8,9},{9,8},{10,11... | collective-permute-start | bytes 2506760 | tf_op jit(solution)/shard_map/ppermute | solution.py:75
  48.7 11.9 %collective-permute-start.12 = (s16[272,768]{1,0:T(8,128)(2,1)S(1)}, s16[272,768]{1,0:T(8,128)(2,1)S(1)}, u32[]{:S(2)}, u32[]{:S(2)}) collective-permute-start(s16[272,768]{1,0:T(8,128)(2,1)S(1)} %grad_3.1), channel_id=1, source_target_pairs={{0,8},{1,25},{2,10},{3,27},{4,12},{5,29},{6,14},{7,31},{8,0},{9,17... | collective-permute-start | bytes 1253384 | tf_op jit(solution)/shard_map/ppermute | solution.py:71
  50.2 11.9 %collective-permute-start.14 = (s16[272,768]{1,0:T(8,128)(2,1)S(1)}, s16[272,768]{1,0:T(8,128)(2,1)S(1)}, u32[]{:S(2)}, u32[]{:S(2)}) collective-permute-start(s16[272,768]{1,0:T(8,128)(2,1)S(1)} %grad_6.1), channel_id=1, source_target_pairs={{0,32},{1,97},{2,34},{3,99},{4,36},{5,101},{6,38},{7,103},{8,40},{... | collective-permute-start | bytes 1253384 | tf_op jit(solution)/shard_map/ppermute | solution.py:71
  53.4 10.8 %collective-permute-start.17 = (s16[272,768]{1,0:T(8,128)(2,1)S(1)}, s16[272,768]{1,0:T(8,128)(2,1)S(1)}, u32[]{:S(2)}, u32[]{:S(2)}) collective-permute-start(s16[272,768]{1,0:T(8,128)(2,1)S(1)} %grad_5.1), channel_id=1, source_target_pairs={{0,2},{1,7},{2,0},{3,5},{4,6},{5,3},{6,4},{7,1},{8,10},{9,15},{10,... | collective-permute-start | bytes 1253384 | tf_op jit(solution)/shard_map/ppermute | solution.py:71
  56.1 13.4 %collective-permute-start.11 = (s16[272,768]{1,0:T(8,128)(2,1)S(1)}, s16[272,768]{1,0:T(8,128)(2,1)S(1)}, u32[]{:S(2)}, u32[]{:S(2)}) collective-permute-start(s16[272,768]{1,0:T(8,128)(2,1)S(1)} %grad_7.1), channel_id=1, source_target_pairs={{0,42},{1,127},{2,40},{3,125},{4,46},{5,123},{6,44},{7,121},{8,34}... | collective-permute-start | bytes 1253384 | tf_op jit(solution)/shard_map/ppermute | solution.py:71
  62.0 9.9 %collective-permute-start.13 = (s16[272,768]{1,0:T(8,128)(2,1)S(1)}, s16[272,768]{1,0:T(8,128)(2,1)S(1)}, u32[]{:S(2)}, u32[]{:S(2)}) collective-permute-start(s16[272,768]{1,0:T(8,128)(2,1)S(1)} %grad_1.1), channel_id=1, source_target_pairs={{0,2},{1,7},{2,0},{3,5},{4,6},{5,3},{6,4},{7,1},{8,10},{9,15},{10,... | collective-permute-start | bytes 1253384 | tf_op jit(solution)/shard_map/ppermute | solution.py:71
  63.5 9.6 %collective-permute-start.15 = (s16[272,768]{1,0:T(8,128)(2,1)S(1)}, s16[272,768]{1,0:T(8,128)(2,1)S(1)}, u32[]{:S(2)}, u32[]{:S(2)}) collective-permute-start(s16[272,768]{1,0:T(8,128)(2,1)S(1)} %grad_2.1), channel_id=1, source_target_pairs={{0,8},{1,25},{2,10},{3,27},{4,12},{5,29},{6,14},{7,31},{8,0},{9,17... | collective-permute-start | bytes 1253384 | tf_op jit(solution)/shard_map/ppermute | solution.py:71
  65.6 12.7 %copy-start = (bf16[128,768]{1,0:T(8,128)(2,1)S(1)}, bf16[128,768]{1,0:T(8,128)(2,1)}, u32[]{:S(2)}) copy-start(bf16[128,768]{1,0:T(8,128)(2,1)} %refs_0_.1) | copy-start | bytes 589828
  65.6 12.7 %copy-start.1 = (bf16[128,768]{1,0:T(8,128)(2,1)S(1)}, bf16[128,768]{1,0:T(8,128)(2,1)}, u32[]{:S(2)}) copy-start(bf16[128,768]{1,0:T(8,128)(2,1)} %refs_1_.1) | copy-start | bytes 589828
  65.6 8.4 %collective-permute-start.18 = (s16[272,768]{1,0:T(8,128)(2,1)S(1)}, s16[272,768]{1,0:T(8,128)(2,1)S(1)}, u32[]{:S(2)}, u32[]{:S(2)}) collective-permute-start(s16[272,768]{1,0:T(8,128)(2,1)S(1)} %grad_4.1), channel_id=1, source_target_pairs={{0,32},{1,97},{2,34},{3,99},{4,36},{5,101},{6,38},{7,103},{8,40},{... | collective-permute-start | bytes 1253384 | tf_op jit(solution)/shard_map/ppermute | solution.py:71
  73.6 3.4 %collective-permute-start.16 = (f32[136,768]{1,0:T(8,128)S(1)}, f32[136,768]{1,0:T(8,128)S(1)}, u32[]{:S(2)}, u32[]{:S(2)}) collective-permute-start(f32[136,768]{1,0:T(8,128)S(1)} %get-tuple-element.41), channel_id=1, source_target_pairs={{0,1},{1,0},{2,3},{3,2},{4,5},{5,4},{6,7},{7,6},{8,9},{9,8},{10,11... | collective-permute-start | bytes 1253384 | tf_op jit(solution)/shard_map/ppermute | solution.py:75
  74.0 4.3 %collective-permute-start.19 = (s16[272,768]{1,0:T(8,128)(2,1)S(1)}, s16[272,768]{1,0:T(8,128)(2,1)S(1)}, u32[]{:S(2)}, u32[]{:S(2)}) collective-permute-start(s16[272,768]{1,0:T(8,128)(2,1)S(1)} %collective-permute-done.18.refs_4_), channel_id=1, source_target_pairs={{0,1},{1,0},{2,3},{3,2},{4,5},{5,4},{6,7},{7,6},{8,9},{9,8},{10,11... | collective-permute-start | bytes 1253384 | tf_op jit(solution)/shard_map/ppermute | solution.py:75

commit v5 on v4

--- a/solution.py
+++ b/solution.py
@@ -16,6 +16,7 @@
 SIDE = CUBE * BLOCK
 WIDTH = 768
 PAD = 16
+PIECES = (48, 48, 40)
 LOSS = 8
 PER = BLOCK // 128
 HALF = CUBE * PER
@@ -51,6 +52,10 @@
                     to = [flip(v) if bits & bit else v for v, bit in ((x, 4), (z, 2), (y, 1))]
                     moves.append((device_index(x, z, y, core), device_index(*to, core)))
     return moves
+
+
+def crossing(bits):
+    return [(source, target ^ 1) for source, target in partners(bits)]
 
 
 def a_cubes():
@@ -281,10 +286,16 @@
     out_ref[BLOCK:, :BLOCK] = tail.astype(jnp.int32).astype(jnp.int16)
 
 
-def decode(ref, at=slice(0, BLOCK)):
+def decode(ref):
     tail = ref[BLOCK:, :BLOCK].astype(jnp.int32).astype(F32)
-    scale = down_rows(jnp.exp2(tail[0:1, at] * (1.0 / 128.0)) * (1.0 / FULL), WIDTH)
-    return ref[at, :].astype(jnp.int32).astype(F32) * scale
+    scale = down_rows(jnp.exp2(tail[0:1, :] * (1.0 / 128.0)) * (1.0 / FULL), WIDTH)
+    return ref[:BLOCK, :].astype(jnp.int32).astype(F32) * scale
+
+
+def decode_half(ref, half):
+    tail = ref[ROWS:, half * ROWS : (half + 1) * ROWS].astype(jnp.int32).astype(F32)
+    scale = down_rows(jnp.exp2(tail[0:1, :] * (1.0 / 128.0)) * (1.0 / FULL), WIDTH)
+    return ref[:ROWS, :].astype(jnp.int32).astype(F32) * scale
 
 
 def digits_of(loss):
@@ -295,8 +306,8 @@
     return high, middle, low
 
 
-def loss_of(ref):
-    tail = ref[BLOCK:, :BLOCK].astype(jnp.int32).astype(F32)[1:2, :]
+def loss_of(ref, rows=BLOCK):
+    tail = ref[rows:, :BLOCK].astype(jnp.int32).astype(F32)[1:2, :]
     lane = lax.broadcasted_iota(jnp.int32, (1, BLOCK), 1)
     unit = jnp.where(lane == 0, 16.0, jnp.where(lane == 1, 1.0 / 1024.0, 1.0 / (1024.0 * 16384.0)))
     return jnp.sum(jnp.where(lane < 3, tail * unit, 0.0))
@@ -351,47 +362,76 @@
         out_ref[BLOCK:, :] = jnp.full((LOSS, WIDTH), loss, F32)
 
 
+def halves_kernel(number, *refs):
+    *given, same_ref, cross_ref, full_ref = refs
+    grad_kernel(number, True, *given, full_ref)
+    low, high, tail = slice(0, ROWS), slice(ROWS, BLOCK), slice(BLOCK, SPAN)
+    same_ref[ROWS:, :] = full_ref[tail, :]
+    cross_ref[ROWS:, :] = full_ref[tail, :]
+    role = role_of()
+
+    @pl.when(role == 0)
+    def _():
+        same_ref[:ROWS, :] = full_ref[low, :]
+        cross_ref[:ROWS, :] = full_ref[high, :]
+
+    @pl.when(role == 1)
+    def _():
+        same_ref[:ROWS, :] = full_ref[high, :]
+        cross_ref[:ROWS, :] = full_ref[low, :]
+
+
 def split_kernel(own_ref, *refs):
-    come, (keep_ref, send_ref) = refs[:-2], refs[-2:]
+    count = len(PIECES) + 1
+    come, keep_ref, send_refs = refs[:-count], refs[-count], refs[1 - count :]
     value, loss = own_ref[:BLOCK, :], own_ref[BLOCK, 0]
     for ref in come:
         value = value + decode(ref)
         loss = loss + loss_of(ref)
     role = role_of()
     keep_ref[ROWS:, :] = jnp.full((LOSS, WIDTH), loss, F32)
-    send_ref[ROWS:, :] = jnp.full((LOSS, WIDTH), loss, F32)
+    send_refs[-1][PIECES[-1] - LOSS :, :] = jnp.full((LOSS, WIDTH), loss, F32)
+
+    def give(half):
+        start = 0
+        for rows, ref in zip(PIECES, send_refs):
+            stop = min(start + rows, ROWS)
+            ref[: stop - start, :] = half[start:stop, :]
+            start = stop
 
     @pl.when(role == 0)
     def _():
         keep_ref[:ROWS, :] = value[:ROWS, :]
-        send_ref[:ROWS, :] = value[ROWS:, :]
+        give(value[ROWS:, :])
 
     @pl.when(role == 1)
     def _():
         keep_ref[:ROWS, :] = value[ROWS:, :]
-        send_ref[:ROWS, :] = value[:ROWS, :]
-
-
-def post_kernel(q_ref, d_ref, keep_ref, come_ref, last_ref, other_ref, loss_ref, gq_ref, gd_ref):
+        give(value[:ROWS, :])
+
+
+def post_kernel(q_ref, d_ref, keep_ref, same_ref, cross_ref, *refs):
+    *come, loss_ref, gq_ref, gd_ref = refs
+    come_ref = jnp.concatenate([ref[...] for ref in come], axis=0)
+
     def project(out_ref, grad, values):
         unit, length = unit_rows(values)
         out_ref[...] = (grad - jnp.sum(grad * unit, axis=1, keepdims=True) * unit) / length
 
     def fill(gq, last_q, gd, last_d, half):
-        at = slice(half * ROWS, (half + 1) * ROWS)
-        project(gq_ref, gq[:ROWS, :] + decode(last_q, at), q_ref[...])
-        project(gd_ref, gd[:ROWS, :] + decode(last_d, at), d_ref[...])
-        loss_ref[...] = (gd[ROWS : ROWS + 1, 0:1] + loss_of(last_d)) * (1.0 / 16384)
+        project(gq_ref, gq[:ROWS, :] + decode_half(last_q, half), q_ref[...])
+        project(gd_ref, gd[:ROWS, :] + decode_half(last_d, half), d_ref[...])
+        loss_ref[...] = (gd[ROWS : ROWS + 1, 0:1] + loss_of(last_d, ROWS)) * (1.0 / 16384)
 
     role = role_of()
 
     @pl.when(role == 0)
     def _():
-        fill(keep_ref, last_ref, come_ref, other_ref, 0)
+        fill(keep_ref, same_ref, come_ref, cross_ref, 0)
 
     @pl.when(role == 1)
     def _():
-        fill(come_ref, other_ref, keep_ref, last_ref, 1)
+        fill(come_ref, cross_ref, keep_ref, same_ref, 1)
 
 
 def local(queries, documents, positives):
@@ -458,18 +498,23 @@
     scales = call(scale_kernel, "scales", pltpu.VMEM((HALF + 8, 128), F32), near(stats))
 
     coded = pltpu.VMEM((SPAN, WIDTH), jnp.int16)
+    half = pltpu.VMEM((ROWS + PAD, WIDTH), jnp.int16)
     plain = pltpu.VMEM((BLOCK + LOSS, WIDTH), F32)
 
     def grad(number, *come, after=(), shape=coded):
+        halves = shape is half
         return call(
-            functools.partial(grad_kernel, number, shape is coded),
+            functools.partial(halves_kernel, number)
+            if halves
+            else functools.partial(grad_kernel, number, shape is coded),
             f"grad_{number}",
-            shape,
+            [half, half] if halves else shape,
             *[near(v[0]) for v in parts],
             *[near(v) for v in y],
             near(scales),
             near(x[number]),
             *[near(v) for v in come],
+            scratch=[coded] if halves else [],
             after=after,
         )
 
@@ -479,19 +524,20 @@
     r6 = send(g6, 4)
     g5 = grad(5)
     r5 = send(g5, 1)
-    g7 = grad(7)
+    g7 = grad(7, after=[g5])
     r7 = send(g7, 7)
     g1 = grad(1, r3)
     r1 = send(g1, 1)
     g2 = grad(2, r6)
     r2 = send(g2, 2)
-    g4 = grad(4, r5)
-    r4 = send(g4, 4)
-    g0 = grad(0, shape=plain)
+    halves = grad(4, r5, shape=half)
+    cross = lax.ppermute(halves[1], "dp", crossing(4))
+    same = send(halves[0], 4)
+    g0 = grad(0, after=[halves[0]], shape=plain)
     part = pltpu.VMEM((ROWS + LOSS, WIDTH), F32)
-    keep, give = call(split_kernel, "split", [part, part], *[near(v) for v in (g0, r7, r1, r2)])
-    come = swap(give)
-    other = swap(r4)
+    pieces = [pltpu.VMEM((rows, WIDTH), F32) for rows in PIECES]
+    keep, *give = call(split_kernel, "split", [part, *pieces], *[near(v) for v in (g0, r7, r1, r2)])
+    come = [swap(v) for v in give]
     loss, gq, gd = call(
         post_kernel,
         "post",
@@ -502,7 +548,7 @@
         ],
         queries,
         documents,
-        *[near(v) for v in (keep, come, r4, other)],
+        *[near(v) for v in (keep, same, cross, *come)],
     )
     return (loss.reshape(()), gq, gd)
 

time: 79.8 us -> 78.5 us (0.984)
  waiting for transfers between devices: 18.3 us -> 16.4 us
    ppermute x0 -> x1, starting transfers between devices: none -> 4.69 us  [local(): cross = lax.ppermute(halves[1], 'dp', crossing(4))]
    ppermute x6 -> x7, starting transfers between devices: 4.78 us -> 2.43 us  [swap(): return lax.ppermute(value, 'dp', SWAP)]
    ppermute x14, starting transfers between devices: 25.7 us -> 23.8 us  [send(): return lax.ppermute(value, 'dp', partners(bits))]
    ppermute x6 -> x7, waiting for transfers between devices: 2.5 us -> 1.12 us  [swap(): return lax.ppermute(value, 'dp', SWAP)]
  transfers between devices with their start and end apart: 20 -> 22, of which waited for: 9 -> 7; matrix products, arithmetic and copies ran while one was open for 0% -> 0% of each run, Pallas kernels for 20% -> 21%
where the time goes in v5:
time: 78.5 us; the launch traced here: 78.3 us
  starting transfers between devices  30.9 us (39%)
  Pallas kernels  22.6 us (29%)
  waiting for transfers between devices  16.4 us (21%)
  blocking collectives  7.53 us (10%)
  between operations  0.84 us (1%)
    ppermute x14, starting transfers between devices, send(): return lax.ppermute(value, 'dp', partners(bits))  23.8 us
    pallas_call x20, Pallas kernels, call(): pl.pallas_call(body, name=name, out_shape=out_shape, scratch_shapes=scrat...  21.4 us
    ppermute x14, waiting for transfers between devices, send(): return lax.ppermute(value, 'dp', partners(bits))  15.3 us
    all_to_all x1, blocking collectives, local(): lax.all_to_all(parts[-1][1], 'dp', 0, 0, axis_index_groups=SUM_GROUPS, ti...  7.53 us
    ppermute x1, starting transfers between devices, local(): cross = lax.ppermute(halves[1], 'dp', crossing(4))  4.69 us
    ppermute x7, starting transfers between devices, swap(): return lax.ppermute(value, 'dp', SWAP)  2.43 us
  transfers between devices with their start and end apart: 22, of which 7 were waited for; matrix products, arithmetic and copies ran while one was open for 0% of the time, Pallas kernels for 21%

profile of v5, /device:TPU:1, one launch (start us, length us, event | category | flops | bytes accessed | tf_op | source)
XLA Modules:
  0.0 78.3 jit_solution(13739157618450157369)
XLA Ops:
  0.6 1.2 %pre.1 = (bf16[144,768]{1,0:T(8,128)(2,1)S(1)}, bf16[144,768]{1,0:T(8,128)(2,1)S(1)}) custom-call(bf16[128,768]{1,0:T(8,128)(2,1)} %refs_0_.1, bf16[128,768]{1,0:T(8,128)(2,1)} %refs_1_.1, s32[1,128]{1,0:T(1,128)} %bitcast.2), custom_call_target="tpu_custom_call" | custom-call | tf_op jit(solution)/shard_map/pre/pallas_call | solution.py:440
  1.9 1.5 %collective-permute-start = (bf16[144,768]{1,0:T(8,128)(2,1)S(1)}, bf16[144,768]{1,0:T(8,128)(2,1)S(1)}, u32[]{:S(2)}, u32[]{:S(2)}) collective-permute-start(bf16[144,768]{1,0:T(8,128)(2,1)S(1)} %get-tuple-element.29), channel_id=1, source_target_pairs={{0,1},{1,0},{2,3},{3,2},{4,5},{5,4},{6,7},{7,6},{8,9},{9,8},{10,11... | collective-permute-start | bytes 663560 | tf_op jit(solution)/shard_map/ppermute | solution.py:80
  4.5 2.9 %collective-permute-start.3 = (bf16[272,768]{1,0:T(8,128)(2,1)S(1)}, bf16[272,768]{1,0:T(8,128)(2,1)S(1)}, u32[]{:S(2)}, u32[]{:S(2)}) collective-permute-start(bf16[272,768]{1,0:T(8,128)(2,1)S(1)} %join.1.refs_0_.refs_9_), channel_id=1, source_target_pairs={{0,2},{1,7},{2,0},{3,5},{4,6},{5,3},{6,4},{7,1},{8,10},{9,15},{10,... | collective-permute-start | bytes 1253384 | tf_op jit(solution)/shard_map/ppermute | solution.py:76
  7.4 3.8 %collective-permute-start.2 = (bf16[272,768]{1,0:T(8,128)(2,1)S(1)}, bf16[272,768]{1,0:T(8,128)(2,1)S(1)}, u32[]{:S(2)}, u32[]{:S(2)}) collective-permute-start(bf16[272,768]{1,0:T(8,128)(2,1)S(1)} %join.1.refs_0_.refs_9_), channel_id=1, source_target_pairs={{0,8},{1,25},{2,10},{3,27},{4,12},{5,29},{6,14},{7,31},{8,0},{9,17... | collective-permute-start | bytes 1253384 | tf_op jit(solution)/shard_map/ppermute | solution.py:76
  11.2 2.5 %collective-permute-start.1 = (bf16[272,768]{1,0:T(8,128)(2,1)S(1)}, bf16[272,768]{1,0:T(8,128)(2,1)S(1)}, u32[]{:S(2)}, u32[]{:S(2)}) collective-permute-start(bf16[272,768]{1,0:T(8,128)(2,1)S(1)} %join.1.refs_0_.refs_9_), channel_id=1, source_target_pairs={{0,32},{1,97},{2,34},{3,99},{4,36},{5,101},{6,38},{7,103},{8,40},{... | collective-permute-start | bytes 1253384 | tf_op jit(solution)/shard_map/ppermute | solution.py:76
  13.7 2.9 %collective-permute-done.2.refs_2_.refs_9_ = bf16[272,768]{1,0:T(8,128)(2,1)S(1)} collective-permute-done((bf16[272,768]{1,0:T(8,128)(2,1)S(1)}, bf16[272,768]{1,0:T(8,128)(2,1)S(1)}, u32[]{:S(2)}, u32[]{:S(2)}) %collective-permute-start.2) | collective-permute-done | bytes 417824 | tf_op jit(solution)/shard_map/ppermute | solution.py:76
  16.6 2.7 %collective-permute-done.1.refs_1_.refs_9_ = bf16[272,768]{1,0:T(8,128)(2,1)S(1)} collective-permute-done((bf16[272,768]{1,0:T(8,128)(2,1)S(1)}, bf16[272,768]{1,0:T(8,128)(2,1)S(1)}, u32[]{:S(2)}, u32[]{:S(2)}) %collective-permute-start.1) | collective-permute-done | bytes 417824 | tf_op jit(solution)/shard_map/ppermute | solution.py:76
  19.5 2.3 %collective-permute-start.5 = (bf16[272,768]{1,0:T(8,128)(2,1)S(1)}, bf16[272,768]{1,0:T(8,128)(2,1)S(1)}, u32[]{:S(2)}, u32[]{:S(2)}) collective-permute-start(bf16[272,768]{1,0:T(8,128)(2,1)S(1)} %collective-permute-done.3.refs_3_.refs_9_), channel_id=1, source_target_pairs={{0,40},{1,121},{2,42},{3,123},{4,44},{5,125},{6,46},{7,127},{8,32}... | collective-permute-start | bytes 1253384 | tf_op jit(solution)/shard_map/ppermute | solution.py:76
  21.8 1.4 %collective-permute-start.6 = (bf16[272,768]{1,0:T(8,128)(2,1)S(1)}, bf16[272,768]{1,0:T(8,128)(2,1)S(1)}, u32[]{:S(2)}, u32[]{:S(2)}) collective-permute-start(bf16[272,768]{1,0:T(8,128)(2,1)S(1)} %collective-permute-done.1.refs_1_.refs_9_), channel_id=1, source_target_pairs={{0,2},{1,7},{2,0},{3,5},{4,6},{5,3},{6,4},{7,1},{8,10},{9,15},{10,... | collective-permute-start | bytes 1253384 | tf_op jit(solution)/shard_map/ppermute | solution.py:76
  23.1 1.4 %collective-permute-start.8 = (bf16[272,768]{1,0:T(8,128)(2,1)S(1)}, bf16[272,768]{1,0:T(8,128)(2,1)S(1)}, u32[]{:S(2)}, u32[]{:S(2)}) collective-permute-start(bf16[272,768]{1,0:T(8,128)(2,1)S(1)} %collective-permute-done.3.refs_3_.refs_9_), channel_id=1, source_target_pairs={{0,8},{1,25},{2,10},{3,27},{4,12},{5,29},{6,14},{7,31},{8,0},{9,17... | collective-permute-start | bytes 1253384 | tf_op jit(solution)/shard_map/ppermute | solution.py:76
  24.7 2.0 %tile_0.1 = (f32[1024,1024]{1,0:T(8,128)S(1)}, f32[1024,128]{1,0:T(8,128)S(1)}, f32[16,1024]{1,0:T(8,128)S(1)}) custom-call(bf16[272,768]{1,0:T(8,128)(2,1)S(1)} %join.1.refs_0_.refs_9_, bf16[272,768]{1,0:T(8,128)(2,1)S(1)} %collective-permute-done.1.refs_1_.refs_9_, bf16[272,768]{1,0:T(8,128)(2,1)S(1)} %collective-permute-done.2.refs_2_.refs_9_, ...), custom_call_target="tpu_custom_call" | custom-call | tf_op jit(solution)/shard_map/tile_0/pallas_call | solution.py:93
  26.7 3.1 %collective-permute-done.5.refs_0_.refs_4_.refs_9_ = bf16[272,768]{1,0:T(8,128)(2,1)S(1)} collective-permute-done((bf16[272,768]{1,0:T(8,128)(2,1)S(1)}, bf16[272,768]{1,0:T(8,128)(2,1)S(1)}, u32[]{:S(2)}, u32[]{:S(2)}) %collective-permute-start.5) | collective-permute-done | bytes 417824 | tf_op jit(solution)/shard_map/ppermute | solution.py:76
  30.0 1.1 %tile_1.1 = (f32[512,1024]{1,0:T(8,128)S(1)}, f32[512,128]{1,0:T(8,128)S(1)}, f32[16,1024]{1,0:T(8,128)S(1)}) custom-call(bf16[272,768]{1,0:T(8,128)(2,1)S(1)} %collective-permute-done.5.refs_0_.refs_4_.refs_9_, bf16[272,768]{1,0:T(8,128)(2,1)S(1)} %collective-permute-done.6.refs_1_.refs_5_.refs_9_, ...), custom_call_target="tpu_custom_call" | custom-call | tf_op jit(solution)/shard_map/tile_1/pallas_call | solution.py:93
  31.2 3.1 %collective-permute-done.8.refs_0_.refs_6_.refs_9_ = bf16[272,768]{1,0:T(8,128)(2,1)S(1)} collective-permute-done((bf16[272,768]{1,0:T(8,128)(2,1)S(1)}, bf16[272,768]{1,0:T(8,128)(2,1)S(1)}, u32[]{:S(2)}, u32[]{:S(2)}) %collective-permute-start.8) | collective-permute-done | bytes 417824 | tf_op jit(solution)/shard_map/ppermute | solution.py:76
  34.4 1.5 %tile_2.1 = (f32[1536,512]{1,0:T(8,128)S(1)}, f32[1536,128]{1,0:T(8,128)S(1)}, f32[16,512]{1,0:T(8,128)S(1)}) custom-call(bf16[272,768]{1,0:T(8,128)(2,1)S(1)} %join.1.refs_0_.refs_9_, bf16[272,768]{1,0:T(8,128)(2,1)S(1)} %collective-permute-done.1.refs_1_.refs_9_, bf16[272,768]{1,0:T(8,128)(2,1)S(1)} %collective-permute-done.2.refs_2_.refs_9_, ...), custom_call_target="tpu_custom_call" | custom-call | tf_op jit(solution)/shard_map/tile_2/pallas_call | solution.py:93
  36.0 1.6 %tile_3.1 = (f32[512,1536]{1,0:T(8,128)S(1)}, f32[512,128]{1,0:T(8,128)S(1)}, f32[16,1536]{1,0:T(8,128)S(1)}) custom-call(bf16[272,768]{1,0:T(8,128)(2,1)S(1)} %collective-permute-done.8.refs_0_.refs_6_.refs_9_, bf16[272,768]{1,0:T(8,128)(2,1)S(1)} %collective-permute-done.9.refs_1_.refs_7_.refs_9_, ...), custom_call_target="tpu_custom_call" | custom-call | tf_op jit(solution)/shard_map/tile_3/pallas_call | solution.py:93
  37.6 2.0 %tile_4.1 = (f32[2048,512]{1,0:T(8,128)S(1)}, f32[8,32,128]{2,1,0:T(8,128)S(1)}) custom-call(bf16[272,768]{1,0:T(8,128)(2,1)S(1)} %join.1.refs_0_.refs_9_, bf16[272,768]{1,0:T(8,128)(2,1)S(1)} %collective-permute-done.1.refs_1_.refs_9_, bf16[272,768]{1,0:T(8,128)(2,1)S(1)} %collective-permute-done.2.refs_2_.refs_9_, ...), custom_call_target="tpu_custom_call" | custom-call | tf_op jit(solution)/shard_map/tile_4/pallas_call | solution.py:93
  39.6 7.5 %all_to_all.5.refs_0_ = f32[8,32,128]{2,1,0:T(8,128)S(1)} all-to-all(f32[8,32,128]{2,1,0:T(8,128)S(1)} %get-tuple-element.43), channel_id=1, replica_groups={{0,2,8,10,32,34,40,42},{4,6,12,14,36,38,44,46},{16,18,24,26,48,50,56,58..., dimensions={0} | all-to-all | bytes 262144 | tf_op jit(solution)/shard_map/all_to_all | solution.py:497
  47.3 1.4 %grad_3.1 = s16[272,768]{1,0:T(8,128)(2,1)S(1)} custom-call(f32[1024,1024]{1,0:T(8,128)S(1)} %get-tuple-element.30.refs_0_, f32[512,1024]{1,0:T(8,128)S(1)} %get-tuple-element.32.refs_1_, f32[1536,512]{1,0:T(8,128)S(1)} %get-tuple-element.34.refs_2_, f32[512,1536]{1,0:T(8,128)S(1)} %get-tuple-element.36.refs_3_, f32[2048,512]{1,0:T(8,128)S(1)} %get-tuple-element.42.refs_4_, ...), custom_call_target="tpu_custom_call" | custom-call | tf_op jit(solution)/shard_map/grad_3/pallas_call | solution.py:93
  48.8 1.4 %grad_6.1 = s16[272,768]{1,0:T(8,128)(2,1)S(1)} custom-call(f32[1024,1024]{1,0:T(8,128)S(1)} %get-tuple-element.30.refs_0_, f32[512,1024]{1,0:T(8,128)S(1)} %get-tuple-element.32.refs_1_, f32[1536,512]{1,0:T(8,128)S(1)} %get-tuple-element.34.refs_2_, f32[512,1536]{1,0:T(8,128)S(1)} %get-tuple-element.36.refs_3_, f32[2048,512]{1,0:T(8,128)S(1)} %get-tuple-element.42.refs_4_, ...), custom_call_target="tpu_custom_call" | custom-call | tf_op jit(solution)/shard_map/grad_6/pallas_call | solution.py:93
  50.2 1.9 %collective-permute-start.15 = (s16[272,768]{1,0:T(8,128)(2,1)S(1)}, s16[272,768]{1,0:T(8,128)(2,1)S(1)}, u32[]{:S(2)}, u32[]{:S(2)}) collective-permute-start(s16[272,768]{1,0:T(8,128)(2,1)S(1)} %grad_6.1), channel_id=1, source_target_pairs={{0,32},{1,97},{2,34},{3,99},{4,36},{5,101},{6,38},{7,103},{8,40},{... | collective-permute-start | bytes 1253384 | tf_op jit(solution)/shard_map/ppermute | solution.py:76
  52.0 1.4 %grad_5.1.refs_10_ = s16[272,768]{1,0:T(8,128)(2,1)S(1)} custom-call(f32[1024,1024]{1,0:T(8,128)S(1)} %get-tuple-element.30.refs_0_, f32[512,1024]{1,0:T(8,128)S(1)} %get-tuple-element.32.refs_1_, f32[1536,512]{1,0:T(8,128)S(1)} %get-tuple-element.34.refs_2_, f32[512,1536]{1,0:T(8,128)S(1)} %get-tuple-element.36.refs_3_, ...), custom_call_target="tpu_custom_call" | custom-call | tf_op jit(solution)/shard_map/grad_5/pallas_call | solution.py:93
  53.4 1.4 %collective-permute-start.11 = (s16[272,768]{1,0:T(8,128)(2,1)S(1)}, s16[272,768]{1,0:T(8,128)(2,1)S(1)}, u32[]{:S(2)}, u32[]{:S(2)}) collective-permute-start(s16[272,768]{1,0:T(8,128)(2,1)S(1)} %grad_5.1.refs_10_), channel_id=1, source_target_pairs={{0,2},{1,7},{2,0},{3,5},{4,6},{5,3},{6,4},{7,1},{8,10},{9,15},{10,... | collective-permute-start | bytes 1253384 | tf_op jit(solution)/shard_map/ppermute | solution.py:76
  54.8 1.4 %grad_7.1 = s16[272,768]{1,0:T(8,128)(2,1)S(1)} custom-call(f32[1024,1024]{1,0:T(8,128)S(1)} %get-tuple-element.30.refs_0_, f32[512,1024]{1,0:T(8,128)S(1)} %get-tuple-element.32.refs_1_, f32[1536,512]{1,0:T(8,128)S(1)} %get-tuple-element.34.refs_2_, f32[512,1536]{1,0:T(8,128)S(1)} %get-tuple-element.36.refs_3_, f32[2048,512]{1,0:T(8,128)S(1)} %get-tuple-element.42.refs_4_, ...), custom_call_target="tpu_custom_call" | custom-call | tf_op jit(solution)/shard_map/grad_7/pallas_call | solution.py:93
  56.1 4.5 %collective-permute-start.12 = (s16[272,768]{1,0:T(8,128)(2,1)S(1)}, s16[272,768]{1,0:T(8,128)(2,1)S(1)}, u32[]{:S(2)}, u32[]{:S(2)}) collective-permute-start(s16[272,768]{1,0:T(8,128)(2,1)S(1)} %grad_7.1), channel_id=1, source_target_pairs={{0,42},{1,127},{2,40},{3,125},{4,46},{5,123},{6,44},{7,121},{8,34}... | collective-permute-start | bytes 1253384 | tf_op jit(solution)/shard_map/ppermute | solution.py:76
  60.6 1.4 %grad_1.1 = s16[272,768]{1,0:T(8,128)(2,1)S(1)} custom-call(f32[1024,1024]{1,0:T(8,128)S(1)} %get-tuple-element.30.refs_0_, f32[512,1024]{1,0:T(8,128)S(1)} %get-tuple-element.32.refs_1_, f32[1536,512]{1,0:T(8,128)S(1)} %get-tuple-element.34.refs_2_, f32[512,1536]{1,0:T(8,128)S(1)} %get-tuple-element.36.refs_3_, f32[2048,512]{1,0:T(8,128)S(1)} %get-tuple-element.42.refs_4_, ...), custom_call_target="tpu_custom_call" | custom-call | tf_op jit(solution)/shard_map/grad_1/pallas_call | solution.py:93
  62.1 1.4 %grad_2.1 = s16[272,768]{1,0:T(8,128)(2,1)S(1)} custom-call(f32[1024,1024]{1,0:T(8,128)S(1)} %get-tuple-element.30.refs_0_, f32[512,1024]{1,0:T(8,128)S(1)} %get-tuple-element.32.refs_1_, f32[1536,512]{1,0:T(8,128)S(1)} %get-tuple-element.34.refs_2_, f32[512,1536]{1,0:T(8,128)S(1)} %get-tuple-element.36.refs_3_, f32[2048,512]{1,0:T(8,128)S(1)} %get-tuple-element.42.refs_4_, ...), custom_call_target="tpu_custom_call" | custom-call | tf_op jit(solution)/shard_map/grad_2/pallas_call | solution.py:93
  64.2 1.4 %grad_4.1 = (s16[144,768]{1,0:T(8,128)(2,1)S(1)}, s16[144,768]{1,0:T(8,128)(2,1)S(1)}) custom-call(f32[1024,1024]{1,0:T(8,128)S(1)} %get-tuple-element.30.refs_0_, f32[512,1024]{1,0:T(8,128)S(1)} %get-tuple-element.32.refs_1_, f32[1536,512]{1,0:T(8,128)S(1)} %get-tuple-element.34.refs_2_, f32[512,1536]{1,0:T(8,128)S(1)} %get-tuple-element.36.refs_3_, ...), custom_call_target="tpu_custom_call" | custom-call | tf_op jit(solution)/shard_map/grad_4/pallas_call | solution.py:93
  65.6 4.7 %collective-permute-start.18 = (s16[144,768]{1,0:T(8,128)(2,1)S(1)}, s16[144,768]{1,0:T(8,128)(2,1)S(1)}, u32[]{:S(2)}, u32[]{:S(2)}) collective-permute-start(s16[144,768]{1,0:T(8,128)(2,1)S(1)} %get-tuple-element.46), channel_id=1, source_target_pairs={{0,33},{1,96},{2,35},{3,98},{4,37},{5,100},{6,39},{7,102},{8,41},{... | collective-permute-start | bytes 663560 | tf_op jit(solution)/shard_map/ppermute | solution.py:534
  71.2 1.1 %grad_0.1.refs_0_ = f32[264,768]{1,0:T(8,128)S(1)} custom-call(f32[1024,1024]{1,0:T(8,128)S(1)} %get-tuple-element.30.refs_0_, f32[512,1024]{1,0:T(8,128)S(1)} %get-tuple-element.32.refs_1_, f32[1536,512]{1,0:T(8,128)S(1)} %get-tuple-element.34.refs_2_, f32[512,1536]{1,0:T(8,128)S(1)} %get-tuple-element.36.refs_3_, ...), custom_call_target="tpu_custom_call" | custom-call | tf_op jit(solution)/shard_map/grad_0/pallas_call | solution.py:93
  74.5 2.4 %collective-permute-done.17.refs_3_ = s16[144,768]{1,0:T(8,128)(2,1)S(1)} collective-permute-done((s16[144,768]{1,0:T(8,128)(2,1)S(1)}, s16[144,768]{1,0:T(8,128)(2,1)S(1)}, u32[]{:S(2)}, u32[]{:S(2)}) %collective-permute-start.17) | collective-permute-done | bytes 221216 | tf_op jit(solution)/shard_map/ppermute | solution.py:76
  76.9 1.3 %post.1 = (f32[1,1]{1,0:T(1,128)}, f32[128,768]{1,0:T(8,128)}, f32[128,768]{1,0:T(8,128)}) custom-call(bf16[128,768]{1,0:T(8,128)(2,1)S(1)} %copy-done, bf16[128,768]{1,0:T(8,128)(2,1)S(1)} %copy-done.1, f32[136,768]{1,0:T(8,128)S(1)} %get-tuple-element.45.refs_2_, s16[144,768]{1,0:T(8,128)(2,1)S(1)} %collective-permute-done.17.refs_3_, ...), custom_call_target="tpu_custom_call" | custom-call | tf_op jit(solution)/shard_map/post/pallas_call | solution.py:93
  (38 shorter events, 5.9 us)
Async XLA Ops:
  1.9 2.6 %collective-permute-start = (bf16[144,768]{1,0:T(8,128)(2,1)S(1)}, bf16[144,768]{1,0:T(8,128)(2,1)S(1)}, u32[]{:S(2)}, u32[]{:S(2)}) collective-permute-start(bf16[144,768]{1,0:T(8,128)(2,1)S(1)} %get-tuple-element.29), channel_id=1, source_target_pairs={{0,1},{1,0},{2,3},{3,2},{4,5},{5,4},{6,7},{7,6},{8,9},{9,8},{10,11... | collective-permute-start | bytes 663560 | tf_op jit(solution)/shard_map/ppermute | solution.py:80
  4.5 9.1 %collective-permute-start.3 = (bf16[272,768]{1,0:T(8,128)(2,1)S(1)}, bf16[272,768]{1,0:T(8,128)(2,1)S(1)}, u32[]{:S(2)}, u32[]{:S(2)}) collective-permute-start(bf16[272,768]{1,0:T(8,128)(2,1)S(1)} %join.1.refs_0_.refs_9_), channel_id=1, source_target_pairs={{0,2},{1,7},{2,0},{3,5},{4,6},{5,3},{6,4},{7,1},{8,10},{9,15},{10,... | collective-permute-start | bytes 1253384 | tf_op jit(solution)/shard_map/ppermute | solution.py:76
  7.4 9.2 %collective-permute-start.2 = (bf16[272,768]{1,0:T(8,128)(2,1)S(1)}, bf16[272,768]{1,0:T(8,128)(2,1)S(1)}, u32[]{:S(2)}, u32[]{:S(2)}) collective-permute-start(bf16[272,768]{1,0:T(8,128)(2,1)S(1)} %join.1.refs_0_.refs_9_), channel_id=1, source_target_pairs={{0,8},{1,25},{2,10},{3,27},{4,12},{5,29},{6,14},{7,31},{8,0},{9,17... | collective-permute-start | bytes 1253384 | tf_op jit(solution)/shard_map/ppermute | solution.py:76
  11.2 8.1 %collective-permute-start.1 = (bf16[272,768]{1,0:T(8,128)(2,1)S(1)}, bf16[272,768]{1,0:T(8,128)(2,1)S(1)}, u32[]{:S(2)}, u32[]{:S(2)}) collective-permute-start(bf16[272,768]{1,0:T(8,128)(2,1)S(1)} %join.1.refs_0_.refs_9_), channel_id=1, source_target_pairs={{0,32},{1,97},{2,34},{3,99},{4,36},{5,101},{6,38},{7,103},{8,40},{... | collective-permute-start | bytes 1253384 | tf_op jit(solution)/shard_map/ppermute | solution.py:76
  19.4 5.3 %collective-permute-start.4 = (bf16[1088,768]{1,0:T(8,128)(2,1)S(1)}, bf16[1088,768]{1,0:T(8,128)(2,1)S(1)}, u32[]{:S(2)}, u32[]{:S(2)}) collective-permute-start(bf16[1088,768]{1,0:T(8,128)(2,1)S(1)} %pack_near.1), channel_id=1, source_target_pairs={{0,1},{1,0},{2,3},{3,2},{4,5},{5,4},{6,7},{7,6},{8,9},{9,8},{10,11... | collective-permute-start | bytes 5013512 | tf_op jit(solution)/shard_map/ppermute | solution.py:80
  19.5 10.4 %collective-permute-start.5 = (bf16[272,768]{1,0:T(8,128)(2,1)S(1)}, bf16[272,768]{1,0:T(8,128)(2,1)S(1)}, u32[]{:S(2)}, u32[]{:S(2)}) collective-permute-start(bf16[272,768]{1,0:T(8,128)(2,1)S(1)} %collective-permute-done.3.refs_3_.refs_9_), channel_id=1, source_target_pairs={{0,40},{1,121},{2,42},{3,123},{4,44},{5,125},{6,46},{7,127},{8,32}... | collective-permute-start | bytes 1253384 | tf_op jit(solution)/shard_map/ppermute | solution.py:76
  21.8 8.1 %collective-permute-start.6 = (bf16[272,768]{1,0:T(8,128)(2,1)S(1)}, bf16[272,768]{1,0:T(8,128)(2,1)S(1)}, u32[]{:S(2)}, u32[]{:S(2)}) collective-permute-start(bf16[272,768]{1,0:T(8,128)(2,1)S(1)} %collective-permute-done.1.refs_1_.refs_9_), channel_id=1, source_target_pairs={{0,2},{1,7},{2,0},{3,5},{4,6},{5,3},{6,4},{7,1},{8,10},{9,15},{10,... | collective-permute-start | bytes 1253384 | tf_op jit(solution)/shard_map/ppermute | solution.py:76
  23.1 11.1 %collective-permute-start.8 = (bf16[272,768]{1,0:T(8,128)(2,1)S(1)}, bf16[272,768]{1,0:T(8,128)(2,1)S(1)}, u32[]{:S(2)}, u32[]{:S(2)}) collective-permute-start(bf16[272,768]{1,0:T(8,128)(2,1)S(1)} %collective-permute-done.3.refs_3_.refs_9_), channel_id=1, source_target_pairs={{0,8},{1,25},{2,10},{3,27},{4,12},{5,29},{6,14},{7,31},{8,0},{9,17... | collective-permute-start | bytes 1253384 | tf_op jit(solution)/shard_map/ppermute | solution.py:76
  24.5 9.7 %collective-permute-start.9 = (bf16[272,768]{1,0:T(8,128)(2,1)S(1)}, bf16[272,768]{1,0:T(8,128)(2,1)S(1)}, u32[]{:S(2)}, u32[]{:S(2)}) collective-permute-start(bf16[272,768]{1,0:T(8,128)(2,1)S(1)} %collective-permute-done.2.refs_2_.refs_9_), channel_id=1, source_target_pairs={{0,32},{1,97},{2,34},{3,99},{4,36},{5,101},{6,38},{7,103},{8,40},{... | collective-permute-start | bytes 1253384 | tf_op jit(solution)/shard_map/ppermute | solution.py:76
  29.9 4.5 %collective-permute-start.7 = (bf16[544,768]{1,0:T(8,128)(2,1)S(1)}, bf16[544,768]{1,0:T(8,128)(2,1)S(1)}, u32[]{:S(2)}, u32[]{:S(2)}) collective-permute-start(bf16[544,768]{1,0:T(8,128)(2,1)S(1)} %pack_first.1), channel_id=1, source_target_pairs={{0,1},{1,0},{2,3},{3,2},{4,5},{5,4},{6,7},{7,6},{8,9},{9,8},{10,11... | collective-permute-start | bytes 2506760 | tf_op jit(solution)/shard_map/ppermute | solution.py:80
  34.3 3.3 %collective-permute-start.10 = (bf16[544,768]{1,0:T(8,128)(2,1)S(1)}, bf16[544,768]{1,0:T(8,128)(2,1)S(1)}, u32[]{:S(2)}, u32[]{:S(2)}) collective-permute-start(bf16[544,768]{1,0:T(8,128)(2,1)S(1)} %pack_second.1), channel_id=1, source_target_pairs={{0,1},{1,0},{2,3},{3,2},{4,5},{5,4},{6,7},{7,6},{8,9},{9,8},{10,11... | collective-permute-start | bytes 2506760 | tf_op jit(solution)/shard_map/ppermute | solution.py:80
  48.7 11.9 %collective-permute-start.13 = (s16[272,768]{1,0:T(8,128)(2,1)S(1)}, s16[272,768]{1,0:T(8,128)(2,1)S(1)}, u32[]{:S(2)}, u32[]{:S(2)}) collective-permute-start(s16[272,768]{1,0:T(8,128)(2,1)S(1)} %grad_3.1), channel_id=1, source_target_pairs={{0,8},{1,25},{2,10},{3,27},{4,12},{5,29},{6,14},{7,31},{8,0},{9,17... | collective-permute-start | bytes 1253384 | tf_op jit(solution)/shard_map/ppermute | solution.py:76
  50.2 11.9 %collective-permute-start.15 = (s16[272,768]{1,0:T(8,128)(2,1)S(1)}, s16[272,768]{1,0:T(8,128)(2,1)S(1)}, u32[]{:S(2)}, u32[]{:S(2)}) collective-permute-start(s16[272,768]{1,0:T(8,128)(2,1)S(1)} %grad_6.1), channel_id=1, source_target_pairs={{0,32},{1,97},{2,34},{3,99},{4,36},{5,101},{6,38},{7,103},{8,40},{... | collective-permute-start | bytes 1253384 | tf_op jit(solution)/shard_map/ppermute | solution.py:76
  53.4 10.8 %collective-permute-start.11 = (s16[272,768]{1,0:T(8,128)(2,1)S(1)}, s16[272,768]{1,0:T(8,128)(2,1)S(1)}, u32[]{:S(2)}, u32[]{:S(2)}) collective-permute-start(s16[272,768]{1,0:T(8,128)(2,1)S(1)} %grad_5.1.refs_10_), channel_id=1, source_target_pairs={{0,2},{1,7},{2,0},{3,5},{4,6},{5,3},{6,4},{7,1},{8,10},{9,15},{10,... | collective-permute-start | bytes 1253384 | tf_op jit(solution)/shard_map/ppermute | solution.py:76
  56.1 16.2 %collective-permute-start.12 = (s16[272,768]{1,0:T(8,128)(2,1)S(1)}, s16[272,768]{1,0:T(8,128)(2,1)S(1)}, u32[]{:S(2)}, u32[]{:S(2)}) collective-permute-start(s16[272,768]{1,0:T(8,128)(2,1)S(1)} %grad_7.1), channel_id=1, source_target_pairs={{0,42},{1,127},{2,40},{3,125},{4,46},{5,123},{6,44},{7,121},{8,34}... | collective-permute-start | bytes 1253384 | tf_op jit(solution)/shard_map/ppermute | solution.py:76
  62.0 10.4 %collective-permute-start.14 = (s16[272,768]{1,0:T(8,128)(2,1)S(1)}, s16[272,768]{1,0:T(8,128)(2,1)S(1)}, u32[]{:S(2)}, u32[]{:S(2)}) collective-permute-start(s16[272,768]{1,0:T(8,128)(2,1)S(1)} %grad_1.1), channel_id=1, source_target_pairs={{0,2},{1,7},{2,0},{3,5},{4,6},{5,3},{6,4},{7,1},{8,10},{9,15},{10,... | collective-permute-start | bytes 1253384 | tf_op jit(solution)/shard_map/ppermute | solution.py:76
  63.5 9.9 %collective-permute-start.16 = (s16[272,768]{1,0:T(8,128)(2,1)S(1)}, s16[272,768]{1,0:T(8,128)(2,1)S(1)}, u32[]{:S(2)}, u32[]{:S(2)}) collective-permute-start(s16[272,768]{1,0:T(8,128)(2,1)S(1)} %grad_2.1), channel_id=1, source_target_pairs={{0,8},{1,25},{2,10},{3,27},{4,12},{5,29},{6,14},{7,31},{8,0},{9,17... | collective-permute-start | bytes 1253384 | tf_op jit(solution)/shard_map/ppermute | solution.py:76
  65.6 8.9 %collective-permute-start.18 = (s16[144,768]{1,0:T(8,128)(2,1)S(1)}, s16[144,768]{1,0:T(8,128)(2,1)S(1)}, u32[]{:S(2)}, u32[]{:S(2)}) collective-permute-start(s16[144,768]{1,0:T(8,128)(2,1)S(1)} %get-tuple-element.46), channel_id=1, source_target_pairs={{0,33},{1,96},{2,35},{3,98},{4,37},{5,100},{6,39},{7,102},{8,41},{... | collective-permute-start | bytes 663560 | tf_op jit(solution)/shard_map/ppermute | solution.py:534
  70.3 6.6 %copy-start = (bf16[128,768]{1,0:T(8,128)(2,1)S(1)}, bf16[128,768]{1,0:T(8,128)(2,1)}, u32[]{:S(2)}) copy-start(bf16[128,768]{1,0:T(8,128)(2,1)} %refs_0_.1) | copy-start | bytes 589828
  70.3 6.6 %copy-start.1 = (bf16[128,768]{1,0:T(8,128)(2,1)S(1)}, bf16[128,768]{1,0:T(8,128)(2,1)}, u32[]{:S(2)}) copy-start(bf16[128,768]{1,0:T(8,128)(2,1)} %refs_1_.1) | copy-start | bytes 589828
  70.3 6.6 %collective-permute-start.17 = (s16[144,768]{1,0:T(8,128)(2,1)S(1)}, s16[144,768]{1,0:T(8,128)(2,1)S(1)}, u32[]{:S(2)}, u32[]{:S(2)}) collective-permute-start(s16[144,768]{1,0:T(8,128)(2,1)S(1)} %get-tuple-element.44.refs_10_), channel_id=1, source_target_pairs={{0,32},{1,97},{2,34},{3,99},{4,36},{5,101},{6,38},{7,103},{8,40},{... | collective-permute-start | bytes 663560 | tf_op jit(solution)/shard_map/ppermute | solution.py:76
  73.9 3.1 %collective-permute-start.19 = (f32[48,768]{1,0:T(8,128)S(1)}, f32[48,768]{1,0:T(8,128)S(1)}, u32[]{:S(2)}, u32[]{:S(2)}) collective-permute-start(f32[48,768]{1,0:T(8,128)S(1)} %get-tuple-element.47), channel_id=1, source_target_pairs={{0,1},{1,0},{2,3},{3,2},{4,5},{5,4},{6,7},{7,6},{8,9},{9,8},{10,11... | collective-permute-start | bytes 442376 | tf_op jit(solution)/shard_map/ppermute | solution.py:80
  73.9 3.0 %collective-permute-start.20 = (f32[48,768]{1,0:T(8,128)S(1)}, f32[48,768]{1,0:T(8,128)S(1)}, u32[]{:S(2)}, u32[]{:S(2)}) collective-permute-start(f32[48,768]{1,0:T(8,128)S(1)} %get-tuple-element.48), channel_id=1, source_target_pairs={{0,1},{1,0},{2,3},{3,2},{4,5},{5,4},{6,7},{7,6},{8,9},{9,8},{10,11... | collective-permute-start | bytes 442376 | tf_op jit(solution)/shard_map/ppermute | solution.py:80
  74.4 2.5 %collective-permute-start.21 = (f32[40,768]{1,0:T(8,128)S(1)}, f32[40,768]{1,0:T(8,128)S(1)}, u32[]{:S(2)}, u32[]{:S(2)}) collective-permute-start(f32[40,768]{1,0:T(8,128)S(1)} %get-tuple-element.49), channel_id=1, source_target_pairs={{0,1},{1,0},{2,3},{3,2},{4,5},{5,4},{6,7},{7,6},{8,9},{9,8},{10,11... | collective-permute-start | bytes 368648 | tf_op jit(solution)/shard_map/ppermute | solution.py:80

commit v6 on v5

--- a/solution.py
+++ b/solution.py
@@ -273,7 +273,7 @@
         piece = jnp.abs(value[:, h * 128 : (h + 1) * 128])
         largest = piece if largest is None else jnp.maximum(largest, piece)
     largest = jnp.max(largest, axis=1, keepdims=True)
-    power = jnp.ceil(jnp.log2(jnp.maximum(largest, 1e-35)) * 128.0)
+    power = jnp.ceil(jnp.log2(jnp.maximum(largest, 1e-30)) * 128.0)
     steps = value * (FULL * jnp.exp2(power * (-1.0 / 128.0)))
     out_ref[:BLOCK, :] = jnp.floor(steps + 0.5).astype(jnp.int32).astype(jnp.int16)
     at = lax.broadcasted_iota(jnp.int32, (PAD, BLOCK), 0)

time: 78.5 us -> 78.5 us (level)
  no operation moved by 1% of the time
where the time goes in v6:
time: 78.5 us; the launch traced here: 78.3 us
  starting transfers between devices  30.9 us (39%)
  Pallas kernels  22.6 us (29%)
  waiting for transfers between devices  16.4 us (21%)
  blocking collectives  7.53 us (10%)
  between operations  0.84 us (1%)
    ppermute x14, starting transfers between devices, send(): return lax.ppermute(value, 'dp', partners(bits))  23.8 us
    pallas_call x20, Pallas kernels, call(): pl.pallas_call(body, name=name, out_shape=out_shape, scratch_shapes=scrat...  21.4 us
    ppermute x14, waiting for transfers between devices, send(): return lax.ppermute(value, 'dp', partners(bits))  15.3 us
    all_to_all x1, blocking collectives, local(): lax.all_to_all(parts[-1][1], 'dp', 0, 0, axis_index_groups=SUM_GROUPS, ti...  7.53 us
    ppermute x1, starting transfers between devices, local(): cross = lax.ppermute(halves[1], 'dp', crossing(4))  4.69 us
    ppermute x7, starting transfers between devices, swap(): return lax.ppermute(value, 'dp', SWAP)  2.43 us
  transfers between devices with their start and end apart: 22, of which 7 were waited for; matrix products, arithmetic and copies ran while one was open for 0% of the time, Pallas kernels for 21%

profile of v6, /device:TPU:1, one launch (start us, length us, event | category | flops | bytes accessed | tf_op | source)
XLA Modules:
  0.0 78.3 jit_solution(13654181433802999397)
XLA Ops:
  0.6 1.2 %pre.1 = (bf16[144,768]{1,0:T(8,128)(2,1)S(1)}, bf16[144,768]{1,0:T(8,128)(2,1)S(1)}) custom-call(bf16[128,768]{1,0:T(8,128)(2,1)} %refs_0_.1, bf16[128,768]{1,0:T(8,128)(2,1)} %refs_1_.1, s32[1,128]{1,0:T(1,128)} %bitcast.2), custom_call_target="tpu_custom_call" | custom-call | tf_op jit(solution)/shard_map/pre/pallas_call | solution.py:440
  1.9 1.5 %collective-permute-start = (bf16[144,768]{1,0:T(8,128)(2,1)S(1)}, bf16[144,768]{1,0:T(8,128)(2,1)S(1)}, u32[]{:S(2)}, u32[]{:S(2)}) collective-permute-start(bf16[144,768]{1,0:T(8,128)(2,1)S(1)} %get-tuple-element.29), channel_id=1, source_target_pairs={{0,1},{1,0},{2,3},{3,2},{4,5},{5,4},{6,7},{7,6},{8,9},{9,8},{10,11... | collective-permute-start | bytes 663560 | tf_op jit(solution)/shard_map/ppermute | solution.py:80
  4.5 2.9 %collective-permute-start.3 = (bf16[272,768]{1,0:T(8,128)(2,1)S(1)}, bf16[272,768]{1,0:T(8,128)(2,1)S(1)}, u32[]{:S(2)}, u32[]{:S(2)}) collective-permute-start(bf16[272,768]{1,0:T(8,128)(2,1)S(1)} %join.1.refs_0_.refs_9_), channel_id=1, source_target_pairs={{0,2},{1,7},{2,0},{3,5},{4,6},{5,3},{6,4},{7,1},{8,10},{9,15},{10,... | collective-permute-start | bytes 1253384 | tf_op jit(solution)/shard_map/ppermute | solution.py:76
  7.4 3.8 %collective-permute-start.2 = (bf16[272,768]{1,0:T(8,128)(2,1)S(1)}, bf16[272,768]{1,0:T(8,128)(2,1)S(1)}, u32[]{:S(2)}, u32[]{:S(2)}) collective-permute-start(bf16[272,768]{1,0:T(8,128)(2,1)S(1)} %join.1.refs_0_.refs_9_), channel_id=1, source_target_pairs={{0,8},{1,25},{2,10},{3,27},{4,12},{5,29},{6,14},{7,31},{8,0},{9,17... | collective-permute-start | bytes 1253384 | tf_op jit(solution)/shard_map/ppermute | solution.py:76
  11.2 2.5 %collective-permute-start.1 = (bf16[272,768]{1,0:T(8,128)(2,1)S(1)}, bf16[272,768]{1,0:T(8,128)(2,1)S(1)}, u32[]{:S(2)}, u32[]{:S(2)}) collective-permute-start(bf16[272,768]{1,0:T(8,128)(2,1)S(1)} %join.1.refs_0_.refs_9_), channel_id=1, source_target_pairs={{0,32},{1,97},{2,34},{3,99},{4,36},{5,101},{6,38},{7,103},{8,40},{... | collective-permute-start | bytes 1253384 | tf_op jit(solution)/shard_map/ppermute | solution.py:76
  13.7 2.9 %collective-permute-done.2.refs_2_.refs_9_ = bf16[272,768]{1,0:T(8,128)(2,1)S(1)} collective-permute-done((bf16[272,768]{1,0:T(8,128)(2,1)S(1)}, bf16[272,768]{1,0:T(8,128)(2,1)S(1)}, u32[]{:S(2)}, u32[]{:S(2)}) %collective-permute-start.2) | collective-permute-done | bytes 417824 | tf_op jit(solution)/shard_map/ppermute | solution.py:76
  16.6 2.7 %collective-permute-done.1.refs_1_.refs_9_ = bf16[272,768]{1,0:T(8,128)(2,1)S(1)} collective-permute-done((bf16[272,768]{1,0:T(8,128)(2,1)S(1)}, bf16[272,768]{1,0:T(8,128)(2,1)S(1)}, u32[]{:S(2)}, u32[]{:S(2)}) %collective-permute-start.1) | collective-permute-done | bytes 417824 | tf_op jit(solution)/shard_map/ppermute | solution.py:76
  19.5 2.3 %collective-permute-start.5 = (bf16[272,768]{1,0:T(8,128)(2,1)S(1)}, bf16[272,768]{1,0:T(8,128)(2,1)S(1)}, u32[]{:S(2)}, u32[]{:S(2)}) collective-permute-start(bf16[272,768]{1,0:T(8,128)(2,1)S(1)} %collective-permute-done.3.refs_3_.refs_9_), channel_id=1, source_target_pairs={{0,40},{1,121},{2,42},{3,123},{4,44},{5,125},{6,46},{7,127},{8,32}... | collective-permute-start | bytes 1253384 | tf_op jit(solution)/shard_map/ppermute | solution.py:76
  21.8 1.4 %collective-permute-start.6 = (bf16[272,768]{1,0:T(8,128)(2,1)S(1)}, bf16[272,768]{1,0:T(8,128)(2,1)S(1)}, u32[]{:S(2)}, u32[]{:S(2)}) collective-permute-start(bf16[272,768]{1,0:T(8,128)(2,1)S(1)} %collective-permute-done.1.refs_1_.refs_9_), channel_id=1, source_target_pairs={{0,2},{1,7},{2,0},{3,5},{4,6},{5,3},{6,4},{7,1},{8,10},{9,15},{10,... | collective-permute-start | bytes 1253384 | tf_op jit(solution)/shard_map/ppermute | solution.py:76
  23.1 1.4 %collective-permute-start.8 = (bf16[272,768]{1,0:T(8,128)(2,1)S(1)}, bf16[272,768]{1,0:T(8,128)(2,1)S(1)}, u32[]{:S(2)}, u32[]{:S(2)}) collective-permute-start(bf16[272,768]{1,0:T(8,128)(2,1)S(1)} %collective-permute-done.3.refs_3_.refs_9_), channel_id=1, source_target_pairs={{0,8},{1,25},{2,10},{3,27},{4,12},{5,29},{6,14},{7,31},{8,0},{9,17... | collective-permute-start | bytes 1253384 | tf_op jit(solution)/shard_map/ppermute | solution.py:76
  24.7 2.0 %tile_0.1 = (f32[1024,1024]{1,0:T(8,128)S(1)}, f32[1024,128]{1,0:T(8,128)S(1)}, f32[16,1024]{1,0:T(8,128)S(1)}) custom-call(bf16[272,768]{1,0:T(8,128)(2,1)S(1)} %join.1.refs_0_.refs_9_, bf16[272,768]{1,0:T(8,128)(2,1)S(1)} %collective-permute-done.1.refs_1_.refs_9_, bf16[272,768]{1,0:T(8,128)(2,1)S(1)} %collective-permute-done.2.refs_2_.refs_9_, ...), custom_call_target="tpu_custom_call" | custom-call | tf_op jit(solution)/shard_map/tile_0/pallas_call | solution.py:93
  26.7 3.1 %collective-permute-done.5.refs_0_.refs_4_.refs_9_ = bf16[272,768]{1,0:T(8,128)(2,1)S(1)} collective-permute-done((bf16[272,768]{1,0:T(8,128)(2,1)S(1)}, bf16[272,768]{1,0:T(8,128)(2,1)S(1)}, u32[]{:S(2)}, u32[]{:S(2)}) %collective-permute-start.5) | collective-permute-done | bytes 417824 | tf_op jit(solution)/shard_map/ppermute | solution.py:76
  30.0 1.1 %tile_1.1 = (f32[512,1024]{1,0:T(8,128)S(1)}, f32[512,128]{1,0:T(8,128)S(1)}, f32[16,1024]{1,0:T(8,128)S(1)}) custom-call(bf16[272,768]{1,0:T(8,128)(2,1)S(1)} %collective-permute-done.5.refs_0_.refs_4_.refs_9_, bf16[272,768]{1,0:T(8,128)(2,1)S(1)} %collective-permute-done.6.refs_1_.refs_5_.refs_9_, ...), custom_call_target="tpu_custom_call" | custom-call | tf_op jit(solution)/shard_map/tile_1/pallas_call | solution.py:93
  31.2 3.1 %collective-permute-done.8.refs_0_.refs_6_.refs_9_ = bf16[272,768]{1,0:T(8,128)(2,1)S(1)} collective-permute-done((bf16[272,768]{1,0:T(8,128)(2,1)S(1)}, bf16[272,768]{1,0:T(8,128)(2,1)S(1)}, u32[]{:S(2)}, u32[]{:S(2)}) %collective-permute-start.8) | collective-permute-done | bytes 417824 | tf_op jit(solution)/shard_map/ppermute | solution.py:76
  34.4 1.5 %tile_2.1 = (f32[1536,512]{1,0:T(8,128)S(1)}, f32[1536,128]{1,0:T(8,128)S(1)}, f32[16,512]{1,0:T(8,128)S(1)}) custom-call(bf16[272,768]{1,0:T(8,128)(2,1)S(1)} %join.1.refs_0_.refs_9_, bf16[272,768]{1,0:T(8,128)(2,1)S(1)} %collective-permute-done.1.refs_1_.refs_9_, bf16[272,768]{1,0:T(8,128)(2,1)S(1)} %collective-permute-done.2.refs_2_.refs_9_, ...), custom_call_target="tpu_custom_call" | custom-call | tf_op jit(solution)/shard_map/tile_2/pallas_call | solution.py:93
  36.0 1.6 %tile_3.1 = (f32[512,1536]{1,0:T(8,128)S(1)}, f32[512,128]{1,0:T(8,128)S(1)}, f32[16,1536]{1,0:T(8,128)S(1)}) custom-call(bf16[272,768]{1,0:T(8,128)(2,1)S(1)} %collective-permute-done.8.refs_0_.refs_6_.refs_9_, bf16[272,768]{1,0:T(8,128)(2,1)S(1)} %collective-permute-done.9.refs_1_.refs_7_.refs_9_, ...), custom_call_target="tpu_custom_call" | custom-call | tf_op jit(solution)/shard_map/tile_3/pallas_call | solution.py:93
  37.6 2.0 %tile_4.1 = (f32[2048,512]{1,0:T(8,128)S(1)}, f32[8,32,128]{2,1,0:T(8,128)S(1)}) custom-call(bf16[272,768]{1,0:T(8,128)(2,1)S(1)} %join.1.refs_0_.refs_9_, bf16[272,768]{1,0:T(8,128)(2,1)S(1)} %collective-permute-done.1.refs_1_.refs_9_, bf16[272,768]{1,0:T(8,128)(2,1)S(1)} %collective-permute-done.2.refs_2_.refs_9_, ...), custom_call_target="tpu_custom_call" | custom-call | tf_op jit(solution)/shard_map/tile_4/pallas_call | solution.py:93
  39.6 7.5 %all_to_all.5.refs_0_ = f32[8,32,128]{2,1,0:T(8,128)S(1)} all-to-all(f32[8,32,128]{2,1,0:T(8,128)S(1)} %get-tuple-element.43), channel_id=1, replica_groups={{0,2,8,10,32,34,40,42},{4,6,12,14,36,38,44,46},{16,18,24,26,48,50,56,58..., dimensions={0} | all-to-all | bytes 262144 | tf_op jit(solution)/shard_map/all_to_all | solution.py:497
  47.3 1.4 %grad_3.1 = s16[272,768]{1,0:T(8,128)(2,1)S(1)} custom-call(f32[1024,1024]{1,0:T(8,128)S(1)} %get-tuple-element.30.refs_0_, f32[512,1024]{1,0:T(8,128)S(1)} %get-tuple-element.32.refs_1_, f32[1536,512]{1,0:T(8,128)S(1)} %get-tuple-element.34.refs_2_, f32[512,1536]{1,0:T(8,128)S(1)} %get-tuple-element.36.refs_3_, f32[2048,512]{1,0:T(8,128)S(1)} %get-tuple-element.42.refs_4_, ...), custom_call_target="tpu_custom_call" | custom-call | tf_op jit(solution)/shard_map/grad_3/pallas_call | solution.py:93
  48.8 1.4 %grad_6.1 = s16[272,768]{1,0:T(8,128)(2,1)S(1)} custom-call(f32[1024,1024]{1,0:T(8,128)S(1)} %get-tuple-element.30.refs_0_, f32[512,1024]{1,0:T(8,128)S(1)} %get-tuple-element.32.refs_1_, f32[1536,512]{1,0:T(8,128)S(1)} %get-tuple-element.34.refs_2_, f32[512,1536]{1,0:T(8,128)S(1)} %get-tuple-element.36.refs_3_, f32[2048,512]{1,0:T(8,128)S(1)} %get-tuple-element.42.refs_4_, ...), custom_call_target="tpu_custom_call" | custom-call | tf_op jit(solution)/shard_map/grad_6/pallas_call | solution.py:93
  50.2 1.9 %collective-permute-start.15 = (s16[272,768]{1,0:T(8,128)(2,1)S(1)}, s16[272,768]{1,0:T(8,128)(2,1)S(1)}, u32[]{:S(2)}, u32[]{:S(2)}) collective-permute-start(s16[272,768]{1,0:T(8,128)(2,1)S(1)} %grad_6.1), channel_id=1, source_target_pairs={{0,32},{1,97},{2,34},{3,99},{4,36},{5,101},{6,38},{7,103},{8,40},{... | collective-permute-start | bytes 1253384 | tf_op jit(solution)/shard_map/ppermute | solution.py:76
  52.0 1.4 %grad_5.1.refs_10_ = s16[272,768]{1,0:T(8,128)(2,1)S(1)} custom-call(f32[1024,1024]{1,0:T(8,128)S(1)} %get-tuple-element.30.refs_0_, f32[512,1024]{1,0:T(8,128)S(1)} %get-tuple-element.32.refs_1_, f32[1536,512]{1,0:T(8,128)S(1)} %get-tuple-element.34.refs_2_, f32[512,1536]{1,0:T(8,128)S(1)} %get-tuple-element.36.refs_3_, ...), custom_call_target="tpu_custom_call" | custom-call | tf_op jit(solution)/shard_map/grad_5/pallas_call | solution.py:93
  53.4 1.4 %collective-permute-start.11 = (s16[272,768]{1,0:T(8,128)(2,1)S(1)}, s16[272,768]{1,0:T(8,128)(2,1)S(1)}, u32[]{:S(2)}, u32[]{:S(2)}) collective-permute-start(s16[272,768]{1,0:T(8,128)(2,1)S(1)} %grad_5.1.refs_10_), channel_id=1, source_target_pairs={{0,2},{1,7},{2,0},{3,5},{4,6},{5,3},{6,4},{7,1},{8,10},{9,15},{10,... | collective-permute-start | bytes 1253384 | tf_op jit(solution)/shard_map/ppermute | solution.py:76
  54.8 1.4 %grad_7.1 = s16[272,768]{1,0:T(8,128)(2,1)S(1)} custom-call(f32[1024,1024]{1,0:T(8,128)S(1)} %get-tuple-element.30.refs_0_, f32[512,1024]{1,0:T(8,128)S(1)} %get-tuple-element.32.refs_1_, f32[1536,512]{1,0:T(8,128)S(1)} %get-tuple-element.34.refs_2_, f32[512,1536]{1,0:T(8,128)S(1)} %get-tuple-element.36.refs_3_, f32[2048,512]{1,0:T(8,128)S(1)} %get-tuple-element.42.refs_4_, ...), custom_call_target="tpu_custom_call" | custom-call | tf_op jit(solution)/shard_map/grad_7/pallas_call | solution.py:93
  56.1 4.5 %collective-permute-start.12 = (s16[272,768]{1,0:T(8,128)(2,1)S(1)}, s16[272,768]{1,0:T(8,128)(2,1)S(1)}, u32[]{:S(2)}, u32[]{:S(2)}) collective-permute-start(s16[272,768]{1,0:T(8,128)(2,1)S(1)} %grad_7.1), channel_id=1, source_target_pairs={{0,42},{1,127},{2,40},{3,125},{4,46},{5,123},{6,44},{7,121},{8,34}... | collective-permute-start | bytes 1253384 | tf_op jit(solution)/shard_map/ppermute | solution.py:76
  60.6 1.4 %grad_1.1 = s16[272,768]{1,0:T(8,128)(2,1)S(1)} custom-call(f32[1024,1024]{1,0:T(8,128)S(1)} %get-tuple-element.30.refs_0_, f32[512,1024]{1,0:T(8,128)S(1)} %get-tuple-element.32.refs_1_, f32[1536,512]{1,0:T(8,128)S(1)} %get-tuple-element.34.refs_2_, f32[512,1536]{1,0:T(8,128)S(1)} %get-tuple-element.36.refs_3_, f32[2048,512]{1,0:T(8,128)S(1)} %get-tuple-element.42.refs_4_, ...), custom_call_target="tpu_custom_call" | custom-call | tf_op jit(solution)/shard_map/grad_1/pallas_call | solution.py:93
  62.1 1.4 %grad_2.1 = s16[272,768]{1,0:T(8,128)(2,1)S(1)} custom-call(f32[1024,1024]{1,0:T(8,128)S(1)} %get-tuple-element.30.refs_0_, f32[512,1024]{1,0:T(8,128)S(1)} %get-tuple-element.32.refs_1_, f32[1536,512]{1,0:T(8,128)S(1)} %get-tuple-element.34.refs_2_, f32[512,1536]{1,0:T(8,128)S(1)} %get-tuple-element.36.refs_3_, f32[2048,512]{1,0:T(8,128)S(1)} %get-tuple-element.42.refs_4_, ...), custom_call_target="tpu_custom_call" | custom-call | tf_op jit(solution)/shard_map/grad_2/pallas_call | solution.py:93
  64.2 1.4 %grad_4.1 = (s16[144,768]{1,0:T(8,128)(2,1)S(1)}, s16[144,768]{1,0:T(8,128)(2,1)S(1)}) custom-call(f32[1024,1024]{1,0:T(8,128)S(1)} %get-tuple-element.30.refs_0_, f32[512,1024]{1,0:T(8,128)S(1)} %get-tuple-element.32.refs_1_, f32[1536,512]{1,0:T(8,128)S(1)} %get-tuple-element.34.refs_2_, f32[512,1536]{1,0:T(8,128)S(1)} %get-tuple-element.36.refs_3_, ...), custom_call_target="tpu_custom_call" | custom-call | tf_op jit(solution)/shard_map/grad_4/pallas_call | solution.py:93
  65.6 4.7 %collective-permute-start.18 = (s16[144,768]{1,0:T(8,128)(2,1)S(1)}, s16[144,768]{1,0:T(8,128)(2,1)S(1)}, u32[]{:S(2)}, u32[]{:S(2)}) collective-permute-start(s16[144,768]{1,0:T(8,128)(2,1)S(1)} %get-tuple-element.46), channel_id=1, source_target_pairs={{0,33},{1,96},{2,35},{3,98},{4,37},{5,100},{6,39},{7,102},{8,41},{... | collective-permute-start | bytes 663560 | tf_op jit(solution)/shard_map/ppermute | solution.py:534
  71.2 1.1 %grad_0.1.refs_0_ = f32[264,768]{1,0:T(8,128)S(1)} custom-call(f32[1024,1024]{1,0:T(8,128)S(1)} %get-tuple-element.30.refs_0_, f32[512,1024]{1,0:T(8,128)S(1)} %get-tuple-element.32.refs_1_, f32[1536,512]{1,0:T(8,128)S(1)} %get-tuple-element.34.refs_2_, f32[512,1536]{1,0:T(8,128)S(1)} %get-tuple-element.36.refs_3_, ...), custom_call_target="tpu_custom_call" | custom-call | tf_op jit(solution)/shard_map/grad_0/pallas_call | solution.py:93
  74.5 2.4 %collective-permute-done.17.refs_3_ = s16[144,768]{1,0:T(8,128)(2,1)S(1)} collective-permute-done((s16[144,768]{1,0:T(8,128)(2,1)S(1)}, s16[144,768]{1,0:T(8,128)(2,1)S(1)}, u32[]{:S(2)}, u32[]{:S(2)}) %collective-permute-start.17) | collective-permute-done | bytes 221216 | tf_op jit(solution)/shard_map/ppermute | solution.py:76
  76.9 1.3 %post.1 = (f32[1,1]{1,0:T(1,128)}, f32[128,768]{1,0:T(8,128)}, f32[128,768]{1,0:T(8,128)}) custom-call(bf16[128,768]{1,0:T(8,128)(2,1)S(1)} %copy-done, bf16[128,768]{1,0:T(8,128)(2,1)S(1)} %copy-done.1, f32[136,768]{1,0:T(8,128)S(1)} %get-tuple-element.45.refs_2_, s16[144,768]{1,0:T(8,128)(2,1)S(1)} %collective-permute-done.17.refs_3_, ...), custom_call_target="tpu_custom_call" | custom-call | tf_op jit(solution)/shard_map/post/pallas_call | solution.py:93
  (38 shorter events, 5.9 us)
Async XLA Ops:
  1.9 2.6 %collective-permute-start = (bf16[144,768]{1,0:T(8,128)(2,1)S(1)}, bf16[144,768]{1,0:T(8,128)(2,1)S(1)}, u32[]{:S(2)}, u32[]{:S(2)}) collective-permute-start(bf16[144,768]{1,0:T(8,128)(2,1)S(1)} %get-tuple-element.29), channel_id=1, source_target_pairs={{0,1},{1,0},{2,3},{3,2},{4,5},{5,4},{6,7},{7,6},{8,9},{9,8},{10,11... | collective-permute-start | bytes 663560 | tf_op jit(solution)/shard_map/ppermute | solution.py:80
  4.5 9.1 %collective-permute-start.3 = (bf16[272,768]{1,0:T(8,128)(2,1)S(1)}, bf16[272,768]{1,0:T(8,128)(2,1)S(1)}, u32[]{:S(2)}, u32[]{:S(2)}) collective-permute-start(bf16[272,768]{1,0:T(8,128)(2,1)S(1)} %join.1.refs_0_.refs_9_), channel_id=1, source_target_pairs={{0,2},{1,7},{2,0},{3,5},{4,6},{5,3},{6,4},{7,1},{8,10},{9,15},{10,... | collective-permute-start | bytes 1253384 | tf_op jit(solution)/shard_map/ppermute | solution.py:76
  7.4 9.2 %collective-permute-start.2 = (bf16[272,768]{1,0:T(8,128)(2,1)S(1)}, bf16[272,768]{1,0:T(8,128)(2,1)S(1)}, u32[]{:S(2)}, u32[]{:S(2)}) collective-permute-start(bf16[272,768]{1,0:T(8,128)(2,1)S(1)} %join.1.refs_0_.refs_9_), channel_id=1, source_target_pairs={{0,8},{1,25},{2,10},{3,27},{4,12},{5,29},{6,14},{7,31},{8,0},{9,17... | collective-permute-start | bytes 1253384 | tf_op jit(solution)/shard_map/ppermute | solution.py:76
  11.2 8.1 %collective-permute-start.1 = (bf16[272,768]{1,0:T(8,128)(2,1)S(1)}, bf16[272,768]{1,0:T(8,128)(2,1)S(1)}, u32[]{:S(2)}, u32[]{:S(2)}) collective-permute-start(bf16[272,768]{1,0:T(8,128)(2,1)S(1)} %join.1.refs_0_.refs_9_), channel_id=1, source_target_pairs={{0,32},{1,97},{2,34},{3,99},{4,36},{5,101},{6,38},{7,103},{8,40},{... | collective-permute-start | bytes 1253384 | tf_op jit(solution)/shard_map/ppermute | solution.py:76
  19.4 5.3 %collective-permute-start.4 = (bf16[1088,768]{1,0:T(8,128)(2,1)S(1)}, bf16[1088,768]{1,0:T(8,128)(2,1)S(1)}, u32[]{:S(2)}, u32[]{:S(2)}) collective-permute-start(bf16[1088,768]{1,0:T(8,128)(2,1)S(1)} %pack_near.1), channel_id=1, source_target_pairs={{0,1},{1,0},{2,3},{3,2},{4,5},{5,4},{6,7},{7,6},{8,9},{9,8},{10,11... | collective-permute-start | bytes 5013512 | tf_op jit(solution)/shard_map/ppermute | solution.py:80
  19.5 10.4 %collective-permute-start.5 = (bf16[272,768]{1,0:T(8,128)(2,1)S(1)}, bf16[272,768]{1,0:T(8,128)(2,1)S(1)}, u32[]{:S(2)}, u32[]{:S(2)}) collective-permute-start(bf16[272,768]{1,0:T(8,128)(2,1)S(1)} %collective-permute-done.3.refs_3_.refs_9_), channel_id=1, source_target_pairs={{0,40},{1,121},{2,42},{3,123},{4,44},{5,125},{6,46},{7,127},{8,32}... | collective-permute-start | bytes 1253384 | tf_op jit(solution)/shard_map/ppermute | solution.py:76
  21.8 8.1 %collective-permute-start.6 = (bf16[272,768]{1,0:T(8,128)(2,1)S(1)}, bf16[272,768]{1,0:T(8,128)(2,1)S(1)}, u32[]{:S(2)}, u32[]{:S(2)}) collective-permute-start(bf16[272,768]{1,0:T(8,128)(2,1)S(1)} %collective-permute-done.1.refs_1_.refs_9_), channel_id=1, source_target_pairs={{0,2},{1,7},{2,0},{3,5},{4,6},{5,3},{6,4},{7,1},{8,10},{9,15},{10,... | collective-permute-start | bytes 1253384 | tf_op jit(solution)/shard_map/ppermute | solution.py:76
  23.1 11.1 %collective-permute-start.8 = (bf16[272,768]{1,0:T(8,128)(2,1)S(1)}, bf16[272,768]{1,0:T(8,128)(2,1)S(1)}, u32[]{:S(2)}, u32[]{:S(2)}) collective-permute-start(bf16[272,768]{1,0:T(8,128)(2,1)S(1)} %collective-permute-done.3.refs_3_.refs_9_), channel_id=1, source_target_pairs={{0,8},{1,25},{2,10},{3,27},{4,12},{5,29},{6,14},{7,31},{8,0},{9,17... | collective-permute-start | bytes 1253384 | tf_op jit(solution)/shard_map/ppermute | solution.py:76
  24.5 9.7 %collective-permute-start.9 = (bf16[272,768]{1,0:T(8,128)(2,1)S(1)}, bf16[272,768]{1,0:T(8,128)(2,1)S(1)}, u32[]{:S(2)}, u32[]{:S(2)}) collective-permute-start(bf16[272,768]{1,0:T(8,128)(2,1)S(1)} %collective-permute-done.2.refs_2_.refs_9_), channel_id=1, source_target_pairs={{0,32},{1,97},{2,34},{3,99},{4,36},{5,101},{6,38},{7,103},{8,40},{... | collective-permute-start | bytes 1253384 | tf_op jit(solution)/shard_map/ppermute | solution.py:76
  29.9 4.5 %collective-permute-start.7 = (bf16[544,768]{1,0:T(8,128)(2,1)S(1)}, bf16[544,768]{1,0:T(8,128)(2,1)S(1)}, u32[]{:S(2)}, u32[]{:S(2)}) collective-permute-start(bf16[544,768]{1,0:T(8,128)(2,1)S(1)} %pack_first.1), channel_id=1, source_target_pairs={{0,1},{1,0},{2,3},{3,2},{4,5},{5,4},{6,7},{7,6},{8,9},{9,8},{10,11... | collective-permute-start | bytes 2506760 | tf_op jit(solution)/shard_map/ppermute | solution.py:80
  34.3 3.3 %collective-permute-start.10 = (bf16[544,768]{1,0:T(8,128)(2,1)S(1)}, bf16[544,768]{1,0:T(8,128)(2,1)S(1)}, u32[]{:S(2)}, u32[]{:S(2)}) collective-permute-start(bf16[544,768]{1,0:T(8,128)(2,1)S(1)} %pack_second.1), channel_id=1, source_target_pairs={{0,1},{1,0},{2,3},{3,2},{4,5},{5,4},{6,7},{7,6},{8,9},{9,8},{10,11... | collective-permute-start | bytes 2506760 | tf_op jit(solution)/shard_map/ppermute | solution.py:80
  48.7 11.9 %collective-permute-start.13 = (s16[272,768]{1,0:T(8,128)(2,1)S(1)}, s16[272,768]{1,0:T(8,128)(2,1)S(1)}, u32[]{:S(2)}, u32[]{:S(2)}) collective-permute-start(s16[272,768]{1,0:T(8,128)(2,1)S(1)} %grad_3.1), channel_id=1, source_target_pairs={{0,8},{1,25},{2,10},{3,27},{4,12},{5,29},{6,14},{7,31},{8,0},{9,17... | collective-permute-start | bytes 1253384 | tf_op jit(solution)/shard_map/ppermute | solution.py:76
  50.2 11.9 %collective-permute-start.15 = (s16[272,768]{1,0:T(8,128)(2,1)S(1)}, s16[272,768]{1,0:T(8,128)(2,1)S(1)}, u32[]{:S(2)}, u32[]{:S(2)}) collective-permute-start(s16[272,768]{1,0:T(8,128)(2,1)S(1)} %grad_6.1), channel_id=1, source_target_pairs={{0,32},{1,97},{2,34},{3,99},{4,36},{5,101},{6,38},{7,103},{8,40},{... | collective-permute-start | bytes 1253384 | tf_op jit(solution)/shard_map/ppermute | solution.py:76
  53.4 10.8 %collective-permute-start.11 = (s16[272,768]{1,0:T(8,128)(2,1)S(1)}, s16[272,768]{1,0:T(8,128)(2,1)S(1)}, u32[]{:S(2)}, u32[]{:S(2)}) collective-permute-start(s16[272,768]{1,0:T(8,128)(2,1)S(1)} %grad_5.1.refs_10_), channel_id=1, source_target_pairs={{0,2},{1,7},{2,0},{3,5},{4,6},{5,3},{6,4},{7,1},{8,10},{9,15},{10,... | collective-permute-start | bytes 1253384 | tf_op jit(solution)/shard_map/ppermute | solution.py:76
  56.1 16.2 %collective-permute-start.12 = (s16[272,768]{1,0:T(8,128)(2,1)S(1)}, s16[272,768]{1,0:T(8,128)(2,1)S(1)}, u32[]{:S(2)}, u32[]{:S(2)}) collective-permute-start(s16[272,768]{1,0:T(8,128)(2,1)S(1)} %grad_7.1), channel_id=1, source_target_pairs={{0,42},{1,127},{2,40},{3,125},{4,46},{5,123},{6,44},{7,121},{8,34}... | collective-permute-start | bytes 1253384 | tf_op jit(solution)/shard_map/ppermute | solution.py:76
  62.0 10.4 %collective-permute-start.14 = (s16[272,768]{1,0:T(8,128)(2,1)S(1)}, s16[272,768]{1,0:T(8,128)(2,1)S(1)}, u32[]{:S(2)}, u32[]{:S(2)}) collective-permute-start(s16[272,768]{1,0:T(8,128)(2,1)S(1)} %grad_1.1), channel_id=1, source_target_pairs={{0,2},{1,7},{2,0},{3,5},{4,6},{5,3},{6,4},{7,1},{8,10},{9,15},{10,... | collective-permute-start | bytes 1253384 | tf_op jit(solution)/shard_map/ppermute | solution.py:76
  63.5 9.9 %collective-permute-start.16 = (s16[272,768]{1,0:T(8,128)(2,1)S(1)}, s16[272,768]{1,0:T(8,128)(2,1)S(1)}, u32[]{:S(2)}, u32[]{:S(2)}) collective-permute-start(s16[272,768]{1,0:T(8,128)(2,1)S(1)} %grad_2.1), channel_id=1, source_target_pairs={{0,8},{1,25},{2,10},{3,27},{4,12},{5,29},{6,14},{7,31},{8,0},{9,17... | collective-permute-start | bytes 1253384 | tf_op jit(solution)/shard_map/ppermute | solution.py:76
  65.6 8.9 %collective-permute-start.18 = (s16[144,768]{1,0:T(8,128)(2,1)S(1)}, s16[144,768]{1,0:T(8,128)(2,1)S(1)}, u32[]{:S(2)}, u32[]{:S(2)}) collective-permute-start(s16[144,768]{1,0:T(8,128)(2,1)S(1)} %get-tuple-element.46), channel_id=1, source_target_pairs={{0,33},{1,96},{2,35},{3,98},{4,37},{5,100},{6,39},{7,102},{8,41},{... | collective-permute-start | bytes 663560 | tf_op jit(solution)/shard_map/ppermute | solution.py:534
  70.3 6.6 %copy-start = (bf16[128,768]{1,0:T(8,128)(2,1)S(1)}, bf16[128,768]{1,0:T(8,128)(2,1)}, u32[]{:S(2)}) copy-start(bf16[128,768]{1,0:T(8,128)(2,1)} %refs_0_.1) | copy-start | bytes 589828
  70.3 6.6 %copy-start.1 = (bf16[128,768]{1,0:T(8,128)(2,1)S(1)}, bf16[128,768]{1,0:T(8,128)(2,1)}, u32[]{:S(2)}) copy-start(bf16[128,768]{1,0:T(8,128)(2,1)} %refs_1_.1) | copy-start | bytes 589828
  70.3 6.6 %collective-permute-start.17 = (s16[144,768]{1,0:T(8,128)(2,1)S(1)}, s16[144,768]{1,0:T(8,128)(2,1)S(1)}, u32[]{:S(2)}, u32[]{:S(2)}) collective-permute-start(s16[144,768]{1,0:T(8,128)(2,1)S(1)} %get-tuple-element.44.refs_10_), channel_id=1, source_target_pairs={{0,32},{1,97},{2,34},{3,99},{4,36},{5,101},{6,38},{7,103},{8,40},{... | collective-permute-start | bytes 663560 | tf_op jit(solution)/shard_map/ppermute | solution.py:76
  73.9 3.1 %collective-permute-start.19 = (f32[48,768]{1,0:T(8,128)S(1)}, f32[48,768]{1,0:T(8,128)S(1)}, u32[]{:S(2)}, u32[]{:S(2)}) collective-permute-start(f32[48,768]{1,0:T(8,128)S(1)} %get-tuple-element.47), channel_id=1, source_target_pairs={{0,1},{1,0},{2,3},{3,2},{4,5},{5,4},{6,7},{7,6},{8,9},{9,8},{10,11... | collective-permute-start | bytes 442376 | tf_op jit(solution)/shard_map/ppermute | solution.py:80
  73.9 3.0 %collective-permute-start.20 = (f32[48,768]{1,0:T(8,128)S(1)}, f32[48,768]{1,0:T(8,128)S(1)}, u32[]{:S(2)}, u32[]{:S(2)}) collective-permute-start(f32[48,768]{1,0:T(8,128)S(1)} %get-tuple-element.48), channel_id=1, source_target_pairs={{0,1},{1,0},{2,3},{3,2},{4,5},{5,4},{6,7},{7,6},{8,9},{9,8},{10,11... | collective-permute-start | bytes 442376 | tf_op jit(solution)/shard_map/ppermute | solution.py:80
  74.4 2.5 %collective-permute-start.21 = (f32[40,768]{1,0:T(8,128)S(1)}, f32[40,768]{1,0:T(8,128)S(1)}, u32[]{:S(2)}, u32[]{:S(2)}) collective-permute-start(f32[40,768]{1,0:T(8,128)S(1)} %get-tuple-element.49), channel_id=1, source_target_pairs={{0,1},{1,0},{2,3},{3,2},{4,5},{5,4},{6,7},{7,6},{8,9},{9,8},{10,11... | collective-permute-start | bytes 368648 | tf_op jit(solution)/shard_map/ppermute | solution.py:80

commit v7 on v6

--- a/solution.py
+++ b/solution.py
@@ -381,7 +381,12 @@
         cross_ref[:ROWS, :] = full_ref[low, :]
 
 
-def split_kernel(own_ref, *refs):
+def split_kernel(q_ref, d_ref, own_ref, *refs):
+    *refs, qn_ref, qr_ref, dn_ref, dr_ref = refs
+    for raw, unit_ref, over_ref in ((q_ref, qn_ref, qr_ref), (d_ref, dn_ref, dr_ref)):
+        unit, length = unit_rows(raw[...])
+        unit_ref[...] = unit
+        over_ref[...] = jnp.broadcast_to(1.0 / length, (ROWS, 128))
     count = len(PIECES) + 1
     come, keep_ref, send_refs = refs[:-count], refs[-count], refs[1 - count :]
     value, loss = own_ref[:BLOCK, :], own_ref[BLOCK, 0]
@@ -410,17 +415,18 @@
         give(value[:ROWS, :])
 
 
-def post_kernel(q_ref, d_ref, keep_ref, same_ref, cross_ref, *refs):
+def post_kernel(qn_ref, qr_ref, dn_ref, dr_ref, keep_ref, same_ref, cross_ref, *refs):
     *come, loss_ref, gq_ref, gd_ref = refs
     come_ref = jnp.concatenate([ref[...] for ref in come], axis=0)
 
-    def project(out_ref, grad, values):
-        unit, length = unit_rows(values)
-        out_ref[...] = (grad - jnp.sum(grad * unit, axis=1, keepdims=True) * unit) / length
+    def project(out_ref, grad, unit_ref, over_ref):
+        unit = unit_ref[...]
+        over = jnp.concatenate([over_ref[...]] * (WIDTH // 128), axis=1)
+        out_ref[...] = (grad - jnp.sum(grad * unit, axis=1, keepdims=True) * unit) * over
 
     def fill(gq, last_q, gd, last_d, half):
-        project(gq_ref, gq[:ROWS, :] + decode_half(last_q, half), q_ref[...])
-        project(gd_ref, gd[:ROWS, :] + decode_half(last_d, half), d_ref[...])
+        project(gq_ref, gq[:ROWS, :] + decode_half(last_q, half), qn_ref, qr_ref)
+        project(gd_ref, gd[:ROWS, :] + decode_half(last_d, half), dn_ref, dr_ref)
         loss_ref[...] = (gd[ROWS : ROWS + 1, 0:1] + loss_of(last_d, ROWS)) * (1.0 / 16384)
 
     role = role_of()
@@ -536,7 +542,13 @@
     g0 = grad(0, after=[halves[0]], shape=plain)
     part = pltpu.VMEM((ROWS + LOSS, WIDTH), F32)
     pieces = [pltpu.VMEM((rows, WIDTH), F32) for rows in PIECES]
-    keep, *give = call(split_kernel, "split", [part, *pieces], *[near(v) for v in (g0, r7, r1, r2)])
+    unit, over = pltpu.VMEM((ROWS, WIDTH), F32), pltpu.VMEM((ROWS, 128), F32)
+    keep, *give, qn, qr, dn, dr = call(
+        split_kernel,
+        "split",
+        [part, *pieces, unit, over, unit, over],
+        *[near(v) for v in (queries, documents, g0, r7, r1, r2)],
+    )
     come = [swap(v) for v in give]
     loss, gq, gd = call(
         post_kernel,
@@ -546,9 +558,7 @@
             jax.ShapeDtypeStruct((ROWS, WIDTH), F32),
             jax.ShapeDtypeStruct((ROWS, WIDTH), F32),
         ],
-        queries,
-        documents,
-        *[near(v) for v in (keep, same, cross, *come)],
+        *[near(v) for v in (qn, qr, dn, dr, keep, same, cross, *come)],
     )
     return (loss.reshape(()), gq, gd)
 

time: 78.5 us -> 78.3 us (level)
  no operation moved by 1% of the time
where the time goes in v7:
time: 78.3 us; the launch traced here: 78.1 us
  starting transfers between devices  30.9 us (39%)
  Pallas kernels  22.6 us (29%)
  waiting for transfers between devices  16.2 us (21%)
  blocking collectives  7.53 us (10%)
  between operations  0.83 us (1%)
    ppermute x14, starting transfers between devices, send(): return lax.ppermute(value, 'dp', partners(bits))  23.8 us
    pallas_call x20, Pallas kernels, call(): pl.pallas_call(body, name=name, out_shape=out_shape, scratch_shapes=scrat...  21.4 us
    ppermute x14, waiting for transfers between devices, send(): return lax.ppermute(value, 'dp', partners(bits))  15.1 us
    all_to_all x1, blocking collectives, local(): lax.all_to_all(parts[-1][1], 'dp', 0, 0, axis_index_groups=SUM_GROUPS, ti...  7.53 us
    ppermute x1, starting transfers between devices, local(): cross = lax.ppermute(halves[1], 'dp', crossing(4))  4.69 us
    ppermute x7, starting transfers between devices, swap(): return lax.ppermute(value, 'dp', SWAP)  2.43 us
  transfers between devices with their start and end apart: 22, of which 7 were waited for; matrix products, arithmetic and copies ran while one was open for 0% of the time, Pallas kernels for 21%

profile of v7, /device:TPU:1, one launch (start us, length us, event | category | flops | bytes accessed | tf_op | source)
XLA Modules:
  0.0 78.1 jit_solution(16176024949985727372)
XLA Ops:
  0.6 1.2 %pre.1 = (bf16[144,768]{1,0:T(8,128)(2,1)S(1)}, bf16[144,768]{1,0:T(8,128)(2,1)S(1)}) custom-call(bf16[128,768]{1,0:T(8,128)(2,1)} %refs_0_.1, bf16[128,768]{1,0:T(8,128)(2,1)} %refs_1_.1, s32[1,128]{1,0:T(1,128)} %bitcast.2), custom_call_target="tpu_custom_call" | custom-call | tf_op jit(solution)/shard_map/pre/pallas_call | solution.py:446
  1.9 1.5 %collective-permute-start = (bf16[144,768]{1,0:T(8,128)(2,1)S(1)}, bf16[144,768]{1,0:T(8,128)(2,1)S(1)}, u32[]{:S(2)}, u32[]{:S(2)}) collective-permute-start(bf16[144,768]{1,0:T(8,128)(2,1)S(1)} %get-tuple-element.33), channel_id=1, source_target_pairs={{0,1},{1,0},{2,3},{3,2},{4,5},{5,4},{6,7},{7,6},{8,9},{9,8},{10,11... | collective-permute-start | bytes 663560 | tf_op jit(solution)/shard_map/ppermute | solution.py:80
  4.5 2.9 %collective-permute-start.3 = (bf16[272,768]{1,0:T(8,128)(2,1)S(1)}, bf16[272,768]{1,0:T(8,128)(2,1)S(1)}, u32[]{:S(2)}, u32[]{:S(2)}) collective-permute-start(bf16[272,768]{1,0:T(8,128)(2,1)S(1)} %join.1.refs_0_.refs_9_), channel_id=1, source_target_pairs={{0,2},{1,7},{2,0},{3,5},{4,6},{5,3},{6,4},{7,1},{8,10},{9,15},{10,... | collective-permute-start | bytes 1253384 | tf_op jit(solution)/shard_map/ppermute | solution.py:76
  7.4 3.8 %collective-permute-start.2 = (bf16[272,768]{1,0:T(8,128)(2,1)S(1)}, bf16[272,768]{1,0:T(8,128)(2,1)S(1)}, u32[]{:S(2)}, u32[]{:S(2)}) collective-permute-start(bf16[272,768]{1,0:T(8,128)(2,1)S(1)} %join.1.refs_0_.refs_9_), channel_id=1, source_target_pairs={{0,8},{1,25},{2,10},{3,27},{4,12},{5,29},{6,14},{7,31},{8,0},{9,17... | collective-permute-start | bytes 1253384 | tf_op jit(solution)/shard_map/ppermute | solution.py:76
  11.2 2.5 %collective-permute-start.1 = (bf16[272,768]{1,0:T(8,128)(2,1)S(1)}, bf16[272,768]{1,0:T(8,128)(2,1)S(1)}, u32[]{:S(2)}, u32[]{:S(2)}) collective-permute-start(bf16[272,768]{1,0:T(8,128)(2,1)S(1)} %join.1.refs_0_.refs_9_), channel_id=1, source_target_pairs={{0,32},{1,97},{2,34},{3,99},{4,36},{5,101},{6,38},{7,103},{8,40},{... | collective-permute-start | bytes 1253384 | tf_op jit(solution)/shard_map/ppermute | solution.py:76
  13.7 2.9 %collective-permute-done.2.refs_2_.refs_9_ = bf16[272,768]{1,0:T(8,128)(2,1)S(1)} collective-permute-done((bf16[272,768]{1,0:T(8,128)(2,1)S(1)}, bf16[272,768]{1,0:T(8,128)(2,1)S(1)}, u32[]{:S(2)}, u32[]{:S(2)}) %collective-permute-start.2) | collective-permute-done | bytes 417824 | tf_op jit(solution)/shard_map/ppermute | solution.py:76
  16.6 2.7 %collective-permute-done.1.refs_1_.refs_9_ = bf16[272,768]{1,0:T(8,128)(2,1)S(1)} collective-permute-done((bf16[272,768]{1,0:T(8,128)(2,1)S(1)}, bf16[272,768]{1,0:T(8,128)(2,1)S(1)}, u32[]{:S(2)}, u32[]{:S(2)}) %collective-permute-start.1) | collective-permute-done | bytes 417824 | tf_op jit(solution)/shard_map/ppermute | solution.py:76
  19.5 2.3 %collective-permute-start.5 = (bf16[272,768]{1,0:T(8,128)(2,1)S(1)}, bf16[272,768]{1,0:T(8,128)(2,1)S(1)}, u32[]{:S(2)}, u32[]{:S(2)}) collective-permute-start(bf16[272,768]{1,0:T(8,128)(2,1)S(1)} %collective-permute-done.3.refs_3_.refs_9_), channel_id=1, source_target_pairs={{0,40},{1,121},{2,42},{3,123},{4,44},{5,125},{6,46},{7,127},{8,32}... | collective-permute-start | bytes 1253384 | tf_op jit(solution)/shard_map/ppermute | solution.py:76
  21.8 1.4 %collective-permute-start.6 = (bf16[272,768]{1,0:T(8,128)(2,1)S(1)}, bf16[272,768]{1,0:T(8,128)(2,1)S(1)}, u32[]{:S(2)}, u32[]{:S(2)}) collective-permute-start(bf16[272,768]{1,0:T(8,128)(2,1)S(1)} %collective-permute-done.1.refs_1_.refs_9_), channel_id=1, source_target_pairs={{0,2},{1,7},{2,0},{3,5},{4,6},{5,3},{6,4},{7,1},{8,10},{9,15},{10,... | collective-permute-start | bytes 1253384 | tf_op jit(solution)/shard_map/ppermute | solution.py:76
  23.1 1.4 %collective-permute-start.8 = (bf16[272,768]{1,0:T(8,128)(2,1)S(1)}, bf16[272,768]{1,0:T(8,128)(2,1)S(1)}, u32[]{:S(2)}, u32[]{:S(2)}) collective-permute-start(bf16[272,768]{1,0:T(8,128)(2,1)S(1)} %collective-permute-done.3.refs_3_.refs_9_), channel_id=1, source_target_pairs={{0,8},{1,25},{2,10},{3,27},{4,12},{5,29},{6,14},{7,31},{8,0},{9,17... | collective-permute-start | bytes 1253384 | tf_op jit(solution)/shard_map/ppermute | solution.py:76
  24.7 2.0 %tile_0.1 = (f32[1024,1024]{1,0:T(8,128)S(1)}, f32[1024,128]{1,0:T(8,128)S(1)}, f32[16,1024]{1,0:T(8,128)S(1)}) custom-call(bf16[272,768]{1,0:T(8,128)(2,1)S(1)} %join.1.refs_0_.refs_9_, bf16[272,768]{1,0:T(8,128)(2,1)S(1)} %collective-permute-done.1.refs_1_.refs_9_, bf16[272,768]{1,0:T(8,128)(2,1)S(1)} %collective-permute-done.2.refs_2_.refs_9_, ...), custom_call_target="tpu_custom_call" | custom-call | tf_op jit(solution)/shard_map/tile_0/pallas_call | solution.py:93
  26.7 3.1 %collective-permute-done.5.refs_0_.refs_4_.refs_9_ = bf16[272,768]{1,0:T(8,128)(2,1)S(1)} collective-permute-done((bf16[272,768]{1,0:T(8,128)(2,1)S(1)}, bf16[272,768]{1,0:T(8,128)(2,1)S(1)}, u32[]{:S(2)}, u32[]{:S(2)}) %collective-permute-start.5) | collective-permute-done | bytes 417824 | tf_op jit(solution)/shard_map/ppermute | solution.py:76
  30.0 1.1 %tile_1.1 = (f32[512,1024]{1,0:T(8,128)S(1)}, f32[512,128]{1,0:T(8,128)S(1)}, f32[16,1024]{1,0:T(8,128)S(1)}) custom-call(bf16[272,768]{1,0:T(8,128)(2,1)S(1)} %collective-permute-done.5.refs_0_.refs_4_.refs_9_, bf16[272,768]{1,0:T(8,128)(2,1)S(1)} %collective-permute-done.6.refs_1_.refs_5_.refs_9_, ...), custom_call_target="tpu_custom_call" | custom-call | tf_op jit(solution)/shard_map/tile_1/pallas_call | solution.py:93
  31.2 3.1 %collective-permute-done.8.refs_0_.refs_6_.refs_9_ = bf16[272,768]{1,0:T(8,128)(2,1)S(1)} collective-permute-done((bf16[272,768]{1,0:T(8,128)(2,1)S(1)}, bf16[272,768]{1,0:T(8,128)(2,1)S(1)}, u32[]{:S(2)}, u32[]{:S(2)}) %collective-permute-start.8) | collective-permute-done | bytes 417824 | tf_op jit(solution)/shard_map/ppermute | solution.py:76
  34.4 1.5 %tile_2.1 = (f32[1536,512]{1,0:T(8,128)S(1)}, f32[1536,128]{1,0:T(8,128)S(1)}, f32[16,512]{1,0:T(8,128)S(1)}) custom-call(bf16[272,768]{1,0:T(8,128)(2,1)S(1)} %join.1.refs_0_.refs_9_, bf16[272,768]{1,0:T(8,128)(2,1)S(1)} %collective-permute-done.1.refs_1_.refs_9_, bf16[272,768]{1,0:T(8,128)(2,1)S(1)} %collective-permute-done.2.refs_2_.refs_9_, ...), custom_call_target="tpu_custom_call" | custom-call | tf_op jit(solution)/shard_map/tile_2/pallas_call | solution.py:93
  36.0 1.6 %tile_3.1 = (f32[512,1536]{1,0:T(8,128)S(1)}, f32[512,128]{1,0:T(8,128)S(1)}, f32[16,1536]{1,0:T(8,128)S(1)}) custom-call(bf16[272,768]{1,0:T(8,128)(2,1)S(1)} %collective-permute-done.8.refs_0_.refs_6_.refs_9_, bf16[272,768]{1,0:T(8,128)(2,1)S(1)} %collective-permute-done.9.refs_1_.refs_7_.refs_9_, ...), custom_call_target="tpu_custom_call" | custom-call | tf_op jit(solution)/shard_map/tile_3/pallas_call | solution.py:93
  37.6 2.0 %tile_4.1 = (f32[2048,512]{1,0:T(8,128)S(1)}, f32[8,32,128]{2,1,0:T(8,128)S(1)}) custom-call(bf16[272,768]{1,0:T(8,128)(2,1)S(1)} %join.1.refs_0_.refs_9_, bf16[272,768]{1,0:T(8,128)(2,1)S(1)} %collective-permute-done.1.refs_1_.refs_9_, bf16[272,768]{1,0:T(8,128)(2,1)S(1)} %collective-permute-done.2.refs_2_.refs_9_, ...), custom_call_target="tpu_custom_call" | custom-call | tf_op jit(solution)/shard_map/tile_4/pallas_call | solution.py:93
  39.6 7.5 %all_to_all.5.refs_0_ = f32[8,32,128]{2,1,0:T(8,128)S(1)} all-to-all(f32[8,32,128]{2,1,0:T(8,128)S(1)} %get-tuple-element.47), channel_id=1, replica_groups={{0,2,8,10,32,34,40,42},{4,6,12,14,36,38,44,46},{16,18,24,26,48,50,56,58..., dimensions={0} | all-to-all | bytes 262144 | tf_op jit(solution)/shard_map/all_to_all | solution.py:503
  47.3 1.4 %grad_3.1 = s16[272,768]{1,0:T(8,128)(2,1)S(1)} custom-call(f32[1024,1024]{1,0:T(8,128)S(1)} %get-tuple-element.34.refs_0_, f32[512,1024]{1,0:T(8,128)S(1)} %get-tuple-element.36.refs_1_, f32[1536,512]{1,0:T(8,128)S(1)} %get-tuple-element.38.refs_2_, f32[512,1536]{1,0:T(8,128)S(1)} %get-tuple-element.40.refs_3_, f32[2048,512]{1,0:T(8,128)S(1)} %get-tuple-element.46.refs_4_, ...), custom_call_target="tpu_custom_call" | custom-call | tf_op jit(solution)/shard_map/grad_3/pallas_call | solution.py:93
  48.8 1.4 %grad_6.1 = s16[272,768]{1,0:T(8,128)(2,1)S(1)} custom-call(f32[1024,1024]{1,0:T(8,128)S(1)} %get-tuple-element.34.refs_0_, f32[512,1024]{1,0:T(8,128)S(1)} %get-tuple-element.36.refs_1_, f32[1536,512]{1,0:T(8,128)S(1)} %get-tuple-element.38.refs_2_, f32[512,1536]{1,0:T(8,128)S(1)} %get-tuple-element.40.refs_3_, f32[2048,512]{1,0:T(8,128)S(1)} %get-tuple-element.46.refs_4_, ...), custom_call_target="tpu_custom_call" | custom-call | tf_op jit(solution)/shard_map/grad_6/pallas_call | solution.py:93
  50.2 1.9 %collective-permute-start.15 = (s16[272,768]{1,0:T(8,128)(2,1)S(1)}, s16[272,768]{1,0:T(8,128)(2,1)S(1)}, u32[]{:S(2)}, u32[]{:S(2)}) collective-permute-start(s16[272,768]{1,0:T(8,128)(2,1)S(1)} %grad_6.1), channel_id=1, source_target_pairs={{0,32},{1,97},{2,34},{3,99},{4,36},{5,101},{6,38},{7,103},{8,40},{... | collective-permute-start | bytes 1253384 | tf_op jit(solution)/shard_map/ppermute | solution.py:76
  52.0 1.4 %grad_5.1.refs_10_ = s16[272,768]{1,0:T(8,128)(2,1)S(1)} custom-call(f32[1024,1024]{1,0:T(8,128)S(1)} %get-tuple-element.34.refs_0_, f32[512,1024]{1,0:T(8,128)S(1)} %get-tuple-element.36.refs_1_, f32[1536,512]{1,0:T(8,128)S(1)} %get-tuple-element.38.refs_2_, f32[512,1536]{1,0:T(8,128)S(1)} %get-tuple-element.40.refs_3_, ...), custom_call_target="tpu_custom_call" | custom-call | tf_op jit(solution)/shard_map/grad_5/pallas_call | solution.py:93
  53.4 1.4 %collective-permute-start.11 = (s16[272,768]{1,0:T(8,128)(2,1)S(1)}, s16[272,768]{1,0:T(8,128)(2,1)S(1)}, u32[]{:S(2)}, u32[]{:S(2)}) collective-permute-start(s16[272,768]{1,0:T(8,128)(2,1)S(1)} %grad_5.1.refs_10_), channel_id=1, source_target_pairs={{0,2},{1,7},{2,0},{3,5},{4,6},{5,3},{6,4},{7,1},{8,10},{9,15},{10,... | collective-permute-start | bytes 1253384 | tf_op jit(solution)/shard_map/ppermute | solution.py:76
  54.8 1.4 %grad_7.1 = s16[272,768]{1,0:T(8,128)(2,1)S(1)} custom-call(f32[1024,1024]{1,0:T(8,128)S(1)} %get-tuple-element.34.refs_0_, f32[512,1024]{1,0:T(8,128)S(1)} %get-tuple-element.36.refs_1_, f32[1536,512]{1,0:T(8,128)S(1)} %get-tuple-element.38.refs_2_, f32[512,1536]{1,0:T(8,128)S(1)} %get-tuple-element.40.refs_3_, f32[2048,512]{1,0:T(8,128)S(1)} %get-tuple-element.46.refs_4_, ...), custom_call_target="tpu_custom_call" | custom-call | tf_op jit(solution)/shard_map/grad_7/pallas_call | solution.py:93
  56.1 4.5 %collective-permute-start.12 = (s16[272,768]{1,0:T(8,128)(2,1)S(1)}, s16[272,768]{1,0:T(8,128)(2,1)S(1)}, u32[]{:S(2)}, u32[]{:S(2)}) collective-permute-start(s16[272,768]{1,0:T(8,128)(2,1)S(1)} %grad_7.1), channel_id=1, source_target_pairs={{0,42},{1,127},{2,40},{3,125},{4,46},{5,123},{6,44},{7,121},{8,34}... | collective-permute-start | bytes 1253384 | tf_op jit(solution)/shard_map/ppermute | solution.py:76
  60.6 1.4 %grad_1.1 = s16[272,768]{1,0:T(8,128)(2,1)S(1)} custom-call(f32[1024,1024]{1,0:T(8,128)S(1)} %get-tuple-element.34.refs_0_, f32[512,1024]{1,0:T(8,128)S(1)} %get-tuple-element.36.refs_1_, f32[1536,512]{1,0:T(8,128)S(1)} %get-tuple-element.38.refs_2_, f32[512,1536]{1,0:T(8,128)S(1)} %get-tuple-element.40.refs_3_, f32[2048,512]{1,0:T(8,128)S(1)} %get-tuple-element.46.refs_4_, ...), custom_call_target="tpu_custom_call" | custom-call | tf_op jit(solution)/shard_map/grad_1/pallas_call | solution.py:93
  62.1 1.4 %grad_2.1 = s16[272,768]{1,0:T(8,128)(2,1)S(1)} custom-call(f32[1024,1024]{1,0:T(8,128)S(1)} %get-tuple-element.34.refs_0_, f32[512,1024]{1,0:T(8,128)S(1)} %get-tuple-element.36.refs_1_, f32[1536,512]{1,0:T(8,128)S(1)} %get-tuple-element.38.refs_2_, f32[512,1536]{1,0:T(8,128)S(1)} %get-tuple-element.40.refs_3_, f32[2048,512]{1,0:T(8,128)S(1)} %get-tuple-element.46.refs_4_, ...), custom_call_target="tpu_custom_call" | custom-call | tf_op jit(solution)/shard_map/grad_2/pallas_call | solution.py:93
  64.2 1.4 %grad_4.1 = (s16[144,768]{1,0:T(8,128)(2,1)S(1)}, s16[144,768]{1,0:T(8,128)(2,1)S(1)}) custom-call(f32[1024,1024]{1,0:T(8,128)S(1)} %get-tuple-element.34.refs_0_, f32[512,1024]{1,0:T(8,128)S(1)} %get-tuple-element.36.refs_1_, f32[1536,512]{1,0:T(8,128)S(1)} %get-tuple-element.38.refs_2_, f32[512,1536]{1,0:T(8,128)S(1)} %get-tuple-element.40.refs_3_, ...), custom_call_target="tpu_custom_call" | custom-call | tf_op jit(solution)/shard_map/grad_4/pallas_call | solution.py:93
  65.6 4.7 %collective-permute-start.18 = (s16[144,768]{1,0:T(8,128)(2,1)S(1)}, s16[144,768]{1,0:T(8,128)(2,1)S(1)}, u32[]{:S(2)}, u32[]{:S(2)}) collective-permute-start(s16[144,768]{1,0:T(8,128)(2,1)S(1)} %get-tuple-element.54), channel_id=1, source_target_pairs={{0,33},{1,96},{2,35},{3,98},{4,37},{5,100},{6,39},{7,102},{8,41},{... | collective-permute-start | bytes 663560 | tf_op jit(solution)/shard_map/ppermute | solution.py:540
  71.2 1.1 %grad_0.1.refs_2_ = f32[264,768]{1,0:T(8,128)S(1)} custom-call(f32[1024,1024]{1,0:T(8,128)S(1)} %get-tuple-element.34.refs_0_, f32[512,1024]{1,0:T(8,128)S(1)} %get-tuple-element.36.refs_1_, f32[1536,512]{1,0:T(8,128)S(1)} %get-tuple-element.38.refs_2_, f32[512,1536]{1,0:T(8,128)S(1)} %get-tuple-element.40.refs_3_, ...), custom_call_target="tpu_custom_call" | custom-call | tf_op jit(solution)/shard_map/grad_0/pallas_call | solution.py:93
  74.7 2.3 %collective-permute-done.17.refs_5_ = s16[144,768]{1,0:T(8,128)(2,1)S(1)} collective-permute-done((s16[144,768]{1,0:T(8,128)(2,1)S(1)}, s16[144,768]{1,0:T(8,128)(2,1)S(1)}, u32[]{:S(2)}, u32[]{:S(2)}) %collective-permute-start.17) | collective-permute-done | bytes 221216 | tf_op jit(solution)/shard_map/ppermute | solution.py:76
  76.9 1.2 %post.1 = (f32[1,1]{1,0:T(1,128)}, f32[128,768]{1,0:T(8,128)}, f32[128,768]{1,0:T(8,128)}) custom-call(f32[128,768]{1,0:T(8,128)S(1)} %get-tuple-element.49.refs_0_, f32[128,128]{1,0:T(8,128)S(1)} %get-tuple-element.50.refs_1_, f32[128,768]{1,0:T(8,128)S(1)} %get-tuple-element.51.refs_2_, f32[128,128]{1,0:T(8,128)S(1)} %get-tuple-element.52.refs_3_, ...), custom_call_target="tpu_custom_call" | custom-call | tf_op jit(solution)/shard_map/post/pallas_call | solution.py:93
  (38 shorter events, 6.0 us)
Async XLA Ops:
  1.9 2.6 %collective-permute-start = (bf16[144,768]{1,0:T(8,128)(2,1)S(1)}, bf16[144,768]{1,0:T(8,128)(2,1)S(1)}, u32[]{:S(2)}, u32[]{:S(2)}) collective-permute-start(bf16[144,768]{1,0:T(8,128)(2,1)S(1)} %get-tuple-element.33), channel_id=1, source_target_pairs={{0,1},{1,0},{2,3},{3,2},{4,5},{5,4},{6,7},{7,6},{8,9},{9,8},{10,11... | collective-permute-start | bytes 663560 | tf_op jit(solution)/shard_map/ppermute | solution.py:80
  4.5 9.1 %collective-permute-start.3 = (bf16[272,768]{1,0:T(8,128)(2,1)S(1)}, bf16[272,768]{1,0:T(8,128)(2,1)S(1)}, u32[]{:S(2)}, u32[]{:S(2)}) collective-permute-start(bf16[272,768]{1,0:T(8,128)(2,1)S(1)} %join.1.refs_0_.refs_9_), channel_id=1, source_target_pairs={{0,2},{1,7},{2,0},{3,5},{4,6},{5,3},{6,4},{7,1},{8,10},{9,15},{10,... | collective-permute-start | bytes 1253384 | tf_op jit(solution)/shard_map/ppermute | solution.py:76
  7.4 9.2 %collective-permute-start.2 = (bf16[272,768]{1,0:T(8,128)(2,1)S(1)}, bf16[272,768]{1,0:T(8,128)(2,1)S(1)}, u32[]{:S(2)}, u32[]{:S(2)}) collective-permute-start(bf16[272,768]{1,0:T(8,128)(2,1)S(1)} %join.1.refs_0_.refs_9_), channel_id=1, source_target_pairs={{0,8},{1,25},{2,10},{3,27},{4,12},{5,29},{6,14},{7,31},{8,0},{9,17... | collective-permute-start | bytes 1253384 | tf_op jit(solution)/shard_map/ppermute | solution.py:76
  11.2 8.1 %collective-permute-start.1 = (bf16[272,768]{1,0:T(8,128)(2,1)S(1)}, bf16[272,768]{1,0:T(8,128)(2,1)S(1)}, u32[]{:S(2)}, u32[]{:S(2)}) collective-permute-start(bf16[272,768]{1,0:T(8,128)(2,1)S(1)} %join.1.refs_0_.refs_9_), channel_id=1, source_target_pairs={{0,32},{1,97},{2,34},{3,99},{4,36},{5,101},{6,38},{7,103},{8,40},{... | collective-permute-start | bytes 1253384 | tf_op jit(solution)/shard_map/ppermute | solution.py:76
  19.4 5.3 %collective-permute-start.4 = (bf16[1088,768]{1,0:T(8,128)(2,1)S(1)}, bf16[1088,768]{1,0:T(8,128)(2,1)S(1)}, u32[]{:S(2)}, u32[]{:S(2)}) collective-permute-start(bf16[1088,768]{1,0:T(8,128)(2,1)S(1)} %pack_near.1), channel_id=1, source_target_pairs={{0,1},{1,0},{2,3},{3,2},{4,5},{5,4},{6,7},{7,6},{8,9},{9,8},{10,11... | collective-permute-start | bytes 5013512 | tf_op jit(solution)/shard_map/ppermute | solution.py:80
  19.5 10.4 %collective-permute-start.5 = (bf16[272,768]{1,0:T(8,128)(2,1)S(1)}, bf16[272,768]{1,0:T(8,128)(2,1)S(1)}, u32[]{:S(2)}, u32[]{:S(2)}) collective-permute-start(bf16[272,768]{1,0:T(8,128)(2,1)S(1)} %collective-permute-done.3.refs_3_.refs_9_), channel_id=1, source_target_pairs={{0,40},{1,121},{2,42},{3,123},{4,44},{5,125},{6,46},{7,127},{8,32}... | collective-permute-start | bytes 1253384 | tf_op jit(solution)/shard_map/ppermute | solution.py:76
  21.8 8.1 %collective-permute-start.6 = (bf16[272,768]{1,0:T(8,128)(2,1)S(1)}, bf16[272,768]{1,0:T(8,128)(2,1)S(1)}, u32[]{:S(2)}, u32[]{:S(2)}) collective-permute-start(bf16[272,768]{1,0:T(8,128)(2,1)S(1)} %collective-permute-done.1.refs_1_.refs_9_), channel_id=1, source_target_pairs={{0,2},{1,7},{2,0},{3,5},{4,6},{5,3},{6,4},{7,1},{8,10},{9,15},{10,... | collective-permute-start | bytes 1253384 | tf_op jit(solution)/shard_map/ppermute | solution.py:76
  23.1 11.1 %collective-permute-start.8 = (bf16[272,768]{1,0:T(8,128)(2,1)S(1)}, bf16[272,768]{1,0:T(8,128)(2,1)S(1)}, u32[]{:S(2)}, u32[]{:S(2)}) collective-permute-start(bf16[272,768]{1,0:T(8,128)(2,1)S(1)} %collective-permute-done.3.refs_3_.refs_9_), channel_id=1, source_target_pairs={{0,8},{1,25},{2,10},{3,27},{4,12},{5,29},{6,14},{7,31},{8,0},{9,17... | collective-permute-start | bytes 1253384 | tf_op jit(solution)/shard_map/ppermute | solution.py:76
  24.5 9.7 %collective-permute-start.9 = (bf16[272,768]{1,0:T(8,128)(2,1)S(1)}, bf16[272,768]{1,0:T(8,128)(2,1)S(1)}, u32[]{:S(2)}, u32[]{:S(2)}) collective-permute-start(bf16[272,768]{1,0:T(8,128)(2,1)S(1)} %collective-permute-done.2.refs_2_.refs_9_), channel_id=1, source_target_pairs={{0,32},{1,97},{2,34},{3,99},{4,36},{5,101},{6,38},{7,103},{8,40},{... | collective-permute-start | bytes 1253384 | tf_op jit(solution)/shard_map/ppermute | solution.py:76
  29.9 4.5 %collective-permute-start.7 = (bf16[544,768]{1,0:T(8,128)(2,1)S(1)}, bf16[544,768]{1,0:T(8,128)(2,1)S(1)}, u32[]{:S(2)}, u32[]{:S(2)}) collective-permute-start(bf16[544,768]{1,0:T(8,128)(2,1)S(1)} %pack_first.1), channel_id=1, source_target_pairs={{0,1},{1,0},{2,3},{3,2},{4,5},{5,4},{6,7},{7,6},{8,9},{9,8},{10,11... | collective-permute-start | bytes 2506760 | tf_op jit(solution)/shard_map/ppermute | solution.py:80
  34.3 3.3 %collective-permute-start.10 = (bf16[544,768]{1,0:T(8,128)(2,1)S(1)}, bf16[544,768]{1,0:T(8,128)(2,1)S(1)}, u32[]{:S(2)}, u32[]{:S(2)}) collective-permute-start(bf16[544,768]{1,0:T(8,128)(2,1)S(1)} %pack_second.1), channel_id=1, source_target_pairs={{0,1},{1,0},{2,3},{3,2},{4,5},{5,4},{6,7},{7,6},{8,9},{9,8},{10,11... | collective-permute-start | bytes 2506760 | tf_op jit(solution)/shard_map/ppermute | solution.py:80
  48.7 11.9 %collective-permute-start.13 = (s16[272,768]{1,0:T(8,128)(2,1)S(1)}, s16[272,768]{1,0:T(8,128)(2,1)S(1)}, u32[]{:S(2)}, u32[]{:S(2)}) collective-permute-start(s16[272,768]{1,0:T(8,128)(2,1)S(1)} %grad_3.1), channel_id=1, source_target_pairs={{0,8},{1,25},{2,10},{3,27},{4,12},{5,29},{6,14},{7,31},{8,0},{9,17... | collective-permute-start | bytes 1253384 | tf_op jit(solution)/shard_map/ppermute | solution.py:76
  50.2 11.9 %collective-permute-start.15 = (s16[272,768]{1,0:T(8,128)(2,1)S(1)}, s16[272,768]{1,0:T(8,128)(2,1)S(1)}, u32[]{:S(2)}, u32[]{:S(2)}) collective-permute-start(s16[272,768]{1,0:T(8,128)(2,1)S(1)} %grad_6.1), channel_id=1, source_target_pairs={{0,32},{1,97},{2,34},{3,99},{4,36},{5,101},{6,38},{7,103},{8,40},{... | collective-permute-start | bytes 1253384 | tf_op jit(solution)/shard_map/ppermute | solution.py:76
  53.4 10.8 %collective-permute-start.11 = (s16[272,768]{1,0:T(8,128)(2,1)S(1)}, s16[272,768]{1,0:T(8,128)(2,1)S(1)}, u32[]{:S(2)}, u32[]{:S(2)}) collective-permute-start(s16[272,768]{1,0:T(8,128)(2,1)S(1)} %grad_5.1.refs_10_), channel_id=1, source_target_pairs={{0,2},{1,7},{2,0},{3,5},{4,6},{5,3},{6,4},{7,1},{8,10},{9,15},{10,... | collective-permute-start | bytes 1253384 | tf_op jit(solution)/shard_map/ppermute | solution.py:76
  56.1 16.2 %collective-permute-start.12 = (s16[272,768]{1,0:T(8,128)(2,1)S(1)}, s16[272,768]{1,0:T(8,128)(2,1)S(1)}, u32[]{:S(2)}, u32[]{:S(2)}) collective-permute-start(s16[272,768]{1,0:T(8,128)(2,1)S(1)} %grad_7.1), channel_id=1, source_target_pairs={{0,42},{1,127},{2,40},{3,125},{4,46},{5,123},{6,44},{7,121},{8,34}... | collective-permute-start | bytes 1253384 | tf_op jit(solution)/shard_map/ppermute | solution.py:76
  62.0 10.4 %collective-permute-start.14 = (s16[272,768]{1,0:T(8,128)(2,1)S(1)}, s16[272,768]{1,0:T(8,128)(2,1)S(1)}, u32[]{:S(2)}, u32[]{:S(2)}) collective-permute-start(s16[272,768]{1,0:T(8,128)(2,1)S(1)} %grad_1.1), channel_id=1, source_target_pairs={{0,2},{1,7},{2,0},{3,5},{4,6},{5,3},{6,4},{7,1},{8,10},{9,15},{10,... | collective-permute-start | bytes 1253384 | tf_op jit(solution)/shard_map/ppermute | solution.py:76
  63.5 9.9 %collective-permute-start.16 = (s16[272,768]{1,0:T(8,128)(2,1)S(1)}, s16[272,768]{1,0:T(8,128)(2,1)S(1)}, u32[]{:S(2)}, u32[]{:S(2)}) collective-permute-start(s16[272,768]{1,0:T(8,128)(2,1)S(1)} %grad_2.1), channel_id=1, source_target_pairs={{0,8},{1,25},{2,10},{3,27},{4,12},{5,29},{6,14},{7,31},{8,0},{9,17... | collective-permute-start | bytes 1253384 | tf_op jit(solution)/shard_map/ppermute | solution.py:76
  65.6 9.1 %collective-permute-start.18 = (s16[144,768]{1,0:T(8,128)(2,1)S(1)}, s16[144,768]{1,0:T(8,128)(2,1)S(1)}, u32[]{:S(2)}, u32[]{:S(2)}) collective-permute-start(s16[144,768]{1,0:T(8,128)(2,1)S(1)} %get-tuple-element.54), channel_id=1, source_target_pairs={{0,33},{1,96},{2,35},{3,98},{4,37},{5,100},{6,39},{7,102},{8,41},{... | collective-permute-start | bytes 663560 | tf_op jit(solution)/shard_map/ppermute | solution.py:540
  70.3 3.1 %copy-start = (bf16[128,768]{1,0:T(8,128)(2,1)S(1)}, bf16[128,768]{1,0:T(8,128)(2,1)}, u32[]{:S(2)}) copy-start(bf16[128,768]{1,0:T(8,128)(2,1)} %refs_0_.1) | copy-start | bytes 589828
  70.3 3.1 %copy-start.1 = (bf16[128,768]{1,0:T(8,128)(2,1)S(1)}, bf16[128,768]{1,0:T(8,128)(2,1)}, u32[]{:S(2)}) copy-start(bf16[128,768]{1,0:T(8,128)(2,1)} %refs_1_.1) | copy-start | bytes 589828
  70.3 6.6 %collective-permute-start.17 = (s16[144,768]{1,0:T(8,128)(2,1)S(1)}, s16[144,768]{1,0:T(8,128)(2,1)S(1)}, u32[]{:S(2)}, u32[]{:S(2)}) collective-permute-start(s16[144,768]{1,0:T(8,128)(2,1)S(1)} %get-tuple-element.48.refs_10_), channel_id=1, source_target_pairs={{0,32},{1,97},{2,34},{3,99},{4,36},{5,101},{6,38},{7,103},{8,40},{... | collective-permute-start | bytes 663560 | tf_op jit(solution)/shard_map/ppermute | solution.py:76
  74.0 2.9 %collective-permute-start.19 = (f32[48,768]{1,0:T(8,128)S(1)}, f32[48,768]{1,0:T(8,128)S(1)}, u32[]{:S(2)}, u32[]{:S(2)}) collective-permute-start(f32[48,768]{1,0:T(8,128)S(1)} %get-tuple-element.55), channel_id=1, source_target_pairs={{0,1},{1,0},{2,3},{3,2},{4,5},{5,4},{6,7},{7,6},{8,9},{9,8},{10,11... | collective-permute-start | bytes 442376 | tf_op jit(solution)/shard_map/ppermute | solution.py:80
  74.1 2.9 %collective-permute-start.20 = (f32[48,768]{1,0:T(8,128)S(1)}, f32[48,768]{1,0:T(8,128)S(1)}, u32[]{:S(2)}, u32[]{:S(2)}) collective-permute-start(f32[48,768]{1,0:T(8,128)S(1)} %get-tuple-element.56), channel_id=1, source_target_pairs={{0,1},{1,0},{2,3},{3,2},{4,5},{5,4},{6,7},{7,6},{8,9},{9,8},{10,11... | collective-permute-start | bytes 442376 | tf_op jit(solution)/shard_map/ppermute | solution.py:80
  74.6 2.4 %collective-permute-start.21 = (f32[40,768]{1,0:T(8,128)S(1)}, f32[40,768]{1,0:T(8,128)S(1)}, u32[]{:S(2)}, u32[]{:S(2)}) collective-permute-start(f32[40,768]{1,0:T(8,128)S(1)} %get-tuple-element.57), channel_id=1, source_target_pairs={{0,1},{1,0},{2,3},{3,2},{4,5},{5,4},{6,7},{7,6},{8,9},{9,8},{10,11... | collective-permute-start | bytes 368648 | tf_op jit(solution)/shard_map/ppermute | solution.py:80

commit v8 on v7

--- a/solution.py
+++ b/solution.py
@@ -416,7 +416,9 @@
 
 
 def post_kernel(qn_ref, qr_ref, dn_ref, dr_ref, keep_ref, same_ref, cross_ref, *refs):
-    *come, loss_ref, gq_ref, gd_ref = refs
+    *come, loss_ref, gq_hbm, gd_hbm, gq_ref, gd_ref, sems = refs
+    out_q = pltpu.make_async_copy(gq_ref, gq_hbm, sems.at[0])
+    out_d = pltpu.make_async_copy(gd_ref, gd_hbm, sems.at[1])
     come_ref = jnp.concatenate([ref[...] for ref in come], axis=0)
 
     def project(out_ref, grad, unit_ref, over_ref):
@@ -426,7 +428,9 @@
 
     def fill(gq, last_q, gd, last_d, half):
         project(gq_ref, gq[:ROWS, :] + decode_half(last_q, half), qn_ref, qr_ref)
+        out_q.start()
         project(gd_ref, gd[:ROWS, :] + decode_half(last_d, half), dn_ref, dr_ref)
+        out_d.start()
         loss_ref[...] = (gd[ROWS : ROWS + 1, 0:1] + loss_of(last_d, ROWS)) * (1.0 / 16384)
 
     role = role_of()
@@ -438,6 +442,9 @@
     @pl.when(role == 1)
     def _():
         fill(come_ref, cross_ref, keep_ref, same_ref, 1)
+
+    out_q.wait()
+    out_d.wait()
 
 
 def local(queries, documents, positives):
@@ -550,16 +557,19 @@
         *[near(v) for v in (queries, documents, g0, r7, r1, r2)],
     )
     come = [swap(v) for v in give]
-    loss, gq, gd = call(
+    grad_shape = jax.ShapeDtypeStruct((ROWS, WIDTH), F32)
+    loss, gq, gd = pl.pallas_call(
         post_kernel,
-        "post",
-        [
-            jax.ShapeDtypeStruct((1, 1), F32),
-            jax.ShapeDtypeStruct((ROWS, WIDTH), F32),
-            jax.ShapeDtypeStruct((ROWS, WIDTH), F32),
+        name="post",
+        out_specs=[pl.BlockSpec(), pl.BlockSpec(memory_space=pltpu.HBM), pl.BlockSpec(memory_space=pltpu.HBM)],
+        out_shape=[jax.ShapeDtypeStruct((1, 1), F32), grad_shape, grad_shape],
+        scratch_shapes=[
+            pltpu.VMEM((ROWS, WIDTH), F32),
+            pltpu.VMEM((ROWS, WIDTH), F32),
+            pltpu.SemaphoreType.DMA((2,)),
         ],
-        *[near(v) for v in (qn, qr, dn, dr, keep, same, cross, *come)],
-    )
+        compiler_params=pltpu.CompilerParams(vmem_limit_bytes=8 * 1024 * 1024),
+    )(*[near(v) for v in (qn, qr, dn, dr, keep, same, cross, *come)])
     return (loss.reshape(()), gq, gd)
 
 

time: 78.3 us -> 79 us (level)
    pallas_call x0 -> x1, Pallas kernels: none -> 1.74 us  [local(): pl.pallas_call(post_kernel, name='post', out_specs=[pl.BlockSpec(), pl.Bl...]
    pallas_call x20 -> x19, Pallas kernels: 21.4 us -> 20.1 us  [call(): pl.pallas_call(body, name=name, out_shape=out_shape, scratch_shapes=scrat...]
where the time goes in v8:
time: 79 us; the launch traced here: 78.8 us
  starting transfers between devices  30.9 us (39%)
  Pallas kernels  23.1 us (29%)
  waiting for transfers between devices  16.2 us (21%)
  blocking collectives  7.53 us (10%)
  between operations  1.01 us (1%)
    ppermute x14, starting transfers between devices, send(): return lax.ppermute(value, 'dp', partners(bits))  23.8 us
    pallas_call x19, Pallas kernels, call(): pl.pallas_call(body, name=name, out_shape=out_shape, scratch_shapes=scrat...  20.1 us
    ppermute x14, waiting for transfers between devices, send(): return lax.ppermute(value, 'dp', partners(bits))  15.1 us
    all_to_all x1, blocking collectives, local(): lax.all_to_all(parts[-1][1], 'dp', 0, 0, axis_index_groups=SUM_GROUPS, ti...  7.53 us
    ppermute x1, starting transfers between devices, local(): cross = lax.ppermute(halves[1], 'dp', crossing(4))  4.69 us
    ppermute x7, starting transfers between devices, swap(): return lax.ppermute(value, 'dp', SWAP)  2.43 us
    pallas_call x1, Pallas kernels, local(): pl.pallas_call(post_kernel, name='post', out_specs=[pl.BlockSpec(), pl.Bl...  1.74 us
  transfers between devices with their start and end apart: 22, of which 7 were waited for; matrix products, arithmetic and copies ran while one was open for 0% of the time, Pallas kernels for 21%

profile of v8, /device:TPU:1, one launch (start us, length us, event | category | flops | bytes accessed | tf_op | source)
XLA Modules:
  0.0 78.8 jit_solution(16821319851410510730)
XLA Ops:
  0.6 1.2 %pre.1 = (bf16[144,768]{1,0:T(8,128)(2,1)S(1)}, bf16[144,768]{1,0:T(8,128)(2,1)S(1)}) custom-call(bf16[128,768]{1,0:T(8,128)(2,1)} %refs_0_.1, bf16[128,768]{1,0:T(8,128)(2,1)} %refs_1_.1, s32[1,128]{1,0:T(1,128)} %bitcast.2), custom_call_target="tpu_custom_call" | custom-call | tf_op jit(solution)/shard_map/pre/pallas_call | solution.py:453
  1.9 1.5 %collective-permute-start = (bf16[144,768]{1,0:T(8,128)(2,1)S(1)}, bf16[144,768]{1,0:T(8,128)(2,1)S(1)}, u32[]{:S(2)}, u32[]{:S(2)}) collective-permute-start(bf16[144,768]{1,0:T(8,128)(2,1)S(1)} %get-tuple-element.33), channel_id=1, source_target_pairs={{0,1},{1,0},{2,3},{3,2},{4,5},{5,4},{6,7},{7,6},{8,9},{9,8},{10,11... | collective-permute-start | bytes 663560 | tf_op jit(solution)/shard_map/ppermute | solution.py:80
  4.5 2.9 %collective-permute-start.3 = (bf16[272,768]{1,0:T(8,128)(2,1)S(1)}, bf16[272,768]{1,0:T(8,128)(2,1)S(1)}, u32[]{:S(2)}, u32[]{:S(2)}) collective-permute-start(bf16[272,768]{1,0:T(8,128)(2,1)S(1)} %join.1.refs_0_.refs_9_), channel_id=1, source_target_pairs={{0,2},{1,7},{2,0},{3,5},{4,6},{5,3},{6,4},{7,1},{8,10},{9,15},{10,... | collective-permute-start | bytes 1253384 | tf_op jit(solution)/shard_map/ppermute | solution.py:76
  7.4 3.8 %collective-permute-start.2 = (bf16[272,768]{1,0:T(8,128)(2,1)S(1)}, bf16[272,768]{1,0:T(8,128)(2,1)S(1)}, u32[]{:S(2)}, u32[]{:S(2)}) collective-permute-start(bf16[272,768]{1,0:T(8,128)(2,1)S(1)} %join.1.refs_0_.refs_9_), channel_id=1, source_target_pairs={{0,8},{1,25},{2,10},{3,27},{4,12},{5,29},{6,14},{7,31},{8,0},{9,17... | collective-permute-start | bytes 1253384 | tf_op jit(solution)/shard_map/ppermute | solution.py:76
  11.2 2.5 %collective-permute-start.1 = (bf16[272,768]{1,0:T(8,128)(2,1)S(1)}, bf16[272,768]{1,0:T(8,128)(2,1)S(1)}, u32[]{:S(2)}, u32[]{:S(2)}) collective-permute-start(bf16[272,768]{1,0:T(8,128)(2,1)S(1)} %join.1.refs_0_.refs_9_), channel_id=1, source_target_pairs={{0,32},{1,97},{2,34},{3,99},{4,36},{5,101},{6,38},{7,103},{8,40},{... | collective-permute-start | bytes 1253384 | tf_op jit(solution)/shard_map/ppermute | solution.py:76
  13.7 2.9 %collective-permute-done.2.refs_2_.refs_9_ = bf16[272,768]{1,0:T(8,128)(2,1)S(1)} collective-permute-done((bf16[272,768]{1,0:T(8,128)(2,1)S(1)}, bf16[272,768]{1,0:T(8,128)(2,1)S(1)}, u32[]{:S(2)}, u32[]{:S(2)}) %collective-permute-start.2) | collective-permute-done | bytes 417824 | tf_op jit(solution)/shard_map/ppermute | solution.py:76
  16.6 2.7 %collective-permute-done.1.refs_1_.refs_9_ = bf16[272,768]{1,0:T(8,128)(2,1)S(1)} collective-permute-done((bf16[272,768]{1,0:T(8,128)(2,1)S(1)}, bf16[272,768]{1,0:T(8,128)(2,1)S(1)}, u32[]{:S(2)}, u32[]{:S(2)}) %collective-permute-start.1) | collective-permute-done | bytes 417824 | tf_op jit(solution)/shard_map/ppermute | solution.py:76
  19.5 2.3 %collective-permute-start.5 = (bf16[272,768]{1,0:T(8,128)(2,1)S(1)}, bf16[272,768]{1,0:T(8,128)(2,1)S(1)}, u32[]{:S(2)}, u32[]{:S(2)}) collective-permute-start(bf16[272,768]{1,0:T(8,128)(2,1)S(1)} %collective-permute-done.3.refs_3_.refs_9_), channel_id=1, source_target_pairs={{0,40},{1,121},{2,42},{3,123},{4,44},{5,125},{6,46},{7,127},{8,32}... | collective-permute-start | bytes 1253384 | tf_op jit(solution)/shard_map/ppermute | solution.py:76
  21.8 1.4 %collective-permute-start.6 = (bf16[272,768]{1,0:T(8,128)(2,1)S(1)}, bf16[272,768]{1,0:T(8,128)(2,1)S(1)}, u32[]{:S(2)}, u32[]{:S(2)}) collective-permute-start(bf16[272,768]{1,0:T(8,128)(2,1)S(1)} %collective-permute-done.1.refs_1_.refs_9_), channel_id=1, source_target_pairs={{0,2},{1,7},{2,0},{3,5},{4,6},{5,3},{6,4},{7,1},{8,10},{9,15},{10,... | collective-permute-start | bytes 1253384 | tf_op jit(solution)/shard_map/ppermute | solution.py:76
  23.1 1.4 %collective-permute-start.8 = (bf16[272,768]{1,0:T(8,128)(2,1)S(1)}, bf16[272,768]{1,0:T(8,128)(2,1)S(1)}, u32[]{:S(2)}, u32[]{:S(2)}) collective-permute-start(bf16[272,768]{1,0:T(8,128)(2,1)S(1)} %collective-permute-done.3.refs_3_.refs_9_), channel_id=1, source_target_pairs={{0,8},{1,25},{2,10},{3,27},{4,12},{5,29},{6,14},{7,31},{8,0},{9,17... | collective-permute-start | bytes 1253384 | tf_op jit(solution)/shard_map/ppermute | solution.py:76
  24.7 2.0 %tile_0.1 = (f32[1024,1024]{1,0:T(8,128)S(1)}, f32[1024,128]{1,0:T(8,128)S(1)}, f32[16,1024]{1,0:T(8,128)S(1)}) custom-call(bf16[272,768]{1,0:T(8,128)(2,1)S(1)} %join.1.refs_0_.refs_9_, bf16[272,768]{1,0:T(8,128)(2,1)S(1)} %collective-permute-done.1.refs_1_.refs_9_, bf16[272,768]{1,0:T(8,128)(2,1)S(1)} %collective-permute-done.2.refs_2_.refs_9_, ...), custom_call_target="tpu_custom_call" | custom-call | tf_op jit(solution)/shard_map/tile_0/pallas_call | solution.py:93
  26.7 3.1 %collective-permute-done.5.refs_0_.refs_4_.refs_9_ = bf16[272,768]{1,0:T(8,128)(2,1)S(1)} collective-permute-done((bf16[272,768]{1,0:T(8,128)(2,1)S(1)}, bf16[272,768]{1,0:T(8,128)(2,1)S(1)}, u32[]{:S(2)}, u32[]{:S(2)}) %collective-permute-start.5) | collective-permute-done | bytes 417824 | tf_op jit(solution)/shard_map/ppermute | solution.py:76
  30.0 1.1 %tile_1.1 = (f32[512,1024]{1,0:T(8,128)S(1)}, f32[512,128]{1,0:T(8,128)S(1)}, f32[16,1024]{1,0:T(8,128)S(1)}) custom-call(bf16[272,768]{1,0:T(8,128)(2,1)S(1)} %collective-permute-done.5.refs_0_.refs_4_.refs_9_, bf16[272,768]{1,0:T(8,128)(2,1)S(1)} %collective-permute-done.6.refs_1_.refs_5_.refs_9_, ...), custom_call_target="tpu_custom_call" | custom-call | tf_op jit(solution)/shard_map/tile_1/pallas_call | solution.py:93
  31.2 3.1 %collective-permute-done.8.refs_0_.refs_6_.refs_9_ = bf16[272,768]{1,0:T(8,128)(2,1)S(1)} collective-permute-done((bf16[272,768]{1,0:T(8,128)(2,1)S(1)}, bf16[272,768]{1,0:T(8,128)(2,1)S(1)}, u32[]{:S(2)}, u32[]{:S(2)}) %collective-permute-start.8) | collective-permute-done | bytes 417824 | tf_op jit(solution)/shard_map/ppermute | solution.py:76
  34.4 1.5 %tile_2.1 = (f32[1536,512]{1,0:T(8,128)S(1)}, f32[1536,128]{1,0:T(8,128)S(1)}, f32[16,512]{1,0:T(8,128)S(1)}) custom-call(bf16[272,768]{1,0:T(8,128)(2,1)S(1)} %join.1.refs_0_.refs_9_, bf16[272,768]{1,0:T(8,128)(2,1)S(1)} %collective-permute-done.1.refs_1_.refs_9_, bf16[272,768]{1,0:T(8,128)(2,1)S(1)} %collective-permute-done.2.refs_2_.refs_9_, ...), custom_call_target="tpu_custom_call" | custom-call | tf_op jit(solution)/shard_map/tile_2/pallas_call | solution.py:93
  36.0 1.6 %tile_3.1 = (f32[512,1536]{1,0:T(8,128)S(1)}, f32[512,128]{1,0:T(8,128)S(1)}, f32[16,1536]{1,0:T(8,128)S(1)}) custom-call(bf16[272,768]{1,0:T(8,128)(2,1)S(1)} %collective-permute-done.8.refs_0_.refs_6_.refs_9_, bf16[272,768]{1,0:T(8,128)(2,1)S(1)} %collective-permute-done.9.refs_1_.refs_7_.refs_9_, ...), custom_call_target="tpu_custom_call" | custom-call | tf_op jit(solution)/shard_map/tile_3/pallas_call | solution.py:93
  37.6 2.0 %tile_4.1 = (f32[2048,512]{1,0:T(8,128)S(1)}, f32[8,32,128]{2,1,0:T(8,128)S(1)}) custom-call(bf16[272,768]{1,0:T(8,128)(2,1)S(1)} %join.1.refs_0_.refs_9_, bf16[272,768]{1,0:T(8,128)(2,1)S(1)} %collective-permute-done.1.refs_1_.refs_9_, bf16[272,768]{1,0:T(8,128)(2,1)S(1)} %collective-permute-done.2.refs_2_.refs_9_, ...), custom_call_target="tpu_custom_call" | custom-call | tf_op jit(solution)/shard_map/tile_4/pallas_call | solution.py:93
  39.6 7.5 %all_to_all.5.refs_0_ = f32[8,32,128]{2,1,0:T(8,128)S(1)} all-to-all(f32[8,32,128]{2,1,0:T(8,128)S(1)} %get-tuple-element.47), channel_id=1, replica_groups={{0,2,8,10,32,34,40,42},{4,6,12,14,36,38,44,46},{16,18,24,26,48,50,56,58..., dimensions={0} | all-to-all | bytes 262144 | tf_op jit(solution)/shard_map/all_to_all | solution.py:510
  47.3 1.4 %grad_3.1 = s16[272,768]{1,0:T(8,128)(2,1)S(1)} custom-call(f32[1024,1024]{1,0:T(8,128)S(1)} %get-tuple-element.34.refs_0_, f32[512,1024]{1,0:T(8,128)S(1)} %get-tuple-element.36.refs_1_, f32[1536,512]{1,0:T(8,128)S(1)} %get-tuple-element.38.refs_2_, f32[512,1536]{1,0:T(8,128)S(1)} %get-tuple-element.40.refs_3_, f32[2048,512]{1,0:T(8,128)S(1)} %get-tuple-element.46.refs_4_, ...), custom_call_target="tpu_custom_call" | custom-call | tf_op jit(solution)/shard_map/grad_3/pallas_call | solution.py:93
  48.8 1.4 %grad_6.1 = s16[272,768]{1,0:T(8,128)(2,1)S(1)} custom-call(f32[1024,1024]{1,0:T(8,128)S(1)} %get-tuple-element.34.refs_0_, f32[512,1024]{1,0:T(8,128)S(1)} %get-tuple-element.36.refs_1_, f32[1536,512]{1,0:T(8,128)S(1)} %get-tuple-element.38.refs_2_, f32[512,1536]{1,0:T(8,128)S(1)} %get-tuple-element.40.refs_3_, f32[2048,512]{1,0:T(8,128)S(1)} %get-tuple-element.46.refs_4_, ...), custom_call_target="tpu_custom_call" | custom-call | tf_op jit(solution)/shard_map/grad_6/pallas_call | solution.py:93
  50.2 1.9 %collective-permute-start.15 = (s16[272,768]{1,0:T(8,128)(2,1)S(1)}, s16[272,768]{1,0:T(8,128)(2,1)S(1)}, u32[]{:S(2)}, u32[]{:S(2)}) collective-permute-start(s16[272,768]{1,0:T(8,128)(2,1)S(1)} %grad_6.1), channel_id=1, source_target_pairs={{0,32},{1,97},{2,34},{3,99},{4,36},{5,101},{6,38},{7,103},{8,40},{... | collective-permute-start | bytes 1253384 | tf_op jit(solution)/shard_map/ppermute | solution.py:76
  52.0 1.4 %grad_5.1.refs_10_ = s16[272,768]{1,0:T(8,128)(2,1)S(1)} custom-call(f32[1024,1024]{1,0:T(8,128)S(1)} %get-tuple-element.34.refs_0_, f32[512,1024]{1,0:T(8,128)S(1)} %get-tuple-element.36.refs_1_, f32[1536,512]{1,0:T(8,128)S(1)} %get-tuple-element.38.refs_2_, f32[512,1536]{1,0:T(8,128)S(1)} %get-tuple-element.40.refs_3_, ...), custom_call_target="tpu_custom_call" | custom-call | tf_op jit(solution)/shard_map/grad_5/pallas_call | solution.py:93
  53.4 1.4 %collective-permute-start.11 = (s16[272,768]{1,0:T(8,128)(2,1)S(1)}, s16[272,768]{1,0:T(8,128)(2,1)S(1)}, u32[]{:S(2)}, u32[]{:S(2)}) collective-permute-start(s16[272,768]{1,0:T(8,128)(2,1)S(1)} %grad_5.1.refs_10_), channel_id=1, source_target_pairs={{0,2},{1,7},{2,0},{3,5},{4,6},{5,3},{6,4},{7,1},{8,10},{9,15},{10,... | collective-permute-start | bytes 1253384 | tf_op jit(solution)/shard_map/ppermute | solution.py:76
  54.8 1.4 %grad_7.1 = s16[272,768]{1,0:T(8,128)(2,1)S(1)} custom-call(f32[1024,1024]{1,0:T(8,128)S(1)} %get-tuple-element.34.refs_0_, f32[512,1024]{1,0:T(8,128)S(1)} %get-tuple-element.36.refs_1_, f32[1536,512]{1,0:T(8,128)S(1)} %get-tuple-element.38.refs_2_, f32[512,1536]{1,0:T(8,128)S(1)} %get-tuple-element.40.refs_3_, f32[2048,512]{1,0:T(8,128)S(1)} %get-tuple-element.46.refs_4_, ...), custom_call_target="tpu_custom_call" | custom-call | tf_op jit(solution)/shard_map/grad_7/pallas_call | solution.py:93
  56.1 4.5 %collective-permute-start.12 = (s16[272,768]{1,0:T(8,128)(2,1)S(1)}, s16[272,768]{1,0:T(8,128)(2,1)S(1)}, u32[]{:S(2)}, u32[]{:S(2)}) collective-permute-start(s16[272,768]{1,0:T(8,128)(2,1)S(1)} %grad_7.1), channel_id=1, source_target_pairs={{0,42},{1,127},{2,40},{3,125},{4,46},{5,123},{6,44},{7,121},{8,34}... | collective-permute-start | bytes 1253384 | tf_op jit(solution)/shard_map/ppermute | solution.py:76
  60.6 1.4 %grad_1.1 = s16[272,768]{1,0:T(8,128)(2,1)S(1)} custom-call(f32[1024,1024]{1,0:T(8,128)S(1)} %get-tuple-element.34.refs_0_, f32[512,1024]{1,0:T(8,128)S(1)} %get-tuple-element.36.refs_1_, f32[1536,512]{1,0:T(8,128)S(1)} %get-tuple-element.38.refs_2_, f32[512,1536]{1,0:T(8,128)S(1)} %get-tuple-element.40.refs_3_, f32[2048,512]{1,0:T(8,128)S(1)} %get-tuple-element.46.refs_4_, ...), custom_call_target="tpu_custom_call" | custom-call | tf_op jit(solution)/shard_map/grad_1/pallas_call | solution.py:93
  62.1 1.4 %grad_2.1 = s16[272,768]{1,0:T(8,128)(2,1)S(1)} custom-call(f32[1024,1024]{1,0:T(8,128)S(1)} %get-tuple-element.34.refs_0_, f32[512,1024]{1,0:T(8,128)S(1)} %get-tuple-element.36.refs_1_, f32[1536,512]{1,0:T(8,128)S(1)} %get-tuple-element.38.refs_2_, f32[512,1536]{1,0:T(8,128)S(1)} %get-tuple-element.40.refs_3_, f32[2048,512]{1,0:T(8,128)S(1)} %get-tuple-element.46.refs_4_, ...), custom_call_target="tpu_custom_call" | custom-call | tf_op jit(solution)/shard_map/grad_2/pallas_call | solution.py:93
  64.2 1.4 %grad_4.1 = (s16[144,768]{1,0:T(8,128)(2,1)S(1)}, s16[144,768]{1,0:T(8,128)(2,1)S(1)}) custom-call(f32[1024,1024]{1,0:T(8,128)S(1)} %get-tuple-element.34.refs_0_, f32[512,1024]{1,0:T(8,128)S(1)} %get-tuple-element.36.refs_1_, f32[1536,512]{1,0:T(8,128)S(1)} %get-tuple-element.38.refs_2_, f32[512,1536]{1,0:T(8,128)S(1)} %get-tuple-element.40.refs_3_, ...), custom_call_target="tpu_custom_call" | custom-call | tf_op jit(solution)/shard_map/grad_4/pallas_call | solution.py:93
  65.6 4.7 %collective-permute-start.18 = (s16[144,768]{1,0:T(8,128)(2,1)S(1)}, s16[144,768]{1,0:T(8,128)(2,1)S(1)}, u32[]{:S(2)}, u32[]{:S(2)}) collective-permute-start(s16[144,768]{1,0:T(8,128)(2,1)S(1)} %get-tuple-element.54), channel_id=1, source_target_pairs={{0,33},{1,96},{2,35},{3,98},{4,37},{5,100},{6,39},{7,102},{8,41},{... | collective-permute-start | bytes 663560 | tf_op jit(solution)/shard_map/ppermute | solution.py:547
  71.2 1.1 %grad_0.1.refs_2_ = f32[264,768]{1,0:T(8,128)S(1)} custom-call(f32[1024,1024]{1,0:T(8,128)S(1)} %get-tuple-element.34.refs_0_, f32[512,1024]{1,0:T(8,128)S(1)} %get-tuple-element.36.refs_1_, f32[1536,512]{1,0:T(8,128)S(1)} %get-tuple-element.38.refs_2_, f32[512,1536]{1,0:T(8,128)S(1)} %get-tuple-element.40.refs_3_, ...), custom_call_target="tpu_custom_call" | custom-call | tf_op jit(solution)/shard_map/grad_0/pallas_call | solution.py:93
  74.7 2.3 %collective-permute-done.17.same_ref = s16[144,768]{1,0:T(8,128)(2,1)S(1)} collective-permute-done((s16[144,768]{1,0:T(8,128)(2,1)S(1)}, s16[144,768]{1,0:T(8,128)(2,1)S(1)}, u32[]{:S(2)}, u32[]{:S(2)}) %collective-permute-start.17) | collective-permute-done | bytes 221216 | tf_op jit(solution)/shard_map/ppermute | solution.py:76
  76.9 1.7 %post.1 = (f32[1,1]{1,0:T(1,128)}, f32[128,768]{1,0:T(8,128)}, f32[128,768]{1,0:T(8,128)}) custom-call(f32[128,768]{1,0:T(8,128)S(1)} %get-tuple-element.49.qn_ref, f32[128,128]{1,0:T(8,128)S(1)} %get-tuple-element.50.qr_ref, f32[128,768]{1,0:T(8,128)S(1)} %get-tuple-element.51.dn_ref, f32[128,128]{1,0:T(8,128)S(1)} %get-tuple-element.52.dr_ref, ...), custom_call_target="tpu_custom_call" | custom-call | tf_op jit(solution)/shard_map/post/pallas_call | solution.py:561
  (38 shorter events, 6.0 us)
Async XLA Ops:
  1.9 2.6 %collective-permute-start = (bf16[144,768]{1,0:T(8,128)(2,1)S(1)}, bf16[144,768]{1,0:T(8,128)(2,1)S(1)}, u32[]{:S(2)}, u32[]{:S(2)}) collective-permute-start(bf16[144,768]{1,0:T(8,128)(2,1)S(1)} %get-tuple-element.33), channel_id=1, source_target_pairs={{0,1},{1,0},{2,3},{3,2},{4,5},{5,4},{6,7},{7,6},{8,9},{9,8},{10,11... | collective-permute-start | bytes 663560 | tf_op jit(solution)/shard_map/ppermute | solution.py:80
  4.5 9.1 %collective-permute-start.3 = (bf16[272,768]{1,0:T(8,128)(2,1)S(1)}, bf16[272,768]{1,0:T(8,128)(2,1)S(1)}, u32[]{:S(2)}, u32[]{:S(2)}) collective-permute-start(bf16[272,768]{1,0:T(8,128)(2,1)S(1)} %join.1.refs_0_.refs_9_), channel_id=1, source_target_pairs={{0,2},{1,7},{2,0},{3,5},{4,6},{5,3},{6,4},{7,1},{8,10},{9,15},{10,... | collective-permute-start | bytes 1253384 | tf_op jit(solution)/shard_map/ppermute | solution.py:76
  7.4 9.2 %collective-permute-start.2 = (bf16[272,768]{1,0:T(8,128)(2,1)S(1)}, bf16[272,768]{1,0:T(8,128)(2,1)S(1)}, u32[]{:S(2)}, u32[]{:S(2)}) collective-permute-start(bf16[272,768]{1,0:T(8,128)(2,1)S(1)} %join.1.refs_0_.refs_9_), channel_id=1, source_target_pairs={{0,8},{1,25},{2,10},{3,27},{4,12},{5,29},{6,14},{7,31},{8,0},{9,17... | collective-permute-start | bytes 1253384 | tf_op jit(solution)/shard_map/ppermute | solution.py:76
  11.2 8.1 %collective-permute-start.1 = (bf16[272,768]{1,0:T(8,128)(2,1)S(1)}, bf16[272,768]{1,0:T(8,128)(2,1)S(1)}, u32[]{:S(2)}, u32[]{:S(2)}) collective-permute-start(bf16[272,768]{1,0:T(8,128)(2,1)S(1)} %join.1.refs_0_.refs_9_), channel_id=1, source_target_pairs={{0,32},{1,97},{2,34},{3,99},{4,36},{5,101},{6,38},{7,103},{8,40},{... | collective-permute-start | bytes 1253384 | tf_op jit(solution)/shard_map/ppermute | solution.py:76
  19.4 5.3 %collective-permute-start.4 = (bf16[1088,768]{1,0:T(8,128)(2,1)S(1)}, bf16[1088,768]{1,0:T(8,128)(2,1)S(1)}, u32[]{:S(2)}, u32[]{:S(2)}) collective-permute-start(bf16[1088,768]{1,0:T(8,128)(2,1)S(1)} %pack_near.1), channel_id=1, source_target_pairs={{0,1},{1,0},{2,3},{3,2},{4,5},{5,4},{6,7},{7,6},{8,9},{9,8},{10,11... | collective-permute-start | bytes 5013512 | tf_op jit(solution)/shard_map/ppermute | solution.py:80
  19.5 10.4 %collective-permute-start.5 = (bf16[272,768]{1,0:T(8,128)(2,1)S(1)}, bf16[272,768]{1,0:T(8,128)(2,1)S(1)}, u32[]{:S(2)}, u32[]{:S(2)}) collective-permute-start(bf16[272,768]{1,0:T(8,128)(2,1)S(1)} %collective-permute-done.3.refs_3_.refs_9_), channel_id=1, source_target_pairs={{0,40},{1,121},{2,42},{3,123},{4,44},{5,125},{6,46},{7,127},{8,32}... | collective-permute-start | bytes 1253384 | tf_op jit(solution)/shard_map/ppermute | solution.py:76
  21.8 8.1 %collective-permute-start.6 = (bf16[272,768]{1,0:T(8,128)(2,1)S(1)}, bf16[272,768]{1,0:T(8,128)(2,1)S(1)}, u32[]{:S(2)}, u32[]{:S(2)}) collective-permute-start(bf16[272,768]{1,0:T(8,128)(2,1)S(1)} %collective-permute-done.1.refs_1_.refs_9_), channel_id=1, source_target_pairs={{0,2},{1,7},{2,0},{3,5},{4,6},{5,3},{6,4},{7,1},{8,10},{9,15},{10,... | collective-permute-start | bytes 1253384 | tf_op jit(solution)/shard_map/ppermute | solution.py:76
  23.1 11.1 %collective-permute-start.8 = (bf16[272,768]{1,0:T(8,128)(2,1)S(1)}, bf16[272,768]{1,0:T(8,128)(2,1)S(1)}, u32[]{:S(2)}, u32[]{:S(2)}) collective-permute-start(bf16[272,768]{1,0:T(8,128)(2,1)S(1)} %collective-permute-done.3.refs_3_.refs_9_), channel_id=1, source_target_pairs={{0,8},{1,25},{2,10},{3,27},{4,12},{5,29},{6,14},{7,31},{8,0},{9,17... | collective-permute-start | bytes 1253384 | tf_op jit(solution)/shard_map/ppermute | solution.py:76
  24.5 9.7 %collective-permute-start.9 = (bf16[272,768]{1,0:T(8,128)(2,1)S(1)}, bf16[272,768]{1,0:T(8,128)(2,1)S(1)}, u32[]{:S(2)}, u32[]{:S(2)}) collective-permute-start(bf16[272,768]{1,0:T(8,128)(2,1)S(1)} %collective-permute-done.2.refs_2_.refs_9_), channel_id=1, source_target_pairs={{0,32},{1,97},{2,34},{3,99},{4,36},{5,101},{6,38},{7,103},{8,40},{... | collective-permute-start | bytes 1253384 | tf_op jit(solution)/shard_map/ppermute | solution.py:76
  29.9 4.5 %collective-permute-start.7 = (bf16[544,768]{1,0:T(8,128)(2,1)S(1)}, bf16[544,768]{1,0:T(8,128)(2,1)S(1)}, u32[]{:S(2)}, u32[]{:S(2)}) collective-permute-start(bf16[544,768]{1,0:T(8,128)(2,1)S(1)} %pack_first.1), channel_id=1, source_target_pairs={{0,1},{1,0},{2,3},{3,2},{4,5},{5,4},{6,7},{7,6},{8,9},{9,8},{10,11... | collective-permute-start | bytes 2506760 | tf_op jit(solution)/shard_map/ppermute | solution.py:80
  34.3 3.3 %collective-permute-start.10 = (bf16[544,768]{1,0:T(8,128)(2,1)S(1)}, bf16[544,768]{1,0:T(8,128)(2,1)S(1)}, u32[]{:S(2)}, u32[]{:S(2)}) collective-permute-start(bf16[544,768]{1,0:T(8,128)(2,1)S(1)} %pack_second.1), channel_id=1, source_target_pairs={{0,1},{1,0},{2,3},{3,2},{4,5},{5,4},{6,7},{7,6},{8,9},{9,8},{10,11... | collective-permute-start | bytes 2506760 | tf_op jit(solution)/shard_map/ppermute | solution.py:80
  48.7 11.9 %collective-permute-start.13 = (s16[272,768]{1,0:T(8,128)(2,1)S(1)}, s16[272,768]{1,0:T(8,128)(2,1)S(1)}, u32[]{:S(2)}, u32[]{:S(2)}) collective-permute-start(s16[272,768]{1,0:T(8,128)(2,1)S(1)} %grad_3.1), channel_id=1, source_target_pairs={{0,8},{1,25},{2,10},{3,27},{4,12},{5,29},{6,14},{7,31},{8,0},{9,17... | collective-permute-start | bytes 1253384 | tf_op jit(solution)/shard_map/ppermute | solution.py:76
  50.2 11.9 %collective-permute-start.15 = (s16[272,768]{1,0:T(8,128)(2,1)S(1)}, s16[272,768]{1,0:T(8,128)(2,1)S(1)}, u32[]{:S(2)}, u32[]{:S(2)}) collective-permute-start(s16[272,768]{1,0:T(8,128)(2,1)S(1)} %grad_6.1), channel_id=1, source_target_pairs={{0,32},{1,97},{2,34},{3,99},{4,36},{5,101},{6,38},{7,103},{8,40},{... | collective-permute-start | bytes 1253384 | tf_op jit(solution)/shard_map/ppermute | solution.py:76
  53.4 10.8 %collective-permute-start.11 = (s16[272,768]{1,0:T(8,128)(2,1)S(1)}, s16[272,768]{1,0:T(8,128)(2,1)S(1)}, u32[]{:S(2)}, u32[]{:S(2)}) collective-permute-start(s16[272,768]{1,0:T(8,128)(2,1)S(1)} %grad_5.1.refs_10_), channel_id=1, source_target_pairs={{0,2},{1,7},{2,0},{3,5},{4,6},{5,3},{6,4},{7,1},{8,10},{9,15},{10,... | collective-permute-start | bytes 1253384 | tf_op jit(solution)/shard_map/ppermute | solution.py:76
  56.1 16.2 %collective-permute-start.12 = (s16[272,768]{1,0:T(8,128)(2,1)S(1)}, s16[272,768]{1,0:T(8,128)(2,1)S(1)}, u32[]{:S(2)}, u32[]{:S(2)}) collective-permute-start(s16[272,768]{1,0:T(8,128)(2,1)S(1)} %grad_7.1), channel_id=1, source_target_pairs={{0,42},{1,127},{2,40},{3,125},{4,46},{5,123},{6,44},{7,121},{8,34}... | collective-permute-start | bytes 1253384 | tf_op jit(solution)/shard_map/ppermute | solution.py:76
  62.0 10.4 %collective-permute-start.14 = (s16[272,768]{1,0:T(8,128)(2,1)S(1)}, s16[272,768]{1,0:T(8,128)(2,1)S(1)}, u32[]{:S(2)}, u32[]{:S(2)}) collective-permute-start(s16[272,768]{1,0:T(8,128)(2,1)S(1)} %grad_1.1), channel_id=1, source_target_pairs={{0,2},{1,7},{2,0},{3,5},{4,6},{5,3},{6,4},{7,1},{8,10},{9,15},{10,... | collective-permute-start | bytes 1253384 | tf_op jit(solution)/shard_map/ppermute | solution.py:76
  63.5 9.9 %collective-permute-start.16 = (s16[272,768]{1,0:T(8,128)(2,1)S(1)}, s16[272,768]{1,0:T(8,128)(2,1)S(1)}, u32[]{:S(2)}, u32[]{:S(2)}) collective-permute-start(s16[272,768]{1,0:T(8,128)(2,1)S(1)} %grad_2.1), channel_id=1, source_target_pairs={{0,8},{1,25},{2,10},{3,27},{4,12},{5,29},{6,14},{7,31},{8,0},{9,17... | collective-permute-start | bytes 1253384 | tf_op jit(solution)/shard_map/ppermute | solution.py:76
  65.6 9.1 %collective-permute-start.18 = (s16[144,768]{1,0:T(8,128)(2,1)S(1)}, s16[144,768]{1,0:T(8,128)(2,1)S(1)}, u32[]{:S(2)}, u32[]{:S(2)}) collective-permute-start(s16[144,768]{1,0:T(8,128)(2,1)S(1)} %get-tuple-element.54), channel_id=1, source_target_pairs={{0,33},{1,96},{2,35},{3,98},{4,37},{5,100},{6,39},{7,102},{8,41},{... | collective-permute-start | bytes 663560 | tf_op jit(solution)/shard_map/ppermute | solution.py:547
  70.3 3.1 %copy-start = (bf16[128,768]{1,0:T(8,128)(2,1)S(1)}, bf16[128,768]{1,0:T(8,128)(2,1)}, u32[]{:S(2)}) copy-start(bf16[128,768]{1,0:T(8,128)(2,1)} %refs_0_.1) | copy-start | bytes 589828
  70.3 3.1 %copy-start.1 = (bf16[128,768]{1,0:T(8,128)(2,1)S(1)}, bf16[128,768]{1,0:T(8,128)(2,1)}, u32[]{:S(2)}) copy-start(bf16[128,768]{1,0:T(8,128)(2,1)} %refs_1_.1) | copy-start | bytes 589828
  70.3 6.6 %collective-permute-start.17 = (s16[144,768]{1,0:T(8,128)(2,1)S(1)}, s16[144,768]{1,0:T(8,128)(2,1)S(1)}, u32[]{:S(2)}, u32[]{:S(2)}) collective-permute-start(s16[144,768]{1,0:T(8,128)(2,1)S(1)} %get-tuple-element.48.refs_10_), channel_id=1, source_target_pairs={{0,32},{1,97},{2,34},{3,99},{4,36},{5,101},{6,38},{7,103},{8,40},{... | collective-permute-start | bytes 663560 | tf_op jit(solution)/shard_map/ppermute | solution.py:76
  74.0 2.9 %collective-permute-start.19 = (f32[48,768]{1,0:T(8,128)S(1)}, f32[48,768]{1,0:T(8,128)S(1)}, u32[]{:S(2)}, u32[]{:S(2)}) collective-permute-start(f32[48,768]{1,0:T(8,128)S(1)} %get-tuple-element.55), channel_id=1, source_target_pairs={{0,1},{1,0},{2,3},{3,2},{4,5},{5,4},{6,7},{7,6},{8,9},{9,8},{10,11... | collective-permute-start | bytes 442376 | tf_op jit(solution)/shard_map/ppermute | solution.py:80
  74.1 2.9 %collective-permute-start.20 = (f32[48,768]{1,0:T(8,128)S(1)}, f32[48,768]{1,0:T(8,128)S(1)}, u32[]{:S(2)}, u32[]{:S(2)}) collective-permute-start(f32[48,768]{1,0:T(8,128)S(1)} %get-tuple-element.56), channel_id=1, source_target_pairs={{0,1},{1,0},{2,3},{3,2},{4,5},{5,4},{6,7},{7,6},{8,9},{9,8},{10,11... | collective-permute-start | bytes 442376 | tf_op jit(solution)/shard_map/ppermute | solution.py:80
  74.6 2.4 %collective-permute-start.21 = (f32[40,768]{1,0:T(8,128)S(1)}, f32[40,768]{1,0:T(8,128)S(1)}, u32[]{:S(2)}, u32[]{:S(2)}) collective-permute-start(f32[40,768]{1,0:T(8,128)S(1)} %get-tuple-element.57), channel_id=1, source_target_pairs={{0,1},{1,0},{2,3},{3,2},{4,5},{5,4},{6,7},{7,6},{8,9},{9,8},{10,11... | collective-permute-start | bytes 368648 | tf_op jit(solution)/shard_map/ppermute | solution.py:80

commit v9 on v7

--- a/solution.py
+++ b/solution.py
@@ -23,7 +23,7 @@
 LOG2E = 1.4426950408889634
 FULL = 32760.0
 NEAR = (0, 4, 2, 1)
-FAR = (7, 5, 3, 6)
+FAR = (7, 5, 6, 3)
 PACKS = (NEAR, FAR[:2], FAR[2:])
 ALL = NEAR + FAR
 PARTS = (

time: 78.3 us -> 78.3 us (level)
  no operation moved by 1% of the time
where the time goes in v9:
time: 78.3 us; the launch traced here: 78.1 us
  starting transfers between devices  30.9 us (39%)
  Pallas kernels  22.6 us (29%)
  waiting for transfers between devices  16.2 us (21%)
  blocking collectives  7.54 us (10%)
  between operations  0.83 us (1%)
    ppermute x14, starting transfers between devices, send(): return lax.ppermute(value, 'dp', partners(bits))  23.8 us
    pallas_call x20, Pallas kernels, call(): pl.pallas_call(body, name=name, out_shape=out_shape, scratch_shapes=scrat...  21.4 us
    ppermute x14, waiting for transfers between devices, send(): return lax.ppermute(value, 'dp', partners(bits))  15.1 us
    all_to_all x1, blocking collectives, local(): lax.all_to_all(parts[-1][1], 'dp', 0, 0, axis_index_groups=SUM_GROUPS, ti...  7.54 us
    ppermute x1, starting transfers between devices, local(): cross = lax.ppermute(halves[1], 'dp', crossing(4))  4.68 us
    ppermute x7, starting transfers between devices, swap(): return lax.ppermute(value, 'dp', SWAP)  2.43 us
  transfers between devices with their start and end apart: 22, of which 7 were waited for; matrix products, arithmetic and copies ran while one was open for 0% of the time, Pallas kernels for 21%

profile of v9, /device:TPU:1, one launch (start us, length us, event | category | flops | bytes accessed | tf_op | source)
XLA Modules:
  0.0 78.1 jit_solution(9122516607701322193)
XLA Ops:
  0.6 1.2 %pre.1 = (bf16[144,768]{1,0:T(8,128)(2,1)S(1)}, bf16[144,768]{1,0:T(8,128)(2,1)S(1)}) custom-call(bf16[128,768]{1,0:T(8,128)(2,1)} %refs_0_.1, bf16[128,768]{1,0:T(8,128)(2,1)} %refs_1_.1, s32[1,128]{1,0:T(1,128)} %bitcast.2), custom_call_target="tpu_custom_call" | custom-call | tf_op jit(solution)/shard_map/pre/pallas_call | solution.py:446
  1.9 1.5 %collective-permute-start = (bf16[144,768]{1,0:T(8,128)(2,1)S(1)}, bf16[144,768]{1,0:T(8,128)(2,1)S(1)}, u32[]{:S(2)}, u32[]{:S(2)}) collective-permute-start(bf16[144,768]{1,0:T(8,128)(2,1)S(1)} %get-tuple-element.33), channel_id=1, source_target_pairs={{0,1},{1,0},{2,3},{3,2},{4,5},{5,4},{6,7},{7,6},{8,9},{9,8},{10,11... | collective-permute-start | bytes 663560 | tf_op jit(solution)/shard_map/ppermute | solution.py:80
  4.5 2.9 %collective-permute-start.3 = (bf16[272,768]{1,0:T(8,128)(2,1)S(1)}, bf16[272,768]{1,0:T(8,128)(2,1)S(1)}, u32[]{:S(2)}, u32[]{:S(2)}) collective-permute-start(bf16[272,768]{1,0:T(8,128)(2,1)S(1)} %join.1.refs_0_.refs_9_), channel_id=1, source_target_pairs={{0,2},{1,7},{2,0},{3,5},{4,6},{5,3},{6,4},{7,1},{8,10},{9,15},{10,... | collective-permute-start | bytes 1253384 | tf_op jit(solution)/shard_map/ppermute | solution.py:76
  7.4 3.8 %collective-permute-start.2 = (bf16[272,768]{1,0:T(8,128)(2,1)S(1)}, bf16[272,768]{1,0:T(8,128)(2,1)S(1)}, u32[]{:S(2)}, u32[]{:S(2)}) collective-permute-start(bf16[272,768]{1,0:T(8,128)(2,1)S(1)} %join.1.refs_0_.refs_9_), channel_id=1, source_target_pairs={{0,8},{1,25},{2,10},{3,27},{4,12},{5,29},{6,14},{7,31},{8,0},{9,17... | collective-permute-start | bytes 1253384 | tf_op jit(solution)/shard_map/ppermute | solution.py:76
  11.2 2.5 %collective-permute-start.1 = (bf16[272,768]{1,0:T(8,128)(2,1)S(1)}, bf16[272,768]{1,0:T(8,128)(2,1)S(1)}, u32[]{:S(2)}, u32[]{:S(2)}) collective-permute-start(bf16[272,768]{1,0:T(8,128)(2,1)S(1)} %join.1.refs_0_.refs_9_), channel_id=1, source_target_pairs={{0,32},{1,97},{2,34},{3,99},{4,36},{5,101},{6,38},{7,103},{8,40},{... | collective-permute-start | bytes 1253384 | tf_op jit(solution)/shard_map/ppermute | solution.py:76
  13.7 2.9 %collective-permute-done.2.refs_2_.refs_9_ = bf16[272,768]{1,0:T(8,128)(2,1)S(1)} collective-permute-done((bf16[272,768]{1,0:T(8,128)(2,1)S(1)}, bf16[272,768]{1,0:T(8,128)(2,1)S(1)}, u32[]{:S(2)}, u32[]{:S(2)}) %collective-permute-start.2) | collective-permute-done | bytes 417824 | tf_op jit(solution)/shard_map/ppermute | solution.py:76
  16.6 2.7 %collective-permute-done.1.refs_1_.refs_9_ = bf16[272,768]{1,0:T(8,128)(2,1)S(1)} collective-permute-done((bf16[272,768]{1,0:T(8,128)(2,1)S(1)}, bf16[272,768]{1,0:T(8,128)(2,1)S(1)}, u32[]{:S(2)}, u32[]{:S(2)}) %collective-permute-start.1) | collective-permute-done | bytes 417824 | tf_op jit(solution)/shard_map/ppermute | solution.py:76
  19.5 2.3 %collective-permute-start.5 = (bf16[272,768]{1,0:T(8,128)(2,1)S(1)}, bf16[272,768]{1,0:T(8,128)(2,1)S(1)}, u32[]{:S(2)}, u32[]{:S(2)}) collective-permute-start(bf16[272,768]{1,0:T(8,128)(2,1)S(1)} %collective-permute-done.3.refs_3_.refs_9_), channel_id=1, source_target_pairs={{0,40},{1,121},{2,42},{3,123},{4,44},{5,125},{6,46},{7,127},{8,32}... | collective-permute-start | bytes 1253384 | tf_op jit(solution)/shard_map/ppermute | solution.py:76
  21.8 1.4 %collective-permute-start.6 = (bf16[272,768]{1,0:T(8,128)(2,1)S(1)}, bf16[272,768]{1,0:T(8,128)(2,1)S(1)}, u32[]{:S(2)}, u32[]{:S(2)}) collective-permute-start(bf16[272,768]{1,0:T(8,128)(2,1)S(1)} %collective-permute-done.1.refs_1_.refs_9_), channel_id=1, source_target_pairs={{0,2},{1,7},{2,0},{3,5},{4,6},{5,3},{6,4},{7,1},{8,10},{9,15},{10,... | collective-permute-start | bytes 1253384 | tf_op jit(solution)/shard_map/ppermute | solution.py:76
  23.1 1.4 %collective-permute-start.9 = (bf16[272,768]{1,0:T(8,128)(2,1)S(1)}, bf16[272,768]{1,0:T(8,128)(2,1)S(1)}, u32[]{:S(2)}, u32[]{:S(2)}) collective-permute-start(bf16[272,768]{1,0:T(8,128)(2,1)S(1)} %collective-permute-done.3.refs_3_.refs_9_), channel_id=1, source_target_pairs={{0,8},{1,25},{2,10},{3,27},{4,12},{5,29},{6,14},{7,31},{8,0},{9,17... | collective-permute-start | bytes 1253384 | tf_op jit(solution)/shard_map/ppermute | solution.py:76
  24.7 2.0 %tile_0.1 = (f32[1024,1024]{1,0:T(8,128)S(1)}, f32[1024,128]{1,0:T(8,128)S(1)}, f32[16,1024]{1,0:T(8,128)S(1)}) custom-call(bf16[272,768]{1,0:T(8,128)(2,1)S(1)} %join.1.refs_0_.refs_9_, bf16[272,768]{1,0:T(8,128)(2,1)S(1)} %collective-permute-done.1.refs_1_.refs_9_, bf16[272,768]{1,0:T(8,128)(2,1)S(1)} %collective-permute-done.2.refs_2_.refs_9_, ...), custom_call_target="tpu_custom_call" | custom-call | tf_op jit(solution)/shard_map/tile_0/pallas_call | solution.py:93
  26.7 3.1 %collective-permute-done.5.refs_0_.refs_4_.refs_9_ = bf16[272,768]{1,0:T(8,128)(2,1)S(1)} collective-permute-done((bf16[272,768]{1,0:T(8,128)(2,1)S(1)}, bf16[272,768]{1,0:T(8,128)(2,1)S(1)}, u32[]{:S(2)}, u32[]{:S(2)}) %collective-permute-start.5) | collective-permute-done | bytes 417824 | tf_op jit(solution)/shard_map/ppermute | solution.py:76
  30.0 1.1 %tile_1.1 = (f32[512,1024]{1,0:T(8,128)S(1)}, f32[512,128]{1,0:T(8,128)S(1)}, f32[16,1024]{1,0:T(8,128)S(1)}) custom-call(bf16[272,768]{1,0:T(8,128)(2,1)S(1)} %collective-permute-done.5.refs_0_.refs_4_.refs_9_, bf16[272,768]{1,0:T(8,128)(2,1)S(1)} %collective-permute-done.6.refs_1_.refs_5_.refs_9_, ...), custom_call_target="tpu_custom_call" | custom-call | tf_op jit(solution)/shard_map/tile_1/pallas_call | solution.py:93
  31.2 3.1 %collective-permute-done.9.refs_1_.refs_7_.refs_9_ = bf16[272,768]{1,0:T(8,128)(2,1)S(1)} collective-permute-done((bf16[272,768]{1,0:T(8,128)(2,1)S(1)}, bf16[272,768]{1,0:T(8,128)(2,1)S(1)}, u32[]{:S(2)}, u32[]{:S(2)}) %collective-permute-start.9) | collective-permute-done | bytes 417824 | tf_op jit(solution)/shard_map/ppermute | solution.py:76
  34.4 1.5 %tile_2.1 = (f32[1536,512]{1,0:T(8,128)S(1)}, f32[1536,128]{1,0:T(8,128)S(1)}, f32[16,512]{1,0:T(8,128)S(1)}) custom-call(bf16[272,768]{1,0:T(8,128)(2,1)S(1)} %join.1.refs_0_.refs_9_, bf16[272,768]{1,0:T(8,128)(2,1)S(1)} %collective-permute-done.1.refs_1_.refs_9_, bf16[272,768]{1,0:T(8,128)(2,1)S(1)} %collective-permute-done.2.refs_2_.refs_9_, ...), custom_call_target="tpu_custom_call" | custom-call | tf_op jit(solution)/shard_map/tile_2/pallas_call | solution.py:93
  36.0 1.6 %tile_3.1 = (f32[512,1536]{1,0:T(8,128)S(1)}, f32[512,128]{1,0:T(8,128)S(1)}, f32[16,1536]{1,0:T(8,128)S(1)}) custom-call(bf16[272,768]{1,0:T(8,128)(2,1)S(1)} %collective-permute-done.8.refs_0_.refs_6_.refs_9_, bf16[272,768]{1,0:T(8,128)(2,1)S(1)} %collective-permute-done.9.refs_1_.refs_7_.refs_9_, ...), custom_call_target="tpu_custom_call" | custom-call | tf_op jit(solution)/shard_map/tile_3/pallas_call | solution.py:93
  37.6 2.0 %tile_4.1 = (f32[2048,512]{1,0:T(8,128)S(1)}, f32[8,32,128]{2,1,0:T(8,128)S(1)}) custom-call(bf16[272,768]{1,0:T(8,128)(2,1)S(1)} %join.1.refs_0_.refs_9_, bf16[272,768]{1,0:T(8,128)(2,1)S(1)} %collective-permute-done.1.refs_1_.refs_9_, bf16[272,768]{1,0:T(8,128)(2,1)S(1)} %collective-permute-done.2.refs_2_.refs_9_, ...), custom_call_target="tpu_custom_call" | custom-call | tf_op jit(solution)/shard_map/tile_4/pallas_call | solution.py:93
  39.6 7.5 %all_to_all.5.refs_0_ = f32[8,32,128]{2,1,0:T(8,128)S(1)} all-to-all(f32[8,32,128]{2,1,0:T(8,128)S(1)} %get-tuple-element.47), channel_id=1, replica_groups={{0,2,8,10,32,34,40,42},{4,6,12,14,36,38,44,46},{16,18,24,26,48,50,56,58..., dimensions={0} | all-to-all | bytes 262144 | tf_op jit(solution)/shard_map/all_to_all | solution.py:503
  47.3 1.4 %grad_3.1 = s16[272,768]{1,0:T(8,128)(2,1)S(1)} custom-call(f32[1024,1024]{1,0:T(8,128)S(1)} %get-tuple-element.34.refs_0_, f32[512,1024]{1,0:T(8,128)S(1)} %get-tuple-element.36.refs_1_, f32[1536,512]{1,0:T(8,128)S(1)} %get-tuple-element.38.refs_2_, f32[512,1536]{1,0:T(8,128)S(1)} %get-tuple-element.40.refs_3_, f32[2048,512]{1,0:T(8,128)S(1)} %get-tuple-element.46.refs_4_, ...), custom_call_target="tpu_custom_call" | custom-call | tf_op jit(solution)/shard_map/grad_3/pallas_call | solution.py:93
  48.8 1.4 %grad_6.1 = s16[272,768]{1,0:T(8,128)(2,1)S(1)} custom-call(f32[1024,1024]{1,0:T(8,128)S(1)} %get-tuple-element.34.refs_0_, f32[512,1024]{1,0:T(8,128)S(1)} %get-tuple-element.36.refs_1_, f32[1536,512]{1,0:T(8,128)S(1)} %get-tuple-element.38.refs_2_, f32[512,1536]{1,0:T(8,128)S(1)} %get-tuple-element.40.refs_3_, f32[2048,512]{1,0:T(8,128)S(1)} %get-tuple-element.46.refs_4_, ...), custom_call_target="tpu_custom_call" | custom-call | tf_op jit(solution)/shard_map/grad_6/pallas_call | solution.py:93
  50.2 1.8 %collective-permute-start.15 = (s16[272,768]{1,0:T(8,128)(2,1)S(1)}, s16[272,768]{1,0:T(8,128)(2,1)S(1)}, u32[]{:S(2)}, u32[]{:S(2)}) collective-permute-start(s16[272,768]{1,0:T(8,128)(2,1)S(1)} %grad_6.1), channel_id=1, source_target_pairs={{0,32},{1,97},{2,34},{3,99},{4,36},{5,101},{6,38},{7,103},{8,40},{... | collective-permute-start | bytes 1253384 | tf_op jit(solution)/shard_map/ppermute | solution.py:76
  52.0 1.4 %grad_5.1.refs_10_ = s16[272,768]{1,0:T(8,128)(2,1)S(1)} custom-call(f32[1024,1024]{1,0:T(8,128)S(1)} %get-tuple-element.34.refs_0_, f32[512,1024]{1,0:T(8,128)S(1)} %get-tuple-element.36.refs_1_, f32[1536,512]{1,0:T(8,128)S(1)} %get-tuple-element.38.refs_2_, f32[512,1536]{1,0:T(8,128)S(1)} %get-tuple-element.40.refs_3_, ...), custom_call_target="tpu_custom_call" | custom-call | tf_op jit(solution)/shard_map/grad_5/pallas_call | solution.py:93
  53.4 1.4 %collective-permute-start.11 = (s16[272,768]{1,0:T(8,128)(2,1)S(1)}, s16[272,768]{1,0:T(8,128)(2,1)S(1)}, u32[]{:S(2)}, u32[]{:S(2)}) collective-permute-start(s16[272,768]{1,0:T(8,128)(2,1)S(1)} %grad_5.1.refs_10_), channel_id=1, source_target_pairs={{0,2},{1,7},{2,0},{3,5},{4,6},{5,3},{6,4},{7,1},{8,10},{9,15},{10,... | collective-permute-start | bytes 1253384 | tf_op jit(solution)/shard_map/ppermute | solution.py:76
  54.8 1.4 %grad_7.1 = s16[272,768]{1,0:T(8,128)(2,1)S(1)} custom-call(f32[1024,1024]{1,0:T(8,128)S(1)} %get-tuple-element.34.refs_0_, f32[512,1024]{1,0:T(8,128)S(1)} %get-tuple-element.36.refs_1_, f32[1536,512]{1,0:T(8,128)S(1)} %get-tuple-element.38.refs_2_, f32[512,1536]{1,0:T(8,128)S(1)} %get-tuple-element.40.refs_3_, f32[2048,512]{1,0:T(8,128)S(1)} %get-tuple-element.46.refs_4_, ...), custom_call_target="tpu_custom_call" | custom-call | tf_op jit(solution)/shard_map/grad_7/pallas_call | solution.py:93
  56.1 4.5 %collective-permute-start.12 = (s16[272,768]{1,0:T(8,128)(2,1)S(1)}, s16[272,768]{1,0:T(8,128)(2,1)S(1)}, u32[]{:S(2)}, u32[]{:S(2)}) collective-permute-start(s16[272,768]{1,0:T(8,128)(2,1)S(1)} %grad_7.1), channel_id=1, source_target_pairs={{0,42},{1,127},{2,40},{3,125},{4,46},{5,123},{6,44},{7,121},{8,34}... | collective-permute-start | bytes 1253384 | tf_op jit(solution)/shard_map/ppermute | solution.py:76
  60.6 1.4 %grad_1.1 = s16[272,768]{1,0:T(8,128)(2,1)S(1)} custom-call(f32[1024,1024]{1,0:T(8,128)S(1)} %get-tuple-element.34.refs_0_, f32[512,1024]{1,0:T(8,128)S(1)} %get-tuple-element.36.refs_1_, f32[1536,512]{1,0:T(8,128)S(1)} %get-tuple-element.38.refs_2_, f32[512,1536]{1,0:T(8,128)S(1)} %get-tuple-element.40.refs_3_, f32[2048,512]{1,0:T(8,128)S(1)} %get-tuple-element.46.refs_4_, ...), custom_call_target="tpu_custom_call" | custom-call | tf_op jit(solution)/shard_map/grad_1/pallas_call | solution.py:93
  62.1 1.4 %grad_2.1 = s16[272,768]{1,0:T(8,128)(2,1)S(1)} custom-call(f32[1024,1024]{1,0:T(8,128)S(1)} %get-tuple-element.34.refs_0_, f32[512,1024]{1,0:T(8,128)S(1)} %get-tuple-element.36.refs_1_, f32[1536,512]{1,0:T(8,128)S(1)} %get-tuple-element.38.refs_2_, f32[512,1536]{1,0:T(8,128)S(1)} %get-tuple-element.40.refs_3_, f32[2048,512]{1,0:T(8,128)S(1)} %get-tuple-element.46.refs_4_, ...), custom_call_target="tpu_custom_call" | custom-call | tf_op jit(solution)/shard_map/grad_2/pallas_call | solution.py:93
  64.2 1.4 %grad_4.1 = (s16[144,768]{1,0:T(8,128)(2,1)S(1)}, s16[144,768]{1,0:T(8,128)(2,1)S(1)}) custom-call(f32[1024,1024]{1,0:T(8,128)S(1)} %get-tuple-element.34.refs_0_, f32[512,1024]{1,0:T(8,128)S(1)} %get-tuple-element.36.refs_1_, f32[1536,512]{1,0:T(8,128)S(1)} %get-tuple-element.38.refs_2_, f32[512,1536]{1,0:T(8,128)S(1)} %get-tuple-element.40.refs_3_, ...), custom_call_target="tpu_custom_call" | custom-call | tf_op jit(solution)/shard_map/grad_4/pallas_call | solution.py:93
  65.6 4.7 %collective-permute-start.18 = (s16[144,768]{1,0:T(8,128)(2,1)S(1)}, s16[144,768]{1,0:T(8,128)(2,1)S(1)}, u32[]{:S(2)}, u32[]{:S(2)}) collective-permute-start(s16[144,768]{1,0:T(8,128)(2,1)S(1)} %get-tuple-element.54), channel_id=1, source_target_pairs={{0,33},{1,96},{2,35},{3,98},{4,37},{5,100},{6,39},{7,102},{8,41},{... | collective-permute-start | bytes 663560 | tf_op jit(solution)/shard_map/ppermute | solution.py:540
  71.2 1.1 %grad_0.1.refs_2_ = f32[264,768]{1,0:T(8,128)S(1)} custom-call(f32[1024,1024]{1,0:T(8,128)S(1)} %get-tuple-element.34.refs_0_, f32[512,1024]{1,0:T(8,128)S(1)} %get-tuple-element.36.refs_1_, f32[1536,512]{1,0:T(8,128)S(1)} %get-tuple-element.38.refs_2_, f32[512,1536]{1,0:T(8,128)S(1)} %get-tuple-element.40.refs_3_, ...), custom_call_target="tpu_custom_call" | custom-call | tf_op jit(solution)/shard_map/grad_0/pallas_call | solution.py:93
  74.7 2.3 %collective-permute-done.17.refs_5_ = s16[144,768]{1,0:T(8,128)(2,1)S(1)} collective-permute-done((s16[144,768]{1,0:T(8,128)(2,1)S(1)}, s16[144,768]{1,0:T(8,128)(2,1)S(1)}, u32[]{:S(2)}, u32[]{:S(2)}) %collective-permute-start.17) | collective-permute-done | bytes 221216 | tf_op jit(solution)/shard_map/ppermute | solution.py:76
  76.9 1.2 %post.1 = (f32[1,1]{1,0:T(1,128)}, f32[128,768]{1,0:T(8,128)}, f32[128,768]{1,0:T(8,128)}) custom-call(f32[128,768]{1,0:T(8,128)S(1)} %get-tuple-element.49.refs_0_, f32[128,128]{1,0:T(8,128)S(1)} %get-tuple-element.50.refs_1_, f32[128,768]{1,0:T(8,128)S(1)} %get-tuple-element.51.refs_2_, f32[128,128]{1,0:T(8,128)S(1)} %get-tuple-element.52.refs_3_, ...), custom_call_target="tpu_custom_call" | custom-call | tf_op jit(solution)/shard_map/post/pallas_call | solution.py:93
  (38 shorter events, 6.0 us)
Async XLA Ops:
  1.9 2.6 %collective-permute-start = (bf16[144,768]{1,0:T(8,128)(2,1)S(1)}, bf16[144,768]{1,0:T(8,128)(2,1)S(1)}, u32[]{:S(2)}, u32[]{:S(2)}) collective-permute-start(bf16[144,768]{1,0:T(8,128)(2,1)S(1)} %get-tuple-element.33), channel_id=1, source_target_pairs={{0,1},{1,0},{2,3},{3,2},{4,5},{5,4},{6,7},{7,6},{8,9},{9,8},{10,11... | collective-permute-start | bytes 663560 | tf_op jit(solution)/shard_map/ppermute | solution.py:80
  4.5 9.1 %collective-permute-start.3 = (bf16[272,768]{1,0:T(8,128)(2,1)S(1)}, bf16[272,768]{1,0:T(8,128)(2,1)S(1)}, u32[]{:S(2)}, u32[]{:S(2)}) collective-permute-start(bf16[272,768]{1,0:T(8,128)(2,1)S(1)} %join.1.refs_0_.refs_9_), channel_id=1, source_target_pairs={{0,2},{1,7},{2,0},{3,5},{4,6},{5,3},{6,4},{7,1},{8,10},{9,15},{10,... | collective-permute-start | bytes 1253384 | tf_op jit(solution)/shard_map/ppermute | solution.py:76
  7.4 9.2 %collective-permute-start.2 = (bf16[272,768]{1,0:T(8,128)(2,1)S(1)}, bf16[272,768]{1,0:T(8,128)(2,1)S(1)}, u32[]{:S(2)}, u32[]{:S(2)}) collective-permute-start(bf16[272,768]{1,0:T(8,128)(2,1)S(1)} %join.1.refs_0_.refs_9_), channel_id=1, source_target_pairs={{0,8},{1,25},{2,10},{3,27},{4,12},{5,29},{6,14},{7,31},{8,0},{9,17... | collective-permute-start | bytes 1253384 | tf_op jit(solution)/shard_map/ppermute | solution.py:76
  11.2 8.1 %collective-permute-start.1 = (bf16[272,768]{1,0:T(8,128)(2,1)S(1)}, bf16[272,768]{1,0:T(8,128)(2,1)S(1)}, u32[]{:S(2)}, u32[]{:S(2)}) collective-permute-start(bf16[272,768]{1,0:T(8,128)(2,1)S(1)} %join.1.refs_0_.refs_9_), channel_id=1, source_target_pairs={{0,32},{1,97},{2,34},{3,99},{4,36},{5,101},{6,38},{7,103},{8,40},{... | collective-permute-start | bytes 1253384 | tf_op jit(solution)/shard_map/ppermute | solution.py:76
  19.4 5.3 %collective-permute-start.4 = (bf16[1088,768]{1,0:T(8,128)(2,1)S(1)}, bf16[1088,768]{1,0:T(8,128)(2,1)S(1)}, u32[]{:S(2)}, u32[]{:S(2)}) collective-permute-start(bf16[1088,768]{1,0:T(8,128)(2,1)S(1)} %pack_near.1), channel_id=1, source_target_pairs={{0,1},{1,0},{2,3},{3,2},{4,5},{5,4},{6,7},{7,6},{8,9},{9,8},{10,11... | collective-permute-start | bytes 5013512 | tf_op jit(solution)/shard_map/ppermute | solution.py:80
  19.5 10.4 %collective-permute-start.5 = (bf16[272,768]{1,0:T(8,128)(2,1)S(1)}, bf16[272,768]{1,0:T(8,128)(2,1)S(1)}, u32[]{:S(2)}, u32[]{:S(2)}) collective-permute-start(bf16[272,768]{1,0:T(8,128)(2,1)S(1)} %collective-permute-done.3.refs_3_.refs_9_), channel_id=1, source_target_pairs={{0,40},{1,121},{2,42},{3,123},{4,44},{5,125},{6,46},{7,127},{8,32}... | collective-permute-start | bytes 1253384 | tf_op jit(solution)/shard_map/ppermute | solution.py:76
  21.8 8.1 %collective-permute-start.6 = (bf16[272,768]{1,0:T(8,128)(2,1)S(1)}, bf16[272,768]{1,0:T(8,128)(2,1)S(1)}, u32[]{:S(2)}, u32[]{:S(2)}) collective-permute-start(bf16[272,768]{1,0:T(8,128)(2,1)S(1)} %collective-permute-done.1.refs_1_.refs_9_), channel_id=1, source_target_pairs={{0,2},{1,7},{2,0},{3,5},{4,6},{5,3},{6,4},{7,1},{8,10},{9,15},{10,... | collective-permute-start | bytes 1253384 | tf_op jit(solution)/shard_map/ppermute | solution.py:76
  23.1 11.1 %collective-permute-start.9 = (bf16[272,768]{1,0:T(8,128)(2,1)S(1)}, bf16[272,768]{1,0:T(8,128)(2,1)S(1)}, u32[]{:S(2)}, u32[]{:S(2)}) collective-permute-start(bf16[272,768]{1,0:T(8,128)(2,1)S(1)} %collective-permute-done.3.refs_3_.refs_9_), channel_id=1, source_target_pairs={{0,8},{1,25},{2,10},{3,27},{4,12},{5,29},{6,14},{7,31},{8,0},{9,17... | collective-permute-start | bytes 1253384 | tf_op jit(solution)/shard_map/ppermute | solution.py:76
  24.5 9.7 %collective-permute-start.8 = (bf16[272,768]{1,0:T(8,128)(2,1)S(1)}, bf16[272,768]{1,0:T(8,128)(2,1)S(1)}, u32[]{:S(2)}, u32[]{:S(2)}) collective-permute-start(bf16[272,768]{1,0:T(8,128)(2,1)S(1)} %collective-permute-done.2.refs_2_.refs_9_), channel_id=1, source_target_pairs={{0,32},{1,97},{2,34},{3,99},{4,36},{5,101},{6,38},{7,103},{8,40},{... | collective-permute-start | bytes 1253384 | tf_op jit(solution)/shard_map/ppermute | solution.py:76
  29.9 4.5 %collective-permute-start.7 = (bf16[544,768]{1,0:T(8,128)(2,1)S(1)}, bf16[544,768]{1,0:T(8,128)(2,1)S(1)}, u32[]{:S(2)}, u32[]{:S(2)}) collective-permute-start(bf16[544,768]{1,0:T(8,128)(2,1)S(1)} %pack_first.1), channel_id=1, source_target_pairs={{0,1},{1,0},{2,3},{3,2},{4,5},{5,4},{6,7},{7,6},{8,9},{9,8},{10,11... | collective-permute-start | bytes 2506760 | tf_op jit(solution)/shard_map/ppermute | solution.py:80
  34.3 3.3 %collective-permute-start.10 = (bf16[544,768]{1,0:T(8,128)(2,1)S(1)}, bf16[544,768]{1,0:T(8,128)(2,1)S(1)}, u32[]{:S(2)}, u32[]{:S(2)}) collective-permute-start(bf16[544,768]{1,0:T(8,128)(2,1)S(1)} %pack_second.1), channel_id=1, source_target_pairs={{0,1},{1,0},{2,3},{3,2},{4,5},{5,4},{6,7},{7,6},{8,9},{9,8},{10,11... | collective-permute-start | bytes 2506760 | tf_op jit(solution)/shard_map/ppermute | solution.py:80
  48.7 11.9 %collective-permute-start.13 = (s16[272,768]{1,0:T(8,128)(2,1)S(1)}, s16[272,768]{1,0:T(8,128)(2,1)S(1)}, u32[]{:S(2)}, u32[]{:S(2)}) collective-permute-start(s16[272,768]{1,0:T(8,128)(2,1)S(1)} %grad_3.1), channel_id=1, source_target_pairs={{0,8},{1,25},{2,10},{3,27},{4,12},{5,29},{6,14},{7,31},{8,0},{9,17... | collective-permute-start | bytes 1253384 | tf_op jit(solution)/shard_map/ppermute | solution.py:76
  50.2 11.9 %collective-permute-start.15 = (s16[272,768]{1,0:T(8,128)(2,1)S(1)}, s16[272,768]{1,0:T(8,128)(2,1)S(1)}, u32[]{:S(2)}, u32[]{:S(2)}) collective-permute-start(s16[272,768]{1,0:T(8,128)(2,1)S(1)} %grad_6.1), channel_id=1, source_target_pairs={{0,32},{1,97},{2,34},{3,99},{4,36},{5,101},{6,38},{7,103},{8,40},{... | collective-permute-start | bytes 1253384 | tf_op jit(solution)/shard_map/ppermute | solution.py:76
  53.4 10.8 %collective-permute-start.11 = (s16[272,768]{1,0:T(8,128)(2,1)S(1)}, s16[272,768]{1,0:T(8,128)(2,1)S(1)}, u32[]{:S(2)}, u32[]{:S(2)}) collective-permute-start(s16[272,768]{1,0:T(8,128)(2,1)S(1)} %grad_5.1.refs_10_), channel_id=1, source_target_pairs={{0,2},{1,7},{2,0},{3,5},{4,6},{5,3},{6,4},{7,1},{8,10},{9,15},{10,... | collective-permute-start | bytes 1253384 | tf_op jit(solution)/shard_map/ppermute | solution.py:76
  56.1 16.2 %collective-permute-start.12 = (s16[272,768]{1,0:T(8,128)(2,1)S(1)}, s16[272,768]{1,0:T(8,128)(2,1)S(1)}, u32[]{:S(2)}, u32[]{:S(2)}) collective-permute-start(s16[272,768]{1,0:T(8,128)(2,1)S(1)} %grad_7.1), channel_id=1, source_target_pairs={{0,42},{1,127},{2,40},{3,125},{4,46},{5,123},{6,44},{7,121},{8,34}... | collective-permute-start | bytes 1253384 | tf_op jit(solution)/shard_map/ppermute | solution.py:76
  62.0 10.4 %collective-permute-start.14 = (s16[272,768]{1,0:T(8,128)(2,1)S(1)}, s16[272,768]{1,0:T(8,128)(2,1)S(1)}, u32[]{:S(2)}, u32[]{:S(2)}) collective-permute-start(s16[272,768]{1,0:T(8,128)(2,1)S(1)} %grad_1.1), channel_id=1, source_target_pairs={{0,2},{1,7},{2,0},{3,5},{4,6},{5,3},{6,4},{7,1},{8,10},{9,15},{10,... | collective-permute-start | bytes 1253384 | tf_op jit(solution)/shard_map/ppermute | solution.py:76
  63.5 9.9 %collective-permute-start.16 = (s16[272,768]{1,0:T(8,128)(2,1)S(1)}, s16[272,768]{1,0:T(8,128)(2,1)S(1)}, u32[]{:S(2)}, u32[]{:S(2)}) collective-permute-start(s16[272,768]{1,0:T(8,128)(2,1)S(1)} %grad_2.1), channel_id=1, source_target_pairs={{0,8},{1,25},{2,10},{3,27},{4,12},{5,29},{6,14},{7,31},{8,0},{9,17... | collective-permute-start | bytes 1253384 | tf_op jit(solution)/shard_map/ppermute | solution.py:76
  65.6 9.0 %collective-permute-start.18 = (s16[144,768]{1,0:T(8,128)(2,1)S(1)}, s16[144,768]{1,0:T(8,128)(2,1)S(1)}, u32[]{:S(2)}, u32[]{:S(2)}) collective-permute-start(s16[144,768]{1,0:T(8,128)(2,1)S(1)} %get-tuple-element.54), channel_id=1, source_target_pairs={{0,33},{1,96},{2,35},{3,98},{4,37},{5,100},{6,39},{7,102},{8,41},{... | collective-permute-start | bytes 663560 | tf_op jit(solution)/shard_map/ppermute | solution.py:540
  70.3 3.1 %copy-start = (bf16[128,768]{1,0:T(8,128)(2,1)S(1)}, bf16[128,768]{1,0:T(8,128)(2,1)}, u32[]{:S(2)}) copy-start(bf16[128,768]{1,0:T(8,128)(2,1)} %refs_0_.1) | copy-start | bytes 589828
  70.3 3.1 %copy-start.1 = (bf16[128,768]{1,0:T(8,128)(2,1)S(1)}, bf16[128,768]{1,0:T(8,128)(2,1)}, u32[]{:S(2)}) copy-start(bf16[128,768]{1,0:T(8,128)(2,1)} %refs_1_.1) | copy-start | bytes 589828
  70.3 6.6 %collective-permute-start.17 = (s16[144,768]{1,0:T(8,128)(2,1)S(1)}, s16[144,768]{1,0:T(8,128)(2,1)S(1)}, u32[]{:S(2)}, u32[]{:S(2)}) collective-permute-start(s16[144,768]{1,0:T(8,128)(2,1)S(1)} %get-tuple-element.48.refs_10_), channel_id=1, source_target_pairs={{0,32},{1,97},{2,34},{3,99},{4,36},{5,101},{6,38},{7,103},{8,40},{... | collective-permute-start | bytes 663560 | tf_op jit(solution)/shard_map/ppermute | solution.py:76
  74.0 2.9 %collective-permute-start.19 = (f32[48,768]{1,0:T(8,128)S(1)}, f32[48,768]{1,0:T(8,128)S(1)}, u32[]{:S(2)}, u32[]{:S(2)}) collective-permute-start(f32[48,768]{1,0:T(8,128)S(1)} %get-tuple-element.55), channel_id=1, source_target_pairs={{0,1},{1,0},{2,3},{3,2},{4,5},{5,4},{6,7},{7,6},{8,9},{9,8},{10,11... | collective-permute-start | bytes 442376 | tf_op jit(solution)/shard_map/ppermute | solution.py:80
  74.1 2.9 %collective-permute-start.20 = (f32[48,768]{1,0:T(8,128)S(1)}, f32[48,768]{1,0:T(8,128)S(1)}, u32[]{:S(2)}, u32[]{:S(2)}) collective-permute-start(f32[48,768]{1,0:T(8,128)S(1)} %get-tuple-element.56), channel_id=1, source_target_pairs={{0,1},{1,0},{2,3},{3,2},{4,5},{5,4},{6,7},{7,6},{8,9},{9,8},{10,11... | collective-permute-start | bytes 442376 | tf_op jit(solution)/shard_map/ppermute | solution.py:80
  74.6 2.4 %collective-permute-start.21 = (f32[40,768]{1,0:T(8,128)S(1)}, f32[40,768]{1,0:T(8,128)S(1)}, u32[]{:S(2)}, u32[]{:S(2)}) collective-permute-start(f32[40,768]{1,0:T(8,128)S(1)} %get-tuple-element.57), channel_id=1, source_target_pairs={{0,1},{1,0},{2,3},{3,2},{4,5},{5,4},{6,7},{7,6},{8,9},{9,8},{10,11... | collective-permute-start | bytes 368648 | tf_op jit(solution)/shard_map/ppermute | solution.py:80
